TPU v7x, 32 devices: a whole 2x2x4 slice. The times are simulated.
32 devices in a mesh: dp: 4 (over y, x), expert: 8 (over z, core).
Axes of the slice: x: 2, y: 2, z: 4, core: 2. Of those that a mesh axis runs over, the one named last changes fastest.
Arguments:
- cell_table: bfloat16 [65536, 256], P(('dp', 'expert')), may hold values from -6 to 6
- sample_index: int32 [32768], P(('dp', 'expert')), may hold values from 0 to 2047
- region: int32 [32768, 1], P(('dp', 'expert')), may hold values from 0 to 7; in each aligned block of 1024 rows (0 to 1023, 1024 to 2047, ...) at most 256 rows name the same one
- targets: bfloat16 [32768, 256], P(('dp', 'expert')), may hold values from -6 to 6
- trunk_weight: bfloat16 [256, 256], replicated, may hold values from -0.375 to 0.375
- expert_params: float32 [8, 2, 256, 2048], P('expert', None, None, 'dp'), may hold values from -0.375 to 0.375
- first_moment: float32 [8, 2, 256, 2048], P('expert', None, None, 'dp'), may hold values from -4 to 4
- second_moment: float32 [8, 2, 256, 2048], P('expert', None, None, 'dp'), may hold values from 0.05 to 1
Outputs:
- trunk_grad: float32 [256, 256], replicated
- row_loss: float32 [32768], P(('dp', 'expert'))
- new_params: float32 [8, 2, 256, 2048], P('expert', None, None, 'dp')
- new_first: float32 [8, 2, 256, 2048], P('expert', None, None, 'dp')
- new_second: float32 [8, 2, 256, 2048], P('expert', None, None, 'dp')
Inputs may be any that keep to these rules, and one draw needn't show every extreme that they name: In the 1024 rows of one device no region is named more than 256 times; some region exactly 256 times. `sample_index`: indexes the rows of the same device's block of cell_table.
All inputs are finite; a program needn't handle non-finite values.
Results may differ from a plain program's by a relative error of at most 0.0044.
Values may be sent and summed in bfloat16 or wider, within the bound.
No kernel may reach another device: no remote copies, remote signals or barrier semaphores. Data moves between devices by JAX's collectives and lax.ppermute only.
A program may use at most 128 MiB of HBM per device.

v0:
```python
import jax
import jax.numpy as jnp
from jax import lax
from jax.sharding import PartitionSpec as P

loss_scale = 1.0 / 32.0
beta_one = 0.9
beta_two = 0.999
learn_rate = 0.05
adam_eps = 1e-08
adam_step = 10


def silu_slope(values):
    sigma = jax.nn.sigmoid(values)
    return sigma * (1.0 + values * (1.0 - sigma))


def expert_forward(arrived, w_up, w_down):
    up_pre = jnp.dot(arrived, w_up, preferred_element_type=jnp.float32)
    hidden = jax.nn.silu(up_pre).astype(jnp.bfloat16)
    predicted = lax.dot_general(
        hidden, w_down, (((1,), (1,)), ((), ())), preferred_element_type=jnp.float32
    )
    return (up_pre, hidden, predicted)


def expert_backward(arrived, up_pre, hidden, scaled_error, w_up, w_down):
    grad_down = lax.dot_general(
        scaled_error, hidden, (((0,), (0,)), ((), ())), preferred_element_type=jnp.float32
    )
    hidden_grad = jnp.dot(scaled_error, w_down, preferred_element_type=jnp.float32)
    pre_grad = (hidden_grad * silu_slope(up_pre)).astype(jnp.bfloat16)
    grad_up = lax.dot_general(
        arrived, pre_grad, (((0,), (0,)), ((), ())), preferred_element_type=jnp.float32
    )
    input_grad = lax.dot_general(
        pre_grad, w_up, (((1,), (1,)), ((), ())), preferred_element_type=jnp.float32
    ).astype(jnp.bfloat16)
    return (grad_up, grad_down, input_grad)


def error_terms(predicted, target):
    errors = predicted - target.astype(jnp.float32)
    losses = jnp.sum(errors * errors, axis=1) * (0.5 * loss_scale)
    return (losses, (errors * loss_scale).astype(jnp.bfloat16))


def adam_update(params, first, second, grads):
    first_new = beta_one * first + (1.0 - beta_one) * grads
    second_new = beta_two * second + (1.0 - beta_two) * grads * grads
    first_hat = first_new / (1.0 - beta_one**adam_step)
    second_hat = second_new / (1.0 - beta_two**adam_step)
    return (
        params - learn_rate * first_hat / (jnp.sqrt(second_hat) + adam_eps),
        first_new,
        second_new,
    )


def on_device(
    cell_table,
    sample_index,
    region,
    targets,
    trunk_weight,
    expert_params,
    first_moment,
    second_moment,
):
    rows = sample_index.shape[0]
    width = cell_table.shape[1]
    experts = lax.axis_size("expert")
    capacity = 2 * rows // experts
    features = jnp.take(cell_table, sample_index, axis=0)
    trunk_pre = jnp.dot(features, trunk_weight, preferred_element_type=jnp.float32)
    trunk_out = (features.astype(jnp.float32) + jax.nn.silu(trunk_pre)).astype(jnp.bfloat16)
    routed = region[:, 0]
    onehot = (routed[:, None] == jnp.arange(experts, dtype=jnp.int32)[None, :]).astype(jnp.int32)
    slots = jnp.sum(jnp.cumsum(onehot, axis=0) * onehot, axis=1) - 1
    places = routed * capacity + slots

    def pack(values):
        empty = jnp.zeros((experts * capacity,) + values.shape[1:], values.dtype)
        return empty.at[places].set(values).reshape((experts, capacity) + values.shape[1:])

    gathered = lax.all_gather(expert_params.astype(jnp.bfloat16), "dp", axis=3, tiled=True)
    w_up = gathered[0, 0]
    w_down = gathered[0, 1]
    arrived = lax.all_to_all(
        pack(trunk_out), "expert", split_axis=0, concat_axis=0, tiled=True
    ).reshape(-1, width)
    up_pre, hidden, predicted = expert_forward(arrived, w_up, w_down)
    returned = lax.all_to_all(
        predicted.reshape(experts, capacity, width),
        "expert",
        split_axis=0,
        concat_axis=0,
        tiled=True,
    )
    row_loss, row_error = error_terms(returned.reshape(-1, width)[places], targets)
    error_there = lax.all_to_all(
        pack(row_error), "expert", split_axis=0, concat_axis=0, tiled=True
    ).reshape(-1, width)
    grad_up, grad_down, input_grad = expert_backward(
        arrived, up_pre, hidden, error_there, w_up, w_down
    )
    back_grad = lax.all_to_all(
        input_grad.reshape(experts, capacity, width),
        "expert",
        split_axis=0,
        concat_axis=0,
        tiled=True,
    )
    row_grad = back_grad.reshape(-1, width)[places]
    trunk_slope = (row_grad.astype(jnp.float32) * silu_slope(trunk_pre)).astype(jnp.bfloat16)
    trunk_local = lax.dot_general(
        features, trunk_slope, (((0,), (0,)), ((), ())), preferred_element_type=jnp.float32
    )
    trunk_grad = lax.psum(trunk_local, ("dp", "expert"))
    grads = jnp.stack([grad_up, grad_down])[None]
    grad_shard = lax.psum_scatter(grads, "dp", scatter_dimension=3, tiled=True)
    new_params, new_first, new_second = adam_update(
        expert_params, first_moment, second_moment, grad_shard
    )
    return (trunk_grad, row_loss, new_params, new_first, new_second)


def solution(mesh):
    placed = (
        P(("dp", "expert"), None),
        P(("dp", "expert")),
        P(("dp", "expert"), None),
        P(("dp", "expert"), None),
        P(),
        P("expert", None, None, "dp"),
        P("expert", None, None, "dp"),
        P("expert", None, None, "dp"),
    )
    return jax.shard_map(
        on_device,
        mesh=mesh,
        in_specs=placed,
        out_specs=(
            P(),
            P(("dp", "expert")),
            P("expert", None, None, "dp"),
            P("expert", None, None, "dp"),
            P("expert", None, None, "dp"),
        ),
        check_vma=False,
    )
```

profile of v0, /device:TPU:0, one launch (start us, length us, event | category | flops | bytes accessed | tf_op | source)
XLA Modules:
  0.0 383.3 jit_solution(5991972244544054535)
XLA Ops:
  10.8 2.3 reduce-window.6
  13.5 3.9 %gather_fusion = bf16[1024,256]{1,0:T(8,128)(2,1)S(1)} fusion(bf16[2048,256]{1,0:T(8,128)(2,1)S(1)} %copy-done, s32[1024]{0:T(1024)S(1)} %fusion.16), kind=kCustom, calls=%fused_computation | custom fusion | bytes 1052672 | tf_op jit(solution)/shard_map/jit(_take)/gather | solution.py:75
  21.0 6.0 %scatter_custom_fusion = bf16[2048,256]{1,0:T(8,128)(2,1)S(1)} fusion(s32[1024]{0:T(1024)S(1)} %bitcast.69, bf16[]{:T(256)} %constant.22.clone.1, f32[1024,256]{1,0:T(8,128)S(1)} %fusion.18, f32[]{:T(128)} %constant.15.clone.1, bf16[1024,256]{1,0:T(8,128)(2,1)S(1)} %gather_fusion, pred[1024]{0:T(1024)(128)(4,1)S(1)} %compare_and_fusion), kind=kCustom, calls=%fused_computation.32 | custom fusion | flops 2097152 | bytes 2622470 | tf_op jit(solution)/shard_map/scatter | solution.py:85
  27.0 32.7 %all_to_all.20 = bf16[8,256,256]{2,1,0:T(8,128)(2,1)S(1)} all-to-all(bf16[8,256,256]{2,1,0:T(8,128)(2,1)S(1)} %bitcast.65), channel_id=1, replica_groups=mesh['dp'=4,'expert'=8] {'expert'}, dimensions={0} | all-to-all | bytes 2097152 | tf_op jit(solution)/shard_map/all_to_all | solution.py:90
  59.7 9.8 %multiply_convert_fusion.1 = (bf16[2048,2048]{1,0:T(8,128)(2,1)S(1)}, f32[2048,2048]{1,0:T(8,128)}) fusion(bf16[2048,256]{1,0:T(8,128)(2,1)S(1)} %bitcast.60, bf16[1,2,256,2048]{3,2,1,0:T(8,128)(2,1)} %all-gather.2.cloned.1.call-done), kind=kOutput, calls=%fused_computation.6 | convolution fusion | flops 2168455168 | bytes 27262976 | tf_op jit(solution)/shard_map/dot_general | solution.py:20
  69.5 3.2 copy-done.2
  72.7 3.8 fusion.1
  76.5 3.6 all-to-all-start.1
  80.4 48.7 %all-to-all-done.1 = f32[8,256,256]{2,1,0:T(8,128)S(1)} async-done(((f32[8,256,256]{2,1,0:T(8,128)}), f32[8,256,256]{2,1,0:T(8,128)S(1)}, u32[]{:S(2)}, u32[]{:S(2)}) %all-to-all-start.1) | async-done | bytes 2097184 | tf_op jit(solution)/shard_map/all_to_all | solution.py:94
  129.1 3.5 gather_fusion.1
  132.6 5.7 %scatter_custom_fusion.1 = bf16[2048,256]{1,0:T(8,128)(2,1)S(1)} fusion(s32[1024]{0:T(1024)S(1)} %bitcast.71, f32[1024,256]{1,0:T(8,128)S(1)} %gather_fusion.1, bf16[1024,256]{1,0:T(8,128)(2,1)} %param.11, f32[]{:T(128)} %constant.16.clone.1, bf16[]{:T(256)} %constant.22.clone.1), kind=kCustom, calls=%fused_computation.29 | custom fusion | flops 1048576 | bytes 2621446 | tf_op jit(solution)/shard_map/scatter | solution.py:85
  138.3 29.0 %all_to_all.21 = bf16[8,256,256]{2,1,0:T(8,128)(2,1)S(1)} all-to-all(bf16[8,256,256]{2,1,0:T(8,128)(2,1)S(1)} %bitcast.64), channel_id=1, replica_groups=mesh['dp'=4,'expert'=8] {'expert'}, dimensions={0} | all-to-all | bytes 2097152 | tf_op jit(solution)/shard_map/all_to_all | solution.py:102
  167.3 5.9 %convolution_bitcast_fusion = f32[1,256,2048]{2,1,0:T(8,128)S(1)} fusion(bf16[2048,256]{1,0:T(8,128)(2,1)S(1)} %bitcast.62, bf16[2048,2048]{1,0:T(8,128)(2,1)} %copy-done.2), kind=kOutput, calls=%fused_computation.9 | convolution fusion | flops 2147483648 | bytes 11534336 | tf_op jit(solution)/shard_map/dot_general | solution.py:29
  173.2 10.4 %multiply_convert_fusion = bf16[2048,2048]{1,0:T(8,128)(2,1)S(1)} fusion(f32[2048,2048]{1,0:T(8,128)} %get-tuple-element.9, bf16[2048,256]{1,0:T(8,128)(2,1)S(1)} %bitcast.63, bf16[1,2,256,2048]{3,2,1,0:T(8,128)(2,1)S(1)} %copy-done.11), kind=kOutput, calls=%fused_computation.5 | convolution fusion | flops 2185232384 | bytes 27262976 | tf_op jit(solution)/shard_map/dot_general | solution.py:32
  183.6 3.2 copy-done.3
  186.8 2.3 convolution_bitcast_fusion.1
  191.4 7.0 %convolution_convert_fusion = bf16[2048,256]{1,0:T(8,128)(2,1)} fusion(bf16[2048,2048]{1,0:T(8,128)(2,1)} %copy-done.3, bf16[1,2,256,2048]{3,2,1,0:T(8,128)(2,1)} %all-gather.2.cloned.1.call-done), kind=kOutput, calls=%fused_computation.11 | convolution fusion | flops 2148007936 | bytes 10485760 | tf_op jit(solution)/shard_map/dot_general | solution.py:37
  198.5 3.7 all-to-all-start.3
  203.1 25.6 %all-to-all-done.3 = bf16[8,256,256]{2,1,0:T(8,128)(2,1)S(1)} async-done(((bf16[8,256,256]{2,1,0:T(8,128)(2,1)}), bf16[8,256,256]{2,1,0:T(8,128)(2,1)S(1)}, u32[]{:S(2)}, u32[]{:S(2)}) %all-to-all-start.3) | async-done | bytes 1048608 | tf_op jit(solution)/shard_map/all_to_all | solution.py:108
  228.7 3.9 %gather_fusion.2 = bf16[1024,256]{1,0:T(8,128)(2,1)S(1)} fusion(bf16[2048,256]{1,0:T(8,128)(2,1)S(1)} %bitcast.58, s32[1024]{0:T(1024)S(1)} %broadcast_clamp_fusion), kind=kCustom, calls=%fused_computation.2 | custom fusion | bytes 1052672 | tf_op jit(solution)/shard_map/gather | solution.py:115
  232.7 2.7 fusion.12
  235.4 7.8 %reduce-scatter.2.cloned.1.call-done = f32[1,2,256,512]{3,2,1,0:T(8,128)} async-done(((f32[1,2,256,2048]{3,2,1,0:T(8,128)}), f32[1,2,256,512]{3,2,1,0:T(8,128)}) %reduce-scatter.2.cloned.1.call-update) | async-done | bytes 1048592 | tf_op jit(solution)/shard_map/reduce_scatter | solution.py:122
  243.2 4.3 %divide_subtract_fusion = (f32[1,2,256,512]{3,2,1,0:T(8,128)}, f32[1,2,256,512]{3,2,1,0:T(8,128)}, f32[1,2,256,512]{3,2,1,0:T(8,128)}) fusion(f32[1,2,256,512]{3,2,1,0:T(8,128)} %param.13, f32[1,2,256,512]{3,2,1,0:T(8,128)} %reduce-scatter.2.cloned.1.call-done, f32[1,2,256,512]{3,2,1,0:T(8,128)} %param.14, f32[1,2,256,512]{3,2,1,0:T(8,128)} %param.15), kind=kLoop, calls=%fused_computation.18 | loop fusion | flops 3145728 | bytes 7340032 | tf_op jit(solution)/shard_map/sub | solution.py:55
  247.5 127.6 %all-reduce.2.cloned.1.call-done = f32[256,256]{1,0:T(8,128)} async-done(((f32[256,256]{1,0:T(8,128)}), f32[256,256]{1,0:T(8,128)}) %all-reduce.2.cloned.1.call-update) | async-done | bytes 262160 | tf_op jit(solution)/shard_map/psum | solution.py:120
  (45 shorter events, 12.6 us)
Async XLA Ops:
  7.2 6.3 %copy-start = (bf16[2048,256]{1,0:T(8,128)(2,1)S(1)}, bf16[2048,256]{1,0:T(8,128)(2,1)}, u32[]{:S(2)}) copy-start(bf16[2048,256]{1,0:T(8,128)(2,1)} %param.8) | copy-start | bytes 3145732
  7.2 52.6 %all-gather.2.cloned.1.call-start = ((), (), s32[]{:S(2)}) async-start(), calls=%async_computation.5 | async-start | bytes 2621440 | tf_op jit(solution)/shard_map/all_gather | solution.py:87
  17.5 52.1 %copy-start.6 = (bf16[1024,256]{1,0:T(8,128)(2,1)}, bf16[1024,256]{1,0:T(8,128)(2,1)S(1)}, u32[]{:S(2)}) copy-start(bf16[1024,256]{1,0:T(8,128)(2,1)S(1)} %gather_fusion) | copy-start | bytes 1572868
  21.0 6.0 %copy-start.8 = (f32[1024,256]{1,0:T(8,128)}, f32[1024,256]{1,0:T(8,128)S(1)}, u32[]{:S(2)}) copy-start(f32[1024,256]{1,0:T(8,128)S(1)} %fusion.18) | copy-start | bytes 3145732
  59.7 9.8 %copy-start.4 = (bf16[8,256,256]{2,1,0:T(8,128)(2,1)}, bf16[8,256,256]{2,1,0:T(8,128)(2,1)S(1)}, u32[]{:S(2)}) copy-start(bf16[8,256,256]{2,1,0:T(8,128)(2,1)S(1)} %all_to_all.20) | copy-start | bytes 3145732
  59.7 13.0 %copy-start.10 = (bf16[1,2,256,2048]{3,2,1,0:T(8,128)(2,1)S(1)}, bf16[1,2,256,2048]{3,2,1,0:T(8,128)(2,1)}, u32[]{:S(2)}) copy-start(bf16[1,2,256,2048]{3,2,1,0:T(8,128)(2,1)} %all-gather.2.cloned.1.call-done) | copy-start | bytes 6291460
  69.5 3.2 copy-start.2
  76.5 52.6 %all-to-all-start.1 = ((f32[8,256,256]{2,1,0:T(8,128)}), f32[8,256,256]{2,1,0:T(8,128)S(1)}, u32[]{:S(2)}, u32[]{:S(2)}) async-start(f32[8,256,256]{2,1,0:T(8,128)} %fusion.1), calls=%async_computation.1 | async-start | bytes 4194304 | tf_op jit(solution)/shard_map/all_to_all | solution.py:94
  80.1 163.1 %reduce-scatter.2.cloned.1.call-start = ((), (), s32[]{:S(2)}) async-start(), calls=%async_computation.7 | async-start | bytes 5242880 | tf_op jit(solution)/shard_map/reduce_scatter | solution.py:122
  167.3 5.9 %copy-start.11 = (bf16[1,2,256,2048]{3,2,1,0:T(8,128)(2,1)S(1)}, bf16[1,2,256,2048]{3,2,1,0:T(8,128)(2,1)}, u32[]{:S(2)}) copy-start(bf16[1,2,256,2048]{3,2,1,0:T(8,128)(2,1)} %all-gather.2.cloned.1.call-done) | copy-start | bytes 6291460
  173.2 13.6 %copy-start.5 = (bf16[8,256,256]{2,1,0:T(8,128)(2,1)S(1)}, bf16[8,256,256]{2,1,0:T(8,128)(2,1)}, u32[]{:S(2)}) copy-start(bf16[8,256,256]{2,1,0:T(8,128)(2,1)} %copy-done.4) | copy-start | bytes 3145732
  183.6 3.2 copy-start.3
  191.4 10.8 %copy-start.9 = (bf16[1024,256]{1,0:T(8,128)(2,1)S(1)}, bf16[1024,256]{1,0:T(8,128)(2,1)}, u32[]{:S(2)}) copy-start(bf16[1024,256]{1,0:T(8,128)(2,1)} %param.11) | copy-start | bytes 1572868
  198.5 34.2 %copy-start.7 = (bf16[1024,256]{1,0:T(8,128)(2,1)S(1)}, bf16[1024,256]{1,0:T(8,128)(2,1)}, u32[]{:S(2)}) copy-start(bf16[1024,256]{1,0:T(8,128)(2,1)} %copy-done.6) | copy-start | bytes 1572868
  198.5 30.2 %all-to-all-start.3 = ((bf16[8,256,256]{2,1,0:T(8,128)(2,1)}), bf16[8,256,256]{2,1,0:T(8,128)(2,1)S(1)}, u32[]{:S(2)}, u32[]{:S(2)}) async-start(bf16[8,256,256]{2,1,0:T(8,128)(2,1)} %bitcast.66), calls=%async_computation.3 | async-start | bytes 2097152 | tf_op jit(solution)/shard_map/all_to_all | solution.py:108
  202.2 172.9 %all-reduce.2.cloned.1.call-start = ((), (), s32[]{:S(2)}) async-start(), calls=%async_computation.6 | async-start | bytes 524288 | tf_op jit(solution)/shard_map/psum | solution.py:120
  228.7 148.1 %copy-start.1 = (bf16[2048,256]{1,0:T(8,128)(2,1)S(1)}, bf16[2048,256]{1,0:T(8,128)(2,1)}, u32[]{:S(2)}) copy-start(bf16[2048,256]{1,0:T(8,128)(2,1)} %param.8) | copy-start | bytes 3145732
Sparse Core Ops, SparseCore 0:
  10.4 37.8 all-gather.1
  191.6 51.5 reduce-scatter.1
  250.2 124.9 all-reduce.1
where the time goes:
time: 384 us; the launch traced here: 383 us
  waiting for transfers between devices  210 us (55%)
  blocking collectives  61.7 us (16%)
  matrix products  43.1 us (11%)
  other arithmetic  27.3 us (7%)
  local copies, waits for them, and re-layouts  19.8 us (5%)
  between operations  13.9 us (4%)
  starting transfers between devices  7.59 us (2%)
    psum x1, waiting for transfers between devices, on_device(): trunk_grad = lax.psum(trunk_local, ('dp', 'expert'))  128 us
    all_to_all x1, waiting for transfers between devices, on_device(): lax.all_to_all(predicted.reshape(experts, capacity, width), 'expert', spl...  48.7 us
    all_to_all x1, blocking collectives, on_device(): lax.all_to_all(pack(trunk_out), 'expert', split_axis=0, concat_axis=0, ti...  32.7 us
    all_to_all x1, blocking collectives, on_device(): lax.all_to_all(pack(row_error), 'expert', split_axis=0, concat_axis=0, ti...  29 us
    all_to_all x1, waiting for transfers between devices, on_device(): lax.all_to_all(input_grad.reshape(experts, capacity, width), 'expert', sp...  25.6 us
    scatter x2, other arithmetic, pack(): empty.at[places].set(values).reshape((experts, capacity) + values.shape[1:])  11.7 us
    dot_general x1, matrix products, expert_backward(): jnp.dot(scaled_error, w_down, preferred_element_type=jnp.float32)  10.4 us
    dot_general x1, matrix products, expert_forward(): up_pre = jnp.dot(arrived, w_up, preferred_element_type=jnp.float32)  9.77 us
  transfers between devices with their start and end apart: 5, of which 4 were waited for; matrix products, arithmetic and copies ran while one was open for 9% of the time, Pallas kernels for 0%

commit v1 on v0

v1 whole, which is shorter than its diff:
```python
import functools

import jax
import jax.numpy as jnp
from jax import lax
from jax.experimental import pallas as pl
from jax.experimental.pallas import tpu as pltpu
from jax.sharding import PartitionSpec as P

loss_scale = 1.0 / 32.0
beta_one = 0.9
beta_two = 0.999
learn_rate = 0.05
adam_eps = 1e-08
adam_step = 10

LANES = 128
F32 = jnp.float32
BF16 = jnp.bfloat16
MIB = 1 << 20


def iota(shape, dim):
    return lax.broadcasted_iota(jnp.int32, shape, dim)


def dot(a, b, ca=1, cb=0):
    return lax.dot_general(a, b, (((ca,), (cb,)), ((), ())), preferred_element_type=F32)


def whole(memory_space=pltpu.VMEM):
    return pl.BlockSpec(memory_space=memory_space)


def pack_kernel(experts, capacity, me_ref, index_ref, region_ref, table_ref, target_ref, *refs):
    blocks, place_ref, rows_ref = refs[:experts], refs[experts], refs[experts + 1]
    me = me_ref[0]
    groups = index_ref.shape[0]
    cells, width = table_ref.shape
    expert_id = iota((experts, LANES), 0)
    starts = ((expert_id ^ me) * capacity).astype(F32)
    ahead = jnp.where(iota((LANES, LANES), 0) <= iota((LANES, LANES), 1), 1.0, 0.0).astype(BF16)
    counted = jnp.zeros((experts, LANES), F32)
    places = []
    for g in range(groups):
        hot = jnp.where(region_ref[g : g + 1, :] == expert_id, 1.0, 0.0)
        upto = dot(hot.astype(BF16), ahead)
        places.append(jnp.sum(hot * (upto - 1.0 + counted + starts), axis=0, keepdims=True))
        counted = counted + jnp.broadcast_to(upto[:, LANES - 1 :], (experts, LANES))
    for g in range(groups):
        place_ref[g : g + 1, :] = places[g].astype(jnp.int32)
    place = jnp.concatenate(places, axis=1)

    step = 2
    cell_id = iota((LANES * step, LANES), 1).astype(F32)
    for g in range(0, groups, step):
        column = jnp.concatenate(
            [
                jnp.broadcast_to(index_ref[h : h + 1, :].astype(F32), (LANES, LANES)).T
                for h in range(g, g + step)
            ],
            axis=0,
        )
        picks = jnp.concatenate(
            [
                jnp.where(column == cell_id + float(LANES * t), 1.0, 0.0).astype(BF16)
                for t in range(cells // LANES)
            ],
            axis=1,
        )
        at = slice(g * LANES, (g + step) * LANES)
        rows_ref[at, :width] = dot(picks, table_ref[...]).astype(BF16)
        rows_ref[at, width:] = target_ref[at, :]

    slot_id = iota((capacity, place.shape[1]), 0).astype(F32)
    for s in range(experts):
        spread = jnp.where(place == slot_id + float(s * capacity), 1.0, 0.0).astype(BF16)
        blocks[s][...] = dot(spread, rows_ref[...]).astype(BF16)


def pack(me, index, region, table, targets, experts, capacity):
    rows, width = targets.shape
    groups = rows // LANES
    return pl.pallas_call(
        functools.partial(pack_kernel, experts, capacity),
        out_shape=[jax.ShapeDtypeStruct((capacity, 2 * width), BF16)] * experts
        + [jax.ShapeDtypeStruct((groups, LANES), jnp.int32)],
        in_specs=[whole(pltpu.SMEM)] + [whole()] * 4,
        out_specs=[whole()] * (experts + 1),
        scratch_shapes=[pltpu.VMEM((rows, 2 * width), BF16)],
        compiler_params=pltpu.CompilerParams(vmem_limit_bytes=32 * MIB),
        cost_estimate=pl.CostEstimate(
            flops=2 * rows * width * (table.shape[0] + 2 * experts * capacity),
            bytes_accessed=6 * MIB,
            transcendentals=0,
        ),
        name="pack_rows",
    )(me, index.reshape(groups, LANES), region.reshape(groups, LANES), table, targets)


def sigmoid(v):
    return 0.5 * jnp.tanh(0.5 * v) + 0.5


def expert_kernel(counts, first, last, *refs):
    blocks, shares, experts, steps, step_rows = counts
    refs = list(refs)

    def take(n):
        got = refs[:n]
        del refs[:n]
        return got

    xs = take(blocks)
    (trunk_ref,) = take(1)
    weights = take(shares)
    if not first:
        prior_ref, prior_trunk_ref = take(2)
    if last:
        loss_refs = take(last - 1)
        (me_ref,) = take(1)
        (own_ref,) = take(1)
        sent = take(shares - 1)
        notes = take(experts)
        part = trunk_part_rows(trunk_ref.shape[0], experts)
        if not part:
            (all_trunk_ref,) = take(1)
    else:
        acc_ref, acc_trunk_ref, loss_ref = take(3)
    x_ref, hid_ref, slope_ref = take(3)
    if last:
        acc_ref, acc_trunk_ref, loss_ref = take(3)

    width = trunk_ref.shape[0]
    share = weights[0].shape[2]
    block_rows = xs[0].shape[0]
    for i, ref in enumerate(xs):
        x_ref[i * block_rows : (i + 1) * block_rows, :] = ref[...]
    if first:
        acc_ref[...] = jnp.zeros(acc_ref.shape, F32)
        acc_trunk_ref[...] = jnp.zeros(acc_trunk_ref.shape, F32)
    else:
        acc_ref[...] = prior_ref[...]
        acc_trunk_ref[...] = prior_trunk_ref[...]

    def step(i, carry):
        at = pl.ds(pl.multiple_of(i * step_rows, step_rows), step_rows)
        feats = x_ref[at, :width]
        feats_f = feats.astype(F32)
        trunk_pre = dot(feats, trunk_ref[...])
        gate = sigmoid(trunk_pre)
        act = trunk_pre * gate
        trunk_slope = gate + act * (1.0 - gate)
        out_f = feats_f + act
        out = out_f.astype(BF16)
        predicted = jnp.zeros((step_rows, width), F32)
        for j in range(shares):
            up = dot(out, weights[j][0])
            s = sigmoid(up)
            h = up * s
            slope_ref[:, j * share : (j + 1) * share] = s + h * (1.0 - s)
            h = h.astype(BF16)
            hid_ref[:, j * share : (j + 1) * share] = h
            predicted = predicted + dot(h, weights[j][1], 1, 1)
        errors = predicted - x_ref[at, width:].astype(F32)
        squares = errors * errors
        half = squares[:, :LANES]
        for k in range(1, width // LANES):
            half = half + squares[:, k * LANES : (k + 1) * LANES]
        loss_ref[pl.ds(i, 1), :] = jnp.sum(half.T, axis=0, keepdims=True) * (0.5 * loss_scale)
        scaled_f = errors * loss_scale
        scaled = scaled_f.astype(BF16)
        scaled_t = scaled_f.T.astype(BF16)
        out_t = out_f.T.astype(BF16)
        row_grad = jnp.zeros((step_rows, width), F32)
        for j in range(shares):
            part = slice(j * share, (j + 1) * share)
            acc_ref[j, 1] += dot(scaled_t, hid_ref[:, part])
            pre = (dot(scaled, weights[j][1]) * slope_ref[:, part]).astype(BF16)
            acc_ref[j, 0] += dot(out_t, pre)
            row_grad = row_grad + dot(pre, weights[j][0], 1, 1)
        slope = (row_grad.astype(BF16).astype(F32) * trunk_slope).astype(BF16)
        acc_trunk_ref[...] += dot(feats_f.T.astype(BF16), slope)
        return carry

    if steps == 1:
        step(0, 0)
    else:
        lax.fori_loop(0, steps, step, 0)
    if last:
        own_ref[...] = acc_ref[0]
        for j in range(1, shares):
            sent[j - 1][...] = acc_ref[j].astype(BF16)
        me = me_ref[0]
        if not part:
            all_trunk_ref[...] = acc_trunk_ref[...]
        for s in range(experts):
            if part:
                mine = pl.ds(pl.multiple_of((me ^ s) * part, part), part)
                notes[s][:part, :] = acc_trunk_ref[mine, :]
            row = loss_row(list(loss_refs) + [loss_ref], s * block_rows // step_rows)
            start = s * block_rows % step_rows
            notes[s][part:, :] = jnp.zeros((8, width), F32)
            notes[s][part:, :block_rows] = jnp.broadcast_to(
                row[:, start : start + block_rows], (8, block_rows)
            )


def loss_row(refs, row):
    for ref in refs:
        if row < ref.shape[0]:
            return ref[row : row + 1, :]
        row -= ref.shape[0]


def expert_call(xs, trunk_weight, weights, prior, losses, me, experts, last):
    block_rows = xs[0].shape[0]
    width = trunk_weight.shape[0]
    shares = len(weights)
    share = weights[0].shape[2]
    rows = block_rows * len(xs)
    step_rows = min(256, rows)
    steps = rows // step_rows
    first = prior is None
    acc = jax.ShapeDtypeStruct((shares, 2, width, share), F32)
    acc_trunk = jax.ShapeDtypeStruct((width, width), F32)
    loss = jax.ShapeDtypeStruct((steps, step_rows), F32)
    args = list(xs) + [trunk_weight] + list(weights)
    if not first:
        args += list(prior)
    in_specs = [whole()] * len(args)
    scratch = [
        pltpu.VMEM((rows, 2 * width), BF16),
        pltpu.VMEM((step_rows, shares * share), BF16),
        pltpu.VMEM((step_rows, shares * share), F32),
    ]
    if last:
        args += list(losses) + [me]
        in_specs += [whole()] * len(losses) + [whole(pltpu.SMEM)]
        outs = [jax.ShapeDtypeStruct((2, width, share), F32)]
        outs += [jax.ShapeDtypeStruct((2, width, share), BF16)] * (shares - 1)
        part = trunk_part_rows(width, experts)
        outs += [jax.ShapeDtypeStruct((part + 8, width), F32)] * experts
        if not part:
            outs += [acc_trunk]
        scratch += [pltpu.VMEM(a.shape, a.dtype) for a in (acc, acc_trunk, loss)]
    else:
        outs = [acc, acc_trunk, loss]
    counts = (len(xs), shares, experts, steps, step_rows)
    return pl.pallas_call(
        functools.partial(expert_kernel, counts, first, len(losses) + 1 if last else 0),
        out_shape=outs,
        in_specs=in_specs,
        out_specs=[whole()] * len(outs),
        scratch_shapes=scratch,
        compiler_params=pltpu.CompilerParams(vmem_limit_bytes=40 * MIB),
        cost_estimate=pl.CostEstimate(
            flops=12 * rows * width * shares * share,
            bytes_accessed=10 * MIB,
            transcendentals=rows * shares * share,
        ),
        name="expert_rows",
    )(*args)


def finish_kernel(experts, me_ref, place_ref, loss_ref, *refs):
    *parts, row_loss_ref, trunk_ref = refs
    me = me_ref[0]
    part = parts[0].shape[0]
    if len(parts) == 1:
        trunk_ref[...] = parts[0][...]
    for s in range(len(parts) if len(parts) > 1 else 0):
        trunk_ref[pl.ds(pl.multiple_of((me ^ s) * part, part), part), :] = parts[s][...]
    capacity = loss_ref.shape[1]
    loss = loss_ref[...]
    for g in range(place_ref.shape[0]):
        place = place_ref[g : g + 1, :]
        block = place // capacity
        slot = place - block * capacity
        picks = jnp.where(iota((capacity, LANES), 0) == slot, 1.0, 0.0)
        found = lax.dot_general(
            loss,
            picks,
            (((1,), (0,)), ((), ())),
            precision=lax.Precision.HIGHEST,
            preferred_element_type=F32,
        )
        mine = jnp.where(iota((experts, LANES), 0) == block, found, 0.0)
        row_loss_ref[g : g + 1, :] = jnp.sum(mine, axis=0, keepdims=True)


def finish(me, place, loss, parts):
    experts = loss.shape[0]
    part, width = parts[0].shape
    return pl.pallas_call(
        functools.partial(finish_kernel, experts),
        out_shape=[
            jax.ShapeDtypeStruct(place.shape, F32),
            jax.ShapeDtypeStruct((len(parts) * part, width), F32),
        ],
        in_specs=[whole(pltpu.SMEM)] + [whole()] * (len(parts) + 2),
        out_specs=[whole()] * 2,
        compiler_params=pltpu.CompilerParams(vmem_limit_bytes=16 * MIB),
        name="finish_rows",
    )(me, place, loss, *parts)


def adam_update(params, first, second, grads):
    first_new = beta_one * first + (1.0 - beta_one) * grads
    second_new = beta_two * second + (1.0 - beta_two) * grads * grads
    first_hat = first_new / (1.0 - beta_one**adam_step)
    second_hat = second_new / (1.0 - beta_two**adam_step)
    return (
        params - learn_rate * first_hat / (jnp.sqrt(second_hat) + adam_eps),
        first_new,
        second_new,
    )


def trunk_part_rows(width, experts):
    return 0 if width % (8 * experts) else width // experts


def swap(value, axis, s):
    if s == 0:
        return value
    return lax.ppermute(value, axis, [(i, i ^ s) for i in range(lax.axis_size(axis))])


def on_device(
    cell_table,
    sample_index,
    region,
    targets,
    trunk_weight,
    expert_params,
    first_moment,
    second_moment,
):
    rows = sample_index.shape[0]
    width = cell_table.shape[1]
    experts = lax.axis_size("expert")
    replicas = lax.axis_size("dp")
    capacity = 2 * rows // experts
    me = lax.axis_index("expert").astype(jnp.int32).reshape(1)

    rounded = expert_params[0].astype(BF16)
    weights = [swap(rounded, "dp", j) for j in range(replicas)]
    *blocks, place = pack(me, sample_index, region[:, 0], cell_table, targets, experts, capacity)
    arrived = [swap(blocks[s], "expert", s) for s in range(experts)]

    cuts = [0, experts // 2, 3 * experts // 4, 7 * experts // 8, experts]
    prior, losses = None, []
    for k in range(len(cuts) - 1):
        xs = arrived[cuts[k] : cuts[k + 1]]
        last = k == len(cuts) - 2
        outs = expert_call(xs, trunk_weight, weights, prior, losses, me, experts, last)
        if not last:
            prior = outs[:2]
            losses.append(outs[2])
    grads = outs[0]
    sent = outs[1:replicas]
    notes = outs[replicas : replicas + experts]

    back = [swap(notes[s], "expert", s) for s in range(experts)]
    part = trunk_part_rows(width, experts)
    if part:
        trunk_part = sum(note[:part] for note in back)
        trunk_part = sum(swap(trunk_part, "dp", j) for j in range(replicas))
        parts = [swap(trunk_part, "expert", s) for s in range(experts)]
    else:
        parts = [lax.psum(outs[-1], ("dp", "expert"))]
    loss = jnp.concatenate([note[part : part + 1, :capacity] for note in back], axis=0)
    row_loss, trunk_grad = finish(me, place, loss, parts)

    for j in range(1, replicas):
        grads = grads + swap(sent[j - 1], "dp", j).astype(F32)
    new_params, new_first, new_second = adam_update(
        expert_params, first_moment, second_moment, grads[None]
    )
    return (trunk_grad, row_loss.reshape(rows), new_params, new_first, new_second)


def solution(mesh):
    placed = (
        P(("dp", "expert"), None),
        P(("dp", "expert")),
        P(("dp", "expert"), None),
        P(("dp", "expert"), None),
        P(),
        P("expert", None, None, "dp"),
        P("expert", None, None, "dp"),
        P("expert", None, None, "dp"),
    )
    return jax.shard_map(
        on_device,
        mesh=mesh,
        in_specs=placed,
        out_specs=(
            P(),
            P(("dp", "expert")),
            P("expert", None, None, "dp"),
            P("expert", None, None, "dp"),
            P("expert", None, None, "dp"),
        ),
        check_vma=False,
    )
```

time: 384 us -> 145 us (0.38)
  waiting for transfers between devices: 210 us -> 69.1 us
  blocking collectives: 61.7 us -> 0 us
  matrix products: 43.1 us -> 0 us
  Pallas kernels: 0 us -> 31.6 us
  starting transfers between devices: 7.59 us -> 34.8 us
  other arithmetic: 27.3 us -> 4.59 us
  local copies, waits for them, and re-layouts: 19.8 us -> 3.69 us
  between operations: 13.9 us -> 0.8 us
    psum x1 -> x0, waiting for transfers between devices: 128 us -> none  [on_device(): trunk_grad = lax.psum(trunk_local, ('dp', 'expert'))]
    all_to_all x2 -> x0, waiting for transfers between devices: 74.4 us -> none  [the longest x1 48.7 us: on_device(): lax.all_to_all(predicted.reshape(experts, capacity, width), 'expert', spl...]
    ppermute x0 -> x30, waiting for transfers between devices: none -> 69.1 us  [swap(): lax.ppermute(value, axis, [(i, i ^ s) for i in range(lax.axis_size(axis))])]
    all_to_all x2 -> x0, blocking collectives: 61.7 us -> none  [the longest x1 32.7 us: on_device(): lax.all_to_all(pack(trunk_out), 'expert', split_axis=0, concat_axis=0, ti...]
    dot_general x8 -> x0, matrix products: 43.1 us -> none  [the longest x1 10.4 us: expert_backward(): jnp.dot(scaled_error, w_down, preferred_element_type=jnp.float32)]
    ppermute x0 -> x30, starting transfers between devices: none -> 34.8 us  [swap(): lax.ppermute(value, axis, [(i, i ^ s) for i in range(lax.axis_size(axis))])]
    pallas_call x0 -> x6, Pallas kernels: none -> 31.6 us  [the longest x4 26.8 us: expert_call(): pl.pallas_call(functools.partial(expert_kernel, counts, first, len(losses...]
    scatter x2 -> x0, other arithmetic: 11.7 us -> none  [pack(): empty.at[places].set(values).reshape((experts, capacity) + values.shape[1:])]
  transfers between devices with their start and end apart: 5 -> 30, of which waited for: 4 -> 13; matrix products, arithmetic and copies ran while one was open for 9% -> 0% of each run, Pallas kernels for 0% -> 17%
where the time goes in v1:
time: 145 us
  waiting for transfers between devices  69.1 us (48%)
  starting transfers between devices  34.8 us (24%)
  Pallas kernels  31.6 us (22%)
  other arithmetic  4.59 us (3%)
  local copies, waits for them, and re-layouts  3.69 us (3%)
    ppermute x30, waiting for transfers between devices, swap(): lax.ppermute(value, axis, [(i, i ^ s) for i in range(lax.axis_size(axis))])  69.1 us
    ppermute x30, starting transfers between devices, swap(): lax.ppermute(value, axis, [(i, i ^ s) for i in range(lax.axis_size(axis))])  34.8 us
    pallas_call x4, Pallas kernels, expert_call(): pl.pallas_call(functools.partial(expert_kernel, counts, first, len(losses...  26.8 us
    sub x1, other arithmetic, adam_update(): params - learn_rate * first_hat / (jnp.sqrt(second_hat) + adam_eps)  4.49 us
    unnamed x12, local copies, waits for them, and re-layouts  3.64 us
    pallas_call x1, Pallas kernels, pack(): pl.pallas_call(functools.partial(pack_kernel, experts, capacity), out_sha...  3.52 us
  transfers between devices with their start and end apart: 30, of which 13 were waited for; matrix products, arithmetic and copies ran while one was open for 0% of the time, Pallas kernels for 17%

profile of v1, /device:TPU:0, one launch (start us, length us, event | category | flops | bytes accessed | tf_op | source)
XLA Modules:
  0.0 144.6 jit_solution(6014568809319635003)
XLA Ops:
  4.3 3.5 %pack_rows.1 = (bf16[256,512]{1,0:T(8,128)(2,1)S(1)}, bf16[256,512]{1,0:T(8,128)(2,1)S(1)}, bf16[256,512]{1,0:T(8,128)(2,1)S(1)}, bf16[256,512]{1,0:T(8,128)(2,1...) custom-call(s32[1]{0:T(128)} %bitcast.me_ref.refs_11_, ...), custom_call_target="tpu_custom_call" | custom-call | flops 3221225472 | bytes 6291456 | tf_op jit(solution)/shard_map/pack_rows/pallas_call | solution.py:84
  8.4 3.5 %collective-permute-start.3 = (bf16[2,256,512]{2,1,0:T(8,128)(2,1)S(1)}, bf16[2,256,512]{2,1,0:T(8,128)(2,1)S(1)}, u32[]{:S(2)}, u32[]{:S(2)}) collective-permute-start(bf16[2,256,512]{2,1,0:T(8,128)(2,1)S(1)} %convert_bitcast_fusion.refs_5_.refs_3_.refs_2_), channel_id=1, source_target_pairs={{0,24},{8,16},{16,8},{24,0},{1,25},{9,17},{17,9},{25,1},{2,26},{10... | collective-permute-start | bytes 1572872 | tf_op jit(solution)/shard_map/ppermute | solution.py:327
  12.6 2.0 %collective-permute-start.8 = (bf16[256,512]{1,0:T(8,128)(2,1)S(1)}, bf16[256,512]{1,0:T(8,128)(2,1)S(1)}, u32[]{:S(2)}, u32[]{:S(2)}) collective-permute-start(bf16[256,512]{1,0:T(8,128)(2,1)S(1)} %get-tuple-element.44), channel_id=1, source_target_pairs={{0,2},{1,3},{2,0},{3,1},{4,6},{5,7},{6,4},{7,5},{8,10},{9,11},{10,... | collective-permute-start | bytes 786440 | tf_op jit(solution)/shard_map/ppermute | solution.py:327
  14.6 7.2 %collective-permute-done.8.refs_2_ = bf16[256,512]{1,0:T(8,128)(2,1)S(1)} collective-permute-done((bf16[256,512]{1,0:T(8,128)(2,1)S(1)}, bf16[256,512]{1,0:T(8,128)(2,1)S(1)}, u32[]{:S(2)}, u32[]{:S(2)}) %collective-permute-start.8) | collective-permute-done | bytes 262176 | tf_op jit(solution)/shard_map/ppermute | solution.py:327
  22.8 2.8 %collective-permute-done.9.refs_3_ = bf16[256,512]{1,0:T(8,128)(2,1)S(1)} collective-permute-done((bf16[256,512]{1,0:T(8,128)(2,1)S(1)}, bf16[256,512]{1,0:T(8,128)(2,1)S(1)}, u32[]{:S(2)}, u32[]{:S(2)}) %collective-permute-start.9) | collective-permute-done | bytes 262176 | tf_op jit(solution)/shard_map/ppermute | solution.py:327
  25.6 3.8 %collective-permute-start.4 = (bf16[256,512]{1,0:T(8,128)(2,1)S(1)}, bf16[256,512]{1,0:T(8,128)(2,1)S(1)}, u32[]{:S(2)}, u32[]{:S(2)}) collective-permute-start(bf16[256,512]{1,0:T(8,128)(2,1)S(1)} %get-tuple-element.39), channel_id=1, source_target_pairs={{0,6},{1,7},{2,4},{3,5},{4,2},{5,3},{6,0},{7,1},{8,14},{9,15},{10,... | collective-permute-start | bytes 786440 | tf_op jit(solution)/shard_map/ppermute | solution.py:327
  29.4 6.3 %collective-permute-done.2.refs_7_.refs_5_.refs_4_ = bf16[2,256,512]{2,1,0:T(8,128)(2,1)S(1)} collective-permute-done((bf16[2,256,512]{2,1,0:T(8,128)(2,1)S(1)}, bf16[2,256,512]{2,1,0:T(8,128)(2,1)S(1)}, u32[]{:S(2)}, u32[]{:S(2)}) %collective-permute-start.2) | collective-permute-done | bytes 524320 | tf_op jit(solution)/shard_map/ppermute | solution.py:327
  35.7 4.8 %collective-permute-start.6 = (bf16[256,512]{1,0:T(8,128)(2,1)S(1)}, bf16[256,512]{1,0:T(8,128)(2,1)S(1)}, u32[]{:S(2)}, u32[]{:S(2)}) collective-permute-start(bf16[256,512]{1,0:T(8,128)(2,1)S(1)} %get-tuple-element.41), channel_id=1, source_target_pairs={{0,5},{1,4},{2,7},{3,6},{4,1},{5,0},{6,3},{7,2},{8,13},{9,12},{10,... | collective-permute-start | bytes 786440 | tf_op jit(solution)/shard_map/ppermute | solution.py:327
  40.6 13.3 %expert_rows.4 = (f32[4,2,256,512]{3,2,1,0:T(8,128)S(1)}, f32[256,256]{1,0:T(8,128)S(1)}, f32[4,256]{1,0:T(4,128)S(1)}) custom-call(bf16[256,512]{1,0:T(8,128)(2,1)S(1)} %get-tuple-element.42.refs_0_, bf16[256,512]{1,0:T(8,128)(2,1)S(1)} %collective-permute-done.7.refs_1_, bf16[256,512]{1,0:T(8,128)(2,1)S(1)} %collective-permute-done.8.refs_2_, ...), custom_call_target="tpu_custom_call" | custom-call | flops 6442450944 | bytes 10485760 | tf_op jit(solution)/shard_map/expert_rows/pallas_call | solution.py:250
  53.9 11.7 %collective-permute-done.5.refs_0_ = bf16[256,512]{1,0:T(8,128)(2,1)S(1)} collective-permute-done((bf16[256,512]{1,0:T(8,128)(2,1)S(1)}, bf16[256,512]{1,0:T(8,128)(2,1)S(1)}, u32[]{:S(2)}, u32[]{:S(2)}) %collective-permute-start.5) | collective-permute-done | bytes 262176 | tf_op jit(solution)/shard_map/ppermute | solution.py:327
  65.7 5.4 %collective-permute-done.6.refs_1_ = bf16[256,512]{1,0:T(8,128)(2,1)S(1)} collective-permute-done((bf16[256,512]{1,0:T(8,128)(2,1)S(1)}, bf16[256,512]{1,0:T(8,128)(2,1)S(1)}, u32[]{:S(2)}, u32[]{:S(2)}) %collective-permute-start.6) | collective-permute-done | bytes 262176 | tf_op jit(solution)/shard_map/ppermute | solution.py:327
  71.0 7.0 %expert_rows.5 = (f32[4,2,256,512]{3,2,1,0:T(8,128)S(1)}, f32[256,256]{1,0:T(8,128)S(1)}, f32[2,256]{1,0:T(2,128)S(1)}) custom-call(bf16[256,512]{1,0:T(8,128)(2,1)S(1)} %collective-permute-done.5.refs_0_, bf16[256,512]{1,0:T(8,128)(2,1)S(1)} %collective-permute-done.6.refs_1_, bf16[256,256]{1,0:T(8,128)(2,1)S(1)} %copy-done, ...), custom_call_target="tpu_custom_call" | custom-call | flops 3221225472 | bytes 10485760 | tf_op jit(solution)/shard_map/expert_rows/pallas_call | solution.py:250
  78.0 3.2 %expert_rows.6 = (f32[4,2,256,512]{3,2,1,0:T(8,128)S(1)}, f32[256,256]{1,0:T(8,128)S(1)}, f32[1,256]{1,0:T(1,128)S(1)}) custom-call(bf16[256,512]{1,0:T(8,128)(2,1)S(1)} %collective-permute-done.4.refs_0_, bf16[256,256]{1,0:T(8,128)(2,1)S(1)} %copy-done, bf16[2,256,512]{2,1,0:T(8,128)(2,1)S(1)} %convert_bitcast_fusion.refs_5_.refs_3_.refs_2_, ...), custom_call_target="tpu_custom_call" | custom-call | flops 1610612736 | bytes 10485760 | tf_op jit(solution)/shard_map/expert_rows/pallas_call | solution.py:250
  81.3 3.2 %expert_rows.7 = (f32[2,256,512]{2,1,0:T(8,128)S(1)}, bf16[2,256,512]{2,1,0:T(8,128)(2,1)S(1)}, bf16[2,256,512]{2,1,0:T(8,128)(2,1)S(1)}, bf16[2,256,512]{2,1,0:...) custom-call(bf16[256,512]{1,0:T(8,128)(2,1)S(1)} %collective-permute, ...), custom_call_target="tpu_custom_call" | custom-call | flops 1610612736 | bytes 10485760 | tf_op jit(solution)/shard_map/expert_rows/pallas_call | solution.py:250
  86.9 2.2 %collective-permute-start.14 = (f32[40,256]{1,0:T(8,128)S(1)}, f32[40,256]{1,0:T(8,128)S(1)}, u32[]{:S(2)}, u32[]{:S(2)}) collective-permute-start(f32[40,256]{1,0:T(8,128)S(1)} %get-tuple-element.60), channel_id=1, source_target_pairs={{0,5},{1,4},{2,7},{3,6},{4,1},{5,0},{6,3},{7,2},{8,13},{9,12},{10,... | collective-permute-start | bytes 122888 | tf_op jit(solution)/shard_map/ppermute | solution.py:327
  90.7 2.0 %collective-permute-start.16 = (f32[40,256]{1,0:T(8,128)S(1)}, f32[40,256]{1,0:T(8,128)S(1)}, u32[]{:S(2)}, u32[]{:S(2)}) collective-permute-start(f32[40,256]{1,0:T(8,128)S(1)} %get-tuple-element.62), channel_id=1, source_target_pairs={{0,7},{1,6},{2,5},{3,4},{4,3},{5,2},{6,1},{7,0},{8,15},{9,14},{10,... | collective-permute-start | bytes 122888 | tf_op jit(solution)/shard_map/ppermute | solution.py:327
  96.2 2.5 %collective-permute-start.19 = (f32[32,256]{1,0:T(8,128)S(1)}, f32[32,256]{1,0:T(8,128)S(1)}, u32[]{:S(2)}, u32[]{:S(2)}) collective-permute-start(f32[32,256]{1,0:T(8,128)S(1)} %slice_add_fusion), channel_id=1, source_target_pairs={{0,24},{8,16},{16,8},{24,0},{1,25},{9,17},{17,9},{25,1},{2,26},{10... | collective-permute-start | bytes 98312 | tf_op jit(solution)/shard_map/ppermute | solution.py:327
  99.2 20.7 %collective-permute-done.19 = f32[32,256]{1,0:T(8,128)S(1)} collective-permute-done((f32[32,256]{1,0:T(8,128)S(1)}, f32[32,256]{1,0:T(8,128)S(1)}, u32[]{:S(2)}, u32[]{:S(2)}) %collective-permute-start.19) | collective-permute-done | bytes 32800 | tf_op jit(solution)/shard_map/ppermute | solution.py:327
  121.3 2.6 %collective-permute-done.17 = f32[32,256]{1,0:T(8,128)S(1)} collective-permute-done((f32[32,256]{1,0:T(8,128)S(1)}, f32[32,256]{1,0:T(8,128)S(1)}, u32[]{:S(2)}, u32[]{:S(2)}) %collective-permute-start.17) | collective-permute-done | bytes 32800 | tf_op jit(solution)/shard_map/ppermute | solution.py:327
  123.9 2.0 %collective-permute-start.25 = (f32[32,256]{1,0:T(8,128)S(1)}, f32[32,256]{1,0:T(8,128)S(1)}, u32[]{:S(2)}, u32[]{:S(2)}) collective-permute-start(f32[32,256]{1,0:T(8,128)S(1)} %add_add_fusion.refs_0_), channel_id=1, source_target_pairs={{0,6},{1,7},{2,4},{3,5},{4,2},{5,3},{6,0},{7,1},{8,14},{9,15},{10,... | collective-permute-start | bytes 98312 | tf_op jit(solution)/shard_map/ppermute | solution.py:327
  125.9 3.2 %collective-permute-done.26.refs_7_ = f32[32,256]{1,0:T(8,128)S(1)} collective-permute-done((f32[32,256]{1,0:T(8,128)S(1)}, f32[32,256]{1,0:T(8,128)S(1)}, u32[]{:S(2)}, u32[]{:S(2)}) %collective-permute-start.26) | collective-permute-done | bytes 32800 | tf_op jit(solution)/shard_map/ppermute | solution.py:327
  130.2 3.1 %collective-permute-done.24.refs_5_ = f32[32,256]{1,0:T(8,128)S(1)} collective-permute-done((f32[32,256]{1,0:T(8,128)S(1)}, f32[32,256]{1,0:T(8,128)S(1)}, u32[]{:S(2)}, u32[]{:S(2)}) %collective-permute-start.24) | collective-permute-done | bytes 32800 | tf_op jit(solution)/shard_map/ppermute | solution.py:327
  136.7 2.1 %collective-permute-done.21.refs_2_ = f32[32,256]{1,0:T(8,128)S(1)} collective-permute-done((f32[32,256]{1,0:T(8,128)S(1)}, f32[32,256]{1,0:T(8,128)S(1)}, u32[]{:S(2)}, u32[]{:S(2)}) %collective-permute-start.21) | collective-permute-done | bytes 32800 | tf_op jit(solution)/shard_map/ppermute | solution.py:327
  140.1 4.5 %divide_subtract_fusion = (f32[1,2,256,512]{3,2,1,0:T(8,128)}, f32[1,2,256,512]{3,2,1,0:T(8,128)}, f32[1,2,256,512]{3,2,1,0:T(8,128)}) fusion(f32[1,2,256,512]{3,2,1,0:T(8,128)} %param.13, bf16[2,256,512]{2,1,0:T(8,128)(2,1)} %collective-permute-done.29, bf16[2,256,512]{2,1,0:T(8,128)(2,1)} %collective-permute-done.28, ...), kind=kLoop, calls=%fused_computation.4 | loop fusion | flops 4718592 | bytes 8912896 | tf_op jit(solution)/shard_map/sub | solution.py:314
  (67 shorter events, 21.0 us)
Async XLA Ops:
  7.8 6.7 %collective-permute-start.7 = (bf16[256,512]{1,0:T(8,128)(2,1)S(1)}, bf16[256,512]{1,0:T(8,128)(2,1)S(1)}, u32[]{:S(2)}, u32[]{:S(2)}) collective-permute-start(bf16[256,512]{1,0:T(8,128)(2,1)S(1)} %get-tuple-element.43), channel_id=1, source_target_pairs={{0,1},{1,0},{2,3},{3,2},{4,5},{5,4},{6,7},{7,6},{8,9},{9,8},{10,11... | collective-permute-start | bytes 786440 | tf_op jit(solution)/shard_map/ppermute | solution.py:327
  8.4 21.0 %collective-permute-start.3 = (bf16[2,256,512]{2,1,0:T(8,128)(2,1)S(1)}, bf16[2,256,512]{2,1,0:T(8,128)(2,1)S(1)}, u32[]{:S(2)}, u32[]{:S(2)}) collective-permute-start(bf16[2,256,512]{2,1,0:T(8,128)(2,1)S(1)} %convert_bitcast_fusion.refs_5_.refs_3_.refs_2_), channel_id=1, source_target_pairs={{0,24},{8,16},{16,8},{24,0},{1,25},{9,17},{17,9},{25,1},{2,26},{10... | collective-permute-start | bytes 1572872 | tf_op jit(solution)/shard_map/ppermute | solution.py:327
  11.9 23.8 %collective-permute-start.2 = (bf16[2,256,512]{2,1,0:T(8,128)(2,1)S(1)}, bf16[2,256,512]{2,1,0:T(8,128)(2,1)S(1)}, u32[]{:S(2)}, u32[]{:S(2)}) collective-permute-start(bf16[2,256,512]{2,1,0:T(8,128)(2,1)S(1)} %convert_bitcast_fusion.refs_5_.refs_3_.refs_2_), channel_id=1, source_target_pairs={{0,16},{8,24},{16,0},{24,8},{1,17},{9,25},{17,1},{25,9},{2,18},{10... | collective-permute-start | bytes 1572872 | tf_op jit(solution)/shard_map/ppermute | solution.py:327
  12.4 28.1 %collective-permute-start.1 = (bf16[2,256,512]{2,1,0:T(8,128)(2,1)S(1)}, bf16[2,256,512]{2,1,0:T(8,128)(2,1)S(1)}, u32[]{:S(2)}, u32[]{:S(2)}) collective-permute-start(bf16[2,256,512]{2,1,0:T(8,128)(2,1)S(1)} %convert_bitcast_fusion.refs_5_.refs_3_.refs_2_), channel_id=1, source_target_pairs={{0,8},{8,0},{16,24},{24,16},{1,9},{9,1},{17,25},{25,17},{2,10},{10... | collective-permute-start | bytes 1572872 | tf_op jit(solution)/shard_map/ppermute | solution.py:327
  12.6 9.2 %collective-permute-start.8 = (bf16[256,512]{1,0:T(8,128)(2,1)S(1)}, bf16[256,512]{1,0:T(8,128)(2,1)S(1)}, u32[]{:S(2)}, u32[]{:S(2)}) collective-permute-start(bf16[256,512]{1,0:T(8,128)(2,1)S(1)} %get-tuple-element.44), channel_id=1, source_target_pairs={{0,2},{1,3},{2,0},{3,1},{4,6},{5,7},{6,4},{7,5},{8,10},{9,11},{10,... | collective-permute-start | bytes 786440 | tf_op jit(solution)/shard_map/ppermute | solution.py:327
  14.6 11.0 %collective-permute-start.9 = (bf16[256,512]{1,0:T(8,128)(2,1)S(1)}, bf16[256,512]{1,0:T(8,128)(2,1)S(1)}, u32[]{:S(2)}, u32[]{:S(2)}) collective-permute-start(bf16[256,512]{1,0:T(8,128)(2,1)S(1)} %get-tuple-element.45), channel_id=1, source_target_pairs={{0,3},{1,2},{2,1},{3,0},{4,7},{5,6},{6,5},{7,4},{8,11},{9,10},{10,... | collective-permute-start | bytes 786440 | tf_op jit(solution)/shard_map/ppermute | solution.py:327
  21.8 59.5 %collective-permute-start = (bf16[256,512]{1,0:T(8,128)(2,1)S(1)}, bf16[256,512]{1,0:T(8,128)(2,1)S(1)}, u32[]{:S(2)}, u32[]{:S(2)}) collective-permute-start(bf16[256,512]{1,0:T(8,128)(2,1)S(1)} %get-tuple-element.38), channel_id=1, source_target_pairs={{0,7},{1,6},{2,5},{3,4},{4,3},{5,2},{6,1},{7,0},{8,15},{9,14},{10,... | collective-permute-start | bytes 786440 | tf_op jit(solution)/shard_map/ppermute | solution.py:327
  25.6 52.5 %collective-permute-start.4 = (bf16[256,512]{1,0:T(8,128)(2,1)S(1)}, bf16[256,512]{1,0:T(8,128)(2,1)S(1)}, u32[]{:S(2)}, u32[]{:S(2)}) collective-permute-start(bf16[256,512]{1,0:T(8,128)(2,1)S(1)} %get-tuple-element.39), channel_id=1, source_target_pairs={{0,6},{1,7},{2,4},{3,5},{4,2},{5,3},{6,0},{7,1},{8,14},{9,15},{10,... | collective-permute-start | bytes 786440 | tf_op jit(solution)/shard_map/ppermute | solution.py:327
  29.4 36.3 %collective-permute-start.5 = (bf16[256,512]{1,0:T(8,128)(2,1)S(1)}, bf16[256,512]{1,0:T(8,128)(2,1)S(1)}, u32[]{:S(2)}, u32[]{:S(2)}) collective-permute-start(bf16[256,512]{1,0:T(8,128)(2,1)S(1)} %get-tuple-element.40), channel_id=1, source_target_pairs={{0,4},{1,5},{2,6},{3,7},{4,0},{5,1},{6,2},{7,3},{8,12},{9,13},{10,... | collective-permute-start | bytes 786440 | tf_op jit(solution)/shard_map/ppermute | solution.py:327
  35.7 35.3 %collective-permute-start.6 = (bf16[256,512]{1,0:T(8,128)(2,1)S(1)}, bf16[256,512]{1,0:T(8,128)(2,1)S(1)}, u32[]{:S(2)}, u32[]{:S(2)}) collective-permute-start(bf16[256,512]{1,0:T(8,128)(2,1)S(1)} %get-tuple-element.41), channel_id=1, source_target_pairs={{0,5},{1,4},{2,7},{3,6},{4,1},{5,0},{6,3},{7,2},{8,13},{9,12},{10,... | collective-permute-start | bytes 786440 | tf_op jit(solution)/shard_map/ppermute | solution.py:327
  84.7 6.0 %collective-permute-start.11 = (f32[40,256]{1,0:T(8,128)S(1)}, f32[40,256]{1,0:T(8,128)S(1)}, u32[]{:S(2)}, u32[]{:S(2)}) collective-permute-start(f32[40,256]{1,0:T(8,128)S(1)} %get-tuple-element.57), channel_id=1, source_target_pairs={{0,2},{1,3},{2,0},{3,1},{4,6},{5,7},{6,4},{7,5},{8,10},{9,11},{10,... | collective-permute-start | bytes 122888 | tf_op jit(solution)/shard_map/ppermute | solution.py:327
  84.7 8.0 %collective-permute-start.12 = (f32[40,256]{1,0:T(8,128)S(1)}, f32[40,256]{1,0:T(8,128)S(1)}, u32[]{:S(2)}, u32[]{:S(2)}) collective-permute-start(f32[40,256]{1,0:T(8,128)S(1)} %get-tuple-element.58), channel_id=1, source_target_pairs={{0,3},{1,2},{2,1},{3,0},{4,7},{5,6},{6,5},{7,4},{8,11},{9,10},{10,... | collective-permute-start | bytes 122888 | tf_op jit(solution)/shard_map/ppermute | solution.py:327
  86.5 7.7 %collective-permute-start.13 = (f32[40,256]{1,0:T(8,128)S(1)}, f32[40,256]{1,0:T(8,128)S(1)}, u32[]{:S(2)}, u32[]{:S(2)}) collective-permute-start(f32[40,256]{1,0:T(8,128)S(1)} %get-tuple-element.59), channel_id=1, source_target_pairs={{0,4},{1,5},{2,6},{3,7},{4,0},{5,1},{6,2},{7,3},{8,12},{9,13},{10,... | collective-permute-start | bytes 122888 | tf_op jit(solution)/shard_map/ppermute | solution.py:327
  86.9 8.8 %collective-permute-start.14 = (f32[40,256]{1,0:T(8,128)S(1)}, f32[40,256]{1,0:T(8,128)S(1)}, u32[]{:S(2)}, u32[]{:S(2)}) collective-permute-start(f32[40,256]{1,0:T(8,128)S(1)} %get-tuple-element.60), channel_id=1, source_target_pairs={{0,5},{1,4},{2,7},{3,6},{4,1},{5,0},{6,3},{7,2},{8,13},{9,12},{10,... | collective-permute-start | bytes 122888 | tf_op jit(solution)/shard_map/ppermute | solution.py:327
  89.1 7.1 %collective-permute-start.15 = (f32[40,256]{1,0:T(8,128)S(1)}, f32[40,256]{1,0:T(8,128)S(1)}, u32[]{:S(2)}, u32[]{:S(2)}) collective-permute-start(f32[40,256]{1,0:T(8,128)S(1)} %get-tuple-element.61), channel_id=1, source_target_pairs={{0,6},{1,7},{2,4},{3,5},{4,2},{5,3},{6,0},{7,1},{8,14},{9,15},{10,... | collective-permute-start | bytes 122888 | tf_op jit(solution)/shard_map/ppermute | solution.py:327
  90.7 5.5 %collective-permute-start.16 = (f32[40,256]{1,0:T(8,128)S(1)}, f32[40,256]{1,0:T(8,128)S(1)}, u32[]{:S(2)}, u32[]{:S(2)}) collective-permute-start(f32[40,256]{1,0:T(8,128)S(1)} %get-tuple-element.62), channel_id=1, source_target_pairs={{0,7},{1,6},{2,5},{3,4},{4,3},{5,2},{6,1},{7,0},{8,15},{9,14},{10,... | collective-permute-start | bytes 122888 | tf_op jit(solution)/shard_map/ppermute | solution.py:327
  92.7 47.4 %collective-permute-start.27 = (bf16[2,256,512]{2,1,0:T(8,128)(2,1)S(1)}, bf16[2,256,512]{2,1,0:T(8,128)(2,1)S(1)}, u32[]{:S(2)}, u32[]{:S(2)}) collective-permute-start(bf16[2,256,512]{2,1,0:T(8,128)(2,1)S(1)} %get-tuple-element.66), channel_id=1, source_target_pairs={{0,8},{8,0},{16,24},{24,16},{1,9},{9,1},{17,25},{25,17},{2,10},{10... | collective-permute-start | bytes 1572872 | tf_op jit(solution)/shard_map/ppermute | solution.py:327
  94.1 45.9 %collective-permute-start.28 = (bf16[2,256,512]{2,1,0:T(8,128)(2,1)S(1)}, bf16[2,256,512]{2,1,0:T(8,128)(2,1)}, u32[]{:S(2)}, u32[]{:S(2)}) collective-permute-start(bf16[2,256,512]{2,1,0:T(8,128)(2,1)S(1)} %get-tuple-element.67), channel_id=1, source_target_pairs={{0,16},{8,24},{16,0},{24,8},{1,17},{9,25},{17,1},{25,9},{2,18},{10... | collective-permute-start | bytes 1572872 | tf_op jit(solution)/shard_map/ppermute | solution.py:327
  95.7 44.4 %collective-permute-start.29 = (bf16[2,256,512]{2,1,0:T(8,128)(2,1)S(1)}, bf16[2,256,512]{2,1,0:T(8,128)(2,1)}, u32[]{:S(2)}, u32[]{:S(2)}) collective-permute-start(bf16[2,256,512]{2,1,0:T(8,128)(2,1)S(1)} %get-tuple-element.68), channel_id=1, source_target_pairs={{0,24},{8,16},{16,8},{24,0},{1,25},{9,17},{17,9},{25,1},{2,26},{10... | collective-permute-start | bytes 1572872 | tf_op jit(solution)/shard_map/ppermute | solution.py:327
  96.2 23.7 %collective-permute-start.19 = (f32[32,256]{1,0:T(8,128)S(1)}, f32[32,256]{1,0:T(8,128)S(1)}, u32[]{:S(2)}, u32[]{:S(2)}) collective-permute-start(f32[32,256]{1,0:T(8,128)S(1)} %slice_add_fusion), channel_id=1, source_target_pairs={{0,24},{8,16},{16,8},{24,0},{1,25},{9,17},{17,9},{25,1},{2,26},{10... | collective-permute-start | bytes 98312 | tf_op jit(solution)/shard_map/ppermute | solution.py:327
  98.7 22.5 %collective-permute-start.18 = (f32[32,256]{1,0:T(8,128)S(1)}, f32[32,256]{1,0:T(8,128)S(1)}, u32[]{:S(2)}, u32[]{:S(2)}) collective-permute-start(f32[32,256]{1,0:T(8,128)S(1)} %slice_add_fusion), channel_id=1, source_target_pairs={{0,16},{8,24},{16,0},{24,8},{1,17},{9,25},{17,1},{25,9},{2,18},{10... | collective-permute-start | bytes 98312 | tf_op jit(solution)/shard_map/ppermute | solution.py:327
  123.9 5.2 %collective-permute-start.26 = (f32[32,256]{1,0:T(8,128)S(1)}, f32[32,256]{1,0:T(8,128)S(1)}, u32[]{:S(2)}, u32[]{:S(2)}) collective-permute-start(f32[32,256]{1,0:T(8,128)S(1)} %add_add_fusion.refs_0_), channel_id=1, source_target_pairs={{0,7},{1,6},{2,5},{3,4},{4,3},{5,2},{6,1},{7,0},{8,15},{9,14},{10,... | collective-permute-start | bytes 98312 | tf_op jit(solution)/shard_map/ppermute | solution.py:327
  123.9 5.8 %collective-permute-start.25 = (f32[32,256]{1,0:T(8,128)S(1)}, f32[32,256]{1,0:T(8,128)S(1)}, u32[]{:S(2)}, u32[]{:S(2)}) collective-permute-start(f32[32,256]{1,0:T(8,128)S(1)} %add_add_fusion.refs_0_), channel_id=1, source_target_pairs={{0,6},{1,7},{2,4},{3,5},{4,2},{5,3},{6,0},{7,1},{8,14},{9,15},{10,... | collective-permute-start | bytes 98312 | tf_op jit(solution)/shard_map/ppermute | solution.py:327
  129.7 5.2 %collective-permute-start.23 = (f32[32,256]{1,0:T(8,128)S(1)}, f32[32,256]{1,0:T(8,128)S(1)}, u32[]{:S(2)}, u32[]{:S(2)}) collective-permute-start(f32[32,256]{1,0:T(8,128)S(1)} %add_add_fusion.refs_0_), channel_id=1, source_target_pairs={{0,4},{1,5},{2,6},{3,7},{4,0},{5,1},{6,2},{7,3},{8,12},{9,13},{10,... | collective-permute-start | bytes 98312 | tf_op jit(solution)/shard_map/ppermute | solution.py:327
  (12 other events, 66.2 us)

commit v2 on v1

--- a/solution.py
+++ b/solution.py
@@ -32,11 +32,21 @@
     return pl.BlockSpec(memory_space=memory_space)
 
 
-def pack_kernel(experts, capacity, me_ref, index_ref, region_ref, table_ref, target_ref, *refs):
-    blocks, place_ref, rows_ref = refs[:experts], refs[experts], refs[experts + 1]
+def pack_kernel(experts, capacity, me_ref, *refs):
+    sources, blocks, place_ref = refs[:4], refs[4 : 4 + experts], refs[4 + experts]
+    rows_ref, index_ref, region_ref, table_ref, target_ref, sems = refs[5 + experts :]
+    loads = [
+        pltpu.make_async_copy(source, held, sems.at[i])
+        for i, (source, held) in enumerate(
+            zip(sources, (index_ref, region_ref, table_ref, target_ref))
+        )
+    ]
+    for load in loads:
+        load.start()
     me = me_ref[0]
     groups = index_ref.shape[0]
     cells, width = table_ref.shape
+    loads[1].wait()
     expert_id = iota((experts, LANES), 0)
     starts = ((expert_id ^ me) * capacity).astype(F32)
     ahead = jnp.where(iota((LANES, LANES), 0) <= iota((LANES, LANES), 1), 1.0, 0.0).astype(BF16)
@@ -51,6 +61,9 @@
         place_ref[g : g + 1, :] = places[g].astype(jnp.int32)
     place = jnp.concatenate(places, axis=1)
 
+    loads[0].wait()
+    loads[2].wait()
+    loads[3].wait()
     step = 2
     cell_id = iota((LANES * step, LANES), 1).astype(F32)
     for g in range(0, groups, step):
@@ -85,10 +98,17 @@
         functools.partial(pack_kernel, experts, capacity),
         out_shape=[jax.ShapeDtypeStruct((capacity, 2 * width), BF16)] * experts
         + [jax.ShapeDtypeStruct((groups, LANES), jnp.int32)],
-        in_specs=[whole(pltpu.SMEM)] + [whole()] * 4,
+        in_specs=[whole(pltpu.SMEM)] + [whole(pltpu.HBM)] * 4,
         out_specs=[whole()] * (experts + 1),
-        scratch_shapes=[pltpu.VMEM((rows, 2 * width), BF16)],
-        compiler_params=pltpu.CompilerParams(vmem_limit_bytes=32 * MIB),
+        scratch_shapes=[
+            pltpu.VMEM((rows, 2 * width), BF16),
+            pltpu.VMEM((groups, LANES), jnp.int32),
+            pltpu.VMEM((groups, LANES), jnp.int32),
+            pltpu.VMEM(table.shape, BF16),
+            pltpu.VMEM(targets.shape, BF16),
+            pltpu.SemaphoreType.DMA((4,)),
+        ],
+        compiler_params=pltpu.CompilerParams(vmem_limit_bytes=58 * MIB),
         cost_estimate=pl.CostEstimate(
             flops=2 * rows * width * (table.shape[0] + 2 * experts * capacity),
             bytes_accessed=6 * MIB,
@@ -102,7 +122,7 @@
     return 0.5 * jnp.tanh(0.5 * v) + 0.5
 
 
-def expert_kernel(counts, first, last, *refs):
+def expert_kernel(counts, order, first, last, *refs):
     blocks, shares, experts, steps, step_rows = counts
     refs = list(refs)
 
@@ -120,11 +140,8 @@
         loss_refs = take(last - 1)
         (me_ref,) = take(1)
         (own_ref,) = take(1)
-        sent = take(shares - 1)
-        notes = take(experts)
-        part = trunk_part_rows(trunk_ref.shape[0], experts)
-        if not part:
-            (all_trunk_ref,) = take(1)
+        sent_up, sent_down = take(shares - 1), take(shares - 1)
+        kept_ref, note_ref = take(2)
     else:
         acc_ref, acc_trunk_ref, loss_ref = take(3)
     x_ref, hid_ref, slope_ref = take(3)
@@ -190,20 +207,28 @@
     if last:
         own_ref[...] = acc_ref[0]
         for j in range(1, shares):
-            sent[j - 1][...] = acc_ref[j].astype(BF16)
+            sent_up[j - 1][...] = acc_ref[j, 0].astype(BF16)
+            sent_down[j - 1][...] = acc_ref[j, 1].astype(BF16)
+        all_losses = list(loss_refs) + [loss_ref]
+        if not in_turns(experts):
+            kept_ref[...] = acc_trunk_ref[...]
+            for row in range(note_ref.shape[0]):
+                note_ref[row : row + 1, :] = loss_row(all_losses, row)
+            return
         me = me_ref[0]
-        if not part:
-            all_trunk_ref[...] = acc_trunk_ref[...]
+        part = width // experts
+        kept_ref[experts // 2 * part :, :] = jnp.zeros((8, width), F32)
+        note_ref[experts // 2 * part :, :] = jnp.zeros((8, width), F32)
         for s in range(experts):
-            if part:
-                mine = pl.ds(pl.multiple_of((me ^ s) * part, part), part)
-                notes[s][:part, :] = acc_trunk_ref[mine, :]
-            row = loss_row(list(loss_refs) + [loss_ref], s * block_rows // step_rows)
-            start = s * block_rows % step_rows
-            notes[s][part:, :] = jnp.zeros((8, width), F32)
-            notes[s][part:, :block_rows] = jnp.broadcast_to(
-                row[:, start : start + block_rows], (8, block_rows)
-            )
+            ref = note_ref if s % 2 else kept_ref
+            mine = pl.ds(pl.multiple_of((me ^ s) * part, part), part)
+            ref[s // 2 * part : (s // 2 + 1) * part, :] = acc_trunk_ref[mine, :]
+            at = experts // 2 * part + s // 2
+            ref[at : at + 1, :] = loss_row(all_losses, order.index(s))
+
+
+def in_turns(experts):
+    return experts == 8
 
 
 def loss_row(refs, row):
@@ -213,7 +238,8 @@
         row -= ref.shape[0]
 
 
-def expert_call(xs, trunk_weight, weights, prior, losses, me, experts, last):
+def expert_call(xs, trunk_weight, weights, prior, losses, me, order, last):
+    experts = len(order)
     block_rows = xs[0].shape[0]
     width = trunk_weight.shape[0]
     shares = len(weights)
@@ -238,17 +264,20 @@
         args += list(losses) + [me]
         in_specs += [whole()] * len(losses) + [whole(pltpu.SMEM)]
         outs = [jax.ShapeDtypeStruct((2, width, share), F32)]
-        outs += [jax.ShapeDtypeStruct((2, width, share), BF16)] * (shares - 1)
-        part = trunk_part_rows(width, experts)
-        outs += [jax.ShapeDtypeStruct((part + 8, width), F32)] * experts
-        if not part:
-            outs += [acc_trunk]
+        outs += [jax.ShapeDtypeStruct((width, share), BF16)] * (2 * (shares - 1))
+        if in_turns(experts):
+            outs += [jax.ShapeDtypeStruct((width // 2 + 8, width), F32)] * 2
+        else:
+            outs += [
+                acc_trunk,
+                jax.ShapeDtypeStruct((experts * block_rows // step_rows, step_rows), F32),
+            ]
         scratch += [pltpu.VMEM(a.shape, a.dtype) for a in (acc, acc_trunk, loss)]
     else:
         outs = [acc, acc_trunk, loss]
     counts = (len(xs), shares, experts, steps, step_rows)
     return pl.pallas_call(
-        functools.partial(expert_kernel, counts, first, len(losses) + 1 if last else 0),
+        functools.partial(expert_kernel, counts, order, first, len(losses) + 1 if last else 0),
         out_shape=outs,
         in_specs=in_specs,
         out_specs=[whole()] * len(outs),
@@ -263,15 +292,60 @@
     )(*args)
 
 
-def finish_kernel(experts, me_ref, place_ref, loss_ref, *refs):
-    *parts, row_loss_ref, trunk_ref = refs
-    me = me_ref[0]
-    part = parts[0].shape[0]
-    if len(parts) == 1:
-        trunk_ref[...] = parts[0][...]
-    for s in range(len(parts) if len(parts) > 1 else 0):
-        trunk_ref[pl.ds(pl.multiple_of((me ^ s) * part, part), part), :] = parts[s][...]
-    capacity = loss_ref.shape[1]
+def turn_one_kernel(part, kept_ref, got_ref, next_ref, note_ref):
+    for s in range(4):
+        ref, k = (note_ref, s // 2) if s % 2 else (next_ref, s // 2)
+        at = slice(s * part, (s + 1) * part)
+        ref[k * part : (k + 1) * part, :] = kept_ref[at, :] + got_ref[at, :]
+    lost = kept_ref[4 * part :, :]
+    found = got_ref[4 * part :, :]
+    for ref, first in ((next_ref, 0), (note_ref, 1)):
+        ref[2 * part :, :] = jnp.concatenate(
+            [
+                lost[first : first + 1],
+                found[first : first + 1],
+                lost[first + 2 : first + 3],
+                found[first + 2 : first + 3],
+                jnp.zeros((4, lost.shape[1]), F32),
+            ],
+            axis=0,
+        )
+
+
+def turn_two_kernel(part, kept_ref, got_ref, next_ref, note_ref):
+    next_ref[:part, :] = kept_ref[:part, :] + got_ref[:part, :]
+    note_ref[:part, :] = kept_ref[part : 2 * part, :] + got_ref[part : 2 * part, :]
+    lost = kept_ref[2 * part :, :]
+    found = got_ref[2 * part :, :]
+    for ref, first in ((next_ref, 0), (note_ref, 2)):
+        ref[part:, :] = jnp.concatenate(
+            [
+                lost[first : first + 2],
+                found[first : first + 2],
+                jnp.zeros((4, lost.shape[1]), F32),
+            ],
+            axis=0,
+        )
+
+
+def turn_three_kernel(part, kept_ref, got_ref, sum_ref, loss_ref):
+    sum_ref[...] = kept_ref[:part, :] + got_ref[:part, :]
+    loss_ref[...] = jnp.concatenate([kept_ref[part : part + 4, :], got_ref[part : part + 4, :]], axis=0)
+
+
+def turn(kernel, kept, got, part, shapes, name):
+    return pl.pallas_call(
+        functools.partial(kernel, part),
+        out_shape=[jax.ShapeDtypeStruct((rows, kept.shape[1]), F32) for rows in shapes],
+        in_specs=[whole()] * 2,
+        out_specs=[whole()] * 2,
+        compiler_params=pltpu.CompilerParams(vmem_limit_bytes=4 * MIB),
+        name=name,
+    )(kept, got)
+
+
+def row_loss_kernel(place_ref, loss_ref, row_loss_ref):
+    experts, capacity = loss_ref.shape
     loss = loss_ref[...]
     for g in range(place_ref.shape[0]):
         place = place_ref[g : g + 1, :]
@@ -289,20 +363,48 @@
         row_loss_ref[g : g + 1, :] = jnp.sum(mine, axis=0, keepdims=True)
 
 
-def finish(me, place, loss, parts):
-    experts = loss.shape[0]
-    part, width = parts[0].shape
+def loss_by_row(place, loss):
     return pl.pallas_call(
-        functools.partial(finish_kernel, experts),
-        out_shape=[
-            jax.ShapeDtypeStruct(place.shape, F32),
-            jax.ShapeDtypeStruct((len(parts) * part, width), F32),
-        ],
-        in_specs=[whole(pltpu.SMEM)] + [whole()] * (len(parts) + 2),
-        out_specs=[whole()] * 2,
+        row_loss_kernel,
+        out_shape=jax.ShapeDtypeStruct(place.shape, F32),
+        in_specs=[whole()] * 2,
+        out_specs=whole(),
         compiler_params=pltpu.CompilerParams(vmem_limit_bytes=16 * MIB),
-        name="finish_rows",
-    )(me, place, loss, *parts)
+        name="row_loss",
+    )(place, loss)
+
+
+def assemble_kernel(part, me_ref, *refs):
+    *held, trunk_ref = refs
+    me = me_ref[0]
+    order = iter((0, 4, 2, 6, 1, 5, 3, 7))
+    for ref in held:
+        for k in range(ref.shape[0] // part):
+            at = pl.ds(pl.multiple_of((me ^ next(order)) * part, part), part)
+            trunk_ref[at, :] = ref[k * part : (k + 1) * part, :]
+
+
+def assemble(me, held, part):
+    width = held[0].shape[1]
+    return pl.pallas_call(
+        functools.partial(assemble_kernel, part),
+        out_shape=jax.ShapeDtypeStruct((8 * part, width), F32),
+        in_specs=[whole(pltpu.SMEM)] + [whole()] * len(held),
+        out_specs=whole(),
+        compiler_params=pltpu.CompilerParams(vmem_limit_bytes=4 * MIB),
+        name="assemble_trunk",
+    )(me, *held)
+
+
+def after(value, *others):
+    return pl.pallas_call(
+        lambda *refs: None,
+        out_shape=jax.ShapeDtypeStruct(value.shape, value.dtype),
+        in_specs=[whole(pl.ANY)] * (1 + len(others)),
+        out_specs=whole(pl.ANY),
+        input_output_aliases={0: 0},
+        name="in_order",
+    )(value, *others)
 
 
 def adam_update(params, first, second, grads):
@@ -315,10 +417,6 @@
         first_new,
         second_new,
     )
-
-
-def trunk_part_rows(width, experts):
-    return 0 if width % (8 * experts) else width // experts
 
 
 def swap(value, axis, s):
@@ -347,34 +445,68 @@
     rounded = expert_params[0].astype(BF16)
     weights = [swap(rounded, "dp", j) for j in range(replicas)]
     *blocks, place = pack(me, sample_index, region[:, 0], cell_table, targets, experts, capacity)
-    arrived = [swap(blocks[s], "expert", s) for s in range(experts)]
-
-    cuts = [0, experts // 2, 3 * experts // 4, 7 * experts // 8, experts]
+    arrived = list(blocks)
+    if in_turns(experts) and replicas == 4:
+        for s in (4, 6):
+            arrived[s] = swap(blocks[s], "expert", s)
+        for s, ahead in (
+            (5, weights[1]),
+            (7, weights[2]),
+            (2, weights[3]),
+            (3, arrived[4]),
+            (1, arrived[6]),
+        ):
+            arrived[s] = swap(after(blocks[s], ahead), "expert", s)
+        batches = ((0, 4, 6), (1, 2, 3), (5,), (7,))
+    else:
+        arrived = [swap(blocks[s], "expert", s) for s in range(experts)]
+        batches = (range(experts // 2), range(experts // 2, experts))
+
+    order = [s for batch in batches for s in batch]
     prior, losses = None, []
-    for k in range(len(cuts) - 1):
-        xs = arrived[cuts[k] : cuts[k + 1]]
-        last = k == len(cuts) - 2
-        outs = expert_call(xs, trunk_weight, weights, prior, losses, me, experts, last)
+    for k, batch in enumerate(batches):
+        last = k == len(batches) - 1
+        outs = expert_call(
+            [arrived[s] for s in batch], trunk_weight, weights, prior, losses, me, order, last
+        )
         if not last:
             prior = outs[:2]
             losses.append(outs[2])
-    grads = outs[0]
-    sent = outs[1:replicas]
-    notes = outs[replicas : replicas + experts]
-
-    back = [swap(notes[s], "expert", s) for s in range(experts)]
-    part = trunk_part_rows(width, experts)
-    if part:
-        trunk_part = sum(note[:part] for note in back)
-        trunk_part = sum(swap(trunk_part, "dp", j) for j in range(replicas))
-        parts = [swap(trunk_part, "expert", s) for s in range(experts)]
+    grads, sent_up, sent_down = outs[0], outs[1:replicas], outs[replicas : 2 * replicas - 1]
+    kept, note = outs[-2:]
+
+    part = width // experts
+    downs = [swap(sent_down[j - 1], "dp", j) for j in range(1, replicas)]
+    if in_turns(experts):
+        kept, note = turn(
+            turn_one_kernel, kept, swap(note, "expert", 1), part, (2 * part + 8,) * 2, "turn_one"
+        )
+        kept, note = turn(
+            turn_two_kernel, kept, swap(note, "expert", 2), part, (part + 8,) * 2, "turn_two"
+        )
+        total, loss = turn(
+            turn_three_kernel, kept, swap(note, "expert", 4), part, (part, experts), "turn_three"
+        )
+        others = [swap(total, "dp", j) for j in range(1, replicas)]
+        sent_up = [after(value, *others) for value in sent_up]
+        if replicas == 4:
+            total = (total + others[0]) + (others[1] + others[2])
+        else:
+            total = total + sum(others)
+        held = [total]
+        for s in (4, 2, 1):
+            message = held[0] if len(held) == 1 else jnp.concatenate(held, axis=0)
+            held.append(swap(message, "expert", s))
+        trunk_grad = assemble(me, held, part)
     else:
-        parts = [lax.psum(outs[-1], ("dp", "expert"))]
-    loss = jnp.concatenate([note[part : part + 1, :capacity] for note in back], axis=0)
-    row_loss, trunk_grad = finish(me, place, loss, parts)
-
-    for j in range(1, replicas):
-        grads = grads + swap(sent[j - 1], "dp", j).astype(F32)
+        trunk_grad = lax.psum(kept, ("dp", "expert"))
+        mine = jnp.arange(experts, dtype=jnp.int32) ^ me
+        note = note.reshape(experts, capacity)
+        loss = lax.all_to_all(note[mine], "expert", split_axis=0, concat_axis=0, tiled=True)[mine]
+    row_loss = loss_by_row(place, loss)
+    ups = [swap(sent_up[j - 1], "dp", j) for j in range(1, replicas)]
+
+    grads = grads + sum(jnp.stack([u, d]).astype(F32) for u, d in zip(ups, downs))
     new_params, new_first, new_second = adam_update(
         expert_params, first_moment, second_moment, grads[None]
     )

time: 145 us -> 137 us (0.945)
  starting transfers between devices: 34.8 us -> 26.6 us
  waiting for transfers between devices: 69.1 us -> 60.9 us
  local copies, waits for them, and re-layouts: 3.69 us -> 8.87 us
  Pallas kernels: 31.6 us -> 34.3 us
    ppermute x30 -> x25, waiting for transfers between devices: 69.1 us -> 60.9 us  [swap(): lax.ppermute(value, axis, [(i, i ^ s) for i in range(lax.axis_size(axis))])]
    ppermute x30 -> x25, starting transfers between devices: 34.8 us -> 26.6 us  [swap(): lax.ppermute(value, axis, [(i, i ^ s) for i in range(lax.axis_size(axis))])]
    unnamed x12 -> x42, local copies, waits for them, and re-layouts: 3.64 us -> 8.87 us
    pallas_call x1, Pallas kernels: 3.52 us -> 5.59 us  [pack(): pl.pallas_call(functools.partial(pack_kernel, experts, capacity), out_sha...]
    pallas_call x5 -> x17, Pallas kernels: 28 us -> 28.8 us  [the longest x4 26.8 us: expert_call(): pl.pallas_call(functools.partial(expert_kernel, counts, order, first, len...]
  transfers between devices with their start and end apart: 30 -> 25, of which waited for: 13 -> 12; matrix products, arithmetic and copies ran while one was open for 0% -> 0% of each run, Pallas kernels for 17% -> 23%
where the time goes in v2:
time: 137 us
  waiting for transfers between devices  60.9 us (44%)
  Pallas kernels  34.3 us (25%)
  starting transfers between devices  26.6 us (19%)
  local copies, waits for them, and re-layouts  8.87 us (6%)
  other arithmetic  5.48 us (4%)
    ppermute x25, waiting for transfers between devices, swap(): lax.ppermute(value, axis, [(i, i ^ s) for i in range(lax.axis_size(axis))])  60.9 us
    pallas_call x4, Pallas kernels, expert_call(): pl.pallas_call(functools.partial(expert_kernel, counts, order, first, len...  26.8 us
    ppermute x25, starting transfers between devices, swap(): lax.ppermute(value, axis, [(i, i ^ s) for i in range(lax.axis_size(axis))])  26.6 us
    unnamed x42, local copies, waits for them, and re-layouts  8.87 us
    pallas_call x1, Pallas kernels, pack(): pl.pallas_call(functools.partial(pack_kernel, experts, capacity), out_sha...  5.59 us
    sub x1, other arithmetic, adam_update(): params - learn_rate * first_hat / (jnp.sqrt(second_hat) + adam_eps)  4.16 us
  transfers between devices with their start and end apart: 25, of which 12 were waited for; matrix products, arithmetic and copies ran while one was open for 0% of the time, Pallas kernels for 23%

profile of v2, /device:TPU:0, one launch (start us, length us, event | category | flops | bytes accessed | tf_op | source)
XLA Modules:
  0.0 137.0 jit_solution(9719829013806921909)
XLA Ops:
  1.9 4.0 %collective-permute-start.3 = (bf16[2,256,512]{2,1,0:T(8,128)(2,1)S(1)}, bf16[2,256,512]{2,1,0:T(8,128)(2,1)S(1)}, u32[]{:S(2)}, u32[]{:S(2)}) collective-permute-start(bf16[2,256,512]{2,1,0:T(8,128)(2,1)S(1)} %convert_bitcast_fusion.refs_4_.refs_2_), channel_id=1, source_target_pairs={{0,24},{8,16},{16,8},{24,0},{1,25},{9,17},{17,9},{25,1},{2,26},{10... | collective-permute-start | bytes 1572872 | tf_op jit(solution)/shard_map/ppermute | solution.py:425
  6.5 5.6 %pack_rows.1 = (bf16[256,512]{1,0:T(8,128)(2,1)}, bf16[256,512]{1,0:T(8,128)(2,1)}, bf16[256,512]{1,0:T(8,128)(2,1)}, bf16[256,512]{1,0:T(8,128)(2,1)}, bf16[256...) custom-call(s32[1]{0:T(128)} %bitcast.me_ref.refs_11_, ...), custom_call_target="tpu_custom_call" | custom-call | flops 3221225472 | bytes 6291456 | tf_op jit(solution)/shard_map/pack_rows/pallas_call | solution.py:97
  12.1 4.1 %collective-permute-start.5 = (bf16[256,512]{1,0:T(8,128)(2,1)}, bf16[256,512]{1,0:T(8,128)(2,1)S(1)}, u32[]{:S(2)}, u32[]{:S(2)}) collective-permute-start(bf16[256,512]{1,0:T(8,128)(2,1)} %get-tuple-element.41), channel_id=1, source_target_pairs={{0,6},{1,7},{2,4},{3,5},{4,2},{5,3},{6,0},{7,1},{8,14},{9,15},{10,... | collective-permute-start | bytes 786440 | tf_op jit(solution)/shard_map/ppermute | solution.py:425
  16.2 7.5 %collective-permute-done.5.refs_1_.refs_2_ = bf16[256,512]{1,0:T(8,128)(2,1)S(1)} collective-permute-done((bf16[256,512]{1,0:T(8,128)(2,1)}, bf16[256,512]{1,0:T(8,128)(2,1)S(1)}, u32[]{:S(2)}, u32[]{:S(2)}) %collective-permute-start.5) | collective-permute-done | bytes 262176 | tf_op jit(solution)/shard_map/ppermute | solution.py:425
  24.4 13.5 %collective-permute-done.8.refs_1_ = bf16[256,512]{1,0:T(8,128)(2,1)S(1)} collective-permute-done((bf16[256,512]{1,0:T(8,128)(2,1)}, bf16[256,512]{1,0:T(8,128)(2,1)S(1)}, u32[]{:S(2)}, u32[]{:S(2)}) %collective-permute-start.8) | collective-permute-done | bytes 262176 | tf_op jit(solution)/shard_map/ppermute | solution.py:425
  40.9 2.0 %collective-permute-start.4 = (bf16[256,512]{1,0:T(8,128)(2,1)}, bf16[256,512]{1,0:T(8,128)(2,1)S(1)}, u32[]{:S(2)}, u32[]{:S(2)}) collective-permute-start(bf16[256,512]{1,0:T(8,128)(2,1)} %in_order.9), channel_id=1, source_target_pairs={{0,5},{1,4},{2,7},{3,6},{4,1},{5,0},{6,3},{7,2},{8,13},{9,12},{10,... | collective-permute-start | bytes 786440 | tf_op jit(solution)/shard_map/ppermute | solution.py:425
  50.2 10.1 %expert_rows.4 = (f32[4,2,256,512]{3,2,1,0:T(8,128)S(1)}, f32[256,256]{1,0:T(8,128)S(1)}, f32[3,256]{1,0:T(4,128)S(1)}) custom-call(bf16[256,512]{1,0:T(8,128)(2,1)S(1)} %copy-done.16, bf16[256,512]{1,0:T(8,128)(2,1)S(1)} %copy-done.11, bf16[256,512]{1,0:T(8,128)(2,1)S(1)} %copy-done.9, bf16[256,256]{1,0:T(8,128)(2,1)S(1)} %copy-done.7, ...), custom_call_target="tpu_custom_call" | custom-call | flops 4831838208 | bytes 10485760 | tf_op jit(solution)/shard_map/expert_rows/pallas_call | solution.py:279
  60.3 10.2 %expert_rows.5 = (f32[4,2,256,512]{3,2,1,0:T(8,128)S(1)}, f32[256,256]{1,0:T(8,128)S(1)}, f32[3,256]{1,0:T(4,128)S(1)}) custom-call(bf16[256,512]{1,0:T(8,128)(2,1)S(1)} %collective-permute-done.6.refs_0_, bf16[256,512]{1,0:T(8,128)(2,1)S(1)} %collective-permute-done.7.refs_1_, bf16[256,512]{1,0:T(8,128)(2,1)S(1)} %collective-permute-done.9.refs_2_, ...), custom_call_target="tpu_custom_call" | custom-call | flops 4831838208 | bytes 10485760 | tf_op jit(solution)/shard_map/expert_rows/pallas_call | solution.py:279
  70.6 3.2 %expert_rows.6 = (f32[4,2,256,512]{3,2,1,0:T(8,128)S(1)}, f32[256,256]{1,0:T(8,128)S(1)}, f32[1,256]{1,0:T(1,128)S(1)}) custom-call(bf16[256,512]{1,0:T(8,128)(2,1)S(1)} %collective-permute-done.4.refs_0_, bf16[256,256]{1,0:T(8,128)(2,1)S(1)} %copy-done.7, bf16[2,256,512]{2,1,0:T(8,128)(2,1)S(1)} %convert_bitcast_fusion.refs_4_.refs_2_, ...), custom_call_target="tpu_custom_call" | custom-call | flops 1610612736 | bytes 10485760 | tf_op jit(solution)/shard_map/expert_rows/pallas_call | solution.py:279
  73.8 3.3 %expert_rows.7 = (f32[2,256,512]{2,1,0:T(8,128)S(1)}, bf16[256,512]{1,0:T(8,128)(2,1)S(1)}, bf16[256,512]{1,0:T(8,128)(2,1)S(1)}, bf16[256,512]{1,0:T(8,128)(2,1...) custom-call(bf16[256,512]{1,0:T(8,128)(2,1)S(1)} %collective-permute, ...), custom_call_target="tpu_custom_call" | custom-call | flops 1610612736 | bytes 10485760 | tf_op jit(solution)/shard_map/expert_rows/pallas_call | solution.py:279
  79.2 3.8 %collective-permute-done.11.got_ref = f32[72,256]{1,0:T(8,128)S(1)} collective-permute-done((f32[72,256]{1,0:T(8,128)S(1)}, f32[72,256]{1,0:T(8,128)S(1)}, u32[]{:S(2)}, u32[]{:S(2)}) %collective-permute-start.11) | collective-permute-done | bytes 73760 | tf_op jit(solution)/shard_map/ppermute | solution.py:425
  83.0 1.8 %collective-permute-start.12 = (f32[40,256]{1,0:T(8,128)S(1)}, f32[40,256]{1,0:T(8,128)S(1)}, u32[]{:S(2)}, u32[]{:S(2)}) collective-permute-start(f32[40,256]{1,0:T(8,128)S(1)} %get-tuple-element.60), channel_id=1, source_target_pairs={{0,4},{1,5},{2,6},{3,7},{4,0},{5,1},{6,2},{7,3},{8,12},{9,13},{10,... | collective-permute-start | bytes 122888 | tf_op jit(solution)/shard_map/ppermute | solution.py:425
  84.8 3.6 %collective-permute-done.12.got_ref = f32[40,256]{1,0:T(8,128)S(1)} collective-permute-done((f32[40,256]{1,0:T(8,128)S(1)}, f32[40,256]{1,0:T(8,128)S(1)}, u32[]{:S(2)}, u32[]{:S(2)}) %collective-permute-start.12) | collective-permute-done | bytes 40992 | tf_op jit(solution)/shard_map/ppermute | solution.py:425
  88.4 2.5 %collective-permute-start.15 = (f32[32,256]{1,0:T(8,128)S(1)}, f32[32,256]{1,0:T(8,128)S(1)}, u32[]{:S(2)}, u32[]{:S(2)}) collective-permute-start(f32[32,256]{1,0:T(8,128)S(1)} %get-tuple-element.61), channel_id=1, source_target_pairs={{0,24},{8,16},{16,8},{24,0},{1,25},{9,17},{17,9},{25,1},{2,26},{10... | collective-permute-start | bytes 98312 | tf_op jit(solution)/shard_map/ppermute | solution.py:425
  91.0 3.1 %collective-permute-start.14 = (f32[32,256]{1,0:T(8,128)S(1)}, f32[32,256]{1,0:T(8,128)S(1)}, u32[]{:S(2)}, u32[]{:S(2)}) collective-permute-start(f32[32,256]{1,0:T(8,128)S(1)} %get-tuple-element.61), channel_id=1, source_target_pairs={{0,16},{8,24},{16,0},{24,8},{1,17},{9,25},{17,1},{25,9},{2,18},{10... | collective-permute-start | bytes 98312 | tf_op jit(solution)/shard_map/ppermute | solution.py:425
  94.1 1.9 %collective-permute-done.14.refs_2_ = f32[32,256]{1,0:T(8,128)S(1)} collective-permute-done((f32[32,256]{1,0:T(8,128)S(1)}, f32[32,256]{1,0:T(8,128)S(1)}, u32[]{:S(2)}, u32[]{:S(2)}) %collective-permute-start.14) | collective-permute-done | bytes 32800 | tf_op jit(solution)/shard_map/ppermute | solution.py:425
  95.9 2.0 %collective-permute-done.13.refs_1_ = f32[32,256]{1,0:T(8,128)S(1)} collective-permute-done((f32[32,256]{1,0:T(8,128)S(1)}, f32[32,256]{1,0:T(8,128)S(1)}, u32[]{:S(2)}, u32[]{:S(2)}) %collective-permute-start.13) | collective-permute-done | bytes 32800 | tf_op jit(solution)/shard_map/ppermute | solution.py:425
  98.0 4.8 %collective-permute-done.16.refs_1_ = f32[32,256]{1,0:T(8,128)S(1)} collective-permute-done((f32[32,256]{1,0:T(8,128)S(1)}, f32[32,256]{1,0:T(8,128)S(1)}, u32[]{:S(2)}, u32[]{:S(2)}) %collective-permute-start.16) | collective-permute-done | bytes 32800 | tf_op jit(solution)/shard_map/ppermute | solution.py:425
  103.1 4.1 %collective-permute-done.17.refs_2_ = f32[64,256]{1,0:T(8,128)S(1)} collective-permute-done((f32[64,256]{1,0:T(8,128)S(1)}, f32[64,256]{1,0:T(8,128)S(1)}, u32[]{:S(2)}, u32[]{:S(2)}) %collective-permute-start.17) | collective-permute-done | bytes 65568 | tf_op jit(solution)/shard_map/ppermute | solution.py:425
  107.4 1.5 %collective-permute-start.24 = (bf16[256,512]{1,0:T(8,128)(2,1)S(1)}, bf16[256,512]{1,0:T(8,128)(2,1)}, u32[]{:S(2)}, u32[]{:S(2)}) collective-permute-start(bf16[256,512]{1,0:T(8,128)(2,1)S(1)} %get-tuple-element.70), channel_id=1, source_target_pairs={{0,24},{8,16},{16,8},{24,0},{1,25},{9,17},{17,9},{25,1},{2,26},{10... | collective-permute-start | bytes 786440 | tf_op jit(solution)/shard_map/ppermute | solution.py:425
  108.9 2.0 %collective-permute-start.19 = (bf16[256,512]{1,0:T(8,128)(2,1)}, bf16[256,512]{1,0:T(8,128)(2,1)}, u32[]{:S(2)}, u32[]{:S(2)}) collective-permute-start(bf16[256,512]{1,0:T(8,128)(2,1)} %in_order.13), channel_id=1, source_target_pairs={{0,8},{8,0},{16,24},{24,16},{1,9},{9,1},{17,25},{25,17},{2,10},{10... | collective-permute-start | bytes 786440 | tf_op jit(solution)/shard_map/ppermute | solution.py:425
  114.4 7.8 %collective-permute-done.22 = bf16[256,512]{1,0:T(8,128)(2,1)} collective-permute-done((bf16[256,512]{1,0:T(8,128)(2,1)S(1)}, bf16[256,512]{1,0:T(8,128)(2,1)}, u32[]{:S(2)}, u32[]{:S(2)}) %collective-permute-start.22) | collective-permute-done | bytes 262176 | tf_op jit(solution)/shard_map/ppermute | solution.py:425
  123.7 9.1 %collective-permute-done.21 = bf16[256,512]{1,0:T(8,128)(2,1)S(1)} collective-permute-done((bf16[256,512]{1,0:T(8,128)(2,1)}, bf16[256,512]{1,0:T(8,128)(2,1)S(1)}, u32[]{:S(2)}, u32[]{:S(2)}) %collective-permute-start.21) | collective-permute-done | bytes 262176 | tf_op jit(solution)/shard_map/ppermute | solution.py:425
  132.9 4.2 %divide_subtract_fusion = (f32[1,2,256,512]{3,2,1,0:T(8,128)}, f32[1,2,256,512]{3,2,1,0:T(8,128)}, f32[1,2,256,512]{3,2,1,0:T(8,128)}) fusion(f32[1,2,256,512]{3,2,1,0:T(8,128)S(1)} %copy-done.17, f32[2,256,512]{2,1,0:T(8,128)S(1)} %get-tuple-element.64, bf16[1,256,512]{2,1,0:T(8,128)(2,1)} %bitcast.10, bf16[1,256,512]{2,1,0:T(8,128)(2,1)S(1)} %bitcast.21, ...), kind=kLoop, calls=%fused_computation.4 | loop fusion | flops 5505024 | bytes 8912896 | tf_op jit(solution)/shard_map/sub | solution.py:416
  (91 shorter events, 20.6 us)
Async XLA Ops:
  1.9 36.7 %collective-permute-start.3 = (bf16[2,256,512]{2,1,0:T(8,128)(2,1)S(1)}, bf16[2,256,512]{2,1,0:T(8,128)(2,1)S(1)}, u32[]{:S(2)}, u32[]{:S(2)}) collective-permute-start(bf16[2,256,512]{2,1,0:T(8,128)(2,1)S(1)} %convert_bitcast_fusion.refs_4_.refs_2_), channel_id=1, source_target_pairs={{0,24},{8,16},{16,8},{24,0},{1,25},{9,17},{17,9},{25,1},{2,26},{10... | collective-permute-start | bytes 1572872 | tf_op jit(solution)/shard_map/ppermute | solution.py:425
  5.9 34.3 %collective-permute-start.2 = (bf16[2,256,512]{2,1,0:T(8,128)(2,1)S(1)}, bf16[2,256,512]{2,1,0:T(8,128)(2,1)S(1)}, u32[]{:S(2)}, u32[]{:S(2)}) collective-permute-start(bf16[2,256,512]{2,1,0:T(8,128)(2,1)S(1)} %convert_bitcast_fusion.refs_4_.refs_2_), channel_id=1, source_target_pairs={{0,8},{8,0},{16,24},{24,16},{1,9},{9,1},{17,25},{25,17},{2,10},{10... | collective-permute-start | bytes 1572872 | tf_op jit(solution)/shard_map/ppermute | solution.py:425
  6.4 36.5 %collective-permute-start = (bf16[2,256,512]{2,1,0:T(8,128)(2,1)S(1)}, bf16[2,256,512]{2,1,0:T(8,128)(2,1)S(1)}, u32[]{:S(2)}, u32[]{:S(2)}) collective-permute-start(bf16[2,256,512]{2,1,0:T(8,128)(2,1)S(1)} %convert_bitcast_fusion.refs_4_.refs_2_), channel_id=1, source_target_pairs={{0,16},{8,24},{16,0},{24,8},{1,17},{9,25},{17,1},{25,9},{2,18},{10... | collective-permute-start | bytes 1572872 | tf_op jit(solution)/shard_map/ppermute | solution.py:425
  12.1 11.6 %collective-permute-start.5 = (bf16[256,512]{1,0:T(8,128)(2,1)}, bf16[256,512]{1,0:T(8,128)(2,1)S(1)}, u32[]{:S(2)}, u32[]{:S(2)}) collective-permute-start(bf16[256,512]{1,0:T(8,128)(2,1)} %get-tuple-element.41), channel_id=1, source_target_pairs={{0,6},{1,7},{2,4},{3,5},{4,2},{5,3},{6,0},{7,1},{8,14},{9,15},{10,... | collective-permute-start | bytes 786440 | tf_op jit(solution)/shard_map/ppermute | solution.py:425
  16.2 21.7 %collective-permute-start.8 = (bf16[256,512]{1,0:T(8,128)(2,1)}, bf16[256,512]{1,0:T(8,128)(2,1)S(1)}, u32[]{:S(2)}, u32[]{:S(2)}) collective-permute-start(bf16[256,512]{1,0:T(8,128)(2,1)} %get-tuple-element.44), channel_id=1, source_target_pairs={{0,4},{1,5},{2,6},{3,7},{4,0},{5,1},{6,2},{7,3},{8,12},{9,13},{10,... | collective-permute-start | bytes 786440 | tf_op jit(solution)/shard_map/ppermute | solution.py:425
  24.4 35.9 %collective-permute-start.6 = (bf16[256,512]{1,0:T(8,128)(2,1)}, bf16[256,512]{1,0:T(8,128)(2,1)S(1)}, u32[]{:S(2)}, u32[]{:S(2)}) collective-permute-start(bf16[256,512]{1,0:T(8,128)(2,1)} %in_order.10), channel_id=1, source_target_pairs={{0,1},{1,0},{2,3},{3,2},{4,5},{5,4},{6,7},{7,6},{8,9},{9,8},{10,11... | collective-permute-start | bytes 786440 | tf_op jit(solution)/shard_map/ppermute | solution.py:425
  38.6 21.7 %collective-permute-start.9 = (bf16[256,512]{1,0:T(8,128)(2,1)}, bf16[256,512]{1,0:T(8,128)(2,1)S(1)}, u32[]{:S(2)}, u32[]{:S(2)}) collective-permute-start(bf16[256,512]{1,0:T(8,128)(2,1)} %in_order.12), channel_id=1, source_target_pairs={{0,3},{1,2},{2,1},{3,0},{4,7},{5,6},{6,5},{7,4},{8,11},{9,10},{10,... | collective-permute-start | bytes 786440 | tf_op jit(solution)/shard_map/ppermute | solution.py:425
  39.4 20.9 %collective-permute-start.7 = (bf16[256,512]{1,0:T(8,128)(2,1)}, bf16[256,512]{1,0:T(8,128)(2,1)S(1)}, u32[]{:S(2)}, u32[]{:S(2)}) collective-permute-start(bf16[256,512]{1,0:T(8,128)(2,1)} %in_order.11), channel_id=1, source_target_pairs={{0,2},{1,3},{2,0},{3,1},{4,6},{5,7},{6,4},{7,5},{8,10},{9,11},{10,... | collective-permute-start | bytes 786440 | tf_op jit(solution)/shard_map/ppermute | solution.py:425
  40.9 29.6 %collective-permute-start.4 = (bf16[256,512]{1,0:T(8,128)(2,1)}, bf16[256,512]{1,0:T(8,128)(2,1)S(1)}, u32[]{:S(2)}, u32[]{:S(2)}) collective-permute-start(bf16[256,512]{1,0:T(8,128)(2,1)} %in_order.9), channel_id=1, source_target_pairs={{0,5},{1,4},{2,7},{3,6},{4,1},{5,0},{6,3},{7,2},{8,13},{9,12},{10,... | collective-permute-start | bytes 786440 | tf_op jit(solution)/shard_map/ppermute | solution.py:425
  43.8 30.1 %collective-permute-start.1 = (bf16[256,512]{1,0:T(8,128)(2,1)}, bf16[256,512]{1,0:T(8,128)(2,1)S(1)}, u32[]{:S(2)}, u32[]{:S(2)}) collective-permute-start(bf16[256,512]{1,0:T(8,128)(2,1)} %in_order.8), channel_id=1, source_target_pairs={{0,7},{1,6},{2,5},{3,4},{4,3},{5,2},{6,1},{7,0},{8,15},{9,14},{10,... | collective-permute-start | bytes 786440 | tf_op jit(solution)/shard_map/ppermute | solution.py:425
  78.6 4.4 %collective-permute-start.11 = (f32[72,256]{1,0:T(8,128)S(1)}, f32[72,256]{1,0:T(8,128)S(1)}, u32[]{:S(2)}, u32[]{:S(2)}) collective-permute-start(f32[72,256]{1,0:T(8,128)S(1)} %get-tuple-element.58), channel_id=1, source_target_pairs={{0,2},{1,3},{2,0},{3,1},{4,6},{5,7},{6,4},{7,5},{8,10},{9,11},{10,... | collective-permute-start | bytes 221192 | tf_op jit(solution)/shard_map/ppermute | solution.py:425
  83.0 5.4 %collective-permute-start.12 = (f32[40,256]{1,0:T(8,128)S(1)}, f32[40,256]{1,0:T(8,128)S(1)}, u32[]{:S(2)}, u32[]{:S(2)}) collective-permute-start(f32[40,256]{1,0:T(8,128)S(1)} %get-tuple-element.60), channel_id=1, source_target_pairs={{0,4},{1,5},{2,6},{3,7},{4,0},{5,1},{6,2},{7,3},{8,12},{9,13},{10,... | collective-permute-start | bytes 122888 | tf_op jit(solution)/shard_map/ppermute | solution.py:425
  88.4 5.6 %collective-permute-start.15 = (f32[32,256]{1,0:T(8,128)S(1)}, f32[32,256]{1,0:T(8,128)S(1)}, u32[]{:S(2)}, u32[]{:S(2)}) collective-permute-start(f32[32,256]{1,0:T(8,128)S(1)} %get-tuple-element.61), channel_id=1, source_target_pairs={{0,24},{8,16},{16,8},{24,0},{1,25},{9,17},{17,9},{25,1},{2,26},{10... | collective-permute-start | bytes 98312 | tf_op jit(solution)/shard_map/ppermute | solution.py:425
  91.0 5.0 %collective-permute-start.14 = (f32[32,256]{1,0:T(8,128)S(1)}, f32[32,256]{1,0:T(8,128)S(1)}, u32[]{:S(2)}, u32[]{:S(2)}) collective-permute-start(f32[32,256]{1,0:T(8,128)S(1)} %get-tuple-element.61), channel_id=1, source_target_pairs={{0,16},{8,24},{16,0},{24,8},{1,17},{9,25},{17,1},{25,9},{2,18},{10... | collective-permute-start | bytes 98312 | tf_op jit(solution)/shard_map/ppermute | solution.py:425
  94.0 3.9 %collective-permute-start.13 = (f32[32,256]{1,0:T(8,128)S(1)}, f32[32,256]{1,0:T(8,128)S(1)}, u32[]{:S(2)}, u32[]{:S(2)}) collective-permute-start(f32[32,256]{1,0:T(8,128)S(1)} %get-tuple-element.61), channel_id=1, source_target_pairs={{0,8},{8,0},{16,24},{24,16},{1,9},{9,1},{17,25},{25,17},{2,10},{10... | collective-permute-start | bytes 98312 | tf_op jit(solution)/shard_map/ppermute | solution.py:425
  98.0 4.9 %collective-permute-start.16 = (f32[32,256]{1,0:T(8,128)S(1)}, f32[32,256]{1,0:T(8,128)S(1)}, u32[]{:S(2)}, u32[]{:S(2)}) collective-permute-start(f32[32,256]{1,0:T(8,128)S(1)} %add_add_fusion.1.refs_0_), channel_id=1, source_target_pairs={{0,4},{1,5},{2,6},{3,7},{4,0},{5,1},{6,2},{7,3},{8,12},{9,13},{10,... | collective-permute-start | bytes 98312 | tf_op jit(solution)/shard_map/ppermute | solution.py:425
  102.9 4.3 %collective-permute-start.17 = (f32[64,256]{1,0:T(8,128)S(1)}, f32[64,256]{1,0:T(8,128)S(1)}, u32[]{:S(2)}, u32[]{:S(2)}) collective-permute-start(f32[64,256]{1,0:T(8,128)S(1)} %pad_maximum_fusion.1), channel_id=1, source_target_pairs={{0,2},{1,3},{2,0},{3,1},{4,6},{5,7},{6,4},{7,5},{8,10},{9,11},{10,... | collective-permute-start | bytes 196616 | tf_op jit(solution)/shard_map/ppermute | solution.py:425
  103.1 7.9 %collective-permute-start.20 = (bf16[256,512]{1,0:T(8,128)(2,1)S(1)}, bf16[256,512]{1,0:T(8,128)(2,1)}, u32[]{:S(2)}, u32[]{:S(2)}) collective-permute-start(bf16[256,512]{1,0:T(8,128)(2,1)S(1)} %get-tuple-element.66), channel_id=1, source_target_pairs={{0,8},{8,0},{16,24},{24,16},{1,9},{9,1},{17,25},{25,17},{2,10},{10... | collective-permute-start | bytes 786440 | tf_op jit(solution)/shard_map/ppermute | solution.py:425
  107.2 3.9 %collective-permute-start.18 = (f32[128,256]{1,0:T(8,128)S(1)}, f32[128,256]{1,0:T(8,128)S(1)}, u32[]{:S(2)}, u32[]{:S(2)}) collective-permute-start(f32[128,256]{1,0:T(8,128)S(1)} %pad_maximum_fusion), channel_id=1, source_target_pairs={{0,1},{1,0},{2,3},{3,2},{4,5},{5,4},{6,7},{7,6},{8,9},{9,8},{10,11... | collective-permute-start | bytes 393224 | tf_op jit(solution)/shard_map/ppermute | solution.py:425
  107.3 15.0 %collective-permute-start.22 = (bf16[256,512]{1,0:T(8,128)(2,1)S(1)}, bf16[256,512]{1,0:T(8,128)(2,1)}, u32[]{:S(2)}, u32[]{:S(2)}) collective-permute-start(bf16[256,512]{1,0:T(8,128)(2,1)S(1)} %get-tuple-element.68), channel_id=1, source_target_pairs={{0,16},{8,24},{16,0},{24,8},{1,17},{9,25},{17,1},{25,9},{2,18},{10... | collective-permute-start | bytes 786440 | tf_op jit(solution)/shard_map/ppermute | solution.py:425
  107.4 14.9 %collective-permute-start.24 = (bf16[256,512]{1,0:T(8,128)(2,1)S(1)}, bf16[256,512]{1,0:T(8,128)(2,1)}, u32[]{:S(2)}, u32[]{:S(2)}) collective-permute-start(bf16[256,512]{1,0:T(8,128)(2,1)S(1)} %get-tuple-element.70), channel_id=1, source_target_pairs={{0,24},{8,16},{16,8},{24,0},{1,25},{9,17},{17,9},{25,1},{2,26},{10... | collective-permute-start | bytes 786440 | tf_op jit(solution)/shard_map/ppermute | solution.py:425
  108.9 14.8 %collective-permute-start.19 = (bf16[256,512]{1,0:T(8,128)(2,1)}, bf16[256,512]{1,0:T(8,128)(2,1)}, u32[]{:S(2)}, u32[]{:S(2)}) collective-permute-start(bf16[256,512]{1,0:T(8,128)(2,1)} %in_order.13), channel_id=1, source_target_pairs={{0,8},{8,0},{16,24},{24,16},{1,9},{9,1},{17,25},{25,17},{2,10},{10... | collective-permute-start | bytes 786440 | tf_op jit(solution)/shard_map/ppermute | solution.py:425
  110.9 21.9 %collective-permute-start.21 = (bf16[256,512]{1,0:T(8,128)(2,1)}, bf16[256,512]{1,0:T(8,128)(2,1)S(1)}, u32[]{:S(2)}, u32[]{:S(2)}) collective-permute-start(bf16[256,512]{1,0:T(8,128)(2,1)} %in_order.14), channel_id=1, source_target_pairs={{0,16},{8,24},{16,0},{24,8},{1,17},{9,25},{17,1},{25,9},{2,18},{10... | collective-permute-start | bytes 786440 | tf_op jit(solution)/shard_map/ppermute | solution.py:425
  111.1 21.8 %collective-permute-start.23 = (bf16[256,512]{1,0:T(8,128)(2,1)}, bf16[256,512]{1,0:T(8,128)(2,1)S(1)}, u32[]{:S(2)}, u32[]{:S(2)}) collective-permute-start(bf16[256,512]{1,0:T(8,128)(2,1)} %in_order.15), channel_id=1, source_target_pairs={{0,24},{8,16},{16,8},{24,0},{1,25},{9,17},{17,9},{25,1},{2,26},{10... | collective-permute-start | bytes 786440 | tf_op jit(solution)/shard_map/ppermute | solution.py:425
  (22 other events, 300.5 us)

commit v3 on v2

--- a/solution.py
+++ b/solution.py
@@ -32,21 +32,11 @@
     return pl.BlockSpec(memory_space=memory_space)
 
 
-def pack_kernel(experts, capacity, me_ref, *refs):
-    sources, blocks, place_ref = refs[:4], refs[4 : 4 + experts], refs[4 + experts]
-    rows_ref, index_ref, region_ref, table_ref, target_ref, sems = refs[5 + experts :]
-    loads = [
-        pltpu.make_async_copy(source, held, sems.at[i])
-        for i, (source, held) in enumerate(
-            zip(sources, (index_ref, region_ref, table_ref, target_ref))
-        )
-    ]
-    for load in loads:
-        load.start()
+def pack_kernel(experts, capacity, me_ref, index_ref, region_ref, table_ref, target_ref, *refs):
+    blocks, place_ref, rows_ref = refs[:experts], refs[experts], refs[experts + 1]
     me = me_ref[0]
     groups = index_ref.shape[0]
     cells, width = table_ref.shape
-    loads[1].wait()
     expert_id = iota((experts, LANES), 0)
     starts = ((expert_id ^ me) * capacity).astype(F32)
     ahead = jnp.where(iota((LANES, LANES), 0) <= iota((LANES, LANES), 1), 1.0, 0.0).astype(BF16)
@@ -61,9 +51,6 @@
         place_ref[g : g + 1, :] = places[g].astype(jnp.int32)
     place = jnp.concatenate(places, axis=1)
 
-    loads[0].wait()
-    loads[2].wait()
-    loads[3].wait()
     step = 2
     cell_id = iota((LANES * step, LANES), 1).astype(F32)
     for g in range(0, groups, step):
@@ -98,17 +85,10 @@
         functools.partial(pack_kernel, experts, capacity),
         out_shape=[jax.ShapeDtypeStruct((capacity, 2 * width), BF16)] * experts
         + [jax.ShapeDtypeStruct((groups, LANES), jnp.int32)],
-        in_specs=[whole(pltpu.SMEM)] + [whole(pltpu.HBM)] * 4,
+        in_specs=[whole(pltpu.SMEM)] + [whole()] * 4,
         out_specs=[whole()] * (experts + 1),
-        scratch_shapes=[
-            pltpu.VMEM((rows, 2 * width), BF16),
-            pltpu.VMEM((groups, LANES), jnp.int32),
-            pltpu.VMEM((groups, LANES), jnp.int32),
-            pltpu.VMEM(table.shape, BF16),
-            pltpu.VMEM(targets.shape, BF16),
-            pltpu.SemaphoreType.DMA((4,)),
-        ],
-        compiler_params=pltpu.CompilerParams(vmem_limit_bytes=58 * MIB),
+        scratch_shapes=[pltpu.VMEM((rows, 2 * width), BF16)],
+        compiler_params=pltpu.CompilerParams(vmem_limit_bytes=32 * MIB),
         cost_estimate=pl.CostEstimate(
             flops=2 * rows * width * (table.shape[0] + 2 * experts * capacity),
             bytes_accessed=6 * MIB,
@@ -139,8 +119,7 @@
     if last:
         loss_refs = take(last - 1)
         (me_ref,) = take(1)
-        (own_ref,) = take(1)
-        sent_up, sent_down = take(shares - 1), take(shares - 1)
+        own_ref, next_up_ref, next_down_ref, sent_up_ref, sent_down_ref = take(5)
         kept_ref, note_ref = take(2)
     else:
         acc_ref, acc_trunk_ref, loss_ref = take(3)
@@ -153,15 +132,30 @@
     block_rows = xs[0].shape[0]
     for i, ref in enumerate(xs):
         x_ref[i * block_rows : (i + 1) * block_rows, :] = ref[...]
-    if first:
+    looped = steps > 3
+    if looped and first:
         acc_ref[...] = jnp.zeros(acc_ref.shape, F32)
         acc_trunk_ref[...] = jnp.zeros(acc_trunk_ref.shape, F32)
-    else:
+    elif looped:
         acc_ref[...] = prior_ref[...]
         acc_trunk_ref[...] = prior_trunk_ref[...]
 
+    def add(i, ref, source, at, value):
+        if looped or i > 0:
+            ref[at] += value
+        elif first:
+            ref[at] = value
+        else:
+            ref[at] = source[at] + value
+
+    prior = None if first else prior_ref
+    prior_trunk = None if first else prior_trunk_ref
+
     def step(i, carry):
-        at = pl.ds(pl.multiple_of(i * step_rows, step_rows), step_rows)
+        if looped:
+            at = pl.ds(pl.multiple_of(i * step_rows, step_rows), step_rows)
+        else:
+            at = slice(i * step_rows, (i + 1) * step_rows)
         feats = x_ref[at, :width]
         feats_f = feats.astype(F32)
         trunk_pre = dot(feats, trunk_ref[...])
@@ -192,23 +186,27 @@
         row_grad = jnp.zeros((step_rows, width), F32)
         for j in range(shares):
             part = slice(j * share, (j + 1) * share)
-            acc_ref[j, 1] += dot(scaled_t, hid_ref[:, part])
+            add(i, acc_ref, prior, (j, 1), dot(scaled_t, hid_ref[:, part]))
             pre = (dot(scaled, weights[j][1]) * slope_ref[:, part]).astype(BF16)
-            acc_ref[j, 0] += dot(out_t, pre)
+            add(i, acc_ref, prior, (j, 0), dot(out_t, pre))
             row_grad = row_grad + dot(pre, weights[j][0], 1, 1)
         slope = (row_grad.astype(BF16).astype(F32) * trunk_slope).astype(BF16)
-        acc_trunk_ref[...] += dot(feats_f.T.astype(BF16), slope)
+        add(i, acc_trunk_ref, prior_trunk, ..., dot(feats_f.T.astype(BF16), slope))
         return carry
 
-    if steps == 1:
-        step(0, 0)
+    if looped:
+        lax.fori_loop(0, steps, step, 0)
     else:
-        lax.fori_loop(0, steps, step, 0)
+        for i in range(steps):
+            step(i, 0)
     if last:
         own_ref[...] = acc_ref[0]
-        for j in range(1, shares):
-            sent_up[j - 1][...] = acc_ref[j, 0].astype(BF16)
-            sent_down[j - 1][...] = acc_ref[j, 1].astype(BF16)
+        next_up_ref[...] = acc_ref[2, 0]
+        next_down_ref[...] = acc_ref[1, 1]
+        for k, j in enumerate((1, 3)):
+            sent_up_ref[k] = acc_ref[j, 0].astype(BF16)
+        for k, j in enumerate((2, 3)):
+            sent_down_ref[k] = acc_ref[j, 1].astype(BF16)
         all_losses = list(loss_refs) + [loss_ref]
         if not in_turns(experts):
             kept_ref[...] = acc_trunk_ref[...]
@@ -264,7 +262,8 @@
         args += list(losses) + [me]
         in_specs += [whole()] * len(losses) + [whole(pltpu.SMEM)]
         outs = [jax.ShapeDtypeStruct((2, width, share), F32)]
-        outs += [jax.ShapeDtypeStruct((width, share), BF16)] * (2 * (shares - 1))
+        outs += [jax.ShapeDtypeStruct((width, share), F32)] * 2
+        outs += [jax.ShapeDtypeStruct((2, width, share), BF16)] * 2
         if in_turns(experts):
             outs += [jax.ShapeDtypeStruct((width // 2 + 8, width), F32)] * 2
         else:
@@ -312,36 +311,54 @@
         )
 
 
-def turn_two_kernel(part, kept_ref, got_ref, next_ref, note_ref):
-    next_ref[:part, :] = kept_ref[:part, :] + got_ref[:part, :]
-    note_ref[:part, :] = kept_ref[part : 2 * part, :] + got_ref[part : 2 * part, :]
+def turn_two_kernel(part, kept_ref, got_ref, both_ref):
+    both_ref[: 2 * part, :] = kept_ref[: 2 * part, :] + got_ref[: 2 * part, :]
     lost = kept_ref[2 * part :, :]
     found = got_ref[2 * part :, :]
-    for ref, first in ((next_ref, 0), (note_ref, 2)):
-        ref[part:, :] = jnp.concatenate(
-            [
-                lost[first : first + 2],
-                found[first : first + 2],
-                jnp.zeros((4, lost.shape[1]), F32),
-            ],
-            axis=0,
-        )
-
-
-def turn_three_kernel(part, kept_ref, got_ref, sum_ref, loss_ref):
-    sum_ref[...] = kept_ref[:part, :] + got_ref[:part, :]
-    loss_ref[...] = jnp.concatenate([kept_ref[part : part + 4, :], got_ref[part : part + 4, :]], axis=0)
-
-
-def turn(kernel, kept, got, part, shapes, name):
+    both_ref[2 * part :, :] = jnp.concatenate(
+        [lost[0:2], found[0:2], lost[2:4], found[2:4]], axis=0
+    )
+
+
+def turn_three_kernel(part, both_ref, got_ref, sum_ref, loss_ref):
+    sum_ref[:part, :] = both_ref[:part, :] + got_ref[part : 2 * part, :]
+    sum_ref[part:, :] = both_ref[part : 2 * part, :] + got_ref[:part, :]
+    loss_ref[...] = jnp.concatenate(
+        [both_ref[2 * part : 2 * part + 4, :], got_ref[2 * part + 4 :, :]], axis=0
+    )
+
+
+def add_kernel(part, one_ref, other_ref, *refs):
+    refs[-1][...] = one_ref[...] + other_ref[...]
+
+
+def turn(kernel, kept, got, part, shapes, name, ahead=()):
     return pl.pallas_call(
         functools.partial(kernel, part),
         out_shape=[jax.ShapeDtypeStruct((rows, kept.shape[1]), F32) for rows in shapes],
-        in_specs=[whole()] * 2,
-        out_specs=[whole()] * 2,
+        in_specs=[whole()] * 2 + [whole(pl.ANY)] * len(ahead),
+        out_specs=[whole()] * len(shapes),
         compiler_params=pltpu.CompilerParams(vmem_limit_bytes=4 * MIB),
         name=name,
-    )(kept, got)
+    )(kept, got, *ahead)
+
+
+def pass_on_kernel(next_up_ref, got_up_ref, next_down_ref, got_down_ref, *refs):
+    up_ref, down_ref = refs[-2:]
+    up_ref[...] = (next_up_ref[...] + got_up_ref[1].astype(F32)).astype(BF16)
+    down_ref[...] = (next_down_ref[...] + got_down_ref[1].astype(F32)).astype(BF16)
+
+
+def pass_on(next_up, got_up, next_down, got_down, ahead=()):
+    up, down = pl.pallas_call(
+        pass_on_kernel,
+        out_shape=[jax.ShapeDtypeStruct(next_up.shape, BF16)] * 2,
+        in_specs=[whole()] * 4 + [whole(pl.ANY)] * len(ahead),
+        out_specs=[whole()] * 2,
+        compiler_params=pltpu.CompilerParams(vmem_limit_bytes=8 * MIB),
+        name="pass_on",
+    )(next_up, got_up, next_down, got_down, *ahead)
+    return swap(up, "dp", 2), swap(down, "dp", 1)
 
 
 def row_loss_kernel(place_ref, loss_ref, row_loss_ref):
@@ -394,17 +411,6 @@
         compiler_params=pltpu.CompilerParams(vmem_limit_bytes=4 * MIB),
         name="assemble_trunk",
     )(me, *held)
-
-
-def after(value, *others):
-    return pl.pallas_call(
-        lambda *refs: None,
-        out_shape=jax.ShapeDtypeStruct(value.shape, value.dtype),
-        in_specs=[whole(pl.ANY)] * (1 + len(others)),
-        out_specs=whole(pl.ANY),
-        input_output_aliases={0: 0},
-        name="in_order",
-    )(value, *others)
 
 
 def adam_update(params, first, second, grads):
@@ -445,21 +451,10 @@
     rounded = expert_params[0].astype(BF16)
     weights = [swap(rounded, "dp", j) for j in range(replicas)]
     *blocks, place = pack(me, sample_index, region[:, 0], cell_table, targets, experts, capacity)
-    arrived = list(blocks)
-    if in_turns(experts) and replicas == 4:
-        for s in (4, 6):
-            arrived[s] = swap(blocks[s], "expert", s)
-        for s, ahead in (
-            (5, weights[1]),
-            (7, weights[2]),
-            (2, weights[3]),
-            (3, arrived[4]),
-            (1, arrived[6]),
-        ):
-            arrived[s] = swap(after(blocks[s], ahead), "expert", s)
-        batches = ((0, 4, 6), (1, 2, 3), (5,), (7,))
+    arrived = [swap(blocks[s], "expert", s) for s in range(experts)]
+    if in_turns(experts):
+        batches = ((0,), (4, 6), (1, 2, 3), (5,), (7,))
     else:
-        arrived = [swap(blocks[s], "expert", s) for s in range(experts)]
         batches = (range(experts // 2), range(experts // 2, experts))
 
     order = [s for batch in batches for s in batch]
@@ -472,41 +467,50 @@
         if not last:
             prior = outs[:2]
             losses.append(outs[2])
-    grads, sent_up, sent_down = outs[0], outs[1:replicas], outs[replicas : 2 * replicas - 1]
-    kept, note = outs[-2:]
-
+    own, next_up, next_down, sent_up, sent_down, kept, note = outs
+
+    got_up = swap(sent_up, "dp", 1)
+    got_down = swap(sent_down, "dp", 2)
     part = width // experts
-    downs = [swap(sent_down[j - 1], "dp", j) for j in range(1, replicas)]
     if in_turns(experts):
         kept, note = turn(
             turn_one_kernel, kept, swap(note, "expert", 1), part, (2 * part + 8,) * 2, "turn_one"
         )
-        kept, note = turn(
-            turn_two_kernel, kept, swap(note, "expert", 2), part, (part + 8,) * 2, "turn_two"
+        (both,) = turn(
+            turn_two_kernel, kept, swap(note, "expert", 2), part, (2 * part + 8,), "turn_two"
         )
         total, loss = turn(
-            turn_three_kernel, kept, swap(note, "expert", 4), part, (part, experts), "turn_three"
-        )
-        others = [swap(total, "dp", j) for j in range(1, replicas)]
-        sent_up = [after(value, *others) for value in sent_up]
-        if replicas == 4:
-            total = (total + others[0]) + (others[1] + others[2])
-        else:
-            total = total + sum(others)
-        held = [total]
-        for s in (4, 2, 1):
-            message = held[0] if len(held) == 1 else jnp.concatenate(held, axis=0)
-            held.append(swap(message, "expert", s))
-        trunk_grad = assemble(me, held, part)
+            turn_three_kernel,
+            both,
+            swap(both, "expert", 4),
+            part,
+            (2 * part, experts),
+            "turn_three",
+        )
+        more_up, more_down = pass_on(next_up, got_up, next_down, got_down, (total,))
+        (total,) = turn(
+            add_kernel, total, swap(total, "dp", 1), part, (2 * part,), "turn_four", (got_up, got_down)
+        )
+        (total,) = turn(
+            add_kernel, total, swap(total, "dp", 2), part, (2 * part,), "turn_five", (more_up, more_down)
+        )
+        other = swap(total, "expert", 2)
+        rest = swap(jnp.concatenate([total, other], axis=0), "expert", 1)
+        trunk_grad = assemble(me, [total, other, rest], part)
     else:
+        more_up, more_down = pass_on(next_up, got_up, next_down, got_down)
         trunk_grad = lax.psum(kept, ("dp", "expert"))
         mine = jnp.arange(experts, dtype=jnp.int32) ^ me
         note = note.reshape(experts, capacity)
         loss = lax.all_to_all(note[mine], "expert", split_axis=0, concat_axis=0, tiled=True)[mine]
     row_loss = loss_by_row(place, loss)
-    ups = [swap(sent_up[j - 1], "dp", j) for j in range(1, replicas)]
-
-    grads = grads + sum(jnp.stack([u, d]).astype(F32) for u, d in zip(ups, downs))
+
+    grads = jnp.stack(
+        [
+            own[0] + got_up[0].astype(F32) + more_up.astype(F32),
+            own[1] + got_down[0].astype(F32) + more_down.astype(F32),
+        ]
+    )
     new_params, new_first, new_second = adam_update(
         expert_params, first_moment, second_moment, grads[None]
     )

time: 137 us -> 120 us (0.88)
  waiting for transfers between devices: 60.9 us -> 46 us
  starting transfers between devices: 26.6 us -> 30.1 us
  Pallas kernels: 34.3 us -> 31.1 us
  other arithmetic: 5.48 us -> 3.67 us
    ppermute x25 -> x21, waiting for transfers between devices: 60.9 us -> 46 us  [swap(): lax.ppermute(value, axis, [(i, i ^ s) for i in range(lax.axis_size(axis))])]
    ppermute x25 -> x21, starting transfers between devices: 26.6 us -> 30.1 us  [swap(): lax.ppermute(value, axis, [(i, i ^ s) for i in range(lax.axis_size(axis))])]
    pallas_call x1, Pallas kernels: 5.59 us -> 3.52 us  [pack(): pl.pallas_call(functools.partial(pack_kernel, experts, capacity), out_sha...]
    sub x1, other arithmetic: 4.16 us -> 2.15 us  [adam_update(): params - learn_rate * first_hat / (jnp.sqrt(second_hat) + adam_eps)]
    pallas_call x4 -> x5, Pallas kernels: 26.8 us -> 25.4 us  [expert_call(): pl.pallas_call(functools.partial(expert_kernel, counts, order, first, len...]
    unnamed x42 -> x20, local copies, waits for them, and re-layouts: 8.87 us -> 7.81 us
  transfers between devices with their start and end apart: 25 -> 21, of which waited for: 12 -> 10; matrix products, arithmetic and copies ran while one was open for 0% -> 2% of each run, Pallas kernels for 23% -> 22%
where the time goes in v3:
time: 120 us
  waiting for transfers between devices  46 us (38%)
  Pallas kernels  31.1 us (26%)
  starting transfers between devices  30.1 us (25%)
  local copies, waits for them, and re-layouts  7.81 us (7%)
  other arithmetic  3.67 us (3%)
    ppermute x21, waiting for transfers between devices, swap(): lax.ppermute(value, axis, [(i, i ^ s) for i in range(lax.axis_size(axis))])  46 us
    ppermute x21, starting transfers between devices, swap(): lax.ppermute(value, axis, [(i, i ^ s) for i in range(lax.axis_size(axis))])  30.1 us
    pallas_call x5, Pallas kernels, expert_call(): pl.pallas_call(functools.partial(expert_kernel, counts, order, first, len...  25.4 us
    unnamed x20, local copies, waits for them, and re-layouts  7.81 us
    pallas_call x1, Pallas kernels, pack(): pl.pallas_call(functools.partial(pack_kernel, experts, capacity), out_sha...  3.52 us
  transfers between devices with their start and end apart: 21, of which 10 were waited for; matrix products, arithmetic and copies ran while one was open for 2% of the time, Pallas kernels for 22%

profile of v3, /device:TPU:0, one launch (start us, length us, event | category | flops | bytes accessed | tf_op | source)
XLA Modules:
  0.0 119.5 jit_solution(8734001625166098058)
XLA Ops:
  1.9 4.0 %collective-permute-start.3 = (bf16[2,256,512]{2,1,0:T(8,128)(2,1)S(1)}, bf16[2,256,512]{2,1,0:T(8,128)(2,1)S(1)}, u32[]{:S(2)}, u32[]{:S(2)}) collective-permute-start(bf16[2,256,512]{2,1,0:T(8,128)(2,1)S(1)} %convert_bitcast_fusion.refs_2_.refs_3_.refs_4_), channel_id=1, source_target_pairs={{0,24},{8,16},{16,8},{24,0},{1,25},{9,17},{17,9},{25,1},{2,26},{10... | collective-permute-start | bytes 1572872 | tf_op jit(solution)/shard_map/ppermute | solution.py:431
  10.2 3.5 %pack_rows.1 = (bf16[256,512]{1,0:T(8,128)(2,1)S(1)}, bf16[256,512]{1,0:T(8,128)(2,1)S(1)}, bf16[256,512]{1,0:T(8,128)(2,1)S(1)}, bf16[256,512]{1,0:T(8,128)(2,1...) custom-call(s32[1]{0:T(128)} %bitcast.me_ref.refs_12_, ...), custom_call_target="tpu_custom_call" | custom-call | flops 3221225472 | bytes 6291456 | tf_op jit(solution)/shard_map/pack_rows/pallas_call | solution.py:84
  13.7 3.1 %collective-permute-start.8 = (bf16[256,512]{1,0:T(8,128)(2,1)S(1)}, bf16[256,512]{1,0:T(8,128)(2,1)S(1)}, u32[]{:S(2)}, u32[]{:S(2)}) collective-permute-start(bf16[256,512]{1,0:T(8,128)(2,1)S(1)} %get-tuple-element.44), channel_id=1, source_target_pairs={{0,4},{1,5},{2,6},{3,7},{4,0},{5,1},{6,2},{7,3},{8,12},{9,13},{10,... | collective-permute-start | bytes 786440 | tf_op jit(solution)/shard_map/ppermute | solution.py:431
  18.7 1.5 %collective-permute-start = (bf16[256,512]{1,0:T(8,128)(2,1)S(1)}, bf16[256,512]{1,0:T(8,128)(2,1)S(1)}, u32[]{:S(2)}, u32[]{:S(2)}) collective-permute-start(bf16[256,512]{1,0:T(8,128)(2,1)S(1)} %get-tuple-element.39), channel_id=1, source_target_pairs={{0,7},{1,6},{2,5},{3,4},{4,3},{5,2},{6,1},{7,0},{8,15},{9,14},{10,... | collective-permute-start | bytes 786440 | tf_op jit(solution)/shard_map/ppermute | solution.py:431
  20.2 8.8 %collective-permute-done.2.refs_4_.refs_5_.refs_6_ = bf16[2,256,512]{2,1,0:T(8,128)(2,1)S(1)} collective-permute-done((bf16[2,256,512]{2,1,0:T(8,128)(2,1)S(1)}, bf16[2,256,512]{2,1,0:T(8,128)(2,1)S(1)}, u32[]{:S(2)}, u32[]{:S(2)}) %collective-permute-start.2) | collective-permute-done | bytes 524320 | tf_op jit(solution)/shard_map/ppermute | solution.py:431
  29.0 2.4 %collective-permute-start.4 = (bf16[256,512]{1,0:T(8,128)(2,1)S(1)}, bf16[256,512]{1,0:T(8,128)(2,1)S(1)}, u32[]{:S(2)}, u32[]{:S(2)}) collective-permute-start(bf16[256,512]{1,0:T(8,128)(2,1)S(1)} %get-tuple-element.40), channel_id=1, source_target_pairs={{0,5},{1,4},{2,7},{3,6},{4,1},{5,0},{6,3},{7,2},{8,13},{9,12},{10,... | collective-permute-start | bytes 786440 | tf_op jit(solution)/shard_map/ppermute | solution.py:431
  31.9 3.1 %expert_rows.5 = (f32[4,2,256,512]{3,2,1,0:T(8,128)S(1)}, f32[256,256]{1,0:T(8,128)S(1)}, f32[1,256]{1,0:T(1,128)S(1)}) custom-call(bf16[256,512]{1,0:T(8,128)(2,1)S(1)} %get-tuple-element.46.refs_0_, bf16[256,256]{1,0:T(8,128)(2,1)S(1)} %copy-done, bf16[2,256,512]{2,1,0:T(8,128)(2,1)S(1)} %convert_bitcast_fusion.refs_2_.refs_3_.refs_4_, ...), custom_call_target="tpu_custom_call" | custom-call | flops 1610612736 | bytes 10485760 | tf_op jit(solution)/shard_map/expert_rows/pallas_call | solution.py:278
  35.1 10.8 %collective-permute-done.8.refs_0_ = bf16[256,512]{1,0:T(8,128)(2,1)S(1)} collective-permute-done((bf16[256,512]{1,0:T(8,128)(2,1)S(1)}, bf16[256,512]{1,0:T(8,128)(2,1)S(1)}, u32[]{:S(2)}, u32[]{:S(2)}) %collective-permute-start.8) | collective-permute-done | bytes 262176 | tf_op jit(solution)/shard_map/ppermute | solution.py:431
  45.9 4.7 %collective-permute-start.7 = (bf16[256,512]{1,0:T(8,128)(2,1)S(1)}, bf16[256,512]{1,0:T(8,128)(2,1)S(1)}, u32[]{:S(2)}, u32[]{:S(2)}) collective-permute-start(bf16[256,512]{1,0:T(8,128)(2,1)S(1)} %get-tuple-element.43), channel_id=1, source_target_pairs={{0,3},{1,2},{2,1},{3,0},{4,7},{5,6},{6,5},{7,4},{8,11},{9,10},{10,... | collective-permute-start | bytes 786440 | tf_op jit(solution)/shard_map/ppermute | solution.py:431
  50.7 6.3 %expert_rows.6 = (f32[4,2,256,512]{3,2,1,0:T(8,128)S(1)}, f32[256,256]{1,0:T(8,128)S(1)}, f32[2,256]{1,0:T(2,128)S(1)}) custom-call(bf16[256,512]{1,0:T(8,128)(2,1)S(1)} %collective-permute-done.8.refs_0_, bf16[256,512]{1,0:T(8,128)(2,1)S(1)} %collective-permute-done.9.refs_1_, bf16[256,256]{1,0:T(8,128)(2,1)S(1)} %copy-done, ...), custom_call_target="tpu_custom_call" | custom-call | flops 3221225472 | bytes 10485760 | tf_op jit(solution)/shard_map/expert_rows/pallas_call | solution.py:278
  57.0 2.0 %copy-done.5 = f32[4,2,256,512]{3,2,1,0:T(8,128)} copy-done((f32[4,2,256,512]{3,2,1,0:T(8,128)}, f32[4,2,256,512]{3,2,1,0:T(8,128)S(1)}, u32[]{:S(2)}) %copy-start.5) | copy-done | bytes 4194328
  59.0 3.1 %collective-permute-done.7.refs_2_ = bf16[256,512]{1,0:T(8,128)(2,1)S(1)} collective-permute-done((bf16[256,512]{1,0:T(8,128)(2,1)S(1)}, bf16[256,512]{1,0:T(8,128)(2,1)S(1)}, u32[]{:S(2)}, u32[]{:S(2)}) %collective-permute-start.7) | collective-permute-done | bytes 262176 | tf_op jit(solution)/shard_map/ppermute | solution.py:431
  62.1 2.2 %copy-done.6 = f32[4,2,256,512]{3,2,1,0:T(8,128)S(1)} copy-done((f32[4,2,256,512]{3,2,1,0:T(8,128)S(1)}, f32[4,2,256,512]{3,2,1,0:T(8,128)}, u32[]{:S(2)}) %copy-start.6) | copy-done | bytes 4194328
  64.3 9.3 %expert_rows.7 = (f32[4,2,256,512]{3,2,1,0:T(8,128)S(1)}, f32[256,256]{1,0:T(8,128)S(1)}, f32[3,256]{1,0:T(4,128)S(1)}) custom-call(bf16[256,512]{1,0:T(8,128)(2,1)S(1)} %collective-permute-done.5.refs_0_, bf16[256,512]{1,0:T(8,128)(2,1)S(1)} %collective-permute-done.6.refs_1_, bf16[256,512]{1,0:T(8,128)(2,1)S(1)} %collective-permute-done.7.refs_2_, ...), custom_call_target="tpu_custom_call" | custom-call | flops 4831838208 | bytes 10485760 | tf_op jit(solution)/shard_map/expert_rows/pallas_call | solution.py:278
  73.6 3.2 %expert_rows.8 = (f32[4,2,256,512]{3,2,1,0:T(8,128)S(1)}, f32[256,256]{1,0:T(8,128)S(1)}, f32[1,256]{1,0:T(1,128)S(1)}) custom-call(bf16[256,512]{1,0:T(8,128)(2,1)S(1)} %collective-permute-done.4.refs_0_, bf16[256,256]{1,0:T(8,128)(2,1)S(1)} %copy-done, bf16[2,256,512]{2,1,0:T(8,128)(2,1)S(1)} %convert_bitcast_fusion.refs_2_.refs_3_.refs_4_, ...), custom_call_target="tpu_custom_call" | custom-call | flops 1610612736 | bytes 10485760 | tf_op jit(solution)/shard_map/expert_rows/pallas_call | solution.py:278
  76.8 3.5 %expert_rows.9 = (f32[2,256,512]{2,1,0:T(8,128)S(1)}, f32[256,512]{1,0:T(8,128)S(1)}, f32[256,512]{1,0:T(8,128)S(1)}, bf16[2,256,512]{2,1,0:T(8,128)(2,1)S(1)}, ...) custom-call(bf16[256,512]{1,0:T(8,128)(2,1)S(1)} %collective-permute-done.refs_0_, ...), custom_call_target="tpu_custom_call" | custom-call | flops 1610612736 | bytes 10485760 | tf_op jit(solution)/shard_map/expert_rows/pallas_call | solution.py:278
  80.3 1.5 %collective-permute-start.14 = (bf16[2,256,512]{2,1,0:T(8,128)(2,1)S(1)}, bf16[2,256,512]{2,1,0:T(8,128)(2,1)S(1)}, u32[]{:S(2)}, u32[]{:S(2)}) collective-permute-start(bf16[2,256,512]{2,1,0:T(8,128)(2,1)S(1)} %get-tuple-element.64), channel_id=1, source_target_pairs={{0,8},{8,0},{16,24},{24,16},{1,9},{9,1},{17,25},{25,17},{2,10},{10... | collective-permute-start | bytes 1572872 | tf_op jit(solution)/shard_map/ppermute | solution.py:431
  85.8 3.9 %collective-permute-done.11.got_ref = f32[72,256]{1,0:T(8,128)S(1)} collective-permute-done((f32[72,256]{1,0:T(8,128)S(1)}, f32[72,256]{1,0:T(8,128)S(1)}, u32[]{:S(2)}, u32[]{:S(2)}) %collective-permute-start.11) | collective-permute-done | bytes 73760 | tf_op jit(solution)/shard_map/ppermute | solution.py:431
  89.7 3.2 %collective-permute-start.12 = (f32[72,256]{1,0:T(8,128)S(1)}, f32[72,256]{1,0:T(8,128)S(1)}, u32[]{:S(2)}, u32[]{:S(2)}) collective-permute-start(f32[72,256]{1,0:T(8,128)S(1)} %turn_two.1.both_ref), channel_id=1, source_target_pairs={{0,4},{1,5},{2,6},{3,7},{4,0},{5,1},{6,2},{7,3},{8,12},{9,13},{10,... | collective-permute-start | bytes 221192 | tf_op jit(solution)/shard_map/ppermute | solution.py:431
  93.0 3.7 %collective-permute-done.12.got_ref = f32[72,256]{1,0:T(8,128)S(1)} collective-permute-done((f32[72,256]{1,0:T(8,128)S(1)}, f32[72,256]{1,0:T(8,128)S(1)}, u32[]{:S(2)}, u32[]{:S(2)}) %collective-permute-start.12) | collective-permute-done | bytes 73760 | tf_op jit(solution)/shard_map/ppermute | solution.py:431
  100.4 7.4 %collective-permute-done.13.other_ref = f32[64,256]{1,0:T(8,128)S(1)} collective-permute-done((f32[64,256]{1,0:T(8,128)S(1)}, f32[64,256]{1,0:T(8,128)S(1)}, u32[]{:S(2)}, u32[]{:S(2)}) %collective-permute-start.13) | collective-permute-done | bytes 65568 | tf_op jit(solution)/shard_map/ppermute | solution.py:431
  109.6 2.6 %collective-permute-done.16.other_ref = f32[64,256]{1,0:T(8,128)S(1)} collective-permute-done((f32[64,256]{1,0:T(8,128)S(1)}, f32[64,256]{1,0:T(8,128)S(1)}, u32[]{:S(2)}, u32[]{:S(2)}) %collective-permute-start.16) | collective-permute-done | bytes 65568 | tf_op jit(solution)/shard_map/ppermute | solution.py:431
  112.5 4.0 %collective-permute-done.19.refs_1_ = f32[64,256]{1,0:T(8,128)S(1)} collective-permute-done((f32[64,256]{1,0:T(8,128)S(1)}, f32[64,256]{1,0:T(8,128)S(1)}, u32[]{:S(2)}, u32[]{:S(2)}) %collective-permute-start.19) | collective-permute-done | bytes 65568 | tf_op jit(solution)/shard_map/ppermute | solution.py:431
  116.6 2.2 %divide_subtract_fusion = (f32[1,2,256,512]{3,2,1,0:T(8,128)}, f32[1,2,256,512]{3,2,1,0:T(8,128)}, f32[1,2,256,512]{3,2,1,0:T(8,128)}) fusion(f32[1,2,256,512]{3,2,1,0:T(8,128)S(1)} %copy-done.7, f32[1,1,256,512]{3,2,1,0:T(8,128)S(1)} %get-tuple-element.77, f32[1,1,256,512]{3,2,1,0:T(8,128)S(1)} %get-tuple-element.76, f32[1,2,256,512]{3,2,1,0:T(8,128)S(1)} %copy-done.8, ...), kind=kLoop, calls=%fused_computation.3 | loop fusion | flops 3407872 | bytes 7340032 | tf_op jit(solution)/shard_map/sub | solution.py:422
  (56 shorter events, 18.5 us)
Async XLA Ops:
  1.9 16.8 %collective-permute-start.3 = (bf16[2,256,512]{2,1,0:T(8,128)(2,1)S(1)}, bf16[2,256,512]{2,1,0:T(8,128)(2,1)S(1)}, u32[]{:S(2)}, u32[]{:S(2)}) collective-permute-start(bf16[2,256,512]{2,1,0:T(8,128)(2,1)S(1)} %convert_bitcast_fusion.refs_2_.refs_3_.refs_4_), channel_id=1, source_target_pairs={{0,24},{8,16},{16,8},{24,0},{1,25},{9,17},{17,9},{25,1},{2,26},{10... | collective-permute-start | bytes 1572872 | tf_op jit(solution)/shard_map/ppermute | solution.py:431
  5.9 23.2 %collective-permute-start.2 = (bf16[2,256,512]{2,1,0:T(8,128)(2,1)S(1)}, bf16[2,256,512]{2,1,0:T(8,128)(2,1)S(1)}, u32[]{:S(2)}, u32[]{:S(2)}) collective-permute-start(bf16[2,256,512]{2,1,0:T(8,128)(2,1)S(1)} %convert_bitcast_fusion.refs_2_.refs_3_.refs_4_), channel_id=1, source_target_pairs={{0,16},{8,24},{16,0},{24,8},{1,17},{9,25},{17,1},{25,9},{2,18},{10... | collective-permute-start | bytes 1572872 | tf_op jit(solution)/shard_map/ppermute | solution.py:431
  6.4 25.1 %collective-permute-start.1 = (bf16[2,256,512]{2,1,0:T(8,128)(2,1)S(1)}, bf16[2,256,512]{2,1,0:T(8,128)(2,1)S(1)}, u32[]{:S(2)}, u32[]{:S(2)}) collective-permute-start(bf16[2,256,512]{2,1,0:T(8,128)(2,1)S(1)} %convert_bitcast_fusion.refs_2_.refs_3_.refs_4_), channel_id=1, source_target_pairs={{0,8},{8,0},{16,24},{24,16},{1,9},{9,1},{17,25},{25,17},{2,10},{10... | collective-permute-start | bytes 1572872 | tf_op jit(solution)/shard_map/ppermute | solution.py:431
  13.7 32.2 %collective-permute-start.8 = (bf16[256,512]{1,0:T(8,128)(2,1)S(1)}, bf16[256,512]{1,0:T(8,128)(2,1)S(1)}, u32[]{:S(2)}, u32[]{:S(2)}) collective-permute-start(bf16[256,512]{1,0:T(8,128)(2,1)S(1)} %get-tuple-element.44), channel_id=1, source_target_pairs={{0,4},{1,5},{2,6},{3,7},{4,0},{5,1},{6,2},{7,3},{8,12},{9,13},{10,... | collective-permute-start | bytes 786440 | tf_op jit(solution)/shard_map/ppermute | solution.py:431
  16.8 29.2 %collective-permute-start.9 = (bf16[256,512]{1,0:T(8,128)(2,1)S(1)}, bf16[256,512]{1,0:T(8,128)(2,1)S(1)}, u32[]{:S(2)}, u32[]{:S(2)}) collective-permute-start(bf16[256,512]{1,0:T(8,128)(2,1)S(1)} %get-tuple-element.45), channel_id=1, source_target_pairs={{0,6},{1,7},{2,4},{3,5},{4,2},{5,3},{6,0},{7,1},{8,14},{9,15},{10,... | collective-permute-start | bytes 786440 | tf_op jit(solution)/shard_map/ppermute | solution.py:431
  18.7 58.1 %collective-permute-start = (bf16[256,512]{1,0:T(8,128)(2,1)S(1)}, bf16[256,512]{1,0:T(8,128)(2,1)S(1)}, u32[]{:S(2)}, u32[]{:S(2)}) collective-permute-start(bf16[256,512]{1,0:T(8,128)(2,1)S(1)} %get-tuple-element.39), channel_id=1, source_target_pairs={{0,7},{1,6},{2,5},{3,4},{4,3},{5,2},{6,1},{7,0},{8,15},{9,14},{10,... | collective-permute-start | bytes 786440 | tf_op jit(solution)/shard_map/ppermute | solution.py:431
  29.0 44.5 %collective-permute-start.4 = (bf16[256,512]{1,0:T(8,128)(2,1)S(1)}, bf16[256,512]{1,0:T(8,128)(2,1)S(1)}, u32[]{:S(2)}, u32[]{:S(2)}) collective-permute-start(bf16[256,512]{1,0:T(8,128)(2,1)S(1)} %get-tuple-element.40), channel_id=1, source_target_pairs={{0,5},{1,4},{2,7},{3,6},{4,1},{5,0},{6,3},{7,2},{8,13},{9,12},{10,... | collective-permute-start | bytes 786440 | tf_op jit(solution)/shard_map/ppermute | solution.py:431
  31.5 27.5 %collective-permute-start.5 = (bf16[256,512]{1,0:T(8,128)(2,1)S(1)}, bf16[256,512]{1,0:T(8,128)(2,1)S(1)}, u32[]{:S(2)}, u32[]{:S(2)}) collective-permute-start(bf16[256,512]{1,0:T(8,128)(2,1)S(1)} %get-tuple-element.41), channel_id=1, source_target_pairs={{0,1},{1,0},{2,3},{3,2},{4,5},{5,4},{6,7},{7,6},{8,9},{9,8},{10,11... | collective-permute-start | bytes 786440 | tf_op jit(solution)/shard_map/ppermute | solution.py:431
  45.9 13.1 %collective-permute-start.6 = (bf16[256,512]{1,0:T(8,128)(2,1)S(1)}, bf16[256,512]{1,0:T(8,128)(2,1)S(1)}, u32[]{:S(2)}, u32[]{:S(2)}) collective-permute-start(bf16[256,512]{1,0:T(8,128)(2,1)S(1)} %get-tuple-element.42), channel_id=1, source_target_pairs={{0,2},{1,3},{2,0},{3,1},{4,6},{5,7},{6,4},{7,5},{8,10},{9,11},{10,... | collective-permute-start | bytes 786440 | tf_op jit(solution)/shard_map/ppermute | solution.py:431
  45.9 16.2 %collective-permute-start.7 = (bf16[256,512]{1,0:T(8,128)(2,1)S(1)}, bf16[256,512]{1,0:T(8,128)(2,1)S(1)}, u32[]{:S(2)}, u32[]{:S(2)}) collective-permute-start(bf16[256,512]{1,0:T(8,128)(2,1)S(1)} %get-tuple-element.43), channel_id=1, source_target_pairs={{0,3},{1,2},{2,1},{3,0},{4,7},{5,6},{6,5},{7,4},{8,11},{9,10},{10,... | collective-permute-start | bytes 786440 | tf_op jit(solution)/shard_map/ppermute | solution.py:431
  80.3 36.3 %copy-start.7 = (f32[1,2,256,512]{3,2,1,0:T(8,128)S(1)}, f32[1,2,256,512]{3,2,1,0:T(8,128)}, u32[]{:S(2)}) copy-start(f32[1,2,256,512]{3,2,1,0:T(8,128)} %param.13) | copy-start | bytes 3145732
  80.3 36.3 %copy-start.8 = (f32[1,2,256,512]{3,2,1,0:T(8,128)S(1)}, f32[1,2,256,512]{3,2,1,0:T(8,128)}, u32[]{:S(2)}) copy-start(f32[1,2,256,512]{3,2,1,0:T(8,128)} %param.14) | copy-start | bytes 3145732
  80.3 36.3 %copy-start.9 = (f32[1,2,256,512]{3,2,1,0:T(8,128)S(1)}, f32[1,2,256,512]{3,2,1,0:T(8,128)}, u32[]{:S(2)}) copy-start(f32[1,2,256,512]{3,2,1,0:T(8,128)} %param.15) | copy-start | bytes 3145732
  80.3 16.4 %collective-permute-start.14 = (bf16[2,256,512]{2,1,0:T(8,128)(2,1)S(1)}, bf16[2,256,512]{2,1,0:T(8,128)(2,1)S(1)}, u32[]{:S(2)}, u32[]{:S(2)}) collective-permute-start(bf16[2,256,512]{2,1,0:T(8,128)(2,1)S(1)} %get-tuple-element.64), channel_id=1, source_target_pairs={{0,8},{8,0},{16,24},{24,16},{1,9},{9,1},{17,25},{25,17},{2,10},{10... | collective-permute-start | bytes 1572872 | tf_op jit(solution)/shard_map/ppermute | solution.py:431
  81.9 14.8 %collective-permute-start.15 = (bf16[2,256,512]{2,1,0:T(8,128)(2,1)S(1)}, bf16[2,256,512]{2,1,0:T(8,128)(2,1)S(1)}, u32[]{:S(2)}, u32[]{:S(2)}) collective-permute-start(bf16[2,256,512]{2,1,0:T(8,128)(2,1)S(1)} %get-tuple-element.65), channel_id=1, source_target_pairs={{0,16},{8,24},{16,0},{24,8},{1,17},{9,25},{17,1},{25,9},{2,18},{10... | collective-permute-start | bytes 1572872 | tf_op jit(solution)/shard_map/ppermute | solution.py:431
  83.4 1.7 %collective-permute-start.10 = (f32[136,256]{1,0:T(8,128)S(1)}, f32[136,256]{1,0:T(8,128)S(1)}, u32[]{:S(2)}, u32[]{:S(2)}) collective-permute-start(f32[136,256]{1,0:T(8,128)S(1)} %get-tuple-element.60), channel_id=1, source_target_pairs={{0,1},{1,0},{2,3},{3,2},{4,5},{5,4},{6,7},{7,6},{8,9},{9,8},{10,11... | collective-permute-start | bytes 417800 | tf_op jit(solution)/shard_map/ppermute | solution.py:431
  85.1 4.6 %collective-permute-start.11 = (f32[72,256]{1,0:T(8,128)S(1)}, f32[72,256]{1,0:T(8,128)S(1)}, u32[]{:S(2)}, u32[]{:S(2)}) collective-permute-start(f32[72,256]{1,0:T(8,128)S(1)} %get-tuple-element.62), channel_id=1, source_target_pairs={{0,2},{1,3},{2,0},{3,1},{4,6},{5,7},{6,4},{7,5},{8,10},{9,11},{10,... | collective-permute-start | bytes 221192 | tf_op jit(solution)/shard_map/ppermute | solution.py:431
  89.7 7.0 %collective-permute-start.12 = (f32[72,256]{1,0:T(8,128)S(1)}, f32[72,256]{1,0:T(8,128)S(1)}, u32[]{:S(2)}, u32[]{:S(2)}) collective-permute-start(f32[72,256]{1,0:T(8,128)S(1)} %turn_two.1.both_ref), channel_id=1, source_target_pairs={{0,4},{1,5},{2,6},{3,7},{4,0},{5,1},{6,2},{7,3},{8,12},{9,13},{10,... | collective-permute-start | bytes 221192 | tf_op jit(solution)/shard_map/ppermute | solution.py:431
  96.9 15.3 %collective-permute-start.17 = (bf16[256,512]{1,0:T(8,128)(2,1)S(1)}, bf16[256,512]{1,0:T(8,128)(2,1)S(1)}, u32[]{:S(2)}, u32[]{:S(2)}) collective-permute-start(bf16[256,512]{1,0:T(8,128)(2,1)S(1)} %get-tuple-element.68), channel_id=1, source_target_pairs={{0,16},{8,24},{16,0},{24,8},{1,17},{9,25},{17,1},{25,9},{2,18},{10... | collective-permute-start | bytes 786440 | tf_op jit(solution)/shard_map/ppermute | solution.py:431
  98.4 13.8 %collective-permute-start.18 = (bf16[256,512]{1,0:T(8,128)(2,1)S(1)}, bf16[256,512]{1,0:T(8,128)(2,1)S(1)}, u32[]{:S(2)}, u32[]{:S(2)}) collective-permute-start(bf16[256,512]{1,0:T(8,128)(2,1)S(1)} %get-tuple-element.69), channel_id=1, source_target_pairs={{0,8},{8,0},{16,24},{24,16},{1,9},{9,1},{17,25},{25,17},{2,10},{10... | collective-permute-start | bytes 786440 | tf_op jit(solution)/shard_map/ppermute | solution.py:431
  98.9 8.9 %collective-permute-start.13 = (f32[64,256]{1,0:T(8,128)S(1)}, f32[64,256]{1,0:T(8,128)S(1)}, u32[]{:S(2)}, u32[]{:S(2)}) collective-permute-start(f32[64,256]{1,0:T(8,128)S(1)} %get-tuple-element.63.one_ref.refs_0_), channel_id=1, source_target_pairs={{0,8},{8,0},{16,24},{24,16},{1,9},{9,1},{17,25},{25,17},{2,10},{10... | collective-permute-start | bytes 196616 | tf_op jit(solution)/shard_map/ppermute | solution.py:431
  107.8 4.3 %collective-permute-start.16 = (f32[64,256]{1,0:T(8,128)S(1)}, f32[64,256]{1,0:T(8,128)S(1)}, u32[]{:S(2)}, u32[]{:S(2)}) collective-permute-start(f32[64,256]{1,0:T(8,128)S(1)} %turn_four.1.one_ref), channel_id=1, source_target_pairs={{0,16},{8,24},{16,0},{24,8},{1,17},{9,25},{17,1},{25,9},{2,18},{10... | collective-permute-start | bytes 196616 | tf_op jit(solution)/shard_map/ppermute | solution.py:431
  112.2 4.3 %collective-permute-start.19 = (f32[64,256]{1,0:T(8,128)S(1)}, f32[64,256]{1,0:T(8,128)S(1)}, u32[]{:S(2)}, u32[]{:S(2)}) collective-permute-start(f32[64,256]{1,0:T(8,128)S(1)} %turn_five.1.refs_0_), channel_id=1, source_target_pairs={{0,2},{1,3},{2,0},{3,1},{4,6},{5,7},{6,4},{7,5},{8,10},{9,11},{10,... | collective-permute-start | bytes 196616 | tf_op jit(solution)/shard_map/ppermute | solution.py:431
  116.5 2.3 %collective-permute-start.20 = (f32[128,256]{1,0:T(8,128)S(1)}, f32[128,256]{1,0:T(8,128)S(1)}, u32[]{:S(2)}, u32[]{:S(2)}) collective-permute-start(f32[128,256]{1,0:T(8,128)S(1)} %pad_maximum_fusion.1), channel_id=1, source_target_pairs={{0,1},{1,0},{2,3},{3,2},{4,5},{5,4},{6,7},{7,6},{8,9},{9,8},{10,11... | collective-permute-start | bytes 393224 | tf_op jit(solution)/shard_map/ppermute | solution.py:431
  (7 other events, 29.6 us)

commit v4 on v3

--- a/solution.py
+++ b/solution.py
@@ -98,6 +98,22 @@
     )(me, index.reshape(groups, LANES), region.reshape(groups, LANES), table, targets)
 
 
+def pair_kernel(one_ref, other_ref, ahead_ref, both_ref):
+    both_ref[0] = one_ref[...]
+    both_ref[1] = other_ref[...]
+
+
+def pair(one, other, ahead):
+    return pl.pallas_call(
+        pair_kernel,
+        out_shape=jax.ShapeDtypeStruct((2, *one.shape), one.dtype),
+        in_specs=[whole()] * 2 + [whole(pl.ANY)],
+        out_specs=whole(),
+        compiler_params=pltpu.CompilerParams(vmem_limit_bytes=4 * MIB),
+        name="pair",
+    )(one, other, ahead)
+
+
 def sigmoid(v):
     return 0.5 * jnp.tanh(0.5 * v) + 0.5
 
@@ -112,8 +128,9 @@
         return got
 
     xs = take(blocks)
-    (trunk_ref,) = take(1)
-    weights = take(shares)
+    trunk_ref, ups_near, ups_far, downs_near, downs_far = take(5)
+    ups = (ups_near.at[0], ups_near.at[1], ups_far.at[0], ups_far.at[1])
+    downs = (downs_near.at[0], downs_far.at[0], downs_near.at[1], downs_far.at[1])
     if not first:
         prior_ref, prior_trunk_ref = take(2)
     if last:
@@ -128,7 +145,7 @@
         acc_ref, acc_trunk_ref, loss_ref = take(3)
 
     width = trunk_ref.shape[0]
-    share = weights[0].shape[2]
+    share = ups_near.shape[2]
     block_rows = xs[0].shape[0]
     for i, ref in enumerate(xs):
         x_ref[i * block_rows : (i + 1) * block_rows, :] = ref[...]
@@ -166,13 +183,13 @@
         out = out_f.astype(BF16)
         predicted = jnp.zeros((step_rows, width), F32)
         for j in range(shares):
-            up = dot(out, weights[j][0])
+            up = dot(out, ups[j][...])
             s = sigmoid(up)
             h = up * s
             slope_ref[:, j * share : (j + 1) * share] = s + h * (1.0 - s)
             h = h.astype(BF16)
             hid_ref[:, j * share : (j + 1) * share] = h
-            predicted = predicted + dot(h, weights[j][1], 1, 1)
+            predicted = predicted + dot(h, downs[j][...], 1, 1)
         errors = predicted - x_ref[at, width:].astype(F32)
         squares = errors * errors
         half = squares[:, :LANES]
@@ -187,9 +204,9 @@
         for j in range(shares):
             part = slice(j * share, (j + 1) * share)
             add(i, acc_ref, prior, (j, 1), dot(scaled_t, hid_ref[:, part]))
-            pre = (dot(scaled, weights[j][1]) * slope_ref[:, part]).astype(BF16)
+            pre = (dot(scaled, downs[j][...]) * slope_ref[:, part]).astype(BF16)
             add(i, acc_ref, prior, (j, 0), dot(out_t, pre))
-            row_grad = row_grad + dot(pre, weights[j][0], 1, 1)
+            row_grad = row_grad + dot(pre, ups[j][...], 1, 1)
         slope = (row_grad.astype(BF16).astype(F32) * trunk_slope).astype(BF16)
         add(i, acc_trunk_ref, prior_trunk, ..., dot(feats_f.T.astype(BF16), slope))
         return carry
@@ -240,8 +257,7 @@
     experts = len(order)
     block_rows = xs[0].shape[0]
     width = trunk_weight.shape[0]
-    shares = len(weights)
-    share = weights[0].shape[2]
+    shares, share = len(weights), weights[0].shape[2]
     rows = block_rows * len(xs)
     step_rows = min(256, rows)
     steps = rows // step_rows
@@ -249,7 +265,7 @@
     acc = jax.ShapeDtypeStruct((shares, 2, width, share), F32)
     acc_trunk = jax.ShapeDtypeStruct((width, width), F32)
     loss = jax.ShapeDtypeStruct((steps, step_rows), F32)
-    args = list(xs) + [trunk_weight] + list(weights)
+    args = list(xs) + [trunk_weight, *weights]
     if not first:
         args += list(prior)
     in_specs = [whole()] * len(args)
@@ -291,56 +307,38 @@
     )(*args)
 
 
-def turn_one_kernel(part, kept_ref, got_ref, next_ref, note_ref):
-    for s in range(4):
-        ref, k = (note_ref, s // 2) if s % 2 else (next_ref, s // 2)
-        at = slice(s * part, (s + 1) * part)
-        ref[k * part : (k + 1) * part, :] = kept_ref[at, :] + got_ref[at, :]
+def turn_one_kernel(part, kept_ref, got_ref, *outs):
     lost = kept_ref[4 * part :, :]
     found = got_ref[4 * part :, :]
-    for ref, first in ((next_ref, 0), (note_ref, 1)):
-        ref[2 * part :, :] = jnp.concatenate(
-            [
-                lost[first : first + 1],
-                found[first : first + 1],
-                lost[first + 2 : first + 3],
-                found[first + 2 : first + 3],
-                jnp.zeros((4, lost.shape[1]), F32),
-            ],
-            axis=0,
-        )
-
-
-def turn_two_kernel(part, kept_ref, got_ref, both_ref):
-    both_ref[: 2 * part, :] = kept_ref[: 2 * part, :] + got_ref[: 2 * part, :]
-    lost = kept_ref[2 * part :, :]
-    found = got_ref[2 * part :, :]
-    both_ref[2 * part :, :] = jnp.concatenate(
-        [lost[0:2], found[0:2], lost[2:4], found[2:4]], axis=0
-    )
-
-
-def turn_three_kernel(part, both_ref, got_ref, sum_ref, loss_ref):
-    sum_ref[:part, :] = both_ref[:part, :] + got_ref[part : 2 * part, :]
-    sum_ref[part:, :] = both_ref[part : 2 * part, :] + got_ref[:part, :]
-    loss_ref[...] = jnp.concatenate(
-        [both_ref[2 * part : 2 * part + 4, :], got_ref[2 * part + 4 :, :]], axis=0
-    )
-
-
-def add_kernel(part, one_ref, other_ref, *refs):
-    refs[-1][...] = one_ref[...] + other_ref[...]
-
-
-def turn(kernel, kept, got, part, shapes, name, ahead=()):
+    for k, ref in enumerate(outs):
+        at = slice(k * part, (k + 1) * part)
+        ref[:part, :] = kept_ref[at, :] + got_ref[at, :]
+        ref[part:, :] = jnp.concatenate(
+            [lost[k : k + 1], found[k : k + 1], jnp.zeros((6, lost.shape[1]), F32)], axis=0
+        )
+
+
+def turn_two_kernel(part, *refs):
+    *notes, sum_ref, loss_ref = refs
+    held = [ref[:part, :] for ref in notes]
+    sum_ref[...] = (held[0] + held[1]) + (held[2] + held[3])
+    loss_ref[...] = jnp.concatenate([ref[part : part + 2, :] for ref in notes], axis=0)
+
+
+def turn_three_kernel(part, *refs):
+    held = [ref[...] for ref in refs[:4]]
+    refs[-1][...] = (held[0] + held[1]) + (held[2] + held[3])
+
+
+def turn(kernel, held, part, shapes, name, ahead=()):
     return pl.pallas_call(
         functools.partial(kernel, part),
-        out_shape=[jax.ShapeDtypeStruct((rows, kept.shape[1]), F32) for rows in shapes],
-        in_specs=[whole()] * 2 + [whole(pl.ANY)] * len(ahead),
+        out_shape=[jax.ShapeDtypeStruct((rows, held[0].shape[1]), F32) for rows in shapes],
+        in_specs=[whole()] * len(held) + [whole(pl.ANY)] * len(ahead),
         out_specs=[whole()] * len(shapes),
         compiler_params=pltpu.CompilerParams(vmem_limit_bytes=4 * MIB),
         name=name,
-    )(kept, got, *ahead)
+    )(*held, *ahead)
 
 
 def pass_on_kernel(next_up_ref, got_up_ref, next_down_ref, got_down_ref, *refs):
@@ -394,7 +392,7 @@
 def assemble_kernel(part, me_ref, *refs):
     *held, trunk_ref = refs
     me = me_ref[0]
-    order = iter((0, 4, 2, 6, 1, 5, 3, 7))
+    order = iter(range(8))
     for ref in held:
         for k in range(ref.shape[0] // part):
             at = pl.ds(pl.multiple_of((me ^ next(order)) * part, part), part)
@@ -448,12 +446,14 @@
     capacity = 2 * rows // experts
     me = lax.axis_index("expert").astype(jnp.int32).reshape(1)
 
-    rounded = expert_params[0].astype(BF16)
-    weights = [swap(rounded, "dp", j) for j in range(replicas)]
+    up, down = expert_params[0, 0].astype(BF16), expert_params[0, 1].astype(BF16)
+    near_up, near_down = swap(up, "dp", 1), swap(down, "dp", 2)
     *blocks, place = pack(me, sample_index, region[:, 0], cell_table, targets, experts, capacity)
+    ups, downs = pair(up, near_up, place), pair(down, near_down, place)
+    weights = [ups, swap(ups, "dp", 2), downs, swap(downs, "dp", 1)]
     arrived = [swap(blocks[s], "expert", s) for s in range(experts)]
     if in_turns(experts):
-        batches = ((0,), (4, 6), (1, 2, 3), (5,), (7,))
+        batches = ((0,), (4, 5), (2, 3, 1), (6,), (7,))
     else:
         batches = (range(experts // 2), range(experts // 2, experts))
 
@@ -473,36 +473,28 @@
     got_down = swap(sent_down, "dp", 2)
     part = width // experts
     if in_turns(experts):
-        kept, note = turn(
-            turn_one_kernel, kept, swap(note, "expert", 1), part, (2 * part + 8,) * 2, "turn_one"
-        )
-        (both,) = turn(
-            turn_two_kernel, kept, swap(note, "expert", 2), part, (2 * part + 8,), "turn_two"
-        )
-        total, loss = turn(
+        ours, *notes = turn(
+            turn_one_kernel, [kept, swap(note, "expert", 1)], part, (part + 8,) * 4, "turn_one"
+        )
+        notes = [swap(note, "expert", s) for note, s in zip(notes, (2, 4, 6))]
+        total, loss = turn(turn_two_kernel, [ours] + notes, part, (part, experts), "turn_two")
+        (total,) = turn(
             turn_three_kernel,
-            both,
-            swap(both, "expert", 4),
+            [total] + [swap(total, "dp", j) for j in range(1, replicas)],
             part,
-            (2 * part, experts),
+            (part,),
             "turn_three",
+            (got_up, got_down),
         )
         more_up, more_down = pass_on(next_up, got_up, next_down, got_down, (total,))
-        (total,) = turn(
-            add_kernel, total, swap(total, "dp", 1), part, (2 * part,), "turn_four", (got_up, got_down)
-        )
-        (total,) = turn(
-            add_kernel, total, swap(total, "dp", 2), part, (2 * part,), "turn_five", (more_up, more_down)
-        )
-        other = swap(total, "expert", 2)
-        rest = swap(jnp.concatenate([total, other], axis=0), "expert", 1)
-        trunk_grad = assemble(me, [total, other, rest], part)
+        chip = jnp.concatenate([total, swap(total, "expert", 1)], axis=0)
+        trunk_grad = assemble(me, [chip] + [swap(chip, "expert", s) for s in (2, 4, 6)], part)
     else:
         more_up, more_down = pass_on(next_up, got_up, next_down, got_down)
         trunk_grad = lax.psum(kept, ("dp", "expert"))
-        mine = jnp.arange(experts, dtype=jnp.int32) ^ me
-        note = note.reshape(experts, capacity)
-        loss = lax.all_to_all(note[mine], "expert", split_axis=0, concat_axis=0, tiled=True)[mine]
+        places = jnp.arange(experts, dtype=jnp.int32) ^ me
+        note = note.reshape(experts, capacity)[places]
+        loss = lax.all_to_all(note, "expert", split_axis=0, concat_axis=0, tiled=True)[places]
     row_loss = loss_by_row(place, loss)
 
     grads = jnp.stack(

time: 120 us -> 111 us (0.925)
  waiting for transfers between devices: 46 us -> 37.9 us
  local copies, waits for them, and re-layouts: 7.81 us -> 3.7 us
  starting transfers between devices: 30.1 us -> 33.5 us
    ppermute x21 -> x26, waiting for transfers between devices: 46 us -> 37.9 us  [swap(): lax.ppermute(value, axis, [(i, i ^ s) for i in range(lax.axis_size(axis))])]
    unnamed x20 -> x16, local copies, waits for them, and re-layouts: 7.81 us -> 3.66 us
    ppermute x21 -> x26, starting transfers between devices: 30.1 us -> 33.5 us  [swap(): lax.ppermute(value, axis, [(i, i ^ s) for i in range(lax.axis_size(axis))])]
    another operation x0 -> x1, other arithmetic: none -> 1.29 us
    convert_element_type x1 -> x0, other arithmetic: 1.29 us -> none  [on_device(): rounded = expert_params[0].astype(BF16)]
  transfers between devices with their start and end apart: 21 -> 26, of which waited for: 10 -> 13; matrix products, arithmetic and copies ran while one was open for 2% -> 0% of each run, Pallas kernels for 22% -> 25%
where the time goes in v4:
time: 111 us
  waiting for transfers between devices  37.9 us (34%)
  starting transfers between devices  33.5 us (30%)
  Pallas kernels  31.4 us (28%)
  local copies, waits for them, and re-layouts  3.7 us (3%)
  other arithmetic  3.67 us (3%)
    ppermute x26, waiting for transfers between devices, swap(): lax.ppermute(value, axis, [(i, i ^ s) for i in range(lax.axis_size(axis))])  37.9 us
    ppermute x26, starting transfers between devices, swap(): lax.ppermute(value, axis, [(i, i ^ s) for i in range(lax.axis_size(axis))])  33.5 us
    pallas_call x5, Pallas kernels, expert_call(): pl.pallas_call(functools.partial(expert_kernel, counts, order, first, len...  25.7 us
    unnamed x16, local copies, waits for them, and re-layouts  3.66 us
    pallas_call x1, Pallas kernels, pack(): pl.pallas_call(functools.partial(pack_kernel, experts, capacity), out_sha...  3.52 us
  transfers between devices with their start and end apart: 26, of which 13 were waited for; matrix products, arithmetic and copies ran while one was open for 0% of the time, Pallas kernels for 25%

profile of v4, /device:TPU:0, one launch (start us, length us, event | category | flops | bytes accessed | tf_op | source)
XLA Modules:
  0.0 111.0 jit_solution(14637832599201750620)
XLA Ops:
  2.0 3.0 %collective-permute-start.3 = (bf16[256,512]{1,0:T(8,128)(2,1)S(1)}, bf16[256,512]{1,0:T(8,128)(2,1)S(1)}, u32[]{:S(2)}, u32[]{:S(2)}) collective-permute-start(bf16[256,512]{1,0:T(8,128)(2,1)S(1)} %get-tuple-element.82.one_ref), channel_id=1, source_target_pairs={{0,16},{8,24},{16,0},{24,8},{1,17},{9,25},{17,1},{25,9},{2,18},{10... | collective-permute-start | bytes 786440 | tf_op jit(solution)/shard_map/ppermute | solution.py:429
  5.0 1.5 %collective-permute-start.1 = (bf16[256,512]{1,0:T(8,128)(2,1)S(1)}, bf16[256,512]{1,0:T(8,128)(2,1)S(1)}, u32[]{:S(2)}, u32[]{:S(2)}) collective-permute-start(bf16[256,512]{1,0:T(8,128)(2,1)S(1)} %get-tuple-element.83.one_ref), channel_id=1, source_target_pairs={{0,8},{8,0},{16,24},{24,16},{1,9},{9,1},{17,25},{25,17},{2,10},{10... | collective-permute-start | bytes 786440 | tf_op jit(solution)/shard_map/ppermute | solution.py:429
  10.1 3.5 %pack_rows.1 = (bf16[256,512]{1,0:T(8,128)(2,1)S(1)}, bf16[256,512]{1,0:T(8,128)(2,1)S(1)}, bf16[256,512]{1,0:T(8,128)(2,1)S(1)}, bf16[256,512]{1,0:T(8,128)(2,1...) custom-call(s32[1]{0:T(128)} %bitcast.me_ref.refs_12_, ...), custom_call_target="tpu_custom_call" | custom-call | flops 3221225472 | bytes 6291456 | tf_op jit(solution)/shard_map/pack_rows/pallas_call | solution.py:84
  15.0 2.6 %collective-permute-start.9 = (bf16[256,512]{1,0:T(8,128)(2,1)S(1)}, bf16[256,512]{1,0:T(8,128)(2,1)S(1)}, u32[]{:S(2)}, u32[]{:S(2)}) collective-permute-start(bf16[256,512]{1,0:T(8,128)(2,1)S(1)} %get-tuple-element.47), channel_id=1, source_target_pairs={{0,4},{1,5},{2,6},{3,7},{4,0},{5,1},{6,2},{7,3},{8,12},{9,13},{10,... | collective-permute-start | bytes 786440 | tf_op jit(solution)/shard_map/ppermute | solution.py:429
  17.6 3.7 %collective-permute-start = (bf16[256,512]{1,0:T(8,128)(2,1)S(1)}, bf16[256,512]{1,0:T(8,128)(2,1)S(1)}, u32[]{:S(2)}, u32[]{:S(2)}) collective-permute-start(bf16[256,512]{1,0:T(8,128)(2,1)S(1)} %get-tuple-element.41), channel_id=1, source_target_pairs={{0,7},{1,6},{2,5},{3,4},{4,3},{5,2},{6,1},{7,0},{8,15},{9,14},{10,... | collective-permute-start | bytes 786440 | tf_op jit(solution)/shard_map/ppermute | solution.py:429
  21.2 5.7 %collective-permute-done.2.refs_3_.refs_4_.refs_5_ = bf16[2,256,512]{2,1,0:T(8,128)(2,1)S(1)} collective-permute-done((bf16[2,256,512]{2,1,0:T(8,128)(2,1)S(1)}, bf16[2,256,512]{2,1,0:T(8,128)(2,1)S(1)}, u32[]{:S(2)}, u32[]{:S(2)}) %collective-permute-start.2) | collective-permute-done | bytes 524320 | tf_op jit(solution)/shard_map/ppermute | solution.py:429
  26.9 3.6 %collective-permute-start.5 = (bf16[256,512]{1,0:T(8,128)(2,1)S(1)}, bf16[256,512]{1,0:T(8,128)(2,1)S(1)}, u32[]{:S(2)}, u32[]{:S(2)}) collective-permute-start(bf16[256,512]{1,0:T(8,128)(2,1)S(1)} %get-tuple-element.43), channel_id=1, source_target_pairs={{0,6},{1,7},{2,4},{3,5},{4,2},{5,3},{6,0},{7,1},{8,14},{9,15},{10,... | collective-permute-start | bytes 786440 | tf_op jit(solution)/shard_map/ppermute | solution.py:429
  30.5 3.2 %expert_rows.5 = (f32[4,2,256,512]{3,2,1,0:T(8,128)S(1)}, f32[256,256]{1,0:T(8,128)S(1)}, f32[1,256]{1,0:T(1,128)S(1)}) custom-call(bf16[256,512]{1,0:T(8,128)(2,1)S(1)} %get-tuple-element.49.refs_0_, bf16[256,256]{1,0:T(8,128)(2,1)S(1)} %copy-done, bf16[2,256,512]{2,1,0:T(8,128)(2,1)S(1)} %pair.2.refs_2_.refs_3_.refs_4_, ...), custom_call_target="tpu_custom_call" | custom-call | flops 1610612736 | bytes 10485760 | tf_op jit(solution)/shard_map/expert_rows/pallas_call | solution.py:294
  33.7 12.8 %collective-permute-done.9.refs_0_ = bf16[256,512]{1,0:T(8,128)(2,1)S(1)} collective-permute-done((bf16[256,512]{1,0:T(8,128)(2,1)S(1)}, bf16[256,512]{1,0:T(8,128)(2,1)S(1)}, u32[]{:S(2)}, u32[]{:S(2)}) %collective-permute-start.9) | collective-permute-done | bytes 262176 | tf_op jit(solution)/shard_map/ppermute | solution.py:429
  46.5 3.2 %collective-permute-done.10.refs_1_ = bf16[256,512]{1,0:T(8,128)(2,1)S(1)} collective-permute-done((bf16[256,512]{1,0:T(8,128)(2,1)S(1)}, bf16[256,512]{1,0:T(8,128)(2,1)S(1)}, u32[]{:S(2)}, u32[]{:S(2)}) %collective-permute-start.10) | collective-permute-done | bytes 262176 | tf_op jit(solution)/shard_map/ppermute | solution.py:429
  49.7 2.2 %collective-permute-start.8 = (bf16[256,512]{1,0:T(8,128)(2,1)S(1)}, bf16[256,512]{1,0:T(8,128)(2,1)S(1)}, u32[]{:S(2)}, u32[]{:S(2)}) collective-permute-start(bf16[256,512]{1,0:T(8,128)(2,1)S(1)} %get-tuple-element.46), channel_id=1, source_target_pairs={{0,1},{1,0},{2,3},{3,2},{4,5},{5,4},{6,7},{7,6},{8,9},{9,8},{10,11... | collective-permute-start | bytes 786440 | tf_op jit(solution)/shard_map/ppermute | solution.py:429
  51.9 6.5 %expert_rows.6 = (f32[4,2,256,512]{3,2,1,0:T(8,128)S(1)}, f32[256,256]{1,0:T(8,128)S(1)}, f32[2,256]{1,0:T(2,128)S(1)}) custom-call(bf16[256,512]{1,0:T(8,128)(2,1)S(1)} %collective-permute-done.9.refs_0_, bf16[256,512]{1,0:T(8,128)(2,1)S(1)} %collective-permute-done.10.refs_1_, bf16[256,256]{1,0:T(8,128)(2,1)S(1)} %copy-done, ...), custom_call_target="tpu_custom_call" | custom-call | flops 3221225472 | bytes 10485760 | tf_op jit(solution)/shard_map/expert_rows/pallas_call | solution.py:294
  58.4 3.5 %collective-permute-done.7.refs_1_ = bf16[256,512]{1,0:T(8,128)(2,1)S(1)} collective-permute-done((bf16[256,512]{1,0:T(8,128)(2,1)S(1)}, bf16[256,512]{1,0:T(8,128)(2,1)S(1)}, u32[]{:S(2)}, u32[]{:S(2)}) %collective-permute-start.7) | collective-permute-done | bytes 262176 | tf_op jit(solution)/shard_map/ppermute | solution.py:429
  61.9 9.4 %expert_rows.7 = (f32[4,2,256,512]{3,2,1,0:T(8,128)S(1)}, f32[256,256]{1,0:T(8,128)S(1)}, f32[3,256]{1,0:T(4,128)S(1)}) custom-call(bf16[256,512]{1,0:T(8,128)(2,1)S(1)} %collective-permute-done.6.refs_0_, bf16[256,512]{1,0:T(8,128)(2,1)S(1)} %collective-permute-done.7.refs_1_, bf16[256,512]{1,0:T(8,128)(2,1)S(1)} %collective-permute-done.8.refs_2_, ...), custom_call_target="tpu_custom_call" | custom-call | flops 4831838208 | bytes 10485760 | tf_op jit(solution)/shard_map/expert_rows/pallas_call | solution.py:294
  71.4 3.2 %expert_rows.8 = (f32[4,2,256,512]{3,2,1,0:T(8,128)S(1)}, f32[256,256]{1,0:T(8,128)S(1)}, f32[1,256]{1,0:T(1,128)S(1)}) custom-call(bf16[256,512]{1,0:T(8,128)(2,1)S(1)} %collective-permute-done.5.refs_0_, bf16[256,256]{1,0:T(8,128)(2,1)S(1)} %copy-done, bf16[2,256,512]{2,1,0:T(8,128)(2,1)S(1)} %pair.2.refs_2_.refs_3_.refs_4_, ...), custom_call_target="tpu_custom_call" | custom-call | flops 1610612736 | bytes 10485760 | tf_op jit(solution)/shard_map/expert_rows/pallas_call | solution.py:294
  74.6 3.5 %expert_rows.9 = (f32[2,256,512]{2,1,0:T(8,128)S(1)}, f32[256,512]{1,0:T(8,128)S(1)}, f32[256,512]{1,0:T(8,128)S(1)}, bf16[2,256,512]{2,1,0:T(8,128)(2,1)S(1)}, ...) custom-call(bf16[256,512]{1,0:T(8,128)(2,1)S(1)} %collective-permute-done.refs_0_, ...), custom_call_target="tpu_custom_call" | custom-call | flops 1610612736 | bytes 10485760 | tf_op jit(solution)/shard_map/expert_rows/pallas_call | solution.py:294
  81.5 2.4 %collective-permute-start.13 = (f32[40,256]{1,0:T(8,128)S(1)}, f32[40,256]{1,0:T(8,128)S(1)}, u32[]{:S(2)}, u32[]{:S(2)}) collective-permute-start(f32[40,256]{1,0:T(8,128)S(1)} %get-tuple-element.66), channel_id=1, source_target_pairs={{0,4},{1,5},{2,6},{3,7},{4,0},{5,1},{6,2},{7,3},{8,12},{9,13},{10,... | collective-permute-start | bytes 122888 | tf_op jit(solution)/shard_map/ppermute | solution.py:429
  85.3 2.3 %collective-permute-done.13.refs_2_ = f32[40,256]{1,0:T(8,128)S(1)} collective-permute-done((f32[40,256]{1,0:T(8,128)S(1)}, f32[40,256]{1,0:T(8,128)S(1)}, u32[]{:S(2)}, u32[]{:S(2)}) %collective-permute-start.13) | collective-permute-done | bytes 40992 | tf_op jit(solution)/shard_map/ppermute | solution.py:429
  87.6 2.1 %collective-permute-done.14.refs_3_ = f32[40,256]{1,0:T(8,128)S(1)} collective-permute-done((f32[40,256]{1,0:T(8,128)S(1)}, f32[40,256]{1,0:T(8,128)S(1)}, u32[]{:S(2)}, u32[]{:S(2)}) %collective-permute-start.14) | collective-permute-done | bytes 40992 | tf_op jit(solution)/shard_map/ppermute | solution.py:429
  90.7 1.5 %collective-permute-start.16 = (f32[32,256]{1,0:T(8,128)S(1)}, f32[32,256]{1,0:T(8,128)S(1)}, u32[]{:S(2)}, u32[]{:S(2)}) collective-permute-start(f32[32,256]{1,0:T(8,128)S(1)} %get-tuple-element.68.refs_0_), channel_id=1, source_target_pairs={{0,16},{8,24},{16,0},{24,8},{1,17},{9,25},{17,1},{25,9},{2,18},{10... | collective-permute-start | bytes 98312 | tf_op jit(solution)/shard_map/ppermute | solution.py:429
  99.1 2.4 %collective-permute-start.23 = (f32[64,256]{1,0:T(8,128)S(1)}, f32[64,256]{1,0:T(8,128)S(1)}, u32[]{:S(2)}, u32[]{:S(2)}) collective-permute-start(f32[64,256]{1,0:T(8,128)S(1)} %pad_maximum_fusion.1.refs_0_), channel_id=1, source_target_pairs={{0,6},{1,7},{2,4},{3,5},{4,2},{5,3},{6,0},{7,1},{8,14},{9,15},{10,... | collective-permute-start | bytes 196616 | tf_op jit(solution)/shard_map/ppermute | solution.py:429
  101.5 1.9 %collective-permute-start.21 = (f32[64,256]{1,0:T(8,128)S(1)}, f32[64,256]{1,0:T(8,128)S(1)}, u32[]{:S(2)}, u32[]{:S(2)}) collective-permute-start(f32[64,256]{1,0:T(8,128)S(1)} %pad_maximum_fusion.1.refs_0_), channel_id=1, source_target_pairs={{0,2},{1,3},{2,0},{3,1},{4,6},{5,7},{6,4},{7,5},{8,10},{9,11},{10,... | collective-permute-start | bytes 196616 | tf_op jit(solution)/shard_map/ppermute | solution.py:429
  105.8 2.0 %collective-permute-done.22.refs_2_ = f32[64,256]{1,0:T(8,128)S(1)} collective-permute-done((f32[64,256]{1,0:T(8,128)S(1)}, f32[64,256]{1,0:T(8,128)S(1)}, u32[]{:S(2)}, u32[]{:S(2)}) %collective-permute-start.22) | collective-permute-done | bytes 65568 | tf_op jit(solution)/shard_map/ppermute | solution.py:429
  108.8 2.2 %divide_subtract_fusion = (f32[1,2,256,512]{3,2,1,0:T(8,128)}, f32[1,2,256,512]{3,2,1,0:T(8,128)}, f32[1,2,256,512]{3,2,1,0:T(8,128)}) fusion(f32[1,2,256,512]{3,2,1,0:T(8,128)S(1)} %copy-done.5, f32[1,1,256,512]{3,2,1,0:T(8,128)S(1)} %get-tuple-element.81, f32[1,1,256,512]{3,2,1,0:T(8,128)S(1)} %get-tuple-element.80, f32[1,2,256,512]{3,2,1,0:T(8,128)S(1)} %copy-done.6, ...), kind=kLoop, calls=%fused_computation.3 | loop fusion | flops 3407872 | bytes 7340032 | tf_op jit(solution)/shard_map/sub | solution.py:420
  (63 shorter events, 22.4 us)
Async XLA Ops:
  2.0 12.3 %collective-permute-start.3 = (bf16[256,512]{1,0:T(8,128)(2,1)S(1)}, bf16[256,512]{1,0:T(8,128)(2,1)S(1)}, u32[]{:S(2)}, u32[]{:S(2)}) collective-permute-start(bf16[256,512]{1,0:T(8,128)(2,1)S(1)} %get-tuple-element.82.one_ref), channel_id=1, source_target_pairs={{0,16},{8,24},{16,0},{24,8},{1,17},{9,25},{17,1},{25,9},{2,18},{10... | collective-permute-start | bytes 786440 | tf_op jit(solution)/shard_map/ppermute | solution.py:429
  5.0 8.7 %collective-permute-start.1 = (bf16[256,512]{1,0:T(8,128)(2,1)S(1)}, bf16[256,512]{1,0:T(8,128)(2,1)S(1)}, u32[]{:S(2)}, u32[]{:S(2)}) collective-permute-start(bf16[256,512]{1,0:T(8,128)(2,1)S(1)} %get-tuple-element.83.one_ref), channel_id=1, source_target_pairs={{0,8},{8,0},{16,24},{24,16},{1,9},{9,1},{17,25},{25,17},{2,10},{10... | collective-permute-start | bytes 786440 | tf_op jit(solution)/shard_map/ppermute | solution.py:429
  13.7 13.2 %collective-permute-start.2 = (bf16[2,256,512]{2,1,0:T(8,128)(2,1)S(1)}, bf16[2,256,512]{2,1,0:T(8,128)(2,1)S(1)}, u32[]{:S(2)}, u32[]{:S(2)}) collective-permute-start(bf16[2,256,512]{2,1,0:T(8,128)(2,1)S(1)} %pair.2.refs_2_.refs_3_.refs_4_), channel_id=1, source_target_pairs={{0,16},{8,24},{16,0},{24,8},{1,17},{9,25},{17,1},{25,9},{2,18},{10... | collective-permute-start | bytes 1572872 | tf_op jit(solution)/shard_map/ppermute | solution.py:429
  14.3 16.2 %collective-permute-start.4 = (bf16[2,256,512]{2,1,0:T(8,128)(2,1)S(1)}, bf16[2,256,512]{2,1,0:T(8,128)(2,1)S(1)}, u32[]{:S(2)}, u32[]{:S(2)}) collective-permute-start(bf16[2,256,512]{2,1,0:T(8,128)(2,1)S(1)} %pair.3.refs_4_.refs_5_.refs_6_), channel_id=1, source_target_pairs={{0,8},{8,0},{16,24},{24,16},{1,9},{9,1},{17,25},{25,17},{2,10},{10... | collective-permute-start | bytes 1572872 | tf_op jit(solution)/shard_map/ppermute | solution.py:429
  15.0 31.5 %collective-permute-start.9 = (bf16[256,512]{1,0:T(8,128)(2,1)S(1)}, bf16[256,512]{1,0:T(8,128)(2,1)S(1)}, u32[]{:S(2)}, u32[]{:S(2)}) collective-permute-start(bf16[256,512]{1,0:T(8,128)(2,1)S(1)} %get-tuple-element.47), channel_id=1, source_target_pairs={{0,4},{1,5},{2,6},{3,7},{4,0},{5,1},{6,2},{7,3},{8,12},{9,13},{10,... | collective-permute-start | bytes 786440 | tf_op jit(solution)/shard_map/ppermute | solution.py:429
  17.6 32.1 %collective-permute-start.10 = (bf16[256,512]{1,0:T(8,128)(2,1)S(1)}, bf16[256,512]{1,0:T(8,128)(2,1)S(1)}, u32[]{:S(2)}, u32[]{:S(2)}) collective-permute-start(bf16[256,512]{1,0:T(8,128)(2,1)S(1)} %get-tuple-element.48), channel_id=1, source_target_pairs={{0,5},{1,4},{2,7},{3,6},{4,1},{5,0},{6,3},{7,2},{8,13},{9,12},{10,... | collective-permute-start | bytes 786440 | tf_op jit(solution)/shard_map/ppermute | solution.py:429
  17.6 57.0 %collective-permute-start = (bf16[256,512]{1,0:T(8,128)(2,1)S(1)}, bf16[256,512]{1,0:T(8,128)(2,1)S(1)}, u32[]{:S(2)}, u32[]{:S(2)}) collective-permute-start(bf16[256,512]{1,0:T(8,128)(2,1)S(1)} %get-tuple-element.41), channel_id=1, source_target_pairs={{0,7},{1,6},{2,5},{3,4},{4,3},{5,2},{6,1},{7,0},{8,15},{9,14},{10,... | collective-permute-start | bytes 786440 | tf_op jit(solution)/shard_map/ppermute | solution.py:429
  26.9 44.5 %collective-permute-start.5 = (bf16[256,512]{1,0:T(8,128)(2,1)S(1)}, bf16[256,512]{1,0:T(8,128)(2,1)S(1)}, u32[]{:S(2)}, u32[]{:S(2)}) collective-permute-start(bf16[256,512]{1,0:T(8,128)(2,1)S(1)} %get-tuple-element.43), channel_id=1, source_target_pairs={{0,6},{1,7},{2,4},{3,5},{4,2},{5,3},{6,0},{7,1},{8,14},{9,15},{10,... | collective-permute-start | bytes 786440 | tf_op jit(solution)/shard_map/ppermute | solution.py:429
  30.5 27.9 %collective-permute-start.6 = (bf16[256,512]{1,0:T(8,128)(2,1)S(1)}, bf16[256,512]{1,0:T(8,128)(2,1)S(1)}, u32[]{:S(2)}, u32[]{:S(2)}) collective-permute-start(bf16[256,512]{1,0:T(8,128)(2,1)S(1)} %get-tuple-element.44), channel_id=1, source_target_pairs={{0,2},{1,3},{2,0},{3,1},{4,6},{5,7},{6,4},{7,5},{8,10},{9,11},{10,... | collective-permute-start | bytes 786440 | tf_op jit(solution)/shard_map/ppermute | solution.py:429
  46.5 15.4 %collective-permute-start.7 = (bf16[256,512]{1,0:T(8,128)(2,1)S(1)}, bf16[256,512]{1,0:T(8,128)(2,1)S(1)}, u32[]{:S(2)}, u32[]{:S(2)}) collective-permute-start(bf16[256,512]{1,0:T(8,128)(2,1)S(1)} %get-tuple-element.45), channel_id=1, source_target_pairs={{0,3},{1,2},{2,1},{3,0},{4,7},{5,6},{6,5},{7,4},{8,11},{9,10},{10,... | collective-permute-start | bytes 786440 | tf_op jit(solution)/shard_map/ppermute | solution.py:429
  49.7 12.3 %collective-permute-start.8 = (bf16[256,512]{1,0:T(8,128)(2,1)S(1)}, bf16[256,512]{1,0:T(8,128)(2,1)S(1)}, u32[]{:S(2)}, u32[]{:S(2)}) collective-permute-start(bf16[256,512]{1,0:T(8,128)(2,1)S(1)} %get-tuple-element.46), channel_id=1, source_target_pairs={{0,1},{1,0},{2,3},{3,2},{4,5},{5,4},{6,7},{7,6},{8,9},{9,8},{10,11... | collective-permute-start | bytes 786440 | tf_op jit(solution)/shard_map/ppermute | solution.py:429
  78.1 18.0 %collective-permute-start.18 = (bf16[2,256,512]{2,1,0:T(8,128)(2,1)S(1)}, bf16[2,256,512]{2,1,0:T(8,128)(2,1)S(1)}, u32[]{:S(2)}, u32[]{:S(2)}) collective-permute-start(bf16[2,256,512]{2,1,0:T(8,128)(2,1)S(1)} %get-tuple-element.69), channel_id=1, source_target_pairs={{0,8},{8,0},{16,24},{24,16},{1,9},{9,1},{17,25},{25,17},{2,10},{10... | collective-permute-start | bytes 1572872 | tf_op jit(solution)/shard_map/ppermute | solution.py:429
  79.0 17.2 %collective-permute-start.19 = (bf16[2,256,512]{2,1,0:T(8,128)(2,1)S(1)}, bf16[2,256,512]{2,1,0:T(8,128)(2,1)S(1)}, u32[]{:S(2)}, u32[]{:S(2)}) collective-permute-start(bf16[2,256,512]{2,1,0:T(8,128)(2,1)S(1)} %get-tuple-element.70), channel_id=1, source_target_pairs={{0,16},{8,24},{16,0},{24,8},{1,17},{9,25},{17,1},{25,9},{2,18},{10... | collective-permute-start | bytes 1572872 | tf_op jit(solution)/shard_map/ppermute | solution.py:429
  80.9 4.5 %collective-permute-start.12 = (f32[40,256]{1,0:T(8,128)S(1)}, f32[40,256]{1,0:T(8,128)S(1)}, u32[]{:S(2)}, u32[]{:S(2)}) collective-permute-start(f32[40,256]{1,0:T(8,128)S(1)} %get-tuple-element.65), channel_id=1, source_target_pairs={{0,2},{1,3},{2,0},{3,1},{4,6},{5,7},{6,4},{7,5},{8,10},{9,11},{10,... | collective-permute-start | bytes 122888 | tf_op jit(solution)/shard_map/ppermute | solution.py:429
  81.5 6.1 %collective-permute-start.13 = (f32[40,256]{1,0:T(8,128)S(1)}, f32[40,256]{1,0:T(8,128)S(1)}, u32[]{:S(2)}, u32[]{:S(2)}) collective-permute-start(f32[40,256]{1,0:T(8,128)S(1)} %get-tuple-element.66), channel_id=1, source_target_pairs={{0,4},{1,5},{2,6},{3,7},{4,0},{5,1},{6,2},{7,3},{8,12},{9,13},{10,... | collective-permute-start | bytes 122888 | tf_op jit(solution)/shard_map/ppermute | solution.py:429
  83.9 5.8 %collective-permute-start.14 = (f32[40,256]{1,0:T(8,128)S(1)}, f32[40,256]{1,0:T(8,128)S(1)}, u32[]{:S(2)}, u32[]{:S(2)}) collective-permute-start(f32[40,256]{1,0:T(8,128)S(1)} %get-tuple-element.67), channel_id=1, source_target_pairs={{0,6},{1,7},{2,4},{3,5},{4,2},{5,3},{6,0},{7,1},{8,14},{9,15},{10,... | collective-permute-start | bytes 122888 | tf_op jit(solution)/shard_map/ppermute | solution.py:429
  89.7 4.9 %collective-permute-start.17 = (f32[32,256]{1,0:T(8,128)S(1)}, f32[32,256]{1,0:T(8,128)S(1)}, u32[]{:S(2)}, u32[]{:S(2)}) collective-permute-start(f32[32,256]{1,0:T(8,128)S(1)} %get-tuple-element.68.refs_0_), channel_id=1, source_target_pairs={{0,24},{8,16},{16,8},{24,0},{1,25},{9,17},{17,9},{25,1},{2,26},{10... | collective-permute-start | bytes 98312 | tf_op jit(solution)/shard_map/ppermute | solution.py:429
  90.7 4.2 %collective-permute-start.16 = (f32[32,256]{1,0:T(8,128)S(1)}, f32[32,256]{1,0:T(8,128)S(1)}, u32[]{:S(2)}, u32[]{:S(2)}) collective-permute-start(f32[32,256]{1,0:T(8,128)S(1)} %get-tuple-element.68.refs_0_), channel_id=1, source_target_pairs={{0,16},{8,24},{16,0},{24,8},{1,17},{9,25},{17,1},{25,9},{2,18},{10... | collective-permute-start | bytes 98312 | tf_op jit(solution)/shard_map/ppermute | solution.py:429
  92.2 3.9 %collective-permute-start.15 = (f32[32,256]{1,0:T(8,128)S(1)}, f32[32,256]{1,0:T(8,128)S(1)}, u32[]{:S(2)}, u32[]{:S(2)}) collective-permute-start(f32[32,256]{1,0:T(8,128)S(1)} %get-tuple-element.68.refs_0_), channel_id=1, source_target_pairs={{0,8},{8,0},{16,24},{24,16},{1,9},{9,1},{17,25},{25,17},{2,10},{10... | collective-permute-start | bytes 98312 | tf_op jit(solution)/shard_map/ppermute | solution.py:429
  96.3 12.3 %collective-permute-start.24 = (bf16[256,512]{1,0:T(8,128)(2,1)S(1)}, bf16[256,512]{1,0:T(8,128)(2,1)S(1)}, u32[]{:S(2)}, u32[]{:S(2)}) collective-permute-start(bf16[256,512]{1,0:T(8,128)(2,1)S(1)} %get-tuple-element.75), channel_id=1, source_target_pairs={{0,16},{8,24},{16,0},{24,8},{1,17},{9,25},{17,1},{25,9},{2,18},{10... | collective-permute-start | bytes 786440 | tf_op jit(solution)/shard_map/ppermute | solution.py:429
  96.8 11.8 %collective-permute-start.25 = (bf16[256,512]{1,0:T(8,128)(2,1)S(1)}, bf16[256,512]{1,0:T(8,128)(2,1)S(1)}, u32[]{:S(2)}, u32[]{:S(2)}) collective-permute-start(bf16[256,512]{1,0:T(8,128)(2,1)S(1)} %get-tuple-element.76), channel_id=1, source_target_pairs={{0,8},{8,0},{16,24},{24,16},{1,9},{9,1},{17,25},{25,17},{2,10},{10... | collective-permute-start | bytes 786440 | tf_op jit(solution)/shard_map/ppermute | solution.py:429
  99.1 6.8 %collective-permute-start.23 = (f32[64,256]{1,0:T(8,128)S(1)}, f32[64,256]{1,0:T(8,128)S(1)}, u32[]{:S(2)}, u32[]{:S(2)}) collective-permute-start(f32[64,256]{1,0:T(8,128)S(1)} %pad_maximum_fusion.1.refs_0_), channel_id=1, source_target_pairs={{0,6},{1,7},{2,4},{3,5},{4,2},{5,3},{6,0},{7,1},{8,14},{9,15},{10,... | collective-permute-start | bytes 196616 | tf_op jit(solution)/shard_map/ppermute | solution.py:429
  101.5 6.3 %collective-permute-start.22 = (f32[64,256]{1,0:T(8,128)S(1)}, f32[64,256]{1,0:T(8,128)S(1)}, u32[]{:S(2)}, u32[]{:S(2)}) collective-permute-start(f32[64,256]{1,0:T(8,128)S(1)} %pad_maximum_fusion.1.refs_0_), channel_id=1, source_target_pairs={{0,4},{1,5},{2,6},{3,7},{4,0},{5,1},{6,2},{7,3},{8,12},{9,13},{10,... | collective-permute-start | bytes 196616 | tf_op jit(solution)/shard_map/ppermute | solution.py:429
  101.5 6.3 %collective-permute-start.21 = (f32[64,256]{1,0:T(8,128)S(1)}, f32[64,256]{1,0:T(8,128)S(1)}, u32[]{:S(2)}, u32[]{:S(2)}) collective-permute-start(f32[64,256]{1,0:T(8,128)S(1)} %pad_maximum_fusion.1.refs_0_), channel_id=1, source_target_pairs={{0,2},{1,3},{2,0},{3,1},{4,6},{5,7},{6,4},{7,5},{8,10},{9,11},{10,... | collective-permute-start | bytes 196616 | tf_op jit(solution)/shard_map/ppermute | solution.py:429
  (10 other events, 118.9 us)

commit v5 on v4

--- a/solution.py
+++ b/solution.py
@@ -119,7 +119,7 @@
 
 
 def expert_kernel(counts, order, first, last, *refs):
-    blocks, shares, experts, steps, step_rows = counts
+    blocks, shares, experts, steps, step_rows, relays = counts
     refs = list(refs)
 
     def take(n):
@@ -133,6 +133,7 @@
     downs = (downs_near.at[0], downs_far.at[0], downs_near.at[1], downs_far.at[1])
     if not first:
         prior_ref, prior_trunk_ref = take(2)
+    held = take(relays)
     if last:
         loss_refs = take(last - 1)
         (me_ref,) = take(1)
@@ -140,6 +141,8 @@
         kept_ref, note_ref = take(2)
     else:
         acc_ref, acc_trunk_ref, loss_ref = take(3)
+        for source, copy in zip(held, take(relays)):
+            copy[...] = source[...]
     x_ref, hid_ref, slope_ref = take(3)
     if last:
         acc_ref, acc_trunk_ref, loss_ref = take(3)
@@ -253,7 +256,7 @@
         row -= ref.shape[0]
 
 
-def expert_call(xs, trunk_weight, weights, prior, losses, me, order, last):
+def expert_call(xs, trunk_weight, weights, prior, losses, me, order, last, relays=()):
     experts = len(order)
     block_rows = xs[0].shape[0]
     width = trunk_weight.shape[0]
@@ -268,6 +271,7 @@
     args = list(xs) + [trunk_weight, *weights]
     if not first:
         args += list(prior)
+    args += relays
     in_specs = [whole()] * len(args)
     scratch = [
         pltpu.VMEM((rows, 2 * width), BF16),
@@ -290,7 +294,8 @@
         scratch += [pltpu.VMEM(a.shape, a.dtype) for a in (acc, acc_trunk, loss)]
     else:
         outs = [acc, acc_trunk, loss]
-    counts = (len(xs), shares, experts, steps, step_rows)
+        outs += [jax.ShapeDtypeStruct(relay.shape, relay.dtype) for relay in relays]
+    counts = (len(xs), shares, experts, steps, step_rows, len(relays))
     return pl.pallas_call(
         functools.partial(expert_kernel, counts, order, first, len(losses) + 1 if last else 0),
         out_shape=outs,
@@ -330,6 +335,11 @@
     refs[-1][...] = (held[0] + held[1]) + (held[2] + held[3])
 
 
+def turn_four_kernel(part, *refs):
+    for k in range(4):
+        refs[-1][k * part : (k + 1) * part, :] = refs[k][...]
+
+
 def turn(kernel, held, part, shapes, name, ahead=()):
     return pl.pallas_call(
         functools.partial(kernel, part),
@@ -392,7 +402,7 @@
 def assemble_kernel(part, me_ref, *refs):
     *held, trunk_ref = refs
     me = me_ref[0]
-    order = iter(range(8))
+    order = iter((0, 2, 4, 6, 1, 3, 5, 7))
     for ref in held:
         for k in range(ref.shape[0] // part):
             at = pl.ds(pl.multiple_of((me ^ next(order)) * part, part), part)
@@ -451,22 +461,24 @@
     *blocks, place = pack(me, sample_index, region[:, 0], cell_table, targets, experts, capacity)
     ups, downs = pair(up, near_up, place), pair(down, near_down, place)
     weights = [ups, swap(ups, "dp", 2), downs, swap(downs, "dp", 1)]
-    arrived = [swap(blocks[s], "expert", s) for s in range(experts)]
     if in_turns(experts):
-        batches = ((0,), (4, 5), (2, 3, 1), (6,), (7,))
+        batches, later = ((0,), (4, 5), (2, 3, 1), (6,), (7,)), (6, 7)
     else:
-        batches = (range(experts // 2), range(experts // 2, experts))
-
+        batches, later = (range(experts // 2), range(experts // 2, experts)), ()
     order = [s for batch in batches for s in batch]
+    arrived = {s: swap(blocks[s], "expert", s) for s in order if s not in later}
     prior, losses = None, []
     for k, batch in enumerate(batches):
         last = k == len(batches) - 1
+        relays = [blocks[s] for s in later] if k == 0 else []
         outs = expert_call(
-            [arrived[s] for s in batch], trunk_weight, weights, prior, losses, me, order, last
+            [arrived[s] for s in batch], trunk_weight, weights, prior, losses, me, order, last, relays
         )
         if not last:
             prior = outs[:2]
             losses.append(outs[2])
+            for s, block in zip(later, outs[3:]):
+                arrived[s] = swap(block, "expert", s)
     own, next_up, next_down, sent_up, sent_down, kept, note = outs
 
     got_up = swap(sent_up, "dp", 1)
@@ -487,8 +499,11 @@
             (got_up, got_down),
         )
         more_up, more_down = pass_on(next_up, got_up, next_down, got_down, (total,))
-        chip = jnp.concatenate([total, swap(total, "expert", 1)], axis=0)
-        trunk_grad = assemble(me, [chip] + [swap(chip, "expert", s) for s in (2, 4, 6)], part)
+        column = [total] + [swap(total, "expert", s) for s in (2, 4, 6)]
+        (column,) = turn(
+            turn_four_kernel, column, part, (4 * part,), "turn_four", (more_up, more_down)
+        )
+        trunk_grad = assemble(me, [column, swap(column, "expert", 1)], part)
     else:
         more_up, more_down = pass_on(next_up, got_up, next_down, got_down)
         trunk_grad = lax.psum(kept, ("dp", "expert"))

time: 111 us -> 104 us (0.937)
  waiting for transfers between devices: 37.9 us -> 25.5 us
  starting transfers between devices: 33.5 us -> 38.1 us
    ppermute x26, waiting for transfers between devices: 37.9 us -> 25.5 us  [swap(): lax.ppermute(value, axis, [(i, i ^ s) for i in range(lax.axis_size(axis))])]
    ppermute x26, starting transfers between devices: 33.5 us -> 38.1 us  [swap(): lax.ppermute(value, axis, [(i, i ^ s) for i in range(lax.axis_size(axis))])]
  transfers between devices with their start and end apart: 26 -> 26, of which waited for: 13 -> 13; matrix products, arithmetic and copies ran while one was open for 0% -> 2% of each run, Pallas kernels for 25% -> 26%
where the time goes in v5:
time: 104 us; the launch traced here: 103 us
  starting transfers between devices  38.1 us (37%)
  Pallas kernels  31.6 us (30%)
  waiting for transfers between devices  25.5 us (25%)
  local copies, waits for them, and re-layouts  3.7 us (4%)
  other arithmetic  3.66 us (4%)
    ppermute x26, starting transfers between devices, swap(): lax.ppermute(value, axis, [(i, i ^ s) for i in range(lax.axis_size(axis))])  38.1 us
    pallas_call x5, Pallas kernels, expert_call(): pl.pallas_call(functools.partial(expert_kernel, counts, order, first, len...  25.9 us
    ppermute x26, waiting for transfers between devices, swap(): lax.ppermute(value, axis, [(i, i ^ s) for i in range(lax.axis_size(axis))])  25.5 us
    unnamed x16, local copies, waits for them, and re-layouts  3.66 us
    pallas_call x1, Pallas kernels, pack(): pl.pallas_call(functools.partial(pack_kernel, experts, capacity), out_sha...  3.52 us
    sub x1, other arithmetic, adam_update(): params - learn_rate * first_hat / (jnp.sqrt(second_hat) + adam_eps)  2.15 us
  transfers between devices with their start and end apart: 26, of which 13 were waited for; matrix products, arithmetic and copies ran while one was open for 2% of the time, Pallas kernels for 26%

profile of v5, /device:TPU:0, one launch (start us, length us, event | category | flops | bytes accessed | tf_op | source)
XLA Modules:
  0.0 103.5 jit_solution(11397973936531829999)
XLA Ops:
  2.0 3.0 %collective-permute-start.2 = (bf16[256,512]{1,0:T(8,128)(2,1)S(1)}, bf16[256,512]{1,0:T(8,128)(2,1)S(1)}, u32[]{:S(2)}, u32[]{:S(2)}) collective-permute-start(bf16[256,512]{1,0:T(8,128)(2,1)S(1)} %get-tuple-element.86.one_ref), channel_id=1, source_target_pairs={{0,16},{8,24},{16,0},{24,8},{1,17},{9,25},{17,1},{25,9},{2,18},{10... | collective-permute-start | bytes 786440 | tf_op jit(solution)/shard_map/ppermute | solution.py:439
  5.0 1.5 %collective-permute-start = (bf16[256,512]{1,0:T(8,128)(2,1)S(1)}, bf16[256,512]{1,0:T(8,128)(2,1)S(1)}, u32[]{:S(2)}, u32[]{:S(2)}) collective-permute-start(bf16[256,512]{1,0:T(8,128)(2,1)S(1)} %get-tuple-element.87.one_ref), channel_id=1, source_target_pairs={{0,8},{8,0},{16,24},{24,16},{1,9},{9,1},{17,25},{25,17},{2,10},{10... | collective-permute-start | bytes 786440 | tf_op jit(solution)/shard_map/ppermute | solution.py:439
  10.1 3.5 %pack_rows.1 = (bf16[256,512]{1,0:T(8,128)(2,1)S(1)}, bf16[256,512]{1,0:T(8,128)(2,1)S(1)}, bf16[256,512]{1,0:T(8,128)(2,1)S(1)}, bf16[256,512]{1,0:T(8,128)(2,1...) custom-call(s32[1]{0:T(128)} %bitcast.me_ref.refs_12_, ...), custom_call_target="tpu_custom_call" | custom-call | flops 3221225472 | bytes 6291456 | tf_op jit(solution)/shard_map/pack_rows/pallas_call | solution.py:84
  15.0 2.6 %collective-permute-start.9 = (bf16[256,512]{1,0:T(8,128)(2,1)S(1)}, bf16[256,512]{1,0:T(8,128)(2,1)S(1)}, u32[]{:S(2)}, u32[]{:S(2)}) collective-permute-start(bf16[256,512]{1,0:T(8,128)(2,1)S(1)} %get-tuple-element.52), channel_id=1, source_target_pairs={{0,4},{1,5},{2,6},{3,7},{4,0},{5,1},{6,2},{7,3},{8,12},{9,13},{10,... | collective-permute-start | bytes 786440 | tf_op jit(solution)/shard_map/ppermute | solution.py:439
  17.6 1.6 %collective-permute-start.6 = (bf16[256,512]{1,0:T(8,128)(2,1)S(1)}, bf16[256,512]{1,0:T(8,128)(2,1)S(1)}, u32[]{:S(2)}, u32[]{:S(2)}) collective-permute-start(bf16[256,512]{1,0:T(8,128)(2,1)S(1)} %get-tuple-element.49), channel_id=1, source_target_pairs={{0,2},{1,3},{2,0},{3,1},{4,6},{5,7},{6,4},{7,5},{8,10},{9,11},{10,... | collective-permute-start | bytes 786440 | tf_op jit(solution)/shard_map/ppermute | solution.py:439
  19.1 7.7 %collective-permute-done.1.refs_3_.refs_4_.refs_5_ = bf16[2,256,512]{2,1,0:T(8,128)(2,1)S(1)} collective-permute-done((bf16[2,256,512]{2,1,0:T(8,128)(2,1)S(1)}, bf16[2,256,512]{2,1,0:T(8,128)(2,1)S(1)}, u32[]{:S(2)}, u32[]{:S(2)}) %collective-permute-start.1) | collective-permute-done | bytes 524320 | tf_op jit(solution)/shard_map/ppermute | solution.py:439
  27.2 1.4 %collective-permute-start.8 = (bf16[256,512]{1,0:T(8,128)(2,1)S(1)}, bf16[256,512]{1,0:T(8,128)(2,1)S(1)}, u32[]{:S(2)}, u32[]{:S(2)}) collective-permute-start(bf16[256,512]{1,0:T(8,128)(2,1)S(1)} %get-tuple-element.51), channel_id=1, source_target_pairs={{0,1},{1,0},{2,3},{3,2},{4,5},{5,4},{6,7},{7,6},{8,9},{9,8},{10,11... | collective-permute-start | bytes 786440 | tf_op jit(solution)/shard_map/ppermute | solution.py:439
  28.6 3.2 %expert_rows.5 = (f32[4,2,256,512]{3,2,1,0:T(8,128)S(1)}, f32[256,256]{1,0:T(8,128)S(1)}, f32[1,256]{1,0:T(1,128)S(1)}, bf16[256,512]{1,0:T(8,128)(2,1)S(1)}, bf16[256,512]{1,0:T(8,128)(2,1)S(1)}) custom-call(bf16[256,512]{1,0:T(8,128)(2,1)S(1)} %get-tuple-element.43.refs_0_, bf16[256,256]{1,0:T(8,128)(2,1)S(1)} %copy-done, ...), custom_call_target="tpu_custom_call" | custom-call | flops 1610612736 | bytes 10485760 | tf_op jit(solution)/shard_map/expert_rows/pallas_call | solution.py:299
  31.8 3.4 %collective-permute-done.9.refs_0_ = bf16[256,512]{1,0:T(8,128)(2,1)S(1)} collective-permute-done((bf16[256,512]{1,0:T(8,128)(2,1)S(1)}, bf16[256,512]{1,0:T(8,128)(2,1)S(1)}, u32[]{:S(2)}, u32[]{:S(2)}) %collective-permute-start.9) | collective-permute-done | bytes 262176 | tf_op jit(solution)/shard_map/ppermute | solution.py:439
  35.3 1.9 %collective-permute-start.4 = (bf16[256,512]{1,0:T(8,128)(2,1)S(1)}, bf16[256,512]{1,0:T(8,128)(2,1)S(1)}, u32[]{:S(2)}, u32[]{:S(2)}) collective-permute-start(bf16[256,512]{1,0:T(8,128)(2,1)S(1)} %get-tuple-element.47), channel_id=1, source_target_pairs={{0,7},{1,6},{2,5},{3,4},{4,3},{5,2},{6,1},{7,0},{8,15},{9,14},{10,... | collective-permute-start | bytes 786440 | tf_op jit(solution)/shard_map/ppermute | solution.py:439
  38.4 5.2 %collective-permute-start.5 = (bf16[256,512]{1,0:T(8,128)(2,1)S(1)}, bf16[256,512]{1,0:T(8,128)(2,1)S(1)}, u32[]{:S(2)}, u32[]{:S(2)}) collective-permute-start(bf16[256,512]{1,0:T(8,128)(2,1)S(1)} %get-tuple-element.48), channel_id=1, source_target_pairs={{0,6},{1,7},{2,4},{3,5},{4,2},{5,3},{6,0},{7,1},{8,14},{9,15},{10,... | collective-permute-start | bytes 786440 | tf_op jit(solution)/shard_map/ppermute | solution.py:439
  43.6 6.5 %expert_rows.6 = (f32[4,2,256,512]{3,2,1,0:T(8,128)S(1)}, f32[256,256]{1,0:T(8,128)S(1)}, f32[2,256]{1,0:T(2,128)S(1)}) custom-call(bf16[256,512]{1,0:T(8,128)(2,1)S(1)} %collective-permute-done.9.refs_0_, bf16[256,512]{1,0:T(8,128)(2,1)S(1)} %collective-permute-done.10.refs_1_, bf16[256,256]{1,0:T(8,128)(2,1)S(1)} %copy-done, ...), custom_call_target="tpu_custom_call" | custom-call | flops 3221225472 | bytes 10485760 | tf_op jit(solution)/shard_map/expert_rows/pallas_call | solution.py:299
  50.2 2.9 %collective-permute-done.7.refs_1_ = bf16[256,512]{1,0:T(8,128)(2,1)S(1)} collective-permute-done((bf16[256,512]{1,0:T(8,128)(2,1)S(1)}, bf16[256,512]{1,0:T(8,128)(2,1)S(1)}, u32[]{:S(2)}, u32[]{:S(2)}) %collective-permute-start.7) | collective-permute-done | bytes 262176 | tf_op jit(solution)/shard_map/ppermute | solution.py:439
  53.1 9.4 %expert_rows.7 = (f32[4,2,256,512]{3,2,1,0:T(8,128)S(1)}, f32[256,256]{1,0:T(8,128)S(1)}, f32[3,256]{1,0:T(4,128)S(1)}) custom-call(bf16[256,512]{1,0:T(8,128)(2,1)S(1)} %collective-permute-done.6.refs_0_, bf16[256,512]{1,0:T(8,128)(2,1)S(1)} %collective-permute-done.7.refs_1_, bf16[256,512]{1,0:T(8,128)(2,1)S(1)} %collective-permute-done.8.refs_2_, ...), custom_call_target="tpu_custom_call" | custom-call | flops 4831838208 | bytes 10485760 | tf_op jit(solution)/shard_map/expert_rows/pallas_call | solution.py:299
  62.6 3.2 %expert_rows.8 = (f32[4,2,256,512]{3,2,1,0:T(8,128)S(1)}, f32[256,256]{1,0:T(8,128)S(1)}, f32[1,256]{1,0:T(1,128)S(1)}) custom-call(bf16[256,512]{1,0:T(8,128)(2,1)S(1)} %collective-permute-done.5.refs_0_, bf16[256,256]{1,0:T(8,128)(2,1)S(1)} %copy-done, bf16[2,256,512]{2,1,0:T(8,128)(2,1)S(1)} %pair.2.refs_2_.refs_3_.refs_4_, ...), custom_call_target="tpu_custom_call" | custom-call | flops 1610612736 | bytes 10485760 | tf_op jit(solution)/shard_map/expert_rows/pallas_call | solution.py:299
  65.8 3.5 %expert_rows.9 = (f32[2,256,512]{2,1,0:T(8,128)S(1)}, f32[256,512]{1,0:T(8,128)S(1)}, f32[256,512]{1,0:T(8,128)S(1)}, bf16[2,256,512]{2,1,0:T(8,128)(2,1)S(1)}, ...) custom-call(bf16[256,512]{1,0:T(8,128)(2,1)S(1)} %collective-permute-done.4.refs_0_, ...), custom_call_target="tpu_custom_call" | custom-call | flops 1610612736 | bytes 10485760 | tf_op jit(solution)/shard_map/expert_rows/pallas_call | solution.py:299
  71.0 3.6 %collective-permute-start.11 = (f32[136,256]{1,0:T(8,128)S(1)}, f32[136,256]{1,0:T(8,128)S(1)}, u32[]{:S(2)}, u32[]{:S(2)}) collective-permute-start(f32[136,256]{1,0:T(8,128)S(1)} %get-tuple-element.67), channel_id=1, source_target_pairs={{0,1},{1,0},{2,3},{3,2},{4,5},{5,4},{6,7},{7,6},{8,9},{9,8},{10,11... | collective-permute-start | bytes 417800 | tf_op jit(solution)/shard_map/ppermute | solution.py:439
  75.7 4.1 %collective-permute-start.13 = (f32[40,256]{1,0:T(8,128)S(1)}, f32[40,256]{1,0:T(8,128)S(1)}, u32[]{:S(2)}, u32[]{:S(2)}) collective-permute-start(f32[40,256]{1,0:T(8,128)S(1)} %get-tuple-element.70), channel_id=1, source_target_pairs={{0,4},{1,5},{2,6},{3,7},{4,0},{5,1},{6,2},{7,3},{8,12},{9,13},{10,... | collective-permute-start | bytes 122888 | tf_op jit(solution)/shard_map/ppermute | solution.py:439
  80.1 2.6 %collective-permute-done.13.refs_2_ = f32[40,256]{1,0:T(8,128)S(1)} collective-permute-done((f32[40,256]{1,0:T(8,128)S(1)}, f32[40,256]{1,0:T(8,128)S(1)}, u32[]{:S(2)}, u32[]{:S(2)}) %collective-permute-start.13) | collective-permute-done | bytes 40992 | tf_op jit(solution)/shard_map/ppermute | solution.py:439
  82.6 2.9 %collective-permute-done.14.refs_3_ = f32[40,256]{1,0:T(8,128)S(1)} collective-permute-done((f32[40,256]{1,0:T(8,128)S(1)}, f32[40,256]{1,0:T(8,128)S(1)}, u32[]{:S(2)}, u32[]{:S(2)}) %collective-permute-start.14) | collective-permute-done | bytes 40992 | tf_op jit(solution)/shard_map/ppermute | solution.py:439
  87.8 1.4 %collective-permute-start.15 = (f32[32,256]{1,0:T(8,128)S(1)}, f32[32,256]{1,0:T(8,128)S(1)}, u32[]{:S(2)}, u32[]{:S(2)}) collective-permute-start(f32[32,256]{1,0:T(8,128)S(1)} %get-tuple-element.72.refs_0_), channel_id=1, source_target_pairs={{0,8},{8,0},{16,24},{24,16},{1,9},{9,1},{17,25},{25,17},{2,10},{10... | collective-permute-start | bytes 98312 | tf_op jit(solution)/shard_map/ppermute | solution.py:439
  89.2 1.3 %collective-permute-done.17.refs_3_ = f32[32,256]{1,0:T(8,128)S(1)} collective-permute-done((f32[32,256]{1,0:T(8,128)S(1)}, f32[32,256]{1,0:T(8,128)S(1)}, u32[]{:S(2)}, u32[]{:S(2)}) %collective-permute-start.17) | collective-permute-done | bytes 32800 | tf_op jit(solution)/shard_map/ppermute | solution.py:439
  94.4 3.9 %collective-permute-start.20 = (f32[32,256]{1,0:T(8,128)S(1)}, f32[32,256]{1,0:T(8,128)S(1)}, u32[]{:S(2)}, u32[]{:S(2)}) collective-permute-start(f32[32,256]{1,0:T(8,128)S(1)} %turn_three.1.refs_0_), channel_id=1, source_target_pairs={{0,2},{1,3},{2,0},{3,1},{4,6},{5,7},{6,4},{7,5},{8,10},{9,11},{10,... | collective-permute-start | bytes 98312 | tf_op jit(solution)/shard_map/ppermute | solution.py:439
  100.6 2.2 %divide_subtract_fusion = (f32[1,2,256,512]{3,2,1,0:T(8,128)}, f32[1,2,256,512]{3,2,1,0:T(8,128)}, f32[1,2,256,512]{3,2,1,0:T(8,128)}) fusion(f32[1,2,256,512]{3,2,1,0:T(8,128)S(1)} %copy-done.5, f32[1,1,256,512]{3,2,1,0:T(8,128)S(1)} %get-tuple-element.85, f32[1,1,256,512]{3,2,1,0:T(8,128)S(1)} %get-tuple-element.84, f32[1,2,256,512]{3,2,1,0:T(8,128)S(1)} %copy-done.6, ...), kind=kLoop, calls=%fused_computation.3 | loop fusion | flops 3407872 | bytes 7340032 | tf_op jit(solution)/shard_map/sub | solution.py:430
  (63 shorter events, 19.9 us)
Async XLA Ops:
  2.0 12.3 %collective-permute-start.2 = (bf16[256,512]{1,0:T(8,128)(2,1)S(1)}, bf16[256,512]{1,0:T(8,128)(2,1)S(1)}, u32[]{:S(2)}, u32[]{:S(2)}) collective-permute-start(bf16[256,512]{1,0:T(8,128)(2,1)S(1)} %get-tuple-element.86.one_ref), channel_id=1, source_target_pairs={{0,16},{8,24},{16,0},{24,8},{1,17},{9,25},{17,1},{25,9},{2,18},{10... | collective-permute-start | bytes 786440 | tf_op jit(solution)/shard_map/ppermute | solution.py:439
  5.0 8.7 %collective-permute-start = (bf16[256,512]{1,0:T(8,128)(2,1)S(1)}, bf16[256,512]{1,0:T(8,128)(2,1)S(1)}, u32[]{:S(2)}, u32[]{:S(2)}) collective-permute-start(bf16[256,512]{1,0:T(8,128)(2,1)S(1)} %get-tuple-element.87.one_ref), channel_id=1, source_target_pairs={{0,8},{8,0},{16,24},{24,16},{1,9},{9,1},{17,25},{25,17},{2,10},{10... | collective-permute-start | bytes 786440 | tf_op jit(solution)/shard_map/ppermute | solution.py:439
  13.7 13.2 %collective-permute-start.1 = (bf16[2,256,512]{2,1,0:T(8,128)(2,1)S(1)}, bf16[2,256,512]{2,1,0:T(8,128)(2,1)S(1)}, u32[]{:S(2)}, u32[]{:S(2)}) collective-permute-start(bf16[2,256,512]{2,1,0:T(8,128)(2,1)S(1)} %pair.2.refs_2_.refs_3_.refs_4_), channel_id=1, source_target_pairs={{0,16},{8,24},{16,0},{24,8},{1,17},{9,25},{17,1},{25,9},{2,18},{10... | collective-permute-start | bytes 1572872 | tf_op jit(solution)/shard_map/ppermute | solution.py:439
  14.3 12.9 %collective-permute-start.3 = (bf16[2,256,512]{2,1,0:T(8,128)(2,1)S(1)}, bf16[2,256,512]{2,1,0:T(8,128)(2,1)S(1)}, u32[]{:S(2)}, u32[]{:S(2)}) collective-permute-start(bf16[2,256,512]{2,1,0:T(8,128)(2,1)S(1)} %pair.3.refs_4_.refs_5_.refs_6_), channel_id=1, source_target_pairs={{0,8},{8,0},{16,24},{24,16},{1,9},{9,1},{17,25},{25,17},{2,10},{10... | collective-permute-start | bytes 1572872 | tf_op jit(solution)/shard_map/ppermute | solution.py:439
  15.0 20.3 %collective-permute-start.9 = (bf16[256,512]{1,0:T(8,128)(2,1)S(1)}, bf16[256,512]{1,0:T(8,128)(2,1)S(1)}, u32[]{:S(2)}, u32[]{:S(2)}) collective-permute-start(bf16[256,512]{1,0:T(8,128)(2,1)S(1)} %get-tuple-element.52), channel_id=1, source_target_pairs={{0,4},{1,5},{2,6},{3,7},{4,0},{5,1},{6,2},{7,3},{8,12},{9,13},{10,... | collective-permute-start | bytes 786440 | tf_op jit(solution)/shard_map/ppermute | solution.py:439
  17.6 20.9 %collective-permute-start.10 = (bf16[256,512]{1,0:T(8,128)(2,1)S(1)}, bf16[256,512]{1,0:T(8,128)(2,1)S(1)}, u32[]{:S(2)}, u32[]{:S(2)}) collective-permute-start(bf16[256,512]{1,0:T(8,128)(2,1)S(1)} %get-tuple-element.53), channel_id=1, source_target_pairs={{0,5},{1,4},{2,7},{3,6},{4,1},{5,0},{6,3},{7,2},{8,13},{9,12},{10,... | collective-permute-start | bytes 786440 | tf_op jit(solution)/shard_map/ppermute | solution.py:439
  17.6 32.6 %collective-permute-start.6 = (bf16[256,512]{1,0:T(8,128)(2,1)S(1)}, bf16[256,512]{1,0:T(8,128)(2,1)S(1)}, u32[]{:S(2)}, u32[]{:S(2)}) collective-permute-start(bf16[256,512]{1,0:T(8,128)(2,1)S(1)} %get-tuple-element.49), channel_id=1, source_target_pairs={{0,2},{1,3},{2,0},{3,1},{4,6},{5,7},{6,4},{7,5},{8,10},{9,11},{10,... | collective-permute-start | bytes 786440 | tf_op jit(solution)/shard_map/ppermute | solution.py:439
  26.9 26.2 %collective-permute-start.7 = (bf16[256,512]{1,0:T(8,128)(2,1)S(1)}, bf16[256,512]{1,0:T(8,128)(2,1)S(1)}, u32[]{:S(2)}, u32[]{:S(2)}) collective-permute-start(bf16[256,512]{1,0:T(8,128)(2,1)S(1)} %get-tuple-element.50), channel_id=1, source_target_pairs={{0,3},{1,2},{2,1},{3,0},{4,7},{5,6},{6,5},{7,4},{8,11},{9,10},{10,... | collective-permute-start | bytes 786440 | tf_op jit(solution)/shard_map/ppermute | solution.py:439
  27.2 25.9 %collective-permute-start.8 = (bf16[256,512]{1,0:T(8,128)(2,1)S(1)}, bf16[256,512]{1,0:T(8,128)(2,1)S(1)}, u32[]{:S(2)}, u32[]{:S(2)}) collective-permute-start(bf16[256,512]{1,0:T(8,128)(2,1)S(1)} %get-tuple-element.51), channel_id=1, source_target_pairs={{0,1},{1,0},{2,3},{3,2},{4,5},{5,4},{6,7},{7,6},{8,9},{9,8},{10,11... | collective-permute-start | bytes 786440 | tf_op jit(solution)/shard_map/ppermute | solution.py:439
  35.3 30.6 %collective-permute-start.4 = (bf16[256,512]{1,0:T(8,128)(2,1)S(1)}, bf16[256,512]{1,0:T(8,128)(2,1)S(1)}, u32[]{:S(2)}, u32[]{:S(2)}) collective-permute-start(bf16[256,512]{1,0:T(8,128)(2,1)S(1)} %get-tuple-element.47), channel_id=1, source_target_pairs={{0,7},{1,6},{2,5},{3,4},{4,3},{5,2},{6,1},{7,0},{8,15},{9,14},{10,... | collective-permute-start | bytes 786440 | tf_op jit(solution)/shard_map/ppermute | solution.py:439
  38.4 24.1 %collective-permute-start.5 = (bf16[256,512]{1,0:T(8,128)(2,1)S(1)}, bf16[256,512]{1,0:T(8,128)(2,1)S(1)}, u32[]{:S(2)}, u32[]{:S(2)}) collective-permute-start(bf16[256,512]{1,0:T(8,128)(2,1)S(1)} %get-tuple-element.48), channel_id=1, source_target_pairs={{0,6},{1,7},{2,4},{3,5},{4,2},{5,3},{6,0},{7,1},{8,14},{9,15},{10,... | collective-permute-start | bytes 786440 | tf_op jit(solution)/shard_map/ppermute | solution.py:439
  69.4 22.3 %collective-permute-start.18 = (bf16[2,256,512]{2,1,0:T(8,128)(2,1)S(1)}, bf16[2,256,512]{2,1,0:T(8,128)(2,1)S(1)}, u32[]{:S(2)}, u32[]{:S(2)}) collective-permute-start(bf16[2,256,512]{2,1,0:T(8,128)(2,1)S(1)} %get-tuple-element.73), channel_id=1, source_target_pairs={{0,8},{8,0},{16,24},{24,16},{1,9},{9,1},{17,25},{25,17},{2,10},{10... | collective-permute-start | bytes 1572872 | tf_op jit(solution)/shard_map/ppermute | solution.py:439
  70.5 21.2 %collective-permute-start.19 = (bf16[2,256,512]{2,1,0:T(8,128)(2,1)S(1)}, bf16[2,256,512]{2,1,0:T(8,128)(2,1)S(1)}, u32[]{:S(2)}, u32[]{:S(2)}) collective-permute-start(bf16[2,256,512]{2,1,0:T(8,128)(2,1)S(1)} %get-tuple-element.74), channel_id=1, source_target_pairs={{0,16},{8,24},{16,0},{24,8},{1,17},{9,25},{17,1},{25,9},{2,18},{10... | collective-permute-start | bytes 1572872 | tf_op jit(solution)/shard_map/ppermute | solution.py:439
  71.0 4.6 %collective-permute-start.11 = (f32[136,256]{1,0:T(8,128)S(1)}, f32[136,256]{1,0:T(8,128)S(1)}, u32[]{:S(2)}, u32[]{:S(2)}) collective-permute-start(f32[136,256]{1,0:T(8,128)S(1)} %get-tuple-element.67), channel_id=1, source_target_pairs={{0,1},{1,0},{2,3},{3,2},{4,5},{5,4},{6,7},{7,6},{8,9},{9,8},{10,11... | collective-permute-start | bytes 417800 | tf_op jit(solution)/shard_map/ppermute | solution.py:439
  75.6 4.5 %collective-permute-start.12 = (f32[40,256]{1,0:T(8,128)S(1)}, f32[40,256]{1,0:T(8,128)S(1)}, u32[]{:S(2)}, u32[]{:S(2)}) collective-permute-start(f32[40,256]{1,0:T(8,128)S(1)} %get-tuple-element.69), channel_id=1, source_target_pairs={{0,2},{1,3},{2,0},{3,1},{4,6},{5,7},{6,4},{7,5},{8,10},{9,11},{10,... | collective-permute-start | bytes 122888 | tf_op jit(solution)/shard_map/ppermute | solution.py:439
  75.7 7.0 %collective-permute-start.13 = (f32[40,256]{1,0:T(8,128)S(1)}, f32[40,256]{1,0:T(8,128)S(1)}, u32[]{:S(2)}, u32[]{:S(2)}) collective-permute-start(f32[40,256]{1,0:T(8,128)S(1)} %get-tuple-element.70), channel_id=1, source_target_pairs={{0,4},{1,5},{2,6},{3,7},{4,0},{5,1},{6,2},{7,3},{8,12},{9,13},{10,... | collective-permute-start | bytes 122888 | tf_op jit(solution)/shard_map/ppermute | solution.py:439
  79.8 5.8 %collective-permute-start.14 = (f32[40,256]{1,0:T(8,128)S(1)}, f32[40,256]{1,0:T(8,128)S(1)}, u32[]{:S(2)}, u32[]{:S(2)}) collective-permute-start(f32[40,256]{1,0:T(8,128)S(1)} %get-tuple-element.71), channel_id=1, source_target_pairs={{0,6},{1,7},{2,4},{3,5},{4,2},{5,3},{6,0},{7,1},{8,14},{9,15},{10,... | collective-permute-start | bytes 122888 | tf_op jit(solution)/shard_map/ppermute | solution.py:439
  85.6 4.9 %collective-permute-start.17 = (f32[32,256]{1,0:T(8,128)S(1)}, f32[32,256]{1,0:T(8,128)S(1)}, u32[]{:S(2)}, u32[]{:S(2)}) collective-permute-start(f32[32,256]{1,0:T(8,128)S(1)} %get-tuple-element.72.refs_0_), channel_id=1, source_target_pairs={{0,24},{8,16},{16,8},{24,0},{1,25},{9,17},{17,9},{25,1},{2,26},{10... | collective-permute-start | bytes 98312 | tf_op jit(solution)/shard_map/ppermute | solution.py:439
  86.8 4.1 %collective-permute-start.16 = (f32[32,256]{1,0:T(8,128)S(1)}, f32[32,256]{1,0:T(8,128)S(1)}, u32[]{:S(2)}, u32[]{:S(2)}) collective-permute-start(f32[32,256]{1,0:T(8,128)S(1)} %get-tuple-element.72.refs_0_), channel_id=1, source_target_pairs={{0,16},{8,24},{16,0},{24,8},{1,17},{9,25},{17,1},{25,9},{2,18},{10... | collective-permute-start | bytes 98312 | tf_op jit(solution)/shard_map/ppermute | solution.py:439
  91.8 8.4 %collective-permute-start.23 = (bf16[256,512]{1,0:T(8,128)(2,1)S(1)}, bf16[256,512]{1,0:T(8,128)(2,1)S(1)}, u32[]{:S(2)}, u32[]{:S(2)}) collective-permute-start(bf16[256,512]{1,0:T(8,128)(2,1)S(1)} %get-tuple-element.77), channel_id=1, source_target_pairs={{0,16},{8,24},{16,0},{24,8},{1,17},{9,25},{17,1},{25,9},{2,18},{10... | collective-permute-start | bytes 786440 | tf_op jit(solution)/shard_map/ppermute | solution.py:439
  92.9 7.3 %collective-permute-start.24 = (bf16[256,512]{1,0:T(8,128)(2,1)S(1)}, bf16[256,512]{1,0:T(8,128)(2,1)S(1)}, u32[]{:S(2)}, u32[]{:S(2)}) collective-permute-start(bf16[256,512]{1,0:T(8,128)(2,1)S(1)} %get-tuple-element.78), channel_id=1, source_target_pairs={{0,8},{8,0},{16,24},{24,16},{1,9},{9,1},{17,25},{25,17},{2,10},{10... | collective-permute-start | bytes 786440 | tf_op jit(solution)/shard_map/ppermute | solution.py:439
  93.9 5.7 %collective-permute-start.22 = (f32[32,256]{1,0:T(8,128)S(1)}, f32[32,256]{1,0:T(8,128)S(1)}, u32[]{:S(2)}, u32[]{:S(2)}) collective-permute-start(f32[32,256]{1,0:T(8,128)S(1)} %turn_three.1.refs_0_), channel_id=1, source_target_pairs={{0,6},{1,7},{2,4},{3,5},{4,2},{5,3},{6,0},{7,1},{8,14},{9,15},{10,... | collective-permute-start | bytes 98312 | tf_op jit(solution)/shard_map/ppermute | solution.py:439
  94.4 5.2 %collective-permute-start.21 = (f32[32,256]{1,0:T(8,128)S(1)}, f32[32,256]{1,0:T(8,128)S(1)}, u32[]{:S(2)}, u32[]{:S(2)}) collective-permute-start(f32[32,256]{1,0:T(8,128)S(1)} %turn_three.1.refs_0_), channel_id=1, source_target_pairs={{0,4},{1,5},{2,6},{3,7},{4,0},{5,1},{6,2},{7,3},{8,12},{9,13},{10,... | collective-permute-start | bytes 98312 | tf_op jit(solution)/shard_map/ppermute | solution.py:439
  94.4 5.8 %collective-permute-start.20 = (f32[32,256]{1,0:T(8,128)S(1)}, f32[32,256]{1,0:T(8,128)S(1)}, u32[]{:S(2)}, u32[]{:S(2)}) collective-permute-start(f32[32,256]{1,0:T(8,128)S(1)} %turn_three.1.refs_0_), channel_id=1, source_target_pairs={{0,2},{1,3},{2,0},{3,1},{4,6},{5,7},{6,4},{7,5},{8,10},{9,11},{10,... | collective-permute-start | bytes 98312 | tf_op jit(solution)/shard_map/ppermute | solution.py:439
  (10 other events, 122.1 us)

commit v6 on v5

--- a/solution.py
+++ b/solution.py
@@ -18,6 +18,7 @@
 F32 = jnp.float32
 BF16 = jnp.bfloat16
 MIB = 1 << 20
+NEAR = 4
 
 
 def iota(shape, dim):
@@ -33,12 +34,17 @@
 
 
 def pack_kernel(experts, capacity, me_ref, index_ref, region_ref, table_ref, target_ref, *refs):
-    blocks, place_ref, rows_ref = refs[:experts], refs[experts], refs[experts + 1]
+    *blocks, place_ref, rows_ref = refs
+    if in_turns(experts):
+        blocks = [blocks[0].at[s] for s in range(NEAR)] + blocks[1:]
     me = me_ref[0]
     groups = index_ref.shape[0]
     cells, width = table_ref.shape
     expert_id = iota((experts, LANES), 0)
-    starts = ((expert_id ^ me) * capacity).astype(F32)
+    block_id = expert_id ^ me
+    if in_turns(experts):
+        block_id = jnp.where(block_id < NEAR, expert_id & (NEAR - 1), block_id)
+    starts = (block_id * capacity).astype(F32)
     ahead = jnp.where(iota((LANES, LANES), 0) <= iota((LANES, LANES), 1), 1.0, 0.0).astype(BF16)
     counted = jnp.zeros((experts, LANES), F32)
     places = []
@@ -81,12 +87,15 @@
 def pack(me, index, region, table, targets, experts, capacity):
     rows, width = targets.shape
     groups = rows // LANES
+    shapes = [(capacity, 2 * width)] * experts
+    if in_turns(experts):
+        shapes = [(NEAR, *shapes[0])] + shapes[NEAR:]
     return pl.pallas_call(
         functools.partial(pack_kernel, experts, capacity),
-        out_shape=[jax.ShapeDtypeStruct((capacity, 2 * width), BF16)] * experts
+        out_shape=[jax.ShapeDtypeStruct(shape, BF16) for shape in shapes]
         + [jax.ShapeDtypeStruct((groups, LANES), jnp.int32)],
         in_specs=[whole(pltpu.SMEM)] + [whole()] * 4,
-        out_specs=[whole()] * (experts + 1),
+        out_specs=[whole()] * (len(shapes) + 1),
         scratch_shapes=[pltpu.VMEM((rows, 2 * width), BF16)],
         compiler_params=pltpu.CompilerParams(vmem_limit_bytes=32 * MIB),
         cost_estimate=pl.CostEstimate(
@@ -118,7 +127,7 @@
     return 0.5 * jnp.tanh(0.5 * v) + 0.5
 
 
-def expert_kernel(counts, order, first, last, *refs):
+def expert_kernel(counts, first, last, *refs):
     blocks, shares, experts, steps, step_rows, relays = counts
     refs = list(refs)
 
@@ -149,9 +158,12 @@
 
     width = trunk_ref.shape[0]
     share = ups_near.shape[2]
-    block_rows = xs[0].shape[0]
-    for i, ref in enumerate(xs):
-        x_ref[i * block_rows : (i + 1) * block_rows, :] = ref[...]
+    block_rows = xs[-1].shape[0]
+    if len(xs) == 1:
+        x_ref = xs[0]
+    else:
+        for i, ref in enumerate(xs):
+            x_ref[i * block_rows : (i + 1) * block_rows, :] = ref[...]
     looped = steps > 3
     if looped and first:
         acc_ref[...] = jnp.zeros(acc_ref.shape, F32)
@@ -242,7 +254,10 @@
             mine = pl.ds(pl.multiple_of((me ^ s) * part, part), part)
             ref[s // 2 * part : (s // 2 + 1) * part, :] = acc_trunk_ref[mine, :]
             at = experts // 2 * part + s // 2
-            ref[at : at + 1, :] = loss_row(all_losses, order.index(s))
+            if s < NEAR:
+                ref[at : at + 1, :] = all_losses[0][pl.ds((me & (NEAR - 1)) ^ s, 1), :]
+            else:
+                ref[at : at + 1, :] = loss_row(all_losses, s)
 
 
 def in_turns(experts):
@@ -256,13 +271,12 @@
         row -= ref.shape[0]
 
 
-def expert_call(xs, trunk_weight, weights, prior, losses, me, order, last, relays=()):
-    experts = len(order)
-    block_rows = xs[0].shape[0]
+def expert_call(xs, trunk_weight, weights, prior, losses, me, experts, last, relays=()):
+    rows = sum(x.shape[0] for x in xs)
     width = trunk_weight.shape[0]
     shares, share = len(weights), weights[0].shape[2]
-    rows = block_rows * len(xs)
     step_rows = min(256, rows)
+    block_rows = 8 * step_rows // experts
     steps = rows // step_rows
     first = prior is None
     acc = jax.ShapeDtypeStruct((shares, 2, width, share), F32)
@@ -274,7 +288,7 @@
     args += relays
     in_specs = [whole()] * len(args)
     scratch = [
-        pltpu.VMEM((rows, 2 * width), BF16),
+        pltpu.VMEM((rows if len(xs) > 1 else 16, 2 * width), BF16),
         pltpu.VMEM((step_rows, shares * share), BF16),
         pltpu.VMEM((step_rows, shares * share), F32),
     ]
@@ -297,7 +311,7 @@
         outs += [jax.ShapeDtypeStruct(relay.shape, relay.dtype) for relay in relays]
     counts = (len(xs), shares, experts, steps, step_rows, len(relays))
     return pl.pallas_call(
-        functools.partial(expert_kernel, counts, order, first, len(losses) + 1 if last else 0),
+        functools.partial(expert_kernel, counts, first, len(losses) + 1 if last else 0),
         out_shape=outs,
         in_specs=in_specs,
         out_specs=[whole()] * len(outs),
@@ -369,13 +383,16 @@
     return swap(up, "dp", 2), swap(down, "dp", 1)
 
 
-def row_loss_kernel(place_ref, loss_ref, row_loss_ref):
+def row_loss_kernel(me_ref, place_ref, loss_ref, row_loss_ref):
     experts, capacity = loss_ref.shape
+    me = me_ref[0]
     loss = loss_ref[...]
     for g in range(place_ref.shape[0]):
         place = place_ref[g : g + 1, :]
         block = place // capacity
         slot = place - block * capacity
+        if in_turns(experts):
+            block = jnp.where(block < NEAR, block ^ (me & (NEAR - 1)), block)
         picks = jnp.where(iota((capacity, LANES), 0) == slot, 1.0, 0.0)
         found = lax.dot_general(
             loss,
@@ -388,15 +405,15 @@
         row_loss_ref[g : g + 1, :] = jnp.sum(mine, axis=0, keepdims=True)
 
 
-def loss_by_row(place, loss):
+def loss_by_row(me, place, loss):
     return pl.pallas_call(
         row_loss_kernel,
         out_shape=jax.ShapeDtypeStruct(place.shape, F32),
-        in_specs=[whole()] * 2,
+        in_specs=[whole(pltpu.SMEM)] + [whole()] * 2,
         out_specs=whole(),
         compiler_params=pltpu.CompilerParams(vmem_limit_bytes=16 * MIB),
         name="row_loss",
-    )(place, loss)
+    )(me, place, loss)
 
 
 def assemble_kernel(part, me_ref, *refs):
@@ -462,23 +479,29 @@
     ups, downs = pair(up, near_up, place), pair(down, near_down, place)
     weights = [ups, swap(ups, "dp", 2), downs, swap(downs, "dp", 1)]
     if in_turns(experts):
-        batches, later = ((0,), (4, 5), (2, 3, 1), (6,), (7,)), (6, 7)
+        near = lax.all_to_all(
+            blocks[0],
+            "expert",
+            split_axis=0,
+            concat_axis=0,
+            tiled=True,
+            axis_index_groups=[list(range(g, g + NEAR)) for g in range(0, experts, NEAR)],
+        )
+        far = [swap(block, "expert", s) for s, block in enumerate(blocks[1:-1], NEAR)]
+        batches, relays = [[near.reshape(-1, 2 * width)], far[:2], far[2:], []], blocks[-1:]
     else:
-        batches, later = (range(experts // 2), range(experts // 2, experts)), ()
-    order = [s for batch in batches for s in batch]
-    arrived = {s: swap(blocks[s], "expert", s) for s in order if s not in later}
+        arrived = [swap(blocks[s], "expert", s) for s in range(experts)]
+        batches, relays = [arrived[: experts // 2], arrived[experts // 2 :]], []
     prior, losses = None, []
-    for k, batch in enumerate(batches):
+    for k, xs in enumerate(batches):
         last = k == len(batches) - 1
-        relays = [blocks[s] for s in later] if k == 0 else []
-        outs = expert_call(
-            [arrived[s] for s in batch], trunk_weight, weights, prior, losses, me, order, last, relays
-        )
+        outs = expert_call(xs, trunk_weight, weights, prior, losses, me, experts, last, relays)
+        if relays:
+            batches[-1].append(swap(outs[-1], "expert", experts - 1))
+            relays = []
         if not last:
             prior = outs[:2]
             losses.append(outs[2])
-            for s, block in zip(later, outs[3:]):
-                arrived[s] = swap(block, "expert", s)
     own, next_up, next_down, sent_up, sent_down, kept, note = outs
 
     got_up = swap(sent_up, "dp", 1)
@@ -510,7 +533,7 @@
         places = jnp.arange(experts, dtype=jnp.int32) ^ me
         note = note.reshape(experts, capacity)[places]
         loss = lax.all_to_all(note, "expert", split_axis=0, concat_axis=0, tiled=True)[places]
-    row_loss = loss_by_row(place, loss)
+    row_loss = loss_by_row(me, place, loss)
 
     grads = jnp.stack(
         [

time: 104 us -> 114 us (1.096)
  waiting for transfers between devices: 25.5 us -> 35.2 us
  local copies, waits for them, and re-layouts: 3.7 us -> 5.36 us
  Pallas kernels: 31.6 us -> 33.2 us
  starting transfers between devices: 38.1 us -> 36.6 us
  other arithmetic: 3.66 us -> 2.47 us
    ppermute x26 -> x23, waiting for transfers between devices: 25.5 us -> 35.2 us  [swap(): lax.ppermute(value, axis, [(i, i ^ s) for i in range(lax.axis_size(axis))])]
    ppermute x26 -> x23, starting transfers between devices: 38.1 us -> 32.2 us  [swap(): lax.ppermute(value, axis, [(i, i ^ s) for i in range(lax.axis_size(axis))])]
    all_to_all x0 -> x1, starting transfers between devices: none -> 4.43 us  [on_device(): lax.all_to_all(blocks[0], 'expert', split_axis=0, concat_axis=0, tiled=Tr...]
    unnamed x16 -> x22, local copies, waits for them, and re-layouts: 3.66 us -> 5.32 us
    another operation x1, other arithmetic: 1.29 us -> 0.07 us
    pallas_call x5 -> x4, Pallas kernels: 25.9 us -> 27 us  [expert_call(): pl.pallas_call(functools.partial(expert_kernel, counts, first, len(losses...]
  transfers between devices with their start and end apart: 26 -> 24, of which waited for: 13 -> 14; matrix products, arithmetic and copies ran while one was open for 2% -> 2% of each run, Pallas kernels for 26% -> 22%
where the time goes in v6:
time: 114 us
  starting transfers between devices  36.6 us (32%)
  waiting for transfers between devices  35.2 us (31%)
  Pallas kernels  33.2 us (29%)
  local copies, waits for them, and re-layouts  5.36 us (5%)
  other arithmetic  2.47 us (2%)
    ppermute x23, waiting for transfers between devices, swap(): lax.ppermute(value, axis, [(i, i ^ s) for i in range(lax.axis_size(axis))])  35.2 us
    ppermute x23, starting transfers between devices, swap(): lax.ppermute(value, axis, [(i, i ^ s) for i in range(lax.axis_size(axis))])  32.2 us
    pallas_call x4, Pallas kernels, expert_call(): pl.pallas_call(functools.partial(expert_kernel, counts, first, len(losses...  27 us
    unnamed x22, local copies, waits for them, and re-layouts  5.32 us
    all_to_all x1, starting transfers between devices, on_device(): lax.all_to_all(blocks[0], 'expert', split_axis=0, concat_axis=0, tiled=Tr...  4.43 us
    pallas_call x1, Pallas kernels, pack(): pl.pallas_call(functools.partial(pack_kernel, experts, capacity), out_sha...  4.12 us
  transfers between devices with their start and end apart: 24, of which 14 were waited for; matrix products, arithmetic and copies ran while one was open for 2% of the time, Pallas kernels for 22%

profile of v6, /device:TPU:0, one launch (start us, length us, event | category | flops | bytes accessed | tf_op | source)
XLA Modules:
  0.0 113.7 jit_solution(5088629929262903773)
XLA Ops:
  4.3 4.1 %pack_rows.1 = (bf16[4,256,512]{2,1,0:T(8,128)(2,1)}, bf16[256,512]{1,0:T(8,128)(2,1)}, bf16[256,512]{1,0:T(8,128)(2,1)}, bf16[256,512]{1,0:T(8,128)(2,1)}, bf16...) custom-call(s32[1]{0:T(128)} %bitcast.me_ref.refs_11_, s32[8,128]{1,0:T(8,128)S(1)} %bitcast.22, s32[8,128]{1,0:T(8,128)S(1)} %bitcast.23, ...), custom_call_target="tpu_custom_call" | custom-call | flops 3221225472 | bytes 6291456 | tf_op jit(solution)/shard_map/pack_rows/pallas_call | solution.py:93
  9.1 4.4 %all-to-all-start = ((bf16[4,256,512]{2,1,0:T(8,128)(2,1)}), bf16[4,256,512]{2,1,0:T(8,128)(2,1)S(1)}, u32[]{:S(2)}, u32[]{:S(2)}) async-start(bf16[4,256,512]{2,1,0:T(8,128)(2,1)} %get-tuple-element.36), calls=%async_computation | async-start | bytes 2097152 | tf_op jit(solution)/shard_map/all_to_all | solution.py:482
  13.7 2.2 %collective-permute-start = (bf16[256,512]{1,0:T(8,128)(2,1)S(1)}, bf16[256,512]{1,0:T(8,128)(2,1)S(1)}, u32[]{:S(2)}, u32[]{:S(2)}) collective-permute-start(bf16[256,512]{1,0:T(8,128)(2,1)S(1)} %get-tuple-element.73.one_ref), channel_id=1, source_target_pairs={{0,8},{8,0},{16,24},{24,16},{1,9},{9,1},{17,25},{25,17},{2,10},{10... | collective-permute-start | bytes 786440 | tf_op jit(solution)/shard_map/ppermute | solution.py:456
  17.4 5.4 %collective-permute-done.other_ref = bf16[256,512]{1,0:T(8,128)(2,1)S(1)} collective-permute-done((bf16[256,512]{1,0:T(8,128)(2,1)S(1)}, bf16[256,512]{1,0:T(8,128)(2,1)S(1)}, u32[]{:S(2)}, u32[]{:S(2)}) %collective-permute-start) | collective-permute-done | bytes 262176 | tf_op jit(solution)/shard_map/ppermute | solution.py:456
  22.9 1.8 %collective-permute-start.1 = (bf16[2,256,512]{2,1,0:T(8,128)(2,1)S(1)}, bf16[2,256,512]{2,1,0:T(8,128)(2,1)S(1)}, u32[]{:S(2)}, u32[]{:S(2)}) collective-permute-start(bf16[2,256,512]{2,1,0:T(8,128)(2,1)S(1)} %pair.2.refs_2_.refs_3_), channel_id=1, source_target_pairs={{0,16},{8,24},{16,0},{24,8},{1,17},{9,25},{17,1},{25,9},{2,18},{10... | collective-permute-start | bytes 1572872 | tf_op jit(solution)/shard_map/ppermute | solution.py:456
  24.8 1.6 %collective-permute-start.3 = (bf16[2,256,512]{2,1,0:T(8,128)(2,1)S(1)}, bf16[2,256,512]{2,1,0:T(8,128)(2,1)S(1)}, u32[]{:S(2)}, u32[]{:S(2)}) collective-permute-start(bf16[2,256,512]{2,1,0:T(8,128)(2,1)S(1)} %pair.3.refs_4_.refs_5_), channel_id=1, source_target_pairs={{0,8},{8,0},{16,24},{24,16},{1,9},{9,1},{17,25},{25,17},{2,10},{10... | collective-permute-start | bytes 1572872 | tf_op jit(solution)/shard_map/ppermute | solution.py:456
  26.3 3.7 %collective-permute-start.5 = (bf16[256,512]{1,0:T(8,128)(2,1)}, bf16[256,512]{1,0:T(8,128)(2,1)S(1)}, u32[]{:S(2)}, u32[]{:S(2)}) collective-permute-start(bf16[256,512]{1,0:T(8,128)(2,1)} %get-tuple-element.40), channel_id=1, source_target_pairs={{0,6},{1,7},{2,4},{3,5},{4,2},{5,3},{6,0},{7,1},{8,14},{9,15},{10,... | collective-permute-start | bytes 786440 | tf_op jit(solution)/shard_map/ppermute | solution.py:456
  30.7 5.9 %collective-permute-done.1.refs_3_.refs_4_ = bf16[2,256,512]{2,1,0:T(8,128)(2,1)S(1)} collective-permute-done((bf16[2,256,512]{2,1,0:T(8,128)(2,1)S(1)}, bf16[2,256,512]{2,1,0:T(8,128)(2,1)S(1)}, u32[]{:S(2)}, u32[]{:S(2)}) %collective-permute-start.1) | collective-permute-done | bytes 524320 | tf_op jit(solution)/shard_map/ppermute | solution.py:456
  39.0 13.3 %expert_rows.4 = (f32[4,2,256,512]{3,2,1,0:T(8,128)S(1)}, f32[256,256]{1,0:T(8,128)S(1)}, f32[4,256]{1,0:T(4,128)S(1)}, bf16[256,512]{1,0:T(8,128)(2,1)S(1)}) custom-call(bf16[1024,512]{1,0:T(8,128)(2,1)S(1)} %bitcast.21, bf16[256,256]{1,0:T(8,128)(2,1)S(1)} %copy-done, bf16[2,256,512]{2,1,0:T(8,128)(2,1)S(1)} %pair.2.refs_2_.refs_3_, ...), custom_call_target="tpu_custom_call" | custom-call | flops 6442450944 | bytes 10485760 | tf_op jit(solution)/shard_map/expert_rows/pallas_call | solution.py:313
  53.4 11.2 %collective-permute-done.6.refs_0_ = bf16[256,512]{1,0:T(8,128)(2,1)} collective-permute-done((bf16[256,512]{1,0:T(8,128)(2,1)}, bf16[256,512]{1,0:T(8,128)(2,1)}, u32[]{:S(2)}, u32[]{:S(2)}) %collective-permute-start.6) | collective-permute-done | bytes 262176 | tf_op jit(solution)/shard_map/ppermute | solution.py:456
  64.6 2.2 %collective-permute-done.7.refs_1_ = bf16[256,512]{1,0:T(8,128)(2,1)} collective-permute-done((bf16[256,512]{1,0:T(8,128)(2,1)}, bf16[256,512]{1,0:T(8,128)(2,1)}, u32[]{:S(2)}, u32[]{:S(2)}) %collective-permute-start.7) | collective-permute-done | bytes 262176 | tf_op jit(solution)/shard_map/ppermute | solution.py:456
  66.8 7.3 %expert_rows.5 = (f32[4,2,256,512]{3,2,1,0:T(8,128)S(1)}, f32[256,256]{1,0:T(8,128)S(1)}, f32[2,256]{1,0:T(2,128)S(1)}) custom-call(bf16[256,512]{1,0:T(8,128)(2,1)} %collective-permute-done.6.refs_0_, bf16[256,512]{1,0:T(8,128)(2,1)} %collective-permute-done.7.refs_1_, bf16[256,256]{1,0:T(8,128)(2,1)S(1)} %copy-done, ...), custom_call_target="tpu_custom_call" | custom-call | flops 3221225472 | bytes 10485760 | tf_op jit(solution)/shard_map/expert_rows/pallas_call | solution.py:313
  74.1 3.2 %expert_rows.6 = (f32[4,2,256,512]{3,2,1,0:T(8,128)S(1)}, f32[256,256]{1,0:T(8,128)S(1)}, f32[1,256]{1,0:T(1,128)S(1)}) custom-call(bf16[256,512]{1,0:T(8,128)(2,1)S(1)} %collective-permute-done.5.refs_0_, bf16[256,256]{1,0:T(8,128)(2,1)S(1)} %copy-done, bf16[2,256,512]{2,1,0:T(8,128)(2,1)S(1)} %pair.2.refs_2_.refs_3_, ...), custom_call_target="tpu_custom_call" | custom-call | flops 1610612736 | bytes 10485760 | tf_op jit(solution)/shard_map/expert_rows/pallas_call | solution.py:313
  77.3 3.2 %expert_rows.7 = (f32[2,256,512]{2,1,0:T(8,128)S(1)}, f32[256,512]{1,0:T(8,128)S(1)}, f32[256,512]{1,0:T(8,128)S(1)}, bf16[2,256,512]{2,1,0:T(8,128)(2,1)S(1)}, ...) custom-call(bf16[256,512]{1,0:T(8,128)(2,1)S(1)} %collective-permute-done.4.refs_0_, ...), custom_call_target="tpu_custom_call" | custom-call | flops 1610612736 | bytes 10485760 | tf_op jit(solution)/shard_map/expert_rows/pallas_call | solution.py:313
  81.7 3.7 %collective-permute-start.8 = (f32[136,256]{1,0:T(8,128)S(1)}, f32[136,256]{1,0:T(8,128)S(1)}, u32[]{:S(2)}, u32[]{:S(2)}) collective-permute-start(f32[136,256]{1,0:T(8,128)S(1)} %get-tuple-element.53), channel_id=1, source_target_pairs={{0,1},{1,0},{2,3},{3,2},{4,5},{5,4},{6,7},{7,6},{8,9},{9,8},{10,11... | collective-permute-start | bytes 417800 | tf_op jit(solution)/shard_map/ppermute | solution.py:456
  87.1 2.3 %collective-permute-start.10 = (f32[40,256]{1,0:T(8,128)S(1)}, f32[40,256]{1,0:T(8,128)S(1)}, u32[]{:S(2)}, u32[]{:S(2)}) collective-permute-start(f32[40,256]{1,0:T(8,128)S(1)} %get-tuple-element.56), channel_id=1, source_target_pairs={{0,4},{1,5},{2,6},{3,7},{4,0},{5,1},{6,2},{7,3},{8,12},{9,13},{10,... | collective-permute-start | bytes 122888 | tf_op jit(solution)/shard_map/ppermute | solution.py:456
  89.4 1.6 %collective-permute-start.11 = (f32[40,256]{1,0:T(8,128)S(1)}, f32[40,256]{1,0:T(8,128)S(1)}, u32[]{:S(2)}, u32[]{:S(2)}) collective-permute-start(f32[40,256]{1,0:T(8,128)S(1)} %get-tuple-element.57), channel_id=1, source_target_pairs={{0,6},{1,7},{2,4},{3,5},{4,2},{5,3},{6,0},{7,1},{8,14},{9,15},{10,... | collective-permute-start | bytes 122888 | tf_op jit(solution)/shard_map/ppermute | solution.py:456
  91.0 2.3 %collective-permute-done.10.refs_2_ = f32[40,256]{1,0:T(8,128)S(1)} collective-permute-done((f32[40,256]{1,0:T(8,128)S(1)}, f32[40,256]{1,0:T(8,128)S(1)}, u32[]{:S(2)}, u32[]{:S(2)}) %collective-permute-start.10) | collective-permute-done | bytes 40992 | tf_op jit(solution)/shard_map/ppermute | solution.py:456
  93.3 1.9 %collective-permute-done.11.refs_3_ = f32[40,256]{1,0:T(8,128)S(1)} collective-permute-done((f32[40,256]{1,0:T(8,128)S(1)}, f32[40,256]{1,0:T(8,128)S(1)}, u32[]{:S(2)}, u32[]{:S(2)}) %collective-permute-start.11) | collective-permute-done | bytes 40992 | tf_op jit(solution)/shard_map/ppermute | solution.py:456
  95.2 1.9 %collective-permute-start.14 = (f32[32,256]{1,0:T(8,128)S(1)}, f32[32,256]{1,0:T(8,128)S(1)}, u32[]{:S(2)}, u32[]{:S(2)}) collective-permute-start(f32[32,256]{1,0:T(8,128)S(1)} %get-tuple-element.58.refs_0_), channel_id=1, source_target_pairs={{0,24},{8,16},{16,8},{24,0},{1,25},{9,17},{17,9},{25,1},{2,26},{10... | collective-permute-start | bytes 98312 | tf_op jit(solution)/shard_map/ppermute | solution.py:456
  101.7 1.6 %collective-permute-start.20 = (bf16[256,512]{1,0:T(8,128)(2,1)S(1)}, bf16[256,512]{1,0:T(8,128)(2,1)S(1)}, u32[]{:S(2)}, u32[]{:S(2)}) collective-permute-start(bf16[256,512]{1,0:T(8,128)(2,1)S(1)} %get-tuple-element.63), channel_id=1, source_target_pairs={{0,16},{8,24},{16,0},{24,8},{1,17},{9,25},{17,1},{25,9},{2,18},{10... | collective-permute-start | bytes 786440 | tf_op jit(solution)/shard_map/ppermute | solution.py:456
  103.8 1.5 %collective-permute-start.19 = (f32[32,256]{1,0:T(8,128)S(1)}, f32[32,256]{1,0:T(8,128)S(1)}, u32[]{:S(2)}, u32[]{:S(2)}) collective-permute-start(f32[32,256]{1,0:T(8,128)S(1)} %turn_three.1.refs_0_), channel_id=1, source_target_pairs={{0,6},{1,7},{2,4},{3,5},{4,2},{5,3},{6,0},{7,1},{8,14},{9,15},{10,... | collective-permute-start | bytes 98312 | tf_op jit(solution)/shard_map/ppermute | solution.py:456
  105.3 2.9 %collective-permute-start.17 = (f32[32,256]{1,0:T(8,128)S(1)}, f32[32,256]{1,0:T(8,128)S(1)}, u32[]{:S(2)}, u32[]{:S(2)}) collective-permute-start(f32[32,256]{1,0:T(8,128)S(1)} %turn_three.1.refs_0_), channel_id=1, source_target_pairs={{0,2},{1,3},{2,0},{3,1},{4,6},{5,7},{6,4},{7,5},{8,10},{9,11},{10,... | collective-permute-start | bytes 98312 | tf_op jit(solution)/shard_map/ppermute | solution.py:456
  110.8 2.1 %divide_subtract_fusion = (f32[1,2,256,512]{3,2,1,0:T(8,128)}, f32[1,2,256,512]{3,2,1,0:T(8,128)}, f32[1,2,256,512]{3,2,1,0:T(8,128)}) fusion(f32[1,2,256,512]{3,2,1,0:T(8,128)S(1)} %copy-done.8, f32[1,1,256,512]{3,2,1,0:T(8,128)S(1)} %get-tuple-element.71, f32[1,1,256,512]{3,2,1,0:T(8,128)S(1)} %get-tuple-element.70, f32[1,2,256,512]{3,2,1,0:T(8,128)S(1)} %copy-done.9, ...), kind=kLoop, calls=%fused_computation.3 | loop fusion | flops 3407872 | bytes 7340032 | tf_op jit(solution)/shard_map/sub | solution.py:447
  (64 shorter events, 21.4 us)
Async XLA Ops:
  9.1 28.9 %all-to-all-start = ((bf16[4,256,512]{2,1,0:T(8,128)(2,1)}), bf16[4,256,512]{2,1,0:T(8,128)(2,1)S(1)}, u32[]{:S(2)}, u32[]{:S(2)}) async-start(bf16[4,256,512]{2,1,0:T(8,128)(2,1)} %get-tuple-element.36), calls=%async_computation | async-start | bytes 2097152 | tf_op jit(solution)/shard_map/all_to_all | solution.py:482
  13.7 9.2 %collective-permute-start = (bf16[256,512]{1,0:T(8,128)(2,1)S(1)}, bf16[256,512]{1,0:T(8,128)(2,1)S(1)}, u32[]{:S(2)}, u32[]{:S(2)}) collective-permute-start(bf16[256,512]{1,0:T(8,128)(2,1)S(1)} %get-tuple-element.73.one_ref), channel_id=1, source_target_pairs={{0,8},{8,0},{16,24},{24,16},{1,9},{9,1},{17,25},{25,17},{2,10},{10... | collective-permute-start | bytes 786440 | tf_op jit(solution)/shard_map/ppermute | solution.py:456
  15.9 8.8 %collective-permute-start.2 = (bf16[256,512]{1,0:T(8,128)(2,1)S(1)}, bf16[256,512]{1,0:T(8,128)(2,1)S(1)}, u32[]{:S(2)}, u32[]{:S(2)}) collective-permute-start(bf16[256,512]{1,0:T(8,128)(2,1)S(1)} %get-tuple-element.72.one_ref), channel_id=1, source_target_pairs={{0,16},{8,24},{16,0},{24,8},{1,17},{9,25},{17,1},{25,9},{2,18},{10... | collective-permute-start | bytes 786440 | tf_op jit(solution)/shard_map/ppermute | solution.py:456
  22.9 13.8 %collective-permute-start.1 = (bf16[2,256,512]{2,1,0:T(8,128)(2,1)S(1)}, bf16[2,256,512]{2,1,0:T(8,128)(2,1)S(1)}, u32[]{:S(2)}, u32[]{:S(2)}) collective-permute-start(bf16[2,256,512]{2,1,0:T(8,128)(2,1)S(1)} %pair.2.refs_2_.refs_3_), channel_id=1, source_target_pairs={{0,16},{8,24},{16,0},{24,8},{1,17},{9,25},{17,1},{25,9},{2,18},{10... | collective-permute-start | bytes 1572872 | tf_op jit(solution)/shard_map/ppermute | solution.py:456
  24.8 13.3 %collective-permute-start.3 = (bf16[2,256,512]{2,1,0:T(8,128)(2,1)S(1)}, bf16[2,256,512]{2,1,0:T(8,128)(2,1)S(1)}, u32[]{:S(2)}, u32[]{:S(2)}) collective-permute-start(bf16[2,256,512]{2,1,0:T(8,128)(2,1)S(1)} %pair.3.refs_4_.refs_5_), channel_id=1, source_target_pairs={{0,8},{8,0},{16,24},{24,16},{1,9},{9,1},{17,25},{25,17},{2,10},{10... | collective-permute-start | bytes 1572872 | tf_op jit(solution)/shard_map/ppermute | solution.py:456
  26.3 47.8 %collective-permute-start.5 = (bf16[256,512]{1,0:T(8,128)(2,1)}, bf16[256,512]{1,0:T(8,128)(2,1)S(1)}, u32[]{:S(2)}, u32[]{:S(2)}) collective-permute-start(bf16[256,512]{1,0:T(8,128)(2,1)} %get-tuple-element.40), channel_id=1, source_target_pairs={{0,6},{1,7},{2,4},{3,5},{4,2},{5,3},{6,0},{7,1},{8,14},{9,15},{10,... | collective-permute-start | bytes 786440 | tf_op jit(solution)/shard_map/ppermute | solution.py:456
  30.0 34.6 %collective-permute-start.6 = (bf16[256,512]{1,0:T(8,128)(2,1)}, bf16[256,512]{1,0:T(8,128)(2,1)}, u32[]{:S(2)}, u32[]{:S(2)}) collective-permute-start(bf16[256,512]{1,0:T(8,128)(2,1)} %get-tuple-element.41), channel_id=1, source_target_pairs={{0,4},{1,5},{2,6},{3,7},{4,0},{5,1},{6,2},{7,3},{8,12},{9,13},{10,... | collective-permute-start | bytes 786440 | tf_op jit(solution)/shard_map/ppermute | solution.py:456
  30.0 36.8 %collective-permute-start.7 = (bf16[256,512]{1,0:T(8,128)(2,1)}, bf16[256,512]{1,0:T(8,128)(2,1)}, u32[]{:S(2)}, u32[]{:S(2)}) collective-permute-start(bf16[256,512]{1,0:T(8,128)(2,1)} %get-tuple-element.42), channel_id=1, source_target_pairs={{0,5},{1,4},{2,7},{3,6},{4,1},{5,0},{6,3},{7,2},{8,13},{9,12},{10,... | collective-permute-start | bytes 786440 | tf_op jit(solution)/shard_map/ppermute | solution.py:456
  52.3 25.0 %collective-permute-start.4 = (bf16[256,512]{1,0:T(8,128)(2,1)S(1)}, bf16[256,512]{1,0:T(8,128)(2,1)S(1)}, u32[]{:S(2)}, u32[]{:S(2)}) collective-permute-start(bf16[256,512]{1,0:T(8,128)(2,1)S(1)} %get-tuple-element.39), channel_id=1, source_target_pairs={{0,7},{1,6},{2,5},{3,4},{4,3},{5,2},{6,1},{7,0},{8,15},{9,14},{10,... | collective-permute-start | bytes 786440 | tf_op jit(solution)/shard_map/ppermute | solution.py:456
  80.6 21.0 %collective-permute-start.15 = (bf16[2,256,512]{2,1,0:T(8,128)(2,1)S(1)}, bf16[2,256,512]{2,1,0:T(8,128)(2,1)S(1)}, u32[]{:S(2)}, u32[]{:S(2)}) collective-permute-start(bf16[2,256,512]{2,1,0:T(8,128)(2,1)S(1)} %get-tuple-element.59), channel_id=1, source_target_pairs={{0,8},{8,0},{16,24},{24,16},{1,9},{9,1},{17,25},{25,17},{2,10},{10... | collective-permute-start | bytes 1572872 | tf_op jit(solution)/shard_map/ppermute | solution.py:456
  80.8 20.8 %collective-permute-start.16 = (bf16[2,256,512]{2,1,0:T(8,128)(2,1)S(1)}, bf16[2,256,512]{2,1,0:T(8,128)(2,1)S(1)}, u32[]{:S(2)}, u32[]{:S(2)}) collective-permute-start(bf16[2,256,512]{2,1,0:T(8,128)(2,1)S(1)} %get-tuple-element.60), channel_id=1, source_target_pairs={{0,16},{8,24},{16,0},{24,8},{1,17},{9,25},{17,1},{25,9},{2,18},{10... | collective-permute-start | bytes 1572872 | tf_op jit(solution)/shard_map/ppermute | solution.py:456
  81.7 4.7 %collective-permute-start.8 = (f32[136,256]{1,0:T(8,128)S(1)}, f32[136,256]{1,0:T(8,128)S(1)}, u32[]{:S(2)}, u32[]{:S(2)}) collective-permute-start(f32[136,256]{1,0:T(8,128)S(1)} %get-tuple-element.53), channel_id=1, source_target_pairs={{0,1},{1,0},{2,3},{3,2},{4,5},{5,4},{6,7},{7,6},{8,9},{9,8},{10,11... | collective-permute-start | bytes 417800 | tf_op jit(solution)/shard_map/ppermute | solution.py:456
  86.5 4.5 %collective-permute-start.9 = (f32[40,256]{1,0:T(8,128)S(1)}, f32[40,256]{1,0:T(8,128)S(1)}, u32[]{:S(2)}, u32[]{:S(2)}) collective-permute-start(f32[40,256]{1,0:T(8,128)S(1)} %get-tuple-element.55), channel_id=1, source_target_pairs={{0,2},{1,3},{2,0},{3,1},{4,6},{5,7},{6,4},{7,5},{8,10},{9,11},{10,... | collective-permute-start | bytes 122888 | tf_op jit(solution)/shard_map/ppermute | solution.py:456
  87.1 6.2 %collective-permute-start.10 = (f32[40,256]{1,0:T(8,128)S(1)}, f32[40,256]{1,0:T(8,128)S(1)}, u32[]{:S(2)}, u32[]{:S(2)}) collective-permute-start(f32[40,256]{1,0:T(8,128)S(1)} %get-tuple-element.56), channel_id=1, source_target_pairs={{0,4},{1,5},{2,6},{3,7},{4,0},{5,1},{6,2},{7,3},{8,12},{9,13},{10,... | collective-permute-start | bytes 122888 | tf_op jit(solution)/shard_map/ppermute | solution.py:456
  89.4 5.8 %collective-permute-start.11 = (f32[40,256]{1,0:T(8,128)S(1)}, f32[40,256]{1,0:T(8,128)S(1)}, u32[]{:S(2)}, u32[]{:S(2)}) collective-permute-start(f32[40,256]{1,0:T(8,128)S(1)} %get-tuple-element.57), channel_id=1, source_target_pairs={{0,6},{1,7},{2,4},{3,5},{4,2},{5,3},{6,0},{7,1},{8,14},{9,15},{10,... | collective-permute-start | bytes 122888 | tf_op jit(solution)/shard_map/ppermute | solution.py:456
  95.2 4.9 %collective-permute-start.14 = (f32[32,256]{1,0:T(8,128)S(1)}, f32[32,256]{1,0:T(8,128)S(1)}, u32[]{:S(2)}, u32[]{:S(2)}) collective-permute-start(f32[32,256]{1,0:T(8,128)S(1)} %get-tuple-element.58.refs_0_), channel_id=1, source_target_pairs={{0,24},{8,16},{16,8},{24,0},{1,25},{9,17},{17,9},{25,1},{2,26},{10... | collective-permute-start | bytes 98312 | tf_op jit(solution)/shard_map/ppermute | solution.py:456
  97.1 3.9 %collective-permute-start.13 = (f32[32,256]{1,0:T(8,128)S(1)}, f32[32,256]{1,0:T(8,128)S(1)}, u32[]{:S(2)}, u32[]{:S(2)}) collective-permute-start(f32[32,256]{1,0:T(8,128)S(1)} %get-tuple-element.58.refs_0_), channel_id=1, source_target_pairs={{0,16},{8,24},{16,0},{24,8},{1,17},{9,25},{17,1},{25,9},{2,18},{10... | collective-permute-start | bytes 98312 | tf_op jit(solution)/shard_map/ppermute | solution.py:456
  97.6 3.9 %collective-permute-start.12 = (f32[32,256]{1,0:T(8,128)S(1)}, f32[32,256]{1,0:T(8,128)S(1)}, u32[]{:S(2)}, u32[]{:S(2)}) collective-permute-start(f32[32,256]{1,0:T(8,128)S(1)} %get-tuple-element.58.refs_0_), channel_id=1, source_target_pairs={{0,8},{8,0},{16,24},{24,16},{1,9},{9,1},{17,25},{25,17},{2,10},{10... | collective-permute-start | bytes 98312 | tf_op jit(solution)/shard_map/ppermute | solution.py:456
  101.7 8.8 %collective-permute-start.20 = (bf16[256,512]{1,0:T(8,128)(2,1)S(1)}, bf16[256,512]{1,0:T(8,128)(2,1)S(1)}, u32[]{:S(2)}, u32[]{:S(2)}) collective-permute-start(bf16[256,512]{1,0:T(8,128)(2,1)S(1)} %get-tuple-element.63), channel_id=1, source_target_pairs={{0,16},{8,24},{16,0},{24,8},{1,17},{9,25},{17,1},{25,9},{2,18},{10... | collective-permute-start | bytes 786440 | tf_op jit(solution)/shard_map/ppermute | solution.py:456
  103.3 7.2 %collective-permute-start.21 = (bf16[256,512]{1,0:T(8,128)(2,1)S(1)}, bf16[256,512]{1,0:T(8,128)(2,1)S(1)}, u32[]{:S(2)}, u32[]{:S(2)}) collective-permute-start(bf16[256,512]{1,0:T(8,128)(2,1)S(1)} %get-tuple-element.64), channel_id=1, source_target_pairs={{0,8},{8,0},{16,24},{24,16},{1,9},{9,1},{17,25},{25,17},{2,10},{10... | collective-permute-start | bytes 786440 | tf_op jit(solution)/shard_map/ppermute | solution.py:456
  103.8 5.7 %collective-permute-start.19 = (f32[32,256]{1,0:T(8,128)S(1)}, f32[32,256]{1,0:T(8,128)S(1)}, u32[]{:S(2)}, u32[]{:S(2)}) collective-permute-start(f32[32,256]{1,0:T(8,128)S(1)} %turn_three.1.refs_0_), channel_id=1, source_target_pairs={{0,6},{1,7},{2,4},{3,5},{4,2},{5,3},{6,0},{7,1},{8,14},{9,15},{10,... | collective-permute-start | bytes 98312 | tf_op jit(solution)/shard_map/ppermute | solution.py:456
  105.3 5.0 %collective-permute-start.18 = (f32[32,256]{1,0:T(8,128)S(1)}, f32[32,256]{1,0:T(8,128)S(1)}, u32[]{:S(2)}, u32[]{:S(2)}) collective-permute-start(f32[32,256]{1,0:T(8,128)S(1)} %turn_three.1.refs_0_), channel_id=1, source_target_pairs={{0,4},{1,5},{2,6},{3,7},{4,0},{5,1},{6,2},{7,3},{8,12},{9,13},{10,... | collective-permute-start | bytes 98312 | tf_op jit(solution)/shard_map/ppermute | solution.py:456
  105.3 5.1 %collective-permute-start.17 = (f32[32,256]{1,0:T(8,128)S(1)}, f32[32,256]{1,0:T(8,128)S(1)}, u32[]{:S(2)}, u32[]{:S(2)}) collective-permute-start(f32[32,256]{1,0:T(8,128)S(1)} %turn_three.1.refs_0_), channel_id=1, source_target_pairs={{0,2},{1,3},{2,0},{3,1},{4,6},{5,7},{6,4},{7,5},{8,10},{9,11},{10,... | collective-permute-start | bytes 98312 | tf_op jit(solution)/shard_map/ppermute | solution.py:456
  110.4 2.5 %collective-permute-start.22 = (f32[128,256]{1,0:T(8,128)S(1)}, f32[128,256]{1,0:T(8,128)S(1)}, u32[]{:S(2)}, u32[]{:S(2)}) collective-permute-start(f32[128,256]{1,0:T(8,128)S(1)} %turn_four.1.refs_0_), channel_id=1, source_target_pairs={{0,1},{1,0},{2,3},{3,2},{4,5},{5,4},{6,7},{7,6},{8,9},{9,8},{10,11... | collective-permute-start | bytes 393224 | tf_op jit(solution)/shard_map/ppermute | solution.py:456
  (11 other events, 134.2 us)

commit v7 on v5

--- a/solution.py
+++ b/solution.py
@@ -304,9 +304,9 @@
         scratch_shapes=scratch,
         compiler_params=pltpu.CompilerParams(vmem_limit_bytes=40 * MIB),
         cost_estimate=pl.CostEstimate(
-            flops=12 * rows * width * shares * share,
-            bytes_accessed=10 * MIB,
-            transcendentals=rows * shares * share,
+            flops=12 * rows * width,
+            bytes_accessed=rows * width,
+            transcendentals=0,
         ),
         name="expert_rows",
     )(*args)
@@ -462,7 +462,7 @@
     ups, downs = pair(up, near_up, place), pair(down, near_down, place)
     weights = [ups, swap(ups, "dp", 2), downs, swap(downs, "dp", 1)]
     if in_turns(experts):
-        batches, later = ((0,), (4, 5), (2, 3, 1), (6,), (7,)), (6, 7)
+        batches, later = ((0, 1), (4, 5), (2, 3), (6,), (7,)), (7,)
     else:
         batches, later = (range(experts // 2), range(experts // 2, experts)), ()
     order = [s for batch in batches for s in batch]

time: 104 us -> 102 us (0.981)
  starting transfers between devices: 38.1 us -> 31.4 us
  waiting for transfers between devices: 25.5 us -> 30.3 us
    ppermute x26, starting transfers between devices: 38.1 us -> 31.4 us  [swap(): lax.ppermute(value, axis, [(i, i ^ s) for i in range(lax.axis_size(axis))])]
    ppermute x26, waiting for transfers between devices: 25.5 us -> 30.3 us  [swap(): lax.ppermute(value, axis, [(i, i ^ s) for i in range(lax.axis_size(axis))])]
  transfers between devices with their start and end apart: 26 -> 26, of which waited for: 13 -> 12; matrix products, arithmetic and copies ran while one was open for 2% -> 2% of each run, Pallas kernels for 26% -> 27%
where the time goes in v7:
time: 102 us; the launch traced here: 101 us
  Pallas kernels  31.5 us (31%)
  starting transfers between devices  31.4 us (31%)
  waiting for transfers between devices  30.3 us (30%)
  local copies, waits for them, and re-layouts  3.7 us (4%)
  other arithmetic  3.65 us (4%)
    ppermute x26, starting transfers between devices, swap(): lax.ppermute(value, axis, [(i, i ^ s) for i in range(lax.axis_size(axis))])  31.4 us
    ppermute x26, waiting for transfers between devices, swap(): lax.ppermute(value, axis, [(i, i ^ s) for i in range(lax.axis_size(axis))])  30.3 us
    pallas_call x5, Pallas kernels, expert_call(): pl.pallas_call(functools.partial(expert_kernel, counts, order, first, len...  25.8 us
    unnamed x16, local copies, waits for them, and re-layouts  3.66 us
    pallas_call x1, Pallas kernels, pack(): pl.pallas_call(functools.partial(pack_kernel, experts, capacity), out_sha...  3.52 us
    sub x1, other arithmetic, adam_update(): params - learn_rate * first_hat / (jnp.sqrt(second_hat) + adam_eps)  2.15 us
  transfers between devices with their start and end apart: 26, of which 12 were waited for; matrix products, arithmetic and copies ran while one was open for 2% of the time, Pallas kernels for 27%

profile of v7, /device:TPU:0, one launch (start us, length us, event | category | flops | bytes accessed | tf_op | source)
XLA Modules:
  0.0 101.4 jit_solution(6092015843396977774)
XLA Ops:
  2.0 3.0 %collective-permute-start.3 = (bf16[256,512]{1,0:T(8,128)(2,1)S(1)}, bf16[256,512]{1,0:T(8,128)(2,1)S(1)}, u32[]{:S(2)}, u32[]{:S(2)}) collective-permute-start(bf16[256,512]{1,0:T(8,128)(2,1)S(1)} %get-tuple-element.84.one_ref), channel_id=1, source_target_pairs={{0,16},{8,24},{16,0},{24,8},{1,17},{9,25},{17,1},{25,9},{2,18},{10... | collective-permute-start | bytes 786440 | tf_op jit(solution)/shard_map/ppermute | solution.py:439
  5.0 1.5 %collective-permute-start.1 = (bf16[256,512]{1,0:T(8,128)(2,1)S(1)}, bf16[256,512]{1,0:T(8,128)(2,1)S(1)}, u32[]{:S(2)}, u32[]{:S(2)}) collective-permute-start(bf16[256,512]{1,0:T(8,128)(2,1)S(1)} %get-tuple-element.85.one_ref), channel_id=1, source_target_pairs={{0,8},{8,0},{16,24},{24,16},{1,9},{9,1},{17,25},{25,17},{2,10},{10... | collective-permute-start | bytes 786440 | tf_op jit(solution)/shard_map/ppermute | solution.py:439
  10.1 3.5 %pack_rows.1 = (bf16[256,512]{1,0:T(8,128)(2,1)S(1)}, bf16[256,512]{1,0:T(8,128)(2,1)S(1)}, bf16[256,512]{1,0:T(8,128)(2,1)S(1)}, bf16[256,512]{1,0:T(8,128)(2,1...) custom-call(s32[1]{0:T(128)} %bitcast.me_ref.refs_12_, ...), custom_call_target="tpu_custom_call" | custom-call | flops 3221225472 | bytes 6291456 | tf_op jit(solution)/shard_map/pack_rows/pallas_call | solution.py:84
  15.0 2.6 %collective-permute-start.9 = (bf16[256,512]{1,0:T(8,128)(2,1)S(1)}, bf16[256,512]{1,0:T(8,128)(2,1)S(1)}, u32[]{:S(2)}, u32[]{:S(2)}) collective-permute-start(bf16[256,512]{1,0:T(8,128)(2,1)S(1)} %get-tuple-element.50), channel_id=1, source_target_pairs={{0,4},{1,5},{2,6},{3,7},{4,0},{5,1},{6,2},{7,3},{8,12},{9,13},{10,... | collective-permute-start | bytes 786440 | tf_op jit(solution)/shard_map/ppermute | solution.py:439
  17.7 1.6 %collective-permute-start.7 = (bf16[256,512]{1,0:T(8,128)(2,1)S(1)}, bf16[256,512]{1,0:T(8,128)(2,1)S(1)}, u32[]{:S(2)}, u32[]{:S(2)}) collective-permute-start(bf16[256,512]{1,0:T(8,128)(2,1)S(1)} %get-tuple-element.48), channel_id=1, source_target_pairs={{0,2},{1,3},{2,0},{3,1},{4,6},{5,7},{6,4},{7,5},{8,10},{9,11},{10,... | collective-permute-start | bytes 786440 | tf_op jit(solution)/shard_map/ppermute | solution.py:439
  19.3 7.6 %collective-permute-done.2.refs_4_.refs_3_ = bf16[2,256,512]{2,1,0:T(8,128)(2,1)S(1)} collective-permute-done((bf16[2,256,512]{2,1,0:T(8,128)(2,1)S(1)}, bf16[2,256,512]{2,1,0:T(8,128)(2,1)S(1)}, u32[]{:S(2)}, u32[]{:S(2)}) %collective-permute-start.2) | collective-permute-done | bytes 524320 | tf_op jit(solution)/shard_map/ppermute | solution.py:439
  27.2 3.6 %collective-permute-start.6 = (bf16[256,512]{1,0:T(8,128)(2,1)S(1)}, bf16[256,512]{1,0:T(8,128)(2,1)S(1)}, u32[]{:S(2)}, u32[]{:S(2)}) collective-permute-start(bf16[256,512]{1,0:T(8,128)(2,1)S(1)} %get-tuple-element.47), channel_id=1, source_target_pairs={{0,6},{1,7},{2,4},{3,5},{4,2},{5,3},{6,0},{7,1},{8,14},{9,15},{10,... | collective-permute-start | bytes 786440 | tf_op jit(solution)/shard_map/ppermute | solution.py:439
  30.8 6.3 %expert_rows.5 = (f32[4,2,256,512]{3,2,1,0:T(8,128)S(1)}, f32[256,256]{1,0:T(8,128)S(1)}, f32[2,256]{1,0:T(2,128)S(1)}, bf16[256,512]{1,0:T(8,128)(2,1)S(1)}) custom-call(bf16[256,512]{1,0:T(8,128)(2,1)S(1)} %get-tuple-element.42.refs_0_, bf16[256,512]{1,0:T(8,128)(2,1)S(1)} %collective-permute-done.refs_1_, bf16[256,256]{1,0:T(8,128)(2,1)S(1)} %copy-done, ...), custom_call_target="tpu_custom_call" | custom-call | flops 1572864 | bytes 131072 | tf_op jit(solution)/shard_map/expert_rows/pallas_call | solution.py:299
  37.1 1.9 %collective-permute-start.5 = (bf16[256,512]{1,0:T(8,128)(2,1)S(1)}, bf16[256,512]{1,0:T(8,128)(2,1)S(1)}, u32[]{:S(2)}, u32[]{:S(2)}) collective-permute-start(bf16[256,512]{1,0:T(8,128)(2,1)S(1)} %get-tuple-element.46), channel_id=1, source_target_pairs={{0,7},{1,6},{2,5},{3,4},{4,3},{5,2},{6,1},{7,0},{8,15},{9,14},{10,... | collective-permute-start | bytes 786440 | tf_op jit(solution)/shard_map/ppermute | solution.py:439
  39.0 2.1 %collective-permute-done.10.refs_1_ = bf16[256,512]{1,0:T(8,128)(2,1)S(1)} collective-permute-done((bf16[256,512]{1,0:T(8,128)(2,1)S(1)}, bf16[256,512]{1,0:T(8,128)(2,1)S(1)}, u32[]{:S(2)}, u32[]{:S(2)}) %collective-permute-start.10) | collective-permute-done | bytes 262176 | tf_op jit(solution)/shard_map/ppermute | solution.py:439
  41.2 6.5 %expert_rows.6 = (f32[4,2,256,512]{3,2,1,0:T(8,128)S(1)}, f32[256,256]{1,0:T(8,128)S(1)}, f32[2,256]{1,0:T(2,128)S(1)}) custom-call(bf16[256,512]{1,0:T(8,128)(2,1)S(1)} %collective-permute-done.9.refs_0_, bf16[256,512]{1,0:T(8,128)(2,1)S(1)} %collective-permute-done.10.refs_1_, bf16[256,256]{1,0:T(8,128)(2,1)S(1)} %copy-done, ...), custom_call_target="tpu_custom_call" | custom-call | flops 1572864 | bytes 131072 | tf_op jit(solution)/shard_map/expert_rows/pallas_call | solution.py:299
  47.7 9.0 %collective-permute-done.8.refs_1_ = bf16[256,512]{1,0:T(8,128)(2,1)S(1)} collective-permute-done((bf16[256,512]{1,0:T(8,128)(2,1)S(1)}, bf16[256,512]{1,0:T(8,128)(2,1)S(1)}, u32[]{:S(2)}, u32[]{:S(2)}) %collective-permute-start.8) | collective-permute-done | bytes 262176 | tf_op jit(solution)/shard_map/ppermute | solution.py:439
  56.7 6.3 %expert_rows.7 = (f32[4,2,256,512]{3,2,1,0:T(8,128)S(1)}, f32[256,256]{1,0:T(8,128)S(1)}, f32[2,256]{1,0:T(2,128)S(1)}) custom-call(bf16[256,512]{1,0:T(8,128)(2,1)S(1)} %collective-permute-done.7.refs_0_, bf16[256,512]{1,0:T(8,128)(2,1)S(1)} %collective-permute-done.8.refs_1_, bf16[256,256]{1,0:T(8,128)(2,1)S(1)} %copy-done, ...), custom_call_target="tpu_custom_call" | custom-call | flops 1572864 | bytes 131072 | tf_op jit(solution)/shard_map/expert_rows/pallas_call | solution.py:299
  63.1 3.2 %expert_rows.8 = (f32[4,2,256,512]{3,2,1,0:T(8,128)S(1)}, f32[256,256]{1,0:T(8,128)S(1)}, f32[1,256]{1,0:T(1,128)S(1)}) custom-call(bf16[256,512]{1,0:T(8,128)(2,1)S(1)} %collective-permute-done.6.refs_0_, bf16[256,256]{1,0:T(8,128)(2,1)S(1)} %copy-done, bf16[2,256,512]{2,1,0:T(8,128)(2,1)S(1)} %pair.2.refs_3_.refs_2_, ...), custom_call_target="tpu_custom_call" | custom-call | flops 786432 | bytes 65536 | tf_op jit(solution)/shard_map/expert_rows/pallas_call | solution.py:299
  66.3 3.5 %expert_rows.9 = (f32[2,256,512]{2,1,0:T(8,128)S(1)}, f32[256,512]{1,0:T(8,128)S(1)}, f32[256,512]{1,0:T(8,128)S(1)}, bf16[2,256,512]{2,1,0:T(8,128)(2,1)S(1)}, ...) custom-call(bf16[256,512]{1,0:T(8,128)(2,1)S(1)} %collective-permute-done.5.refs_0_, ...), custom_call_target="tpu_custom_call" | custom-call | flops 786432 | bytes 65536 | tf_op jit(solution)/shard_map/expert_rows/pallas_call | solution.py:299
  70.6 1.4 %collective-permute-done.11.got_ref = f32[136,256]{1,0:T(8,128)S(1)} collective-permute-done((f32[136,256]{1,0:T(8,128)S(1)}, f32[136,256]{1,0:T(8,128)S(1)}, u32[]{:S(2)}, u32[]{:S(2)}) %collective-permute-start.11) | collective-permute-done | bytes 139296 | tf_op jit(solution)/shard_map/ppermute | solution.py:439
  72.6 4.0 %collective-permute-start.13 = (f32[40,256]{1,0:T(8,128)S(1)}, f32[40,256]{1,0:T(8,128)S(1)}, u32[]{:S(2)}, u32[]{:S(2)}) collective-permute-start(f32[40,256]{1,0:T(8,128)S(1)} %get-tuple-element.68), channel_id=1, source_target_pairs={{0,4},{1,5},{2,6},{3,7},{4,0},{5,1},{6,2},{7,3},{8,12},{9,13},{10,... | collective-permute-start | bytes 122888 | tf_op jit(solution)/shard_map/ppermute | solution.py:439
  76.7 2.8 %collective-permute-done.13.refs_2_ = f32[40,256]{1,0:T(8,128)S(1)} collective-permute-done((f32[40,256]{1,0:T(8,128)S(1)}, f32[40,256]{1,0:T(8,128)S(1)}, u32[]{:S(2)}, u32[]{:S(2)}) %collective-permute-start.13) | collective-permute-done | bytes 40992 | tf_op jit(solution)/shard_map/ppermute | solution.py:439
  79.5 3.0 %collective-permute-done.14.refs_3_ = f32[40,256]{1,0:T(8,128)S(1)} collective-permute-done((f32[40,256]{1,0:T(8,128)S(1)}, f32[40,256]{1,0:T(8,128)S(1)}, u32[]{:S(2)}, u32[]{:S(2)}) %collective-permute-start.14) | collective-permute-done | bytes 40992 | tf_op jit(solution)/shard_map/ppermute | solution.py:439
  82.5 2.5 %collective-permute-start.17 = (f32[32,256]{1,0:T(8,128)S(1)}, f32[32,256]{1,0:T(8,128)S(1)}, u32[]{:S(2)}, u32[]{:S(2)}) collective-permute-start(f32[32,256]{1,0:T(8,128)S(1)} %get-tuple-element.70.refs_0_), channel_id=1, source_target_pairs={{0,24},{8,16},{16,8},{24,0},{1,25},{9,17},{17,9},{25,1},{2,26},{10... | collective-permute-start | bytes 98312 | tf_op jit(solution)/shard_map/ppermute | solution.py:439
  86.1 1.6 %collective-permute-done.17.refs_3_ = f32[32,256]{1,0:T(8,128)S(1)} collective-permute-done((f32[32,256]{1,0:T(8,128)S(1)}, f32[32,256]{1,0:T(8,128)S(1)}, u32[]{:S(2)}, u32[]{:S(2)}) %collective-permute-start.17) | collective-permute-done | bytes 32800 | tf_op jit(solution)/shard_map/ppermute | solution.py:439
  89.6 1.7 %collective-permute-start.23 = (bf16[256,512]{1,0:T(8,128)(2,1)S(1)}, bf16[256,512]{1,0:T(8,128)(2,1)S(1)}, u32[]{:S(2)}, u32[]{:S(2)}) collective-permute-start(bf16[256,512]{1,0:T(8,128)(2,1)S(1)} %get-tuple-element.75), channel_id=1, source_target_pairs={{0,16},{8,24},{16,0},{24,8},{1,17},{9,25},{17,1},{25,9},{2,18},{10... | collective-permute-start | bytes 786440 | tf_op jit(solution)/shard_map/ppermute | solution.py:439
  92.2 4.1 %collective-permute-start.20 = (f32[32,256]{1,0:T(8,128)S(1)}, f32[32,256]{1,0:T(8,128)S(1)}, u32[]{:S(2)}, u32[]{:S(2)}) collective-permute-start(f32[32,256]{1,0:T(8,128)S(1)} %turn_three.1.refs_0_), channel_id=1, source_target_pairs={{0,2},{1,3},{2,0},{3,1},{4,6},{5,7},{6,4},{7,5},{8,10},{9,11},{10,... | collective-permute-start | bytes 98312 | tf_op jit(solution)/shard_map/ppermute | solution.py:439
  98.6 2.2 %divide_subtract_fusion = (f32[1,2,256,512]{3,2,1,0:T(8,128)}, f32[1,2,256,512]{3,2,1,0:T(8,128)}, f32[1,2,256,512]{3,2,1,0:T(8,128)}) fusion(f32[1,2,256,512]{3,2,1,0:T(8,128)S(1)} %copy-done.5, f32[1,1,256,512]{3,2,1,0:T(8,128)S(1)} %get-tuple-element.83, f32[1,1,256,512]{3,2,1,0:T(8,128)S(1)} %get-tuple-element.82, f32[1,2,256,512]{3,2,1,0:T(8,128)S(1)} %copy-done.6, ...), kind=kLoop, calls=%fused_computation.3 | loop fusion | flops 3407872 | bytes 7340032 | tf_op jit(solution)/shard_map/sub | solution.py:430
  (63 shorter events, 15.0 us)
Async XLA Ops:
  2.0 12.3 %collective-permute-start.3 = (bf16[256,512]{1,0:T(8,128)(2,1)S(1)}, bf16[256,512]{1,0:T(8,128)(2,1)S(1)}, u32[]{:S(2)}, u32[]{:S(2)}) collective-permute-start(bf16[256,512]{1,0:T(8,128)(2,1)S(1)} %get-tuple-element.84.one_ref), channel_id=1, source_target_pairs={{0,16},{8,24},{16,0},{24,8},{1,17},{9,25},{17,1},{25,9},{2,18},{10... | collective-permute-start | bytes 786440 | tf_op jit(solution)/shard_map/ppermute | solution.py:439
  5.0 8.7 %collective-permute-start.1 = (bf16[256,512]{1,0:T(8,128)(2,1)S(1)}, bf16[256,512]{1,0:T(8,128)(2,1)S(1)}, u32[]{:S(2)}, u32[]{:S(2)}) collective-permute-start(bf16[256,512]{1,0:T(8,128)(2,1)S(1)} %get-tuple-element.85.one_ref), channel_id=1, source_target_pairs={{0,8},{8,0},{16,24},{24,16},{1,9},{9,1},{17,25},{25,17},{2,10},{10... | collective-permute-start | bytes 786440 | tf_op jit(solution)/shard_map/ppermute | solution.py:439
  13.7 13.2 %collective-permute-start.2 = (bf16[2,256,512]{2,1,0:T(8,128)(2,1)S(1)}, bf16[2,256,512]{2,1,0:T(8,128)(2,1)S(1)}, u32[]{:S(2)}, u32[]{:S(2)}) collective-permute-start(bf16[2,256,512]{2,1,0:T(8,128)(2,1)S(1)} %pair.2.refs_3_.refs_2_), channel_id=1, source_target_pairs={{0,16},{8,24},{16,0},{24,8},{1,17},{9,25},{17,1},{25,9},{2,18},{10... | collective-permute-start | bytes 1572872 | tf_op jit(solution)/shard_map/ppermute | solution.py:439
  14.3 12.9 %collective-permute-start.4 = (bf16[2,256,512]{2,1,0:T(8,128)(2,1)S(1)}, bf16[2,256,512]{2,1,0:T(8,128)(2,1)S(1)}, u32[]{:S(2)}, u32[]{:S(2)}) collective-permute-start(bf16[2,256,512]{2,1,0:T(8,128)(2,1)S(1)} %pair.3.refs_5_.refs_4_), channel_id=1, source_target_pairs={{0,8},{8,0},{16,24},{24,16},{1,9},{9,1},{17,25},{25,17},{2,10},{10... | collective-permute-start | bytes 1572872 | tf_op jit(solution)/shard_map/ppermute | solution.py:439
  15.0 2.8 %collective-permute-start = (bf16[256,512]{1,0:T(8,128)(2,1)S(1)}, bf16[256,512]{1,0:T(8,128)(2,1)S(1)}, u32[]{:S(2)}, u32[]{:S(2)}) collective-permute-start(bf16[256,512]{1,0:T(8,128)(2,1)S(1)} %get-tuple-element.43), channel_id=1, source_target_pairs={{0,1},{1,0},{2,3},{3,2},{4,5},{5,4},{6,7},{7,6},{8,9},{9,8},{10,11... | collective-permute-start | bytes 786440 | tf_op jit(solution)/shard_map/ppermute | solution.py:439
  15.0 22.2 %collective-permute-start.9 = (bf16[256,512]{1,0:T(8,128)(2,1)S(1)}, bf16[256,512]{1,0:T(8,128)(2,1)S(1)}, u32[]{:S(2)}, u32[]{:S(2)}) collective-permute-start(bf16[256,512]{1,0:T(8,128)(2,1)S(1)} %get-tuple-element.50), channel_id=1, source_target_pairs={{0,4},{1,5},{2,6},{3,7},{4,0},{5,1},{6,2},{7,3},{8,12},{9,13},{10,... | collective-permute-start | bytes 786440 | tf_op jit(solution)/shard_map/ppermute | solution.py:439
  17.6 23.6 %collective-permute-start.10 = (bf16[256,512]{1,0:T(8,128)(2,1)S(1)}, bf16[256,512]{1,0:T(8,128)(2,1)S(1)}, u32[]{:S(2)}, u32[]{:S(2)}) collective-permute-start(bf16[256,512]{1,0:T(8,128)(2,1)S(1)} %get-tuple-element.51), channel_id=1, source_target_pairs={{0,5},{1,4},{2,7},{3,6},{4,1},{5,0},{6,3},{7,2},{8,13},{9,12},{10,... | collective-permute-start | bytes 786440 | tf_op jit(solution)/shard_map/ppermute | solution.py:439
  17.7 30.0 %collective-permute-start.7 = (bf16[256,512]{1,0:T(8,128)(2,1)S(1)}, bf16[256,512]{1,0:T(8,128)(2,1)S(1)}, u32[]{:S(2)}, u32[]{:S(2)}) collective-permute-start(bf16[256,512]{1,0:T(8,128)(2,1)S(1)} %get-tuple-element.48), channel_id=1, source_target_pairs={{0,2},{1,3},{2,0},{3,1},{4,6},{5,7},{6,4},{7,5},{8,10},{9,11},{10,... | collective-permute-start | bytes 786440 | tf_op jit(solution)/shard_map/ppermute | solution.py:439
  26.9 29.8 %collective-permute-start.8 = (bf16[256,512]{1,0:T(8,128)(2,1)S(1)}, bf16[256,512]{1,0:T(8,128)(2,1)S(1)}, u32[]{:S(2)}, u32[]{:S(2)}) collective-permute-start(bf16[256,512]{1,0:T(8,128)(2,1)S(1)} %get-tuple-element.49), channel_id=1, source_target_pairs={{0,3},{1,2},{2,1},{3,0},{4,7},{5,6},{6,5},{7,4},{8,11},{9,10},{10,... | collective-permute-start | bytes 786440 | tf_op jit(solution)/shard_map/ppermute | solution.py:439
  27.2 35.8 %collective-permute-start.6 = (bf16[256,512]{1,0:T(8,128)(2,1)S(1)}, bf16[256,512]{1,0:T(8,128)(2,1)S(1)}, u32[]{:S(2)}, u32[]{:S(2)}) collective-permute-start(bf16[256,512]{1,0:T(8,128)(2,1)S(1)} %get-tuple-element.47), channel_id=1, source_target_pairs={{0,6},{1,7},{2,4},{3,5},{4,2},{5,3},{6,0},{7,1},{8,14},{9,15},{10,... | collective-permute-start | bytes 786440 | tf_op jit(solution)/shard_map/ppermute | solution.py:439
  37.1 29.2 %collective-permute-start.5 = (bf16[256,512]{1,0:T(8,128)(2,1)S(1)}, bf16[256,512]{1,0:T(8,128)(2,1)S(1)}, u32[]{:S(2)}, u32[]{:S(2)}) collective-permute-start(bf16[256,512]{1,0:T(8,128)(2,1)S(1)} %get-tuple-element.46), channel_id=1, source_target_pairs={{0,7},{1,6},{2,5},{3,4},{4,3},{5,2},{6,1},{7,0},{8,15},{9,14},{10,... | collective-permute-start | bytes 786440 | tf_op jit(solution)/shard_map/ppermute | solution.py:439
  69.8 19.6 %collective-permute-start.18 = (bf16[2,256,512]{2,1,0:T(8,128)(2,1)S(1)}, bf16[2,256,512]{2,1,0:T(8,128)(2,1)S(1)}, u32[]{:S(2)}, u32[]{:S(2)}) collective-permute-start(bf16[2,256,512]{2,1,0:T(8,128)(2,1)S(1)} %get-tuple-element.71), channel_id=1, source_target_pairs={{0,8},{8,0},{16,24},{24,16},{1,9},{9,1},{17,25},{25,17},{2,10},{10... | collective-permute-start | bytes 1572872 | tf_op jit(solution)/shard_map/ppermute | solution.py:439
  70.4 19.0 %collective-permute-start.19 = (bf16[2,256,512]{2,1,0:T(8,128)(2,1)S(1)}, bf16[2,256,512]{2,1,0:T(8,128)(2,1)S(1)}, u32[]{:S(2)}, u32[]{:S(2)}) collective-permute-start(bf16[2,256,512]{2,1,0:T(8,128)(2,1)S(1)} %get-tuple-element.72), channel_id=1, source_target_pairs={{0,16},{8,24},{16,0},{24,8},{1,17},{9,25},{17,1},{25,9},{2,18},{10... | collective-permute-start | bytes 1572872 | tf_op jit(solution)/shard_map/ppermute | solution.py:439
  72.0 4.7 %collective-permute-start.12 = (f32[40,256]{1,0:T(8,128)S(1)}, f32[40,256]{1,0:T(8,128)S(1)}, u32[]{:S(2)}, u32[]{:S(2)}) collective-permute-start(f32[40,256]{1,0:T(8,128)S(1)} %get-tuple-element.67), channel_id=1, source_target_pairs={{0,2},{1,3},{2,0},{3,1},{4,6},{5,7},{6,4},{7,5},{8,10},{9,11},{10,... | collective-permute-start | bytes 122888 | tf_op jit(solution)/shard_map/ppermute | solution.py:439
  72.6 6.9 %collective-permute-start.13 = (f32[40,256]{1,0:T(8,128)S(1)}, f32[40,256]{1,0:T(8,128)S(1)}, u32[]{:S(2)}, u32[]{:S(2)}) collective-permute-start(f32[40,256]{1,0:T(8,128)S(1)} %get-tuple-element.68), channel_id=1, source_target_pairs={{0,4},{1,5},{2,6},{3,7},{4,0},{5,1},{6,2},{7,3},{8,12},{9,13},{10,... | collective-permute-start | bytes 122888 | tf_op jit(solution)/shard_map/ppermute | solution.py:439
  76.7 5.8 %collective-permute-start.14 = (f32[40,256]{1,0:T(8,128)S(1)}, f32[40,256]{1,0:T(8,128)S(1)}, u32[]{:S(2)}, u32[]{:S(2)}) collective-permute-start(f32[40,256]{1,0:T(8,128)S(1)} %get-tuple-element.69), channel_id=1, source_target_pairs={{0,6},{1,7},{2,4},{3,5},{4,2},{5,3},{6,0},{7,1},{8,14},{9,15},{10,... | collective-permute-start | bytes 122888 | tf_op jit(solution)/shard_map/ppermute | solution.py:439
  82.5 5.2 %collective-permute-start.17 = (f32[32,256]{1,0:T(8,128)S(1)}, f32[32,256]{1,0:T(8,128)S(1)}, u32[]{:S(2)}, u32[]{:S(2)}) collective-permute-start(f32[32,256]{1,0:T(8,128)S(1)} %get-tuple-element.70.refs_0_), channel_id=1, source_target_pairs={{0,24},{8,16},{16,8},{24,0},{1,25},{9,17},{17,9},{25,1},{2,26},{10... | collective-permute-start | bytes 98312 | tf_op jit(solution)/shard_map/ppermute | solution.py:439
  85.0 3.9 %collective-permute-start.16 = (f32[32,256]{1,0:T(8,128)S(1)}, f32[32,256]{1,0:T(8,128)S(1)}, u32[]{:S(2)}, u32[]{:S(2)}) collective-permute-start(f32[32,256]{1,0:T(8,128)S(1)} %get-tuple-element.70.refs_0_), channel_id=1, source_target_pairs={{0,16},{8,24},{16,0},{24,8},{1,17},{9,25},{17,1},{25,9},{2,18},{10... | collective-permute-start | bytes 98312 | tf_op jit(solution)/shard_map/ppermute | solution.py:439
  85.5 3.9 %collective-permute-start.15 = (f32[32,256]{1,0:T(8,128)S(1)}, f32[32,256]{1,0:T(8,128)S(1)}, u32[]{:S(2)}, u32[]{:S(2)}) collective-permute-start(f32[32,256]{1,0:T(8,128)S(1)} %get-tuple-element.70.refs_0_), channel_id=1, source_target_pairs={{0,8},{8,0},{16,24},{24,16},{1,9},{9,1},{17,25},{25,17},{2,10},{10... | collective-permute-start | bytes 98312 | tf_op jit(solution)/shard_map/ppermute | solution.py:439
  89.6 8.6 %collective-permute-start.23 = (bf16[256,512]{1,0:T(8,128)(2,1)S(1)}, bf16[256,512]{1,0:T(8,128)(2,1)S(1)}, u32[]{:S(2)}, u32[]{:S(2)}) collective-permute-start(bf16[256,512]{1,0:T(8,128)(2,1)S(1)} %get-tuple-element.75), channel_id=1, source_target_pairs={{0,16},{8,24},{16,0},{24,8},{1,17},{9,25},{17,1},{25,9},{2,18},{10... | collective-permute-start | bytes 786440 | tf_op jit(solution)/shard_map/ppermute | solution.py:439
  91.3 6.9 %collective-permute-start.24 = (bf16[256,512]{1,0:T(8,128)(2,1)S(1)}, bf16[256,512]{1,0:T(8,128)(2,1)S(1)}, u32[]{:S(2)}, u32[]{:S(2)}) collective-permute-start(bf16[256,512]{1,0:T(8,128)(2,1)S(1)} %get-tuple-element.76), channel_id=1, source_target_pairs={{0,8},{8,0},{16,24},{24,16},{1,9},{9,1},{17,25},{25,17},{2,10},{10... | collective-permute-start | bytes 786440 | tf_op jit(solution)/shard_map/ppermute | solution.py:439
  91.9 5.7 %collective-permute-start.22 = (f32[32,256]{1,0:T(8,128)S(1)}, f32[32,256]{1,0:T(8,128)S(1)}, u32[]{:S(2)}, u32[]{:S(2)}) collective-permute-start(f32[32,256]{1,0:T(8,128)S(1)} %turn_three.1.refs_0_), channel_id=1, source_target_pairs={{0,6},{1,7},{2,4},{3,5},{4,2},{5,3},{6,0},{7,1},{8,14},{9,15},{10,... | collective-permute-start | bytes 98312 | tf_op jit(solution)/shard_map/ppermute | solution.py:439
  92.2 5.5 %collective-permute-start.21 = (f32[32,256]{1,0:T(8,128)S(1)}, f32[32,256]{1,0:T(8,128)S(1)}, u32[]{:S(2)}, u32[]{:S(2)}) collective-permute-start(f32[32,256]{1,0:T(8,128)S(1)} %turn_three.1.refs_0_), channel_id=1, source_target_pairs={{0,4},{1,5},{2,6},{3,7},{4,0},{5,1},{6,2},{7,3},{8,12},{9,13},{10,... | collective-permute-start | bytes 98312 | tf_op jit(solution)/shard_map/ppermute | solution.py:439
  92.2 6.0 %collective-permute-start.20 = (f32[32,256]{1,0:T(8,128)S(1)}, f32[32,256]{1,0:T(8,128)S(1)}, u32[]{:S(2)}, u32[]{:S(2)}) collective-permute-start(f32[32,256]{1,0:T(8,128)S(1)} %turn_three.1.refs_0_), channel_id=1, source_target_pairs={{0,2},{1,3},{2,0},{3,1},{4,6},{5,7},{6,4},{7,5},{8,10},{9,11},{10,... | collective-permute-start | bytes 98312 | tf_op jit(solution)/shard_map/ppermute | solution.py:439
  (10 other events, 114.4 us)

commit v8 on v7

--- a/solution.py
+++ b/solution.py
@@ -136,16 +136,17 @@
     held = take(relays)
     if last:
         loss_refs = take(last - 1)
-        (me_ref,) = take(1)
-        own_ref, next_up_ref, next_down_ref, sent_up_ref, sent_down_ref = take(5)
-        kept_ref, note_ref = take(2)
+        (ids_ref,) = take(1)
+        (acc_ref,) = take(1)
+        trunk_parts = take(shares if in_turns(experts) else 1)
+        (all_loss_ref,) = take(1)
     else:
         acc_ref, acc_trunk_ref, loss_ref = take(3)
         for source, copy in zip(held, take(relays)):
             copy[...] = source[...]
     x_ref, hid_ref, slope_ref = take(3)
     if last:
-        acc_ref, acc_trunk_ref, loss_ref = take(3)
+        acc_trunk_ref, loss_ref = take(2)
 
     width = trunk_ref.shape[0]
     share = ups_near.shape[2]
@@ -220,29 +221,18 @@
         for i in range(steps):
             step(i, 0)
     if last:
-        own_ref[...] = acc_ref[0]
-        next_up_ref[...] = acc_ref[2, 0]
-        next_down_ref[...] = acc_ref[1, 1]
-        for k, j in enumerate((1, 3)):
-            sent_up_ref[k] = acc_ref[j, 0].astype(BF16)
-        for k, j in enumerate((2, 3)):
-            sent_down_ref[k] = acc_ref[j, 1].astype(BF16)
         all_losses = list(loss_refs) + [loss_ref]
         if not in_turns(experts):
-            kept_ref[...] = acc_trunk_ref[...]
-            for row in range(note_ref.shape[0]):
-                note_ref[row : row + 1, :] = loss_row(all_losses, row)
+            trunk_parts[0][...] = acc_trunk_ref[...]
+            for row in range(all_loss_ref.shape[0]):
+                all_loss_ref[row : row + 1, :] = loss_row(all_losses, row)
             return
-        me = me_ref[0]
-        part = width // experts
-        kept_ref[experts // 2 * part :, :] = jnp.zeros((8, width), F32)
-        note_ref[experts // 2 * part :, :] = jnp.zeros((8, width), F32)
+        quarter = width // shares
+        for j, ref in enumerate(trunk_parts):
+            at = pl.multiple_of((ids_ref[1] ^ j) * quarter, quarter)
+            ref[...] = acc_trunk_ref[pl.ds(at, quarter), :]
         for s in range(experts):
-            ref = note_ref if s % 2 else kept_ref
-            mine = pl.ds(pl.multiple_of((me ^ s) * part, part), part)
-            ref[s // 2 * part : (s // 2 + 1) * part, :] = acc_trunk_ref[mine, :]
-            at = experts // 2 * part + s // 2
-            ref[at : at + 1, :] = loss_row(all_losses, order.index(s))
+            all_loss_ref[s : s + 1, :] = loss_row(all_losses, order.index(s))
 
 
 def in_turns(experts):
@@ -256,7 +246,7 @@
         row -= ref.shape[0]
 
 
-def expert_call(xs, trunk_weight, weights, prior, losses, me, order, last, relays=()):
+def expert_call(xs, trunk_weight, weights, prior, losses, ids, order, last, relays=()):
     experts = len(order)
     block_rows = xs[0].shape[0]
     width = trunk_weight.shape[0]
@@ -279,19 +269,15 @@
         pltpu.VMEM((step_rows, shares * share), F32),
     ]
     if last:
-        args += list(losses) + [me]
+        args += list(losses) + [ids]
         in_specs += [whole()] * len(losses) + [whole(pltpu.SMEM)]
-        outs = [jax.ShapeDtypeStruct((2, width, share), F32)]
-        outs += [jax.ShapeDtypeStruct((width, share), F32)] * 2
-        outs += [jax.ShapeDtypeStruct((2, width, share), BF16)] * 2
+        outs = [acc]
         if in_turns(experts):
-            outs += [jax.ShapeDtypeStruct((width // 2 + 8, width), F32)] * 2
+            outs += [jax.ShapeDtypeStruct((width // shares, width), F32)] * shares
         else:
-            outs += [
-                acc_trunk,
-                jax.ShapeDtypeStruct((experts * block_rows // step_rows, step_rows), F32),
-            ]
-        scratch += [pltpu.VMEM(a.shape, a.dtype) for a in (acc, acc_trunk, loss)]
+            outs += [acc_trunk]
+        outs += [jax.ShapeDtypeStruct((experts * block_rows // step_rows, step_rows), F32)]
+        scratch += [pltpu.VMEM(a.shape, a.dtype) for a in (acc_trunk, loss)]
     else:
         outs = [acc, acc_trunk, loss]
         outs += [jax.ShapeDtypeStruct(relay.shape, relay.dtype) for relay in relays]
@@ -312,61 +298,87 @@
     )(*args)
 
 
-def turn_one_kernel(part, kept_ref, got_ref, *outs):
-    lost = kept_ref[4 * part :, :]
-    found = got_ref[4 * part :, :]
+def four(refs):
+    return (refs[0][...] + refs[1][...]) + (refs[2][...] + refs[3][...])
+
+
+def dp_turn_kernel(q0, q1, q2, q3, loss_ref, total_ref, note_ref):
+    total = four((q0, q1, q2, q3))
+    total_ref[...] = total
+    rows = total.shape[0]
+    note_ref[:rows, :] = total
+    for k in range(4):
+        note_ref[rows + k : rows + k + 1, :] = loss_ref[2 * k + 1 : 2 * k + 2, :]
+    note_ref[rows + 4 :, :] = jnp.zeros((4, total.shape[1]), F32)
+
+
+def pair_turn_kernel(ids_ref, total_ref, got_ref, loss_ref, *outs):
+    rows, width = total_ref.shape
+    half = rows // 2
+    at = pl.ds(pl.multiple_of((ids_ref[0] & 1) * half, half), half)
     for k, ref in enumerate(outs):
-        at = slice(k * part, (k + 1) * part)
-        ref[:part, :] = kept_ref[at, :] + got_ref[at, :]
-        ref[part:, :] = jnp.concatenate(
-            [lost[k : k + 1], found[k : k + 1], jnp.zeros((6, lost.shape[1]), F32)], axis=0
-        )
-
-
-def turn_two_kernel(part, *refs):
-    *notes, sum_ref, loss_ref = refs
-    held = [ref[:part, :] for ref in notes]
-    sum_ref[...] = (held[0] + held[1]) + (held[2] + held[3])
-    loss_ref[...] = jnp.concatenate([ref[part : part + 2, :] for ref in notes], axis=0)
-
-
-def turn_three_kernel(part, *refs):
-    held = [ref[...] for ref in refs[:4]]
-    refs[-1][...] = (held[0] + held[1]) + (held[2] + held[3])
-
-
-def turn_four_kernel(part, *refs):
-    for k in range(4):
-        refs[-1][k * part : (k + 1) * part, :] = refs[k][...]
-
-
-def turn(kernel, held, part, shapes, name, ahead=()):
-    return pl.pallas_call(
-        functools.partial(kernel, part),
-        out_shape=[jax.ShapeDtypeStruct((rows, held[0].shape[1]), F32) for rows in shapes],
-        in_specs=[whole()] * len(held) + [whole(pl.ANY)] * len(ahead),
+        ref[:half, :] = total_ref[at, :] + got_ref[at, :]
+        ref[half : half + 1, :] = loss_ref[2 * k : 2 * k + 1, :]
+        ref[half + 1 : half + 2, :] = got_ref[rows + k : rows + k + 1, :]
+        ref[half + 2 :, :] = jnp.zeros((6, width), F32)
+
+
+def z_turn_kernel(*refs):
+    *notes, total_ref, loss_ref = refs
+    half = total_ref.shape[0]
+    total_ref[...] = four([note.at[:half, :] for note in notes])
+    for k, note in enumerate(notes):
+        loss_ref[2 * k : 2 * k + 2, :] = note[half : half + 2, :]
+
+
+def join_kernel(ids_ref, own_ref, other_ref, both_ref):
+    half = own_ref.shape[0]
+    core = ids_ref[0] & 1
+    both_ref[pl.ds(pl.multiple_of(core * half, half), half), :] = own_ref[...]
+    both_ref[pl.ds(pl.multiple_of((1 - core) * half, half), half), :] = other_ref[...]
+
+
+def assemble_kernel(ids_ref, *refs):
+    *held, _, trunk_ref = refs
+    for j, ref in enumerate(held):
+        rows = ref.shape[0]
+        at = pl.multiple_of((ids_ref[1] ^ j) * rows, rows)
+        trunk_ref[pl.ds(at, rows), :] = ref[...]
+
+
+def turn(kernel, held, shapes, name, ids=None):
+    first = [] if ids is None else [ids]
+    width = held[0].shape[1]
+    return pl.pallas_call(
+        kernel,
+        out_shape=[jax.ShapeDtypeStruct((rows, width), F32) for rows in shapes],
+        in_specs=[whole(pltpu.SMEM)] * len(first) + [whole()] * len(held),
         out_specs=[whole()] * len(shapes),
         compiler_params=pltpu.CompilerParams(vmem_limit_bytes=4 * MIB),
         name=name,
-    )(*held, *ahead)
-
-
-def pass_on_kernel(next_up_ref, got_up_ref, next_down_ref, got_down_ref, *refs):
-    up_ref, down_ref = refs[-2:]
-    up_ref[...] = (next_up_ref[...] + got_up_ref[1].astype(F32)).astype(BF16)
-    down_ref[...] = (next_down_ref[...] + got_down_ref[1].astype(F32)).astype(BF16)
-
-
-def pass_on(next_up, got_up, next_down, got_down, ahead=()):
-    up, down = pl.pallas_call(
-        pass_on_kernel,
-        out_shape=[jax.ShapeDtypeStruct(next_up.shape, BF16)] * 2,
-        in_specs=[whole()] * 4 + [whole(pl.ANY)] * len(ahead),
+    )(*first, *held)
+
+
+def send_kernel(acc_ref, ahead_ref, up_ref, down_ref):
+    for k in range(2):
+        up_ref[k] = acc_ref[2 * k + 1, 0].astype(BF16)
+        down_ref[k] = acc_ref[k + 2, 1].astype(BF16)
+
+
+def pass_on_kernel(acc_ref, got_up_ref, got_down_ref, ahead_ref, up_ref, down_ref):
+    up_ref[...] = (acc_ref[2, 0] + got_up_ref[1].astype(F32)).astype(BF16)
+    down_ref[...] = (acc_ref[1, 1] + got_down_ref[1].astype(F32)).astype(BF16)
+
+
+def messages(kernel, held, ahead, shape, name):
+    return pl.pallas_call(
+        kernel,
+        out_shape=[jax.ShapeDtypeStruct(shape, BF16)] * 2,
+        in_specs=[whole()] * len(held) + [whole(pl.ANY)],
         out_specs=[whole()] * 2,
-        compiler_params=pltpu.CompilerParams(vmem_limit_bytes=8 * MIB),
-        name="pass_on",
-    )(next_up, got_up, next_down, got_down, *ahead)
-    return swap(up, "dp", 2), swap(down, "dp", 1)
+        compiler_params=pltpu.CompilerParams(vmem_limit_bytes=16 * MIB),
+        name=name,
+    )(*held, ahead)
 
 
 def row_loss_kernel(place_ref, loss_ref, row_loss_ref):
@@ -399,28 +411,6 @@
     )(place, loss)
 
 
-def assemble_kernel(part, me_ref, *refs):
-    *held, trunk_ref = refs
-    me = me_ref[0]
-    order = iter((0, 2, 4, 6, 1, 3, 5, 7))
-    for ref in held:
-        for k in range(ref.shape[0] // part):
-            at = pl.ds(pl.multiple_of((me ^ next(order)) * part, part), part)
-            trunk_ref[at, :] = ref[k * part : (k + 1) * part, :]
-
-
-def assemble(me, held, part):
-    width = held[0].shape[1]
-    return pl.pallas_call(
-        functools.partial(assemble_kernel, part),
-        out_shape=jax.ShapeDtypeStruct((8 * part, width), F32),
-        in_specs=[whole(pltpu.SMEM)] + [whole()] * len(held),
-        out_specs=whole(),
-        compiler_params=pltpu.CompilerParams(vmem_limit_bytes=4 * MIB),
-        name="assemble_trunk",
-    )(me, *held)
-
-
 def adam_update(params, first, second, grads):
     first_new = beta_one * first + (1.0 - beta_one) * grads
     second_new = beta_two * second + (1.0 - beta_two) * grads * grads
@@ -431,6 +421,32 @@
         first_new,
         second_new,
     )
+
+
+def adam_kernel(*refs):
+    params_ref, first_ref, second_ref, acc_ref, *got = refs[:8]
+    *outs, done_ref = refs[8:]
+    for k in range(2):
+        grads = acc_ref[0, k] + got[k][0].astype(F32) + got[2 + k][...].astype(F32)
+        news = adam_update(params_ref[0, k], first_ref[0, k], second_ref[0, k], grads)
+        for ref, new in zip(outs, news):
+            ref[0, k] = new
+    done_ref[...] = jnp.zeros(done_ref.shape, F32)
+
+
+def adam(params, first, second, acc, got):
+    shape = jax.ShapeDtypeStruct(params.shape, F32)
+    return pl.pallas_call(
+        adam_kernel,
+        out_shape=[shape] * 3 + [jax.ShapeDtypeStruct((8, LANES), F32)],
+        in_specs=[whole()] * 8,
+        out_specs=[whole()] * 4,
+        compiler_params=pltpu.CompilerParams(vmem_limit_bytes=24 * MIB),
+        cost_estimate=pl.CostEstimate(
+            flops=20 * params.size, bytes_accessed=8 * params.size, transcendentals=params.size
+        ),
+        name="adam",
+    )(params, first, second, acc, *got)
 
 
 def swap(value, axis, s):
@@ -455,6 +471,7 @@
     replicas = lax.axis_size("dp")
     capacity = 2 * rows // experts
     me = lax.axis_index("expert").astype(jnp.int32).reshape(1)
+    ids = jnp.concatenate([me, lax.axis_index("dp").astype(jnp.int32).reshape(1)])
 
     up, down = expert_params[0, 0].astype(BF16), expert_params[0, 1].astype(BF16)
     near_up, near_down = swap(up, "dp", 1), swap(down, "dp", 2)
@@ -462,7 +479,7 @@
     ups, downs = pair(up, near_up, place), pair(down, near_down, place)
     weights = [ups, swap(ups, "dp", 2), downs, swap(downs, "dp", 1)]
     if in_turns(experts):
-        batches, later = ((0, 1), (4, 5), (2, 3), (6,), (7,)), (7,)
+        batches, later = ((0, 1), (4, 5), (2,), (3,), (6,), (7,)), (7,)
     else:
         batches, later = (range(experts // 2), range(experts // 2, experts)), ()
     order = [s for batch in batches for s in batch]
@@ -472,56 +489,57 @@
         last = k == len(batches) - 1
         relays = [blocks[s] for s in later] if k == 0 else []
         outs = expert_call(
-            [arrived[s] for s in batch], trunk_weight, weights, prior, losses, me, order, last, relays
+            [arrived[s] for s in batch], trunk_weight, weights, prior, losses, ids, order, last, relays
         )
         if not last:
             prior = outs[:2]
             losses.append(outs[2])
             for s, block in zip(later, outs[3:]):
                 arrived[s] = swap(block, "expert", s)
-    own, next_up, next_down, sent_up, sent_down, kept, note = outs
-
-    got_up = swap(sent_up, "dp", 1)
-    got_down = swap(sent_down, "dp", 2)
-    part = width // experts
+    acc, *parts, losses = outs
+
+    def send(ahead):
+        up, down = messages(send_kernel, [acc], ahead, (2, *acc.shape[2:]), "send")
+        return swap(up, "dp", 1), swap(down, "dp", 2)
+
+    def pass_on(got, ahead):
+        up, down = messages(pass_on_kernel, [acc, *got], ahead, acc.shape[2:], "pass_on")
+        return swap(up, "dp", 2), swap(down, "dp", 1)
+
     if in_turns(experts):
-        ours, *notes = turn(
-            turn_one_kernel, [kept, swap(note, "expert", 1)], part, (part + 8,) * 4, "turn_one"
-        )
-        notes = [swap(note, "expert", s) for note, s in zip(notes, (2, 4, 6))]
-        total, loss = turn(turn_two_kernel, [ours] + notes, part, (part, experts), "turn_two")
-        (total,) = turn(
-            turn_three_kernel,
-            [total] + [swap(total, "dp", j) for j in range(1, replicas)],
-            part,
-            (part,),
-            "turn_three",
-            (got_up, got_down),
-        )
-        more_up, more_down = pass_on(next_up, got_up, next_down, got_down, (total,))
-        column = [total] + [swap(total, "expert", s) for s in (2, 4, 6)]
-        (column,) = turn(
-            turn_four_kernel, column, part, (4 * part,), "turn_four", (more_up, more_down)
-        )
-        trunk_grad = assemble(me, [column, swap(column, "expert", 1)], part)
+        quarter = width // replicas
+        parts = [swap(part, "dp", j) for j, part in enumerate(parts)]
+        total, note = turn(dp_turn_kernel, parts + [losses], (quarter, quarter + 8), "dp_turn")
+        got = send(total)
+        notes = turn(
+            pair_turn_kernel,
+            [total, swap(note, "expert", 1), losses],
+            (quarter // 2 + 8,) * 4,
+            "pair_turn",
+            ids,
+        )
+        notes = [swap(note, "expert", 2 * k) for k, note in enumerate(notes)]
+        total, loss = turn(z_turn_kernel, notes, (quarter // 2, experts), "z_turn")
+        more_up, more_down = pass_on(got, total)
+        (total,) = turn(join_kernel, [total, swap(total, "expert", 1)], (quarter,), "join", ids)
+        parts = [swap(total, "dp", j) for j in range(replicas)]
+        *news, done = adam(
+            expert_params, first_moment, second_moment, acc, [*got, more_up, more_down]
+        )
+        (trunk_grad,) = turn(assemble_kernel, parts + [done], (width,), "assemble_trunk", ids)
     else:
-        more_up, more_down = pass_on(next_up, got_up, next_down, got_down)
-        trunk_grad = lax.psum(kept, ("dp", "expert"))
+        got = send(losses)
+        more_up, more_down = pass_on(got, losses)
+        *news, _ = adam(
+            expert_params, first_moment, second_moment, acc, [*got, more_up, more_down]
+        )
+        trunk_grad = lax.psum(parts[0], ("dp", "expert"))
         places = jnp.arange(experts, dtype=jnp.int32) ^ me
-        note = note.reshape(experts, capacity)[places]
-        loss = lax.all_to_all(note, "expert", split_axis=0, concat_axis=0, tiled=True)[places]
+        losses = losses.reshape(experts, capacity)[places]
+        loss = lax.all_to_all(losses, "expert", split_axis=0, concat_axis=0, tiled=True)[places]
     row_loss = loss_by_row(place, loss)
 
-    grads = jnp.stack(
-        [
-            own[0] + got_up[0].astype(F32) + more_up.astype(F32),
-            own[1] + got_down[0].astype(F32) + more_down.astype(F32),
-        ]
-    )
-    new_params, new_first, new_second = adam_update(
-        expert_params, first_moment, second_moment, grads[None]
-    )
-    return (trunk_grad, row_loss.reshape(rows), new_params, new_first, new_second)
+    return (trunk_grad, row_loss.reshape(rows), *news)
 
 
 def solution(mesh):

time: 102 us -> 107 us (1.049)
  Pallas kernels: 31.5 us -> 38.7 us
  local copies, waits for them, and re-layouts: 3.7 us -> 7.84 us
  waiting for transfers between devices: 30.3 us -> 27.4 us
  other arithmetic: 3.65 us -> 1.37 us
  starting transfers between devices: 31.4 us -> 30.3 us
    unnamed x16 -> x20, local copies, waits for them, and re-layouts: 3.66 us -> 7.81 us
    pallas_call x6 -> x8, Pallas kernels: 0.89 us -> 4.71 us  [the longest x5 2.41 us: turn(): pl.pallas_call(kernel, out_shape=[jax.ShapeDtypeStruct((rows, width), F32...]
    ppermute x26, waiting for transfers between devices: 30.3 us -> 27.4 us  [swap(): lax.ppermute(value, axis, [(i, i ^ s) for i in range(lax.axis_size(axis))])]
    pallas_call x5 -> x6, Pallas kernels: 25.8 us -> 28.7 us  [expert_call(): pl.pallas_call(functools.partial(expert_kernel, counts, order, first, len...]
    sub x1 -> x0, other arithmetic: 2.15 us -> none  [adam_update(): params - learn_rate * first_hat / (jnp.sqrt(second_hat) + adam_eps)]
    ppermute x26, starting transfers between devices: 31.4 us -> 30.3 us  [swap(): lax.ppermute(value, axis, [(i, i ^ s) for i in range(lax.axis_size(axis))])]
  transfers between devices with their start and end apart: 26 -> 26, of which waited for: 12 -> 9; matrix products, arithmetic and copies ran while one was open for 2% -> 0% of each run, Pallas kernels for 27% -> 31%
where the time goes in v8:
time: 107 us; the launch traced here: 106 us
  Pallas kernels  38.7 us (36%)
  starting transfers between devices  30.3 us (28%)
  waiting for transfers between devices  27.4 us (26%)
  local copies, waits for them, and re-layouts  7.84 us (7%)
  other arithmetic  1.37 us (1%)
    ppermute x26, starting transfers between devices, swap(): lax.ppermute(value, axis, [(i, i ^ s) for i in range(lax.axis_size(axis))])  30.3 us
    pallas_call x6, Pallas kernels, expert_call(): pl.pallas_call(functools.partial(expert_kernel, counts, order, first, len...  28.7 us
    ppermute x26, waiting for transfers between devices, swap(): lax.ppermute(value, axis, [(i, i ^ s) for i in range(lax.axis_size(axis))])  27.4 us
    unnamed x20, local copies, waits for them, and re-layouts  7.81 us
    pallas_call x1, Pallas kernels, pack(): pl.pallas_call(functools.partial(pack_kernel, experts, capacity), out_sha...  4.12 us
    pallas_call x5, Pallas kernels, turn(): pl.pallas_call(kernel, out_shape=[jax.ShapeDtypeStruct((rows, width), F32...  2.41 us
  transfers between devices with their start and end apart: 26, of which 9 were waited for; matrix products, arithmetic and copies ran while one was open for 0% of the time, Pallas kernels for 31%

profile of v8, /device:TPU:0, one launch (start us, length us, event | category | flops | bytes accessed | tf_op | source)
XLA Modules:
  0.0 106.5 jit_solution(30569019894308820)
XLA Ops:
  2.0 3.0 %collective-permute-start.3 = (bf16[256,512]{1,0:T(8,128)(2,1)S(1)}, bf16[256,512]{1,0:T(8,128)(2,1)S(1)}, u32[]{:S(2)}, u32[]{:S(2)}) collective-permute-start(bf16[256,512]{1,0:T(8,128)(2,1)S(1)} %get-tuple-element.99.one_ref), channel_id=1, source_target_pairs={{0,16},{8,24},{16,0},{24,8},{1,17},{9,25},{17,1},{25,9},{2,18},{10... | collective-permute-start | bytes 786440 | tf_op jit(solution)/shard_map/ppermute | solution.py:455
  10.1 4.1 %pack_rows.1 = (bf16[256,512]{1,0:T(8,128)(2,1)S(1)}, bf16[256,512]{1,0:T(8,128)(2,1)S(1)}, bf16[256,512]{1,0:T(8,128)(2,1)}, bf16[256,512]{1,0:T(8,128)(2,1)}, ...) custom-call(s32[1]{0:T(128)} %bitcast.me_ref, ...), custom_call_target="tpu_custom_call" | custom-call | flops 3221225472 | bytes 6291456 | tf_op jit(solution)/shard_map/pack_rows/pallas_call | solution.py:84
  15.1 3.0 %collective-permute-start.9 = (bf16[256,512]{1,0:T(8,128)(2,1)S(1)}, bf16[256,512]{1,0:T(8,128)(2,1)S(1)}, u32[]{:S(2)}, u32[]{:S(2)}) collective-permute-start(bf16[256,512]{1,0:T(8,128)(2,1)S(1)} %get-tuple-element.60), channel_id=1, source_target_pairs={{0,4},{1,5},{2,6},{3,7},{4,0},{5,1},{6,2},{7,3},{8,12},{9,13},{10,... | collective-permute-start | bytes 786440 | tf_op jit(solution)/shard_map/ppermute | solution.py:455
  18.3 1.6 %collective-permute-start.8 = (bf16[256,512]{1,0:T(8,128)(2,1)}, bf16[256,512]{1,0:T(8,128)(2,1)}, u32[]{:S(2)}, u32[]{:S(2)}) collective-permute-start(bf16[256,512]{1,0:T(8,128)(2,1)} %get-tuple-element.59), channel_id=1, source_target_pairs={{0,2},{1,3},{2,0},{3,1},{4,6},{5,7},{6,4},{7,5},{8,10},{9,11},{10,... | collective-permute-start | bytes 786440 | tf_op jit(solution)/shard_map/ppermute | solution.py:455
  19.9 7.6 %collective-permute-done.2.refs_4_.refs_3_ = bf16[2,256,512]{2,1,0:T(8,128)(2,1)S(1)} collective-permute-done((bf16[2,256,512]{2,1,0:T(8,128)(2,1)S(1)}, bf16[2,256,512]{2,1,0:T(8,128)(2,1)S(1)}, u32[]{:S(2)}, u32[]{:S(2)}) %collective-permute-start.2) | collective-permute-done | bytes 524320 | tf_op jit(solution)/shard_map/ppermute | solution.py:455
  27.5 3.6 %collective-permute-start.6 = (bf16[256,512]{1,0:T(8,128)(2,1)}, bf16[256,512]{1,0:T(8,128)(2,1)S(1)}, u32[]{:S(2)}, u32[]{:S(2)}) collective-permute-start(bf16[256,512]{1,0:T(8,128)(2,1)} %get-tuple-element.57), channel_id=1, source_target_pairs={{0,6},{1,7},{2,4},{3,5},{4,2},{5,3},{6,0},{7,1},{8,14},{9,15},{10,... | collective-permute-start | bytes 786440 | tf_op jit(solution)/shard_map/ppermute | solution.py:455
  31.1 6.8 %expert_rows.6 = (f32[4,2,256,512]{3,2,1,0:T(8,128)S(1)}, f32[256,256]{1,0:T(8,128)S(1)}, f32[2,256]{1,0:T(2,128)S(1)}, bf16[256,512]{1,0:T(8,128)(2,1)}) custom-call(bf16[256,512]{1,0:T(8,128)(2,1)S(1)} %get-tuple-element.52.refs_0_, bf16[256,512]{1,0:T(8,128)(2,1)S(1)} %collective-permute-done.refs_1_, bf16[256,256]{1,0:T(8,128)(2,1)S(1)} %copy-done, ...), custom_call_target="tpu_custom_call" | custom-call | flops 1572864 | bytes 131072 | tf_op jit(solution)/shard_map/expert_rows/pallas_call | solution.py:285
  37.9 2.0 %copy-done.1 = f32[4,2,256,512]{3,2,1,0:T(8,128)} copy-done((f32[4,2,256,512]{3,2,1,0:T(8,128)}, f32[4,2,256,512]{3,2,1,0:T(8,128)S(1)}, u32[]{:S(2)}) %copy-start.1) | copy-done | bytes 4194328
  40.5 6.9 %collective-permute-done.10.refs_1_ = bf16[256,512]{1,0:T(8,128)(2,1)S(1)} collective-permute-done((bf16[256,512]{1,0:T(8,128)(2,1)}, bf16[256,512]{1,0:T(8,128)(2,1)S(1)}, u32[]{:S(2)}, u32[]{:S(2)}) %collective-permute-start.10) | collective-permute-done | bytes 262176 | tf_op jit(solution)/shard_map/ppermute | solution.py:455
  47.5 2.2 %copy-done.2 = f32[4,2,256,512]{3,2,1,0:T(8,128)S(1)} copy-done((f32[4,2,256,512]{3,2,1,0:T(8,128)S(1)}, f32[4,2,256,512]{3,2,1,0:T(8,128)}, u32[]{:S(2)}) %copy-start.2) | copy-done | bytes 4194328
  49.7 6.4 %expert_rows.7 = (f32[4,2,256,512]{3,2,1,0:T(8,128)S(1)}, f32[256,256]{1,0:T(8,128)S(1)}, f32[2,256]{1,0:T(2,128)S(1)}) custom-call(bf16[256,512]{1,0:T(8,128)(2,1)S(1)} %collective-permute-done.9.refs_0_, bf16[256,512]{1,0:T(8,128)(2,1)S(1)} %collective-permute-done.10.refs_1_, bf16[256,256]{1,0:T(8,128)(2,1)S(1)} %copy-done, ...), custom_call_target="tpu_custom_call" | custom-call | flops 1572864 | bytes 131072 | tf_op jit(solution)/shard_map/expert_rows/pallas_call | solution.py:285
  56.1 4.2 %expert_rows.8 = (f32[4,2,256,512]{3,2,1,0:T(8,128)S(1)}, f32[256,256]{1,0:T(8,128)S(1)}, f32[1,256]{1,0:T(1,128)S(1)}) custom-call(bf16[256,512]{1,0:T(8,128)(2,1)} %collective-permute-done.8.refs_0_, bf16[256,256]{1,0:T(8,128)(2,1)S(1)} %copy-done, bf16[2,256,512]{2,1,0:T(8,128)(2,1)S(1)} %pair.2.refs_3_.refs_2_, ...), custom_call_target="tpu_custom_call" | custom-call | flops 786432 | bytes 65536 | tf_op jit(solution)/shard_map/expert_rows/pallas_call | solution.py:285
  60.2 4.2 %expert_rows.9 = (f32[4,2,256,512]{3,2,1,0:T(8,128)S(1)}, f32[256,256]{1,0:T(8,128)S(1)}, f32[1,256]{1,0:T(1,128)S(1)}) custom-call(bf16[256,512]{1,0:T(8,128)(2,1)} %collective-permute-done.7.refs_0_, bf16[256,256]{1,0:T(8,128)(2,1)S(1)} %copy-done, bf16[2,256,512]{2,1,0:T(8,128)(2,1)S(1)} %pair.2.refs_3_.refs_2_, ...), custom_call_target="tpu_custom_call" | custom-call | flops 786432 | bytes 65536 | tf_op jit(solution)/shard_map/expert_rows/pallas_call | solution.py:285
  64.4 3.1 %expert_rows.10 = (f32[4,2,256,512]{3,2,1,0:T(8,128)S(1)}, f32[256,256]{1,0:T(8,128)S(1)}, f32[1,256]{1,0:T(1,128)S(1)}) custom-call(bf16[256,512]{1,0:T(8,128)(2,1)S(1)} %collective-permute-done.6.refs_0_, bf16[256,256]{1,0:T(8,128)(2,1)S(1)} %copy-done, bf16[2,256,512]{2,1,0:T(8,128)(2,1)S(1)} %pair.2.refs_3_.refs_2_, ...), custom_call_target="tpu_custom_call" | custom-call | flops 786432 | bytes 65536 | tf_op jit(solution)/shard_map/expert_rows/pallas_call | solution.py:285
  67.6 4.0 %expert_rows.11 = (f32[4,2,256,512]{3,2,1,0:T(8,128)S(1)}, f32[64,256]{1,0:T(8,128)S(1)}, f32[64,256]{1,0:T(8,128)S(1)}, f32[64,256]{1,0:T(8,128)S(1)}, f32[64,256]{1,0:T(8,128)S(1)}, /*index=5*/f32[8,256]{1,0:T(8,128)S(1)}) custom-call(bf16[256,512]{1,0:T(8,128)(2,1)S(1)} %collective-permute-done.5.refs_0_, bf16[256,256]{1,0:T(8,128)(2,1)S(1)} %copy-done, ...), custom_call_target="tpu_custom_call" | custom-call | flops 786432 | bytes 65536 | tf_op jit(solution)/shard_map/expert_rows/pallas_call | solution.py:285
  73.0 1.5 %collective-permute-start.12 = (f32[64,256]{1,0:T(8,128)S(1)}, f32[64,256]{1,0:T(8,128)S(1)}, u32[]{:S(2)}, u32[]{:S(2)}) collective-permute-start(f32[64,256]{1,0:T(8,128)S(1)} %get-tuple-element.79), channel_id=1, source_target_pairs={{0,16},{8,24},{16,0},{24,8},{1,17},{9,25},{17,1},{25,9},{2,18},{10... | collective-permute-start | bytes 196616 | tf_op jit(solution)/shard_map/ppermute | solution.py:455
  77.3 2.4 %collective-permute-done.13.q3 = f32[64,256]{1,0:T(8,128)S(1)} collective-permute-done((f32[64,256]{1,0:T(8,128)S(1)}, f32[64,256]{1,0:T(8,128)S(1)}, u32[]{:S(2)}, u32[]{:S(2)}) %collective-permute-start.13) | collective-permute-done | bytes 65568 | tf_op jit(solution)/shard_map/ppermute | solution.py:455
  84.2 3.4 %collective-permute-start.16 = (f32[40,256]{1,0:T(8,128)S(1)}, f32[40,256]{1,0:T(8,128)S(1)}, u32[]{:S(2)}, u32[]{:S(2)}) collective-permute-start(f32[40,256]{1,0:T(8,128)S(1)} %get-tuple-element.86), channel_id=1, source_target_pairs={{0,4},{1,5},{2,6},{3,7},{4,0},{5,1},{6,2},{7,3},{8,12},{9,13},{10,... | collective-permute-start | bytes 122888 | tf_op jit(solution)/shard_map/ppermute | solution.py:455
  87.6 2.8 %collective-permute-done.16.refs_2_ = f32[40,256]{1,0:T(8,128)S(1)} collective-permute-done((f32[40,256]{1,0:T(8,128)S(1)}, f32[40,256]{1,0:T(8,128)S(1)}, u32[]{:S(2)}, u32[]{:S(2)}) %collective-permute-start.16) | collective-permute-done | bytes 40992 | tf_op jit(solution)/shard_map/ppermute | solution.py:455
  90.4 3.0 %collective-permute-done.17.refs_3_ = f32[40,256]{1,0:T(8,128)S(1)} collective-permute-done((f32[40,256]{1,0:T(8,128)S(1)}, f32[40,256]{1,0:T(8,128)S(1)}, u32[]{:S(2)}, u32[]{:S(2)}) %collective-permute-start.17) | collective-permute-done | bytes 40992 | tf_op jit(solution)/shard_map/ppermute | solution.py:455
  93.5 1.6 %collective-permute-start.24 = (bf16[256,512]{1,0:T(8,128)(2,1)S(1)}, bf16[256,512]{1,0:T(8,128)(2,1)S(1)}, u32[]{:S(2)}, u32[]{:S(2)}) collective-permute-start(bf16[256,512]{1,0:T(8,128)(2,1)S(1)} %get-tuple-element.92), channel_id=1, source_target_pairs={{0,16},{8,24},{16,0},{24,8},{1,17},{9,25},{17,1},{25,9},{2,18},{10... | collective-permute-start | bytes 786440 | tf_op jit(solution)/shard_map/ppermute | solution.py:455
  98.9 1.5 %collective-permute-start.20 = (f32[64,256]{1,0:T(8,128)S(1)}, f32[64,256]{1,0:T(8,128)S(1)}, u32[]{:S(2)}, u32[]{:S(2)}) collective-permute-start(f32[64,256]{1,0:T(8,128)S(1)} %join.1.refs_0_), channel_id=1, source_target_pairs={{0,16},{8,24},{16,0},{24,8},{1,17},{9,25},{17,1},{25,9},{2,18},{10... | collective-permute-start | bytes 196616 | tf_op jit(solution)/shard_map/ppermute | solution.py:455
  100.4 1.5 %collective-permute-start.19 = (f32[64,256]{1,0:T(8,128)S(1)}, f32[64,256]{1,0:T(8,128)S(1)}, u32[]{:S(2)}, u32[]{:S(2)}) collective-permute-start(f32[64,256]{1,0:T(8,128)S(1)} %join.1.refs_0_), channel_id=1, source_target_pairs={{0,8},{8,0},{16,24},{24,16},{1,9},{9,1},{17,25},{25,17},{2,10},{10... | collective-permute-start | bytes 196616 | tf_op jit(solution)/shard_map/ppermute | solution.py:455
  103.1 2.1 %adam.1 = (f32[1,2,256,512]{3,2,1,0:T(8,128)}, f32[1,2,256,512]{3,2,1,0:T(8,128)}, f32[1,2,256,512]{3,2,1,0:T(8,128)}, f32[8,128]{1,0:T(8,128)S(1)}) custom-call(f32[1,2,256,512]{3,2,1,0:T(8,128)S(1)} %copy-done.3, f32[1,2,256,512]{3,2,1,0:T(8,128)S(1)} %copy-done.4, f32[1,2,256,512]{3,2,1,0:T(8,128)S(1)} %copy-done.5, ...), custom_call_target="tpu_custom_call" | custom-call | flops 5242880 | bytes 2097152 | tf_op jit(solution)/shard_map/adam/pallas_call | solution.py:439
  (69 shorter events, 23.1 us)
Async XLA Ops:
  2.0 12.9 %collective-permute-start.3 = (bf16[256,512]{1,0:T(8,128)(2,1)S(1)}, bf16[256,512]{1,0:T(8,128)(2,1)S(1)}, u32[]{:S(2)}, u32[]{:S(2)}) collective-permute-start(bf16[256,512]{1,0:T(8,128)(2,1)S(1)} %get-tuple-element.99.one_ref), channel_id=1, source_target_pairs={{0,16},{8,24},{16,0},{24,8},{1,17},{9,25},{17,1},{25,9},{2,18},{10... | collective-permute-start | bytes 786440 | tf_op jit(solution)/shard_map/ppermute | solution.py:455
  5.0 9.3 %collective-permute-start.1 = (bf16[256,512]{1,0:T(8,128)(2,1)S(1)}, bf16[256,512]{1,0:T(8,128)(2,1)S(1)}, u32[]{:S(2)}, u32[]{:S(2)}) collective-permute-start(bf16[256,512]{1,0:T(8,128)(2,1)S(1)} %get-tuple-element.100.one_ref), channel_id=1, source_target_pairs={{0,8},{8,0},{16,24},{24,16},{1,9},{9,1},{17,25},{25,17},{2,10},{10... | collective-permute-start | bytes 786440 | tf_op jit(solution)/shard_map/ppermute | solution.py:455
  14.3 13.2 %collective-permute-start.2 = (bf16[2,256,512]{2,1,0:T(8,128)(2,1)S(1)}, bf16[2,256,512]{2,1,0:T(8,128)(2,1)S(1)}, u32[]{:S(2)}, u32[]{:S(2)}) collective-permute-start(bf16[2,256,512]{2,1,0:T(8,128)(2,1)S(1)} %pair.2.refs_3_.refs_2_), channel_id=1, source_target_pairs={{0,16},{8,24},{16,0},{24,8},{1,17},{9,25},{17,1},{25,9},{2,18},{10... | collective-permute-start | bytes 1572872 | tf_op jit(solution)/shard_map/ppermute | solution.py:455
  14.9 16.2 %collective-permute-start.4 = (bf16[2,256,512]{2,1,0:T(8,128)(2,1)S(1)}, bf16[2,256,512]{2,1,0:T(8,128)(2,1)S(1)}, u32[]{:S(2)}, u32[]{:S(2)}) collective-permute-start(bf16[2,256,512]{2,1,0:T(8,128)(2,1)S(1)} %pair.3.refs_5_.refs_4_), channel_id=1, source_target_pairs={{0,8},{8,0},{16,24},{24,16},{1,9},{9,1},{17,25},{25,17},{2,10},{10... | collective-permute-start | bytes 1572872 | tf_op jit(solution)/shard_map/ppermute | solution.py:455
  15.1 3.2 %collective-permute-start = (bf16[256,512]{1,0:T(8,128)(2,1)S(1)}, bf16[256,512]{1,0:T(8,128)(2,1)S(1)}, u32[]{:S(2)}, u32[]{:S(2)}) collective-permute-start(bf16[256,512]{1,0:T(8,128)(2,1)S(1)} %get-tuple-element.53), channel_id=1, source_target_pairs={{0,1},{1,0},{2,3},{3,2},{4,5},{5,4},{6,7},{7,6},{8,9},{9,8},{10,11... | collective-permute-start | bytes 786440 | tf_op jit(solution)/shard_map/ppermute | solution.py:455
  15.1 24.8 %collective-permute-start.9 = (bf16[256,512]{1,0:T(8,128)(2,1)S(1)}, bf16[256,512]{1,0:T(8,128)(2,1)S(1)}, u32[]{:S(2)}, u32[]{:S(2)}) collective-permute-start(bf16[256,512]{1,0:T(8,128)(2,1)S(1)} %get-tuple-element.60), channel_id=1, source_target_pairs={{0,4},{1,5},{2,6},{3,7},{4,0},{5,1},{6,2},{7,3},{8,12},{9,13},{10,... | collective-permute-start | bytes 786440 | tf_op jit(solution)/shard_map/ppermute | solution.py:455
  18.1 29.4 %collective-permute-start.10 = (bf16[256,512]{1,0:T(8,128)(2,1)}, bf16[256,512]{1,0:T(8,128)(2,1)S(1)}, u32[]{:S(2)}, u32[]{:S(2)}) collective-permute-start(bf16[256,512]{1,0:T(8,128)(2,1)} %get-tuple-element.61), channel_id=1, source_target_pairs={{0,5},{1,4},{2,7},{3,6},{4,1},{5,0},{6,3},{7,2},{8,13},{9,12},{10,... | collective-permute-start | bytes 786440 | tf_op jit(solution)/shard_map/ppermute | solution.py:455
  18.3 37.8 %collective-permute-start.8 = (bf16[256,512]{1,0:T(8,128)(2,1)}, bf16[256,512]{1,0:T(8,128)(2,1)}, u32[]{:S(2)}, u32[]{:S(2)}) collective-permute-start(bf16[256,512]{1,0:T(8,128)(2,1)} %get-tuple-element.59), channel_id=1, source_target_pairs={{0,2},{1,3},{2,0},{3,1},{4,6},{5,7},{6,4},{7,5},{8,10},{9,11},{10,... | collective-permute-start | bytes 786440 | tf_op jit(solution)/shard_map/ppermute | solution.py:455
  27.5 37.0 %collective-permute-start.6 = (bf16[256,512]{1,0:T(8,128)(2,1)}, bf16[256,512]{1,0:T(8,128)(2,1)S(1)}, u32[]{:S(2)}, u32[]{:S(2)}) collective-permute-start(bf16[256,512]{1,0:T(8,128)(2,1)} %get-tuple-element.57), channel_id=1, source_target_pairs={{0,6},{1,7},{2,4},{3,5},{4,2},{5,3},{6,0},{7,1},{8,14},{9,15},{10,... | collective-permute-start | bytes 786440 | tf_op jit(solution)/shard_map/ppermute | solution.py:455
  31.1 29.2 %collective-permute-start.7 = (bf16[256,512]{1,0:T(8,128)(2,1)}, bf16[256,512]{1,0:T(8,128)(2,1)}, u32[]{:S(2)}, u32[]{:S(2)}) collective-permute-start(bf16[256,512]{1,0:T(8,128)(2,1)} %get-tuple-element.58), channel_id=1, source_target_pairs={{0,3},{1,2},{2,1},{3,0},{4,7},{5,6},{6,5},{7,4},{8,11},{9,10},{10,... | collective-permute-start | bytes 786440 | tf_op jit(solution)/shard_map/ppermute | solution.py:455
  39.9 27.7 %collective-permute-start.5 = (bf16[256,512]{1,0:T(8,128)(2,1)}, bf16[256,512]{1,0:T(8,128)(2,1)S(1)}, u32[]{:S(2)}, u32[]{:S(2)}) collective-permute-start(bf16[256,512]{1,0:T(8,128)(2,1)} %get-tuple-element.56), channel_id=1, source_target_pairs={{0,7},{1,6},{2,5},{3,4},{4,3},{5,2},{6,1},{7,0},{8,15},{9,14},{10,... | collective-permute-start | bytes 786440 | tf_op jit(solution)/shard_map/ppermute | solution.py:455
  71.6 4.3 %collective-permute-start.11 = (f32[64,256]{1,0:T(8,128)S(1)}, f32[64,256]{1,0:T(8,128)S(1)}, u32[]{:S(2)}, u32[]{:S(2)}) collective-permute-start(f32[64,256]{1,0:T(8,128)S(1)} %get-tuple-element.78), channel_id=1, source_target_pairs={{0,8},{8,0},{16,24},{24,16},{1,9},{9,1},{17,25},{25,17},{2,10},{10... | collective-permute-start | bytes 196616 | tf_op jit(solution)/shard_map/ppermute | solution.py:455
  73.0 4.3 %collective-permute-start.12 = (f32[64,256]{1,0:T(8,128)S(1)}, f32[64,256]{1,0:T(8,128)S(1)}, u32[]{:S(2)}, u32[]{:S(2)}) collective-permute-start(f32[64,256]{1,0:T(8,128)S(1)} %get-tuple-element.79), channel_id=1, source_target_pairs={{0,16},{8,24},{16,0},{24,8},{1,17},{9,25},{17,1},{25,9},{2,18},{10... | collective-permute-start | bytes 196616 | tf_op jit(solution)/shard_map/ppermute | solution.py:455
  74.5 5.2 %collective-permute-start.13 = (f32[64,256]{1,0:T(8,128)S(1)}, f32[64,256]{1,0:T(8,128)S(1)}, u32[]{:S(2)}, u32[]{:S(2)}) collective-permute-start(f32[64,256]{1,0:T(8,128)S(1)} %get-tuple-element.80), channel_id=1, source_target_pairs={{0,24},{8,16},{16,8},{24,0},{1,25},{9,17},{17,9},{25,1},{2,26},{10... | collective-permute-start | bytes 196616 | tf_op jit(solution)/shard_map/ppermute | solution.py:455
  79.9 13.5 %collective-permute-start.22 = (bf16[2,256,512]{2,1,0:T(8,128)(2,1)S(1)}, bf16[2,256,512]{2,1,0:T(8,128)(2,1)S(1)}, u32[]{:S(2)}, u32[]{:S(2)}) collective-permute-start(bf16[2,256,512]{2,1,0:T(8,128)(2,1)S(1)} %get-tuple-element.90), channel_id=1, source_target_pairs={{0,8},{8,0},{16,24},{24,16},{1,9},{9,1},{17,25},{25,17},{2,10},{10... | collective-permute-start | bytes 1572872 | tf_op jit(solution)/shard_map/ppermute | solution.py:455
  80.4 12.9 %collective-permute-start.23 = (bf16[2,256,512]{2,1,0:T(8,128)(2,1)S(1)}, bf16[2,256,512]{2,1,0:T(8,128)(2,1)S(1)}, u32[]{:S(2)}, u32[]{:S(2)}) collective-permute-start(bf16[2,256,512]{2,1,0:T(8,128)(2,1)S(1)} %get-tuple-element.91), channel_id=1, source_target_pairs={{0,16},{8,24},{16,0},{24,8},{1,17},{9,25},{17,1},{25,9},{2,18},{10... | collective-permute-start | bytes 1572872 | tf_op jit(solution)/shard_map/ppermute | solution.py:455
  82.9 4.6 %collective-permute-start.15 = (f32[40,256]{1,0:T(8,128)S(1)}, f32[40,256]{1,0:T(8,128)S(1)}, u32[]{:S(2)}, u32[]{:S(2)}) collective-permute-start(f32[40,256]{1,0:T(8,128)S(1)} %get-tuple-element.85), channel_id=1, source_target_pairs={{0,2},{1,3},{2,0},{3,1},{4,6},{5,7},{6,4},{7,5},{8,10},{9,11},{10,... | collective-permute-start | bytes 122888 | tf_op jit(solution)/shard_map/ppermute | solution.py:455
  84.2 6.2 %collective-permute-start.16 = (f32[40,256]{1,0:T(8,128)S(1)}, f32[40,256]{1,0:T(8,128)S(1)}, u32[]{:S(2)}, u32[]{:S(2)}) collective-permute-start(f32[40,256]{1,0:T(8,128)S(1)} %get-tuple-element.86), channel_id=1, source_target_pairs={{0,4},{1,5},{2,6},{3,7},{4,0},{5,1},{6,2},{7,3},{8,12},{9,13},{10,... | collective-permute-start | bytes 122888 | tf_op jit(solution)/shard_map/ppermute | solution.py:455
  87.5 5.8 %collective-permute-start.17 = (f32[40,256]{1,0:T(8,128)S(1)}, f32[40,256]{1,0:T(8,128)S(1)}, u32[]{:S(2)}, u32[]{:S(2)}) collective-permute-start(f32[40,256]{1,0:T(8,128)S(1)} %get-tuple-element.87), channel_id=1, source_target_pairs={{0,6},{1,7},{2,4},{3,5},{4,2},{5,3},{6,0},{7,1},{8,14},{9,15},{10,... | collective-permute-start | bytes 122888 | tf_op jit(solution)/shard_map/ppermute | solution.py:455
  93.5 9.6 %collective-permute-start.24 = (bf16[256,512]{1,0:T(8,128)(2,1)S(1)}, bf16[256,512]{1,0:T(8,128)(2,1)S(1)}, u32[]{:S(2)}, u32[]{:S(2)}) collective-permute-start(bf16[256,512]{1,0:T(8,128)(2,1)S(1)} %get-tuple-element.92), channel_id=1, source_target_pairs={{0,16},{8,24},{16,0},{24,8},{1,17},{9,25},{17,1},{25,9},{2,18},{10... | collective-permute-start | bytes 786440 | tf_op jit(solution)/shard_map/ppermute | solution.py:455
  95.1 8.0 %collective-permute-start.25 = (bf16[256,512]{1,0:T(8,128)(2,1)S(1)}, bf16[256,512]{1,0:T(8,128)(2,1)S(1)}, u32[]{:S(2)}, u32[]{:S(2)}) collective-permute-start(bf16[256,512]{1,0:T(8,128)(2,1)S(1)} %get-tuple-element.93), channel_id=1, source_target_pairs={{0,8},{8,0},{16,24},{24,16},{1,9},{9,1},{17,25},{25,17},{2,10},{10... | collective-permute-start | bytes 786440 | tf_op jit(solution)/shard_map/ppermute | solution.py:455
  98.3 6.9 %collective-permute-start.21 = (f32[64,256]{1,0:T(8,128)S(1)}, f32[64,256]{1,0:T(8,128)S(1)}, u32[]{:S(2)}, u32[]{:S(2)}) collective-permute-start(f32[64,256]{1,0:T(8,128)S(1)} %join.1.refs_0_), channel_id=1, source_target_pairs={{0,24},{8,16},{16,8},{24,0},{1,25},{9,17},{17,9},{25,1},{2,26},{10... | collective-permute-start | bytes 196616 | tf_op jit(solution)/shard_map/ppermute | solution.py:455
  98.9 6.3 %collective-permute-start.20 = (f32[64,256]{1,0:T(8,128)S(1)}, f32[64,256]{1,0:T(8,128)S(1)}, u32[]{:S(2)}, u32[]{:S(2)}) collective-permute-start(f32[64,256]{1,0:T(8,128)S(1)} %join.1.refs_0_), channel_id=1, source_target_pairs={{0,16},{8,24},{16,0},{24,8},{1,17},{9,25},{17,1},{25,9},{2,18},{10... | collective-permute-start | bytes 196616 | tf_op jit(solution)/shard_map/ppermute | solution.py:455
  100.4 4.8 %collective-permute-start.19 = (f32[64,256]{1,0:T(8,128)S(1)}, f32[64,256]{1,0:T(8,128)S(1)}, u32[]{:S(2)}, u32[]{:S(2)}) collective-permute-start(f32[64,256]{1,0:T(8,128)S(1)} %join.1.refs_0_), channel_id=1, source_target_pairs={{0,8},{8,0},{16,24},{24,16},{1,9},{9,1},{17,25},{25,17},{2,10},{10... | collective-permute-start | bytes 196616 | tf_op jit(solution)/shard_map/ppermute | solution.py:455
  (12 other events, 101.3 us)

commit v9 on v8

--- a/solution.py
+++ b/solution.py
@@ -88,7 +88,7 @@
         in_specs=[whole(pltpu.SMEM)] + [whole()] * 4,
         out_specs=[whole()] * (experts + 1),
         scratch_shapes=[pltpu.VMEM((rows, 2 * width), BF16)],
-        compiler_params=pltpu.CompilerParams(vmem_limit_bytes=32 * MIB),
+        compiler_params=pltpu.CompilerParams(vmem_limit_bytes=20 * MIB),
         cost_estimate=pl.CostEstimate(
             flops=2 * rows * width * (table.shape[0] + 2 * experts * capacity),
             bytes_accessed=6 * MIB,
@@ -288,7 +288,7 @@
         in_specs=in_specs,
         out_specs=[whole()] * len(outs),
         scratch_shapes=scratch,
-        compiler_params=pltpu.CompilerParams(vmem_limit_bytes=40 * MIB),
+        compiler_params=pltpu.CompilerParams(vmem_limit_bytes=24 * MIB),
         cost_estimate=pl.CostEstimate(
             flops=12 * rows * width,
             bytes_accessed=rows * width,
@@ -312,30 +312,22 @@
     note_ref[rows + 4 :, :] = jnp.zeros((4, total.shape[1]), F32)
 
 
-def pair_turn_kernel(ids_ref, total_ref, got_ref, loss_ref, *outs):
+def pair_turn_kernel(total_ref, got_ref, loss_ref, *outs):
     rows, width = total_ref.shape
-    half = rows // 2
-    at = pl.ds(pl.multiple_of((ids_ref[0] & 1) * half, half), half)
+    total = total_ref[...] + got_ref[:rows, :]
     for k, ref in enumerate(outs):
-        ref[:half, :] = total_ref[at, :] + got_ref[at, :]
-        ref[half : half + 1, :] = loss_ref[2 * k : 2 * k + 1, :]
-        ref[half + 1 : half + 2, :] = got_ref[rows + k : rows + k + 1, :]
-        ref[half + 2 :, :] = jnp.zeros((6, width), F32)
+        ref[:rows, :] = total
+        ref[rows : rows + 1, :] = loss_ref[2 * k : 2 * k + 1, :]
+        ref[rows + 1 : rows + 2, :] = got_ref[rows + k : rows + k + 1, :]
+        ref[rows + 2 :, :] = jnp.zeros((6, width), F32)
 
 
 def z_turn_kernel(*refs):
     *notes, total_ref, loss_ref = refs
-    half = total_ref.shape[0]
-    total_ref[...] = four([note.at[:half, :] for note in notes])
+    rows = total_ref.shape[0]
+    total_ref[...] = four([note.at[:rows, :] for note in notes])
     for k, note in enumerate(notes):
-        loss_ref[2 * k : 2 * k + 2, :] = note[half : half + 2, :]
-
-
-def join_kernel(ids_ref, own_ref, other_ref, both_ref):
-    half = own_ref.shape[0]
-    core = ids_ref[0] & 1
-    both_ref[pl.ds(pl.multiple_of(core * half, half), half), :] = own_ref[...]
-    both_ref[pl.ds(pl.multiple_of((1 - core) * half, half), half), :] = other_ref[...]
+        loss_ref[2 * k : 2 * k + 2, :] = note[rows : rows + 2, :]
 
 
 def assemble_kernel(ids_ref, *refs):
@@ -479,7 +471,7 @@
     ups, downs = pair(up, near_up, place), pair(down, near_down, place)
     weights = [ups, swap(ups, "dp", 2), downs, swap(downs, "dp", 1)]
     if in_turns(experts):
-        batches, later = ((0, 1), (4, 5), (2,), (3,), (6,), (7,)), (7,)
+        batches, later = ((0, 1), (4, 5), (2,), (3,), (6,), (7,)), (6, 7)
     else:
         batches, later = (range(experts // 2), range(experts // 2, experts)), ()
     order = [s for batch in batches for s in batch]
@@ -514,14 +506,12 @@
         notes = turn(
             pair_turn_kernel,
             [total, swap(note, "expert", 1), losses],
-            (quarter // 2 + 8,) * 4,
+            (quarter + 8,) * 4,
             "pair_turn",
-            ids,
         )
         notes = [swap(note, "expert", 2 * k) for k, note in enumerate(notes)]
-        total, loss = turn(z_turn_kernel, notes, (quarter // 2, experts), "z_turn")
+        total, loss = turn(z_turn_kernel, notes, (quarter, experts), "z_turn")
         more_up, more_down = pass_on(got, total)
-        (total,) = turn(join_kernel, [total, swap(total, "expert", 1)], (quarter,), "join", ids)
         parts = [swap(total, "dp", j) for j in range(replicas)]
         *news, done = adam(
             expert_params, first_moment, second_moment, acc, [*got, more_up, more_down]

time: 107 us -> 106 us (level)
  starting transfers between devices: 30.3 us -> 31.4 us
    ppermute x26 -> x25, starting transfers between devices: 30.3 us -> 31.4 us  [swap(): lax.ppermute(value, axis, [(i, i ^ s) for i in range(lax.axis_size(axis))])]
    pallas_call x5 -> x4, Pallas kernels: 2.41 us -> 1.33 us  [turn(): pl.pallas_call(kernel, out_shape=[jax.ShapeDtypeStruct((rows, width), F32...]
    ppermute x26 -> x25, waiting for transfers between devices: 27.4 us -> 26.7 us  [swap(): lax.ppermute(value, axis, [(i, i ^ s) for i in range(lax.axis_size(axis))])]
  transfers between devices with their start and end apart: 26 -> 25, of which waited for: 9 -> 11; matrix products, arithmetic and copies ran while one was open for 0% -> 0% of each run, Pallas kernels for 31% -> 30%
where the time goes in v9:
time: 106 us
  Pallas kernels  37.7 us (36%)
  starting transfers between devices  31.4 us (30%)
  waiting for transfers between devices  26.7 us (25%)
  local copies, waits for them, and re-layouts  7.85 us (7%)
  other arithmetic  1.37 us (1%)
    ppermute x25, starting transfers between devices, swap(): lax.ppermute(value, axis, [(i, i ^ s) for i in range(lax.axis_size(axis))])  31.4 us
    pallas_call x6, Pallas kernels, expert_call(): pl.pallas_call(functools.partial(expert_kernel, counts, order, first, len...  28.7 us
    ppermute x25, waiting for transfers between devices, swap(): lax.ppermute(value, axis, [(i, i ^ s) for i in range(lax.axis_size(axis))])  26.7 us
    unnamed x20, local copies, waits for them, and re-layouts  7.81 us
    pallas_call x1, Pallas kernels, pack(): pl.pallas_call(functools.partial(pack_kernel, experts, capacity), out_sha...  4.09 us
  transfers between devices with their start and end apart: 25, of which 11 were waited for; matrix products, arithmetic and copies ran while one was open for 0% of the time, Pallas kernels for 30%

profile of v9, /device:TPU:0, one launch (start us, length us, event | category | flops | bytes accessed | tf_op | source)
XLA Modules:
  0.0 105.8 jit_solution(7524414687844224313)
XLA Ops:
  2.0 3.0 %collective-permute-start.3 = (bf16[256,512]{1,0:T(8,128)(2,1)S(1)}, bf16[256,512]{1,0:T(8,128)(2,1)S(1)}, u32[]{:S(2)}, u32[]{:S(2)}) collective-permute-start(bf16[256,512]{1,0:T(8,128)(2,1)S(1)} %get-tuple-element.101.one_ref), channel_id=1, source_target_pairs={{0,16},{8,24},{16,0},{24,8},{1,17},{9,25},{17,1},{25,9},{2,18},{10... | collective-permute-start | bytes 786440 | tf_op jit(solution)/shard_map/ppermute | solution.py:447
  5.0 1.5 %collective-permute-start.1 = (bf16[256,512]{1,0:T(8,128)(2,1)S(1)}, bf16[256,512]{1,0:T(8,128)(2,1)S(1)}, u32[]{:S(2)}, u32[]{:S(2)}) collective-permute-start(bf16[256,512]{1,0:T(8,128)(2,1)S(1)} %get-tuple-element.102.one_ref), channel_id=1, source_target_pairs={{0,8},{8,0},{16,24},{24,16},{1,9},{9,1},{17,25},{25,17},{2,10},{10... | collective-permute-start | bytes 786440 | tf_op jit(solution)/shard_map/ppermute | solution.py:447
  10.1 4.1 %pack_rows.1 = (bf16[256,512]{1,0:T(8,128)(2,1)S(1)}, bf16[256,512]{1,0:T(8,128)(2,1)S(1)}, bf16[256,512]{1,0:T(8,128)(2,1)}, bf16[256,512]{1,0:T(8,128)(2,1)}, ...) custom-call(s32[1]{0:T(128)} %bitcast.me_ref, ...), custom_call_target="tpu_custom_call" | custom-call | flops 3221225472 | bytes 6291456 | tf_op jit(solution)/shard_map/pack_rows/pallas_call | solution.py:84
  15.1 3.0 %collective-permute-start.9 = (bf16[256,512]{1,0:T(8,128)(2,1)S(1)}, bf16[256,512]{1,0:T(8,128)(2,1)S(1)}, u32[]{:S(2)}, u32[]{:S(2)}) collective-permute-start(bf16[256,512]{1,0:T(8,128)(2,1)S(1)} %get-tuple-element.62), channel_id=1, source_target_pairs={{0,4},{1,5},{2,6},{3,7},{4,0},{5,1},{6,2},{7,3},{8,12},{9,13},{10,... | collective-permute-start | bytes 786440 | tf_op jit(solution)/shard_map/ppermute | solution.py:447
  19.7 7.7 %collective-permute-done.2.refs_4_.refs_3_ = bf16[2,256,512]{2,1,0:T(8,128)(2,1)S(1)} collective-permute-done((bf16[2,256,512]{2,1,0:T(8,128)(2,1)S(1)}, bf16[2,256,512]{2,1,0:T(8,128)(2,1)S(1)}, u32[]{:S(2)}, u32[]{:S(2)}) %collective-permute-start.2) | collective-permute-done | bytes 524320 | tf_op jit(solution)/shard_map/ppermute | solution.py:447
  27.4 1.6 %collective-permute-start.8 = (bf16[256,512]{1,0:T(8,128)(2,1)}, bf16[256,512]{1,0:T(8,128)(2,1)}, u32[]{:S(2)}, u32[]{:S(2)}) collective-permute-start(bf16[256,512]{1,0:T(8,128)(2,1)} %get-tuple-element.61), channel_id=1, source_target_pairs={{0,2},{1,3},{2,0},{3,1},{4,6},{5,7},{6,4},{7,5},{8,10},{9,11},{10,... | collective-permute-start | bytes 786440 | tf_op jit(solution)/shard_map/ppermute | solution.py:447
  29.0 6.9 %expert_rows.6 = (f32[4,2,256,512]{3,2,1,0:T(8,128)S(1)}, f32[256,256]{1,0:T(8,128)S(1)}, f32[2,256]{1,0:T(2,128)S(1)}, bf16[256,512]{1,0:T(8,128)(2,1)}, bf16[256,512]{1,0:T(8,128)(2,1)}) custom-call(bf16[256,512]{1,0:T(8,128)(2,1)S(1)} %get-tuple-element.53.refs_0_, bf16[256,512]{1,0:T(8,128)(2,1)S(1)} %collective-permute-done.refs_1_, ...), custom_call_target="tpu_custom_call" | custom-call | flops 1572864 | bytes 131072 | tf_op jit(solution)/shard_map/expert_rows/pallas_call | solution.py:285
  35.9 2.0 %copy-done.1 = f32[4,2,256,512]{3,2,1,0:T(8,128)} copy-done((f32[4,2,256,512]{3,2,1,0:T(8,128)}, f32[4,2,256,512]{3,2,1,0:T(8,128)S(1)}, u32[]{:S(2)}) %copy-start.1) | copy-done | bytes 4194328
  37.9 2.5 %collective-permute-start.6 = (bf16[256,512]{1,0:T(8,128)(2,1)}, bf16[256,512]{1,0:T(8,128)(2,1)}, u32[]{:S(2)}, u32[]{:S(2)}) collective-permute-start(bf16[256,512]{1,0:T(8,128)(2,1)} %get-tuple-element.59), channel_id=1, source_target_pairs={{0,6},{1,7},{2,4},{3,5},{4,2},{5,3},{6,0},{7,1},{8,14},{9,15},{10,... | collective-permute-start | bytes 786440 | tf_op jit(solution)/shard_map/ppermute | solution.py:447
  41.8 2.2 %copy-done.2 = f32[4,2,256,512]{3,2,1,0:T(8,128)S(1)} copy-done((f32[4,2,256,512]{3,2,1,0:T(8,128)S(1)}, f32[4,2,256,512]{3,2,1,0:T(8,128)}, u32[]{:S(2)}) %copy-start.2) | copy-done | bytes 4194328
  44.0 6.4 %expert_rows.7 = (f32[4,2,256,512]{3,2,1,0:T(8,128)S(1)}, f32[256,256]{1,0:T(8,128)S(1)}, f32[2,256]{1,0:T(2,128)S(1)}) custom-call(bf16[256,512]{1,0:T(8,128)(2,1)S(1)} %collective-permute-done.9.refs_0_, bf16[256,512]{1,0:T(8,128)(2,1)S(1)} %collective-permute-done.10.refs_1_, bf16[256,256]{1,0:T(8,128)(2,1)S(1)} %copy-done, ...), custom_call_target="tpu_custom_call" | custom-call | flops 1572864 | bytes 131072 | tf_op jit(solution)/shard_map/expert_rows/pallas_call | solution.py:285
  50.4 5.2 %collective-permute-done.8.refs_0_ = bf16[256,512]{1,0:T(8,128)(2,1)} collective-permute-done((bf16[256,512]{1,0:T(8,128)(2,1)}, bf16[256,512]{1,0:T(8,128)(2,1)}, u32[]{:S(2)}, u32[]{:S(2)}) %collective-permute-start.8) | collective-permute-done | bytes 262176 | tf_op jit(solution)/shard_map/ppermute | solution.py:447
  55.6 4.2 %expert_rows.8 = (f32[4,2,256,512]{3,2,1,0:T(8,128)S(1)}, f32[256,256]{1,0:T(8,128)S(1)}, f32[1,256]{1,0:T(1,128)S(1)}) custom-call(bf16[256,512]{1,0:T(8,128)(2,1)} %collective-permute-done.8.refs_0_, bf16[256,256]{1,0:T(8,128)(2,1)S(1)} %copy-done, bf16[2,256,512]{2,1,0:T(8,128)(2,1)S(1)} %pair.2.refs_3_.refs_2_, ...), custom_call_target="tpu_custom_call" | custom-call | flops 786432 | bytes 65536 | tf_op jit(solution)/shard_map/expert_rows/pallas_call | solution.py:285
  59.8 3.1 %expert_rows.9 = (f32[4,2,256,512]{3,2,1,0:T(8,128)S(1)}, f32[256,256]{1,0:T(8,128)S(1)}, f32[1,256]{1,0:T(1,128)S(1)}) custom-call(bf16[256,512]{1,0:T(8,128)(2,1)S(1)} %collective-permute-done.7.refs_0_, bf16[256,256]{1,0:T(8,128)(2,1)S(1)} %copy-done, bf16[2,256,512]{2,1,0:T(8,128)(2,1)S(1)} %pair.2.refs_3_.refs_2_, ...), custom_call_target="tpu_custom_call" | custom-call | flops 786432 | bytes 65536 | tf_op jit(solution)/shard_map/expert_rows/pallas_call | solution.py:285
  63.0 4.1 %expert_rows.10 = (f32[4,2,256,512]{3,2,1,0:T(8,128)S(1)}, f32[256,256]{1,0:T(8,128)S(1)}, f32[1,256]{1,0:T(1,128)S(1)}) custom-call(bf16[256,512]{1,0:T(8,128)(2,1)} %collective-permute-done.6.refs_0_, bf16[256,256]{1,0:T(8,128)(2,1)S(1)} %copy-done, bf16[2,256,512]{2,1,0:T(8,128)(2,1)S(1)} %pair.2.refs_3_.refs_2_, ...), custom_call_target="tpu_custom_call" | custom-call | flops 786432 | bytes 65536 | tf_op jit(solution)/shard_map/expert_rows/pallas_call | solution.py:285
  67.1 4.0 %expert_rows.11 = (f32[4,2,256,512]{3,2,1,0:T(8,128)S(1)}, f32[64,256]{1,0:T(8,128)S(1)}, f32[64,256]{1,0:T(8,128)S(1)}, f32[64,256]{1,0:T(8,128)S(1)}, f32[64,256]{1,0:T(8,128)S(1)}, /*index=5*/f32[8,256]{1,0:T(8,128)S(1)}) custom-call(bf16[256,512]{1,0:T(8,128)(2,1)S(1)} %collective-permute-done.5.refs_0_, bf16[256,256]{1,0:T(8,128)(2,1)S(1)} %copy-done, ...), custom_call_target="tpu_custom_call" | custom-call | flops 786432 | bytes 65536 | tf_op jit(solution)/shard_map/expert_rows/pallas_call | solution.py:285
  71.8 2.9 %collective-permute-start.13 = (f32[64,256]{1,0:T(8,128)S(1)}, f32[64,256]{1,0:T(8,128)S(1)}, u32[]{:S(2)}, u32[]{:S(2)}) collective-permute-start(f32[64,256]{1,0:T(8,128)S(1)} %get-tuple-element.82), channel_id=1, source_target_pairs={{0,24},{8,16},{16,8},{24,0},{1,25},{9,17},{17,9},{25,1},{2,26},{10... | collective-permute-start | bytes 196616 | tf_op jit(solution)/shard_map/ppermute | solution.py:447
  77.8 2.1 %collective-permute-start.21 = (bf16[2,256,512]{2,1,0:T(8,128)(2,1)S(1)}, bf16[2,256,512]{2,1,0:T(8,128)(2,1)S(1)}, u32[]{:S(2)}, u32[]{:S(2)}) collective-permute-start(bf16[2,256,512]{2,1,0:T(8,128)(2,1)S(1)} %get-tuple-element.92), channel_id=1, source_target_pairs={{0,8},{8,0},{16,24},{24,16},{1,9},{9,1},{17,25},{25,17},{2,10},{10... | collective-permute-start | bytes 1572872 | tf_op jit(solution)/shard_map/ppermute | solution.py:447
  82.7 5.1 %collective-permute-start.16 = (f32[72,256]{1,0:T(8,128)S(1)}, f32[72,256]{1,0:T(8,128)S(1)}, u32[]{:S(2)}, u32[]{:S(2)}) collective-permute-start(f32[72,256]{1,0:T(8,128)S(1)} %get-tuple-element.88), channel_id=1, source_target_pairs={{0,4},{1,5},{2,6},{3,7},{4,0},{5,1},{6,2},{7,3},{8,12},{9,13},{10,... | collective-permute-start | bytes 221192 | tf_op jit(solution)/shard_map/ppermute | solution.py:447
  87.9 5.2 %collective-permute-done.16.refs_2_ = f32[72,256]{1,0:T(8,128)S(1)} collective-permute-done((f32[72,256]{1,0:T(8,128)S(1)}, f32[72,256]{1,0:T(8,128)S(1)}, u32[]{:S(2)}, u32[]{:S(2)}) %collective-permute-start.16) | collective-permute-done | bytes 73760 | tf_op jit(solution)/shard_map/ppermute | solution.py:447
  94.4 1.5 %collective-permute-start.24 = (bf16[256,512]{1,0:T(8,128)(2,1)S(1)}, bf16[256,512]{1,0:T(8,128)(2,1)S(1)}, u32[]{:S(2)}, u32[]{:S(2)}) collective-permute-start(bf16[256,512]{1,0:T(8,128)(2,1)S(1)} %get-tuple-element.95), channel_id=1, source_target_pairs={{0,8},{8,0},{16,24},{24,16},{1,9},{9,1},{17,25},{25,17},{2,10},{10... | collective-permute-start | bytes 786440 | tf_op jit(solution)/shard_map/ppermute | solution.py:447
  95.9 2.0 %collective-permute-start.20 = (f32[64,256]{1,0:T(8,128)S(1)}, f32[64,256]{1,0:T(8,128)S(1)}, u32[]{:S(2)}, u32[]{:S(2)}) collective-permute-start(f32[64,256]{1,0:T(8,128)S(1)} %get-tuple-element.90.ahead_ref.refs_0_), channel_id=1, source_target_pairs={{0,24},{8,16},{16,8},{24,0},{1,25},{9,17},{17,9},{25,1},{2,26},{10... | collective-permute-start | bytes 196616 | tf_op jit(solution)/shard_map/ppermute | solution.py:447
  100.5 1.8 %collective-permute-done.23.refs_6_ = bf16[256,512]{1,0:T(8,128)(2,1)S(1)} collective-permute-done((bf16[256,512]{1,0:T(8,128)(2,1)S(1)}, bf16[256,512]{1,0:T(8,128)(2,1)S(1)}, u32[]{:S(2)}, u32[]{:S(2)}) %collective-permute-start.23) | collective-permute-done | bytes 262176 | tf_op jit(solution)/shard_map/ppermute | solution.py:447
  102.4 2.1 %adam.1 = (f32[1,2,256,512]{3,2,1,0:T(8,128)}, f32[1,2,256,512]{3,2,1,0:T(8,128)}, f32[1,2,256,512]{3,2,1,0:T(8,128)}, f32[8,128]{1,0:T(8,128)S(1)}) custom-call(f32[1,2,256,512]{3,2,1,0:T(8,128)S(1)} %copy-done.3, f32[1,2,256,512]{3,2,1,0:T(8,128)S(1)} %copy-done.4, f32[1,2,256,512]{3,2,1,0:T(8,128)S(1)} %copy-done.5, ...), custom_call_target="tpu_custom_call" | custom-call | flops 5242880 | bytes 2097152 | tf_op jit(solution)/shard_map/adam/pallas_call | solution.py:431
  (66 shorter events, 20.8 us)
Async XLA Ops:
  2.0 12.9 %collective-permute-start.3 = (bf16[256,512]{1,0:T(8,128)(2,1)S(1)}, bf16[256,512]{1,0:T(8,128)(2,1)S(1)}, u32[]{:S(2)}, u32[]{:S(2)}) collective-permute-start(bf16[256,512]{1,0:T(8,128)(2,1)S(1)} %get-tuple-element.101.one_ref), channel_id=1, source_target_pairs={{0,16},{8,24},{16,0},{24,8},{1,17},{9,25},{17,1},{25,9},{2,18},{10... | collective-permute-start | bytes 786440 | tf_op jit(solution)/shard_map/ppermute | solution.py:447
  5.0 9.2 %collective-permute-start.1 = (bf16[256,512]{1,0:T(8,128)(2,1)S(1)}, bf16[256,512]{1,0:T(8,128)(2,1)S(1)}, u32[]{:S(2)}, u32[]{:S(2)}) collective-permute-start(bf16[256,512]{1,0:T(8,128)(2,1)S(1)} %get-tuple-element.102.one_ref), channel_id=1, source_target_pairs={{0,8},{8,0},{16,24},{24,16},{1,9},{9,1},{17,25},{25,17},{2,10},{10... | collective-permute-start | bytes 786440 | tf_op jit(solution)/shard_map/ppermute | solution.py:447
  14.3 13.2 %collective-permute-start.2 = (bf16[2,256,512]{2,1,0:T(8,128)(2,1)S(1)}, bf16[2,256,512]{2,1,0:T(8,128)(2,1)S(1)}, u32[]{:S(2)}, u32[]{:S(2)}) collective-permute-start(bf16[2,256,512]{2,1,0:T(8,128)(2,1)S(1)} %pair.2.refs_3_.refs_2_), channel_id=1, source_target_pairs={{0,16},{8,24},{16,0},{24,8},{1,17},{9,25},{17,1},{25,9},{2,18},{10... | collective-permute-start | bytes 1572872 | tf_op jit(solution)/shard_map/ppermute | solution.py:447
  14.9 14.1 %collective-permute-start.4 = (bf16[2,256,512]{2,1,0:T(8,128)(2,1)S(1)}, bf16[2,256,512]{2,1,0:T(8,128)(2,1)S(1)}, u32[]{:S(2)}, u32[]{:S(2)}) collective-permute-start(bf16[2,256,512]{2,1,0:T(8,128)(2,1)S(1)} %pair.3.refs_5_.refs_4_), channel_id=1, source_target_pairs={{0,8},{8,0},{16,24},{24,16},{1,9},{9,1},{17,25},{25,17},{2,10},{10... | collective-permute-start | bytes 1572872 | tf_op jit(solution)/shard_map/ppermute | solution.py:447
  15.1 3.2 %collective-permute-start = (bf16[256,512]{1,0:T(8,128)(2,1)S(1)}, bf16[256,512]{1,0:T(8,128)(2,1)S(1)}, u32[]{:S(2)}, u32[]{:S(2)}) collective-permute-start(bf16[256,512]{1,0:T(8,128)(2,1)S(1)} %get-tuple-element.54), channel_id=1, source_target_pairs={{0,1},{1,0},{2,3},{3,2},{4,5},{5,4},{6,7},{7,6},{8,9},{9,8},{10,11... | collective-permute-start | bytes 786440 | tf_op jit(solution)/shard_map/ppermute | solution.py:447
  15.1 25.3 %collective-permute-start.9 = (bf16[256,512]{1,0:T(8,128)(2,1)S(1)}, bf16[256,512]{1,0:T(8,128)(2,1)S(1)}, u32[]{:S(2)}, u32[]{:S(2)}) collective-permute-start(bf16[256,512]{1,0:T(8,128)(2,1)S(1)} %get-tuple-element.62), channel_id=1, source_target_pairs={{0,4},{1,5},{2,6},{3,7},{4,0},{5,1},{6,2},{7,3},{8,12},{9,13},{10,... | collective-permute-start | bytes 786440 | tf_op jit(solution)/shard_map/ppermute | solution.py:447
  18.1 23.7 %collective-permute-start.10 = (bf16[256,512]{1,0:T(8,128)(2,1)}, bf16[256,512]{1,0:T(8,128)(2,1)S(1)}, u32[]{:S(2)}, u32[]{:S(2)}) collective-permute-start(bf16[256,512]{1,0:T(8,128)(2,1)} %get-tuple-element.63), channel_id=1, source_target_pairs={{0,5},{1,4},{2,7},{3,6},{4,1},{5,0},{6,3},{7,2},{8,13},{9,12},{10,... | collective-permute-start | bytes 786440 | tf_op jit(solution)/shard_map/ppermute | solution.py:447
  18.2 41.6 %collective-permute-start.7 = (bf16[256,512]{1,0:T(8,128)(2,1)}, bf16[256,512]{1,0:T(8,128)(2,1)S(1)}, u32[]{:S(2)}, u32[]{:S(2)}) collective-permute-start(bf16[256,512]{1,0:T(8,128)(2,1)} %get-tuple-element.60), channel_id=1, source_target_pairs={{0,3},{1,2},{2,1},{3,0},{4,7},{5,6},{6,5},{7,4},{8,11},{9,10},{10,... | collective-permute-start | bytes 786440 | tf_op jit(solution)/shard_map/ppermute | solution.py:447
  27.4 28.2 %collective-permute-start.8 = (bf16[256,512]{1,0:T(8,128)(2,1)}, bf16[256,512]{1,0:T(8,128)(2,1)}, u32[]{:S(2)}, u32[]{:S(2)}) collective-permute-start(bf16[256,512]{1,0:T(8,128)(2,1)} %get-tuple-element.61), channel_id=1, source_target_pairs={{0,2},{1,3},{2,0},{3,1},{4,6},{5,7},{6,4},{7,5},{8,10},{9,11},{10,... | collective-permute-start | bytes 786440 | tf_op jit(solution)/shard_map/ppermute | solution.py:447
  37.9 25.1 %collective-permute-start.6 = (bf16[256,512]{1,0:T(8,128)(2,1)}, bf16[256,512]{1,0:T(8,128)(2,1)}, u32[]{:S(2)}, u32[]{:S(2)}) collective-permute-start(bf16[256,512]{1,0:T(8,128)(2,1)} %get-tuple-element.59), channel_id=1, source_target_pairs={{0,6},{1,7},{2,4},{3,5},{4,2},{5,3},{6,0},{7,1},{8,14},{9,15},{10,... | collective-permute-start | bytes 786440 | tf_op jit(solution)/shard_map/ppermute | solution.py:447
  40.4 26.7 %collective-permute-start.5 = (bf16[256,512]{1,0:T(8,128)(2,1)}, bf16[256,512]{1,0:T(8,128)(2,1)S(1)}, u32[]{:S(2)}, u32[]{:S(2)}) collective-permute-start(bf16[256,512]{1,0:T(8,128)(2,1)} %get-tuple-element.58), channel_id=1, source_target_pairs={{0,7},{1,6},{2,5},{3,4},{4,3},{5,2},{6,1},{7,0},{8,15},{9,14},{10,... | collective-permute-start | bytes 786440 | tf_op jit(solution)/shard_map/ppermute | solution.py:447
  71.1 4.3 %collective-permute-start.11 = (f32[64,256]{1,0:T(8,128)S(1)}, f32[64,256]{1,0:T(8,128)S(1)}, u32[]{:S(2)}, u32[]{:S(2)}) collective-permute-start(f32[64,256]{1,0:T(8,128)S(1)} %get-tuple-element.80), channel_id=1, source_target_pairs={{0,8},{8,0},{16,24},{24,16},{1,9},{9,1},{17,25},{25,17},{2,10},{10... | collective-permute-start | bytes 196616 | tf_op jit(solution)/shard_map/ppermute | solution.py:447
  71.7 4.4 %collective-permute-start.12 = (f32[64,256]{1,0:T(8,128)S(1)}, f32[64,256]{1,0:T(8,128)S(1)}, u32[]{:S(2)}, u32[]{:S(2)}) collective-permute-start(f32[64,256]{1,0:T(8,128)S(1)} %get-tuple-element.81), channel_id=1, source_target_pairs={{0,16},{8,24},{16,0},{24,8},{1,17},{9,25},{17,1},{25,9},{2,18},{10... | collective-permute-start | bytes 196616 | tf_op jit(solution)/shard_map/ppermute | solution.py:447
  71.8 5.8 %collective-permute-start.13 = (f32[64,256]{1,0:T(8,128)S(1)}, f32[64,256]{1,0:T(8,128)S(1)}, u32[]{:S(2)}, u32[]{:S(2)}) collective-permute-start(f32[64,256]{1,0:T(8,128)S(1)} %get-tuple-element.82), channel_id=1, source_target_pairs={{0,24},{8,16},{16,8},{24,0},{1,25},{9,17},{17,9},{25,1},{2,26},{10... | collective-permute-start | bytes 196616 | tf_op jit(solution)/shard_map/ppermute | solution.py:447
  77.8 16.4 %collective-permute-start.21 = (bf16[2,256,512]{2,1,0:T(8,128)(2,1)S(1)}, bf16[2,256,512]{2,1,0:T(8,128)(2,1)S(1)}, u32[]{:S(2)}, u32[]{:S(2)}) collective-permute-start(bf16[2,256,512]{2,1,0:T(8,128)(2,1)S(1)} %get-tuple-element.92), channel_id=1, source_target_pairs={{0,8},{8,0},{16,24},{24,16},{1,9},{9,1},{17,25},{25,17},{2,10},{10... | collective-permute-start | bytes 1572872 | tf_op jit(solution)/shard_map/ppermute | solution.py:447
  79.9 14.2 %collective-permute-start.22 = (bf16[2,256,512]{2,1,0:T(8,128)(2,1)S(1)}, bf16[2,256,512]{2,1,0:T(8,128)(2,1)S(1)}, u32[]{:S(2)}, u32[]{:S(2)}) collective-permute-start(bf16[2,256,512]{2,1,0:T(8,128)(2,1)S(1)} %get-tuple-element.93), channel_id=1, source_target_pairs={{0,16},{8,24},{16,0},{24,8},{1,17},{9,25},{17,1},{25,9},{2,18},{10... | collective-permute-start | bytes 1572872 | tf_op jit(solution)/shard_map/ppermute | solution.py:447
  82.7 5.2 %collective-permute-start.15 = (f32[72,256]{1,0:T(8,128)S(1)}, f32[72,256]{1,0:T(8,128)S(1)}, u32[]{:S(2)}, u32[]{:S(2)}) collective-permute-start(f32[72,256]{1,0:T(8,128)S(1)} %get-tuple-element.87), channel_id=1, source_target_pairs={{0,2},{1,3},{2,0},{3,1},{4,6},{5,7},{6,4},{7,5},{8,10},{9,11},{10,... | collective-permute-start | bytes 221192 | tf_op jit(solution)/shard_map/ppermute | solution.py:447
  82.7 10.4 %collective-permute-start.16 = (f32[72,256]{1,0:T(8,128)S(1)}, f32[72,256]{1,0:T(8,128)S(1)}, u32[]{:S(2)}, u32[]{:S(2)}) collective-permute-start(f32[72,256]{1,0:T(8,128)S(1)} %get-tuple-element.88), channel_id=1, source_target_pairs={{0,4},{1,5},{2,6},{3,7},{4,0},{5,1},{6,2},{7,3},{8,12},{9,13},{10,... | collective-permute-start | bytes 221192 | tf_op jit(solution)/shard_map/ppermute | solution.py:447
  87.8 6.3 %collective-permute-start.17 = (f32[72,256]{1,0:T(8,128)S(1)}, f32[72,256]{1,0:T(8,128)S(1)}, u32[]{:S(2)}, u32[]{:S(2)}) collective-permute-start(f32[72,256]{1,0:T(8,128)S(1)} %get-tuple-element.89), channel_id=1, source_target_pairs={{0,6},{1,7},{2,4},{3,5},{4,2},{5,3},{6,0},{7,1},{8,14},{9,15},{10,... | collective-permute-start | bytes 221192 | tf_op jit(solution)/shard_map/ppermute | solution.py:447
  94.3 8.0 %collective-permute-start.23 = (bf16[256,512]{1,0:T(8,128)(2,1)S(1)}, bf16[256,512]{1,0:T(8,128)(2,1)S(1)}, u32[]{:S(2)}, u32[]{:S(2)}) collective-permute-start(bf16[256,512]{1,0:T(8,128)(2,1)S(1)} %get-tuple-element.94), channel_id=1, source_target_pairs={{0,16},{8,24},{16,0},{24,8},{1,17},{9,25},{17,1},{25,9},{2,18},{10... | collective-permute-start | bytes 786440 | tf_op jit(solution)/shard_map/ppermute | solution.py:447
  94.4 8.0 %collective-permute-start.24 = (bf16[256,512]{1,0:T(8,128)(2,1)S(1)}, bf16[256,512]{1,0:T(8,128)(2,1)S(1)}, u32[]{:S(2)}, u32[]{:S(2)}) collective-permute-start(bf16[256,512]{1,0:T(8,128)(2,1)S(1)} %get-tuple-element.95), channel_id=1, source_target_pairs={{0,8},{8,0},{16,24},{24,16},{1,9},{9,1},{17,25},{25,17},{2,10},{10... | collective-permute-start | bytes 786440 | tf_op jit(solution)/shard_map/ppermute | solution.py:447
  95.9 8.6 %collective-permute-start.20 = (f32[64,256]{1,0:T(8,128)S(1)}, f32[64,256]{1,0:T(8,128)S(1)}, u32[]{:S(2)}, u32[]{:S(2)}) collective-permute-start(f32[64,256]{1,0:T(8,128)S(1)} %get-tuple-element.90.ahead_ref.refs_0_), channel_id=1, source_target_pairs={{0,24},{8,16},{16,8},{24,0},{1,25},{9,17},{17,9},{25,1},{2,26},{10... | collective-permute-start | bytes 196616 | tf_op jit(solution)/shard_map/ppermute | solution.py:447
  97.9 6.7 %collective-permute-start.19 = (f32[64,256]{1,0:T(8,128)S(1)}, f32[64,256]{1,0:T(8,128)S(1)}, u32[]{:S(2)}, u32[]{:S(2)}) collective-permute-start(f32[64,256]{1,0:T(8,128)S(1)} %get-tuple-element.90.ahead_ref.refs_0_), channel_id=1, source_target_pairs={{0,16},{8,24},{16,0},{24,8},{1,17},{9,25},{17,1},{25,9},{2,18},{10... | collective-permute-start | bytes 196616 | tf_op jit(solution)/shard_map/ppermute | solution.py:447
  97.9 6.6 %collective-permute-start.18 = (f32[64,256]{1,0:T(8,128)S(1)}, f32[64,256]{1,0:T(8,128)S(1)}, u32[]{:S(2)}, u32[]{:S(2)}) collective-permute-start(f32[64,256]{1,0:T(8,128)S(1)} %get-tuple-element.90.ahead_ref.refs_0_), channel_id=1, source_target_pairs={{0,8},{8,0},{16,24},{24,16},{1,9},{9,1},{17,25},{25,17},{2,10},{10... | collective-permute-start | bytes 196616 | tf_op jit(solution)/shard_map/ppermute | solution.py:447
  (11 other events, 102.3 us)

commit v10 on v8

--- a/solution.py
+++ b/solution.py
@@ -18,6 +18,7 @@
 F32 = jnp.float32
 BF16 = jnp.bfloat16
 MIB = 1 << 20
+LOSSES = 256
 
 
 def iota(shape, dim):
@@ -88,7 +89,7 @@
         in_specs=[whole(pltpu.SMEM)] + [whole()] * 4,
         out_specs=[whole()] * (experts + 1),
         scratch_shapes=[pltpu.VMEM((rows, 2 * width), BF16)],
-        compiler_params=pltpu.CompilerParams(vmem_limit_bytes=32 * MIB),
+        compiler_params=pltpu.CompilerParams(vmem_limit_bytes=24 * MIB),
         cost_estimate=pl.CostEstimate(
             flops=2 * rows * width * (table.shape[0] + 2 * experts * capacity),
             bytes_accessed=6 * MIB,
@@ -136,7 +137,7 @@
     held = take(relays)
     if last:
         loss_refs = take(last - 1)
-        (ids_ref,) = take(1)
+        (mine_ref,) = take(1)
         (acc_ref,) = take(1)
         trunk_parts = take(shares if in_turns(experts) else 1)
         (all_loss_ref,) = take(1)
@@ -199,7 +200,10 @@
         half = squares[:, :LANES]
         for k in range(1, width // LANES):
             half = half + squares[:, k * LANES : (k + 1) * LANES]
-        loss_ref[pl.ds(i, 1), :] = jnp.sum(half.T, axis=0, keepdims=True) * (0.5 * loss_scale)
+        lost = jnp.sum(half.T, axis=0, keepdims=True) * (0.5 * loss_scale)
+        for k in range(step_rows // LOSSES):
+            row = pl.ds(i * (step_rows // LOSSES) + k, 1)
+            loss_ref[row, :] = lost[:, k * LOSSES : (k + 1) * LOSSES]
         scaled_f = errors * loss_scale
         scaled = scaled_f.astype(BF16)
         scaled_t = scaled_f.T.astype(BF16)
@@ -229,7 +233,7 @@
             return
         quarter = width // shares
         for j, ref in enumerate(trunk_parts):
-            at = pl.multiple_of((ids_ref[1] ^ j) * quarter, quarter)
+            at = pl.multiple_of((mine_ref[0] ^ j) * quarter, quarter)
             ref[...] = acc_trunk_ref[pl.ds(at, quarter), :]
         for s in range(experts):
             all_loss_ref[s : s + 1, :] = loss_row(all_losses, order.index(s))
@@ -246,18 +250,18 @@
         row -= ref.shape[0]
 
 
-def expert_call(xs, trunk_weight, weights, prior, losses, ids, order, last, relays=()):
+def expert_call(xs, trunk_weight, weights, prior, losses, mine, order, last, relays=()):
     experts = len(order)
     block_rows = xs[0].shape[0]
     width = trunk_weight.shape[0]
     shares, share = len(weights), weights[0].shape[2]
     rows = block_rows * len(xs)
-    step_rows = min(256, rows)
+    step_rows = min(512, rows)
     steps = rows // step_rows
     first = prior is None
     acc = jax.ShapeDtypeStruct((shares, 2, width, share), F32)
     acc_trunk = jax.ShapeDtypeStruct((width, width), F32)
-    loss = jax.ShapeDtypeStruct((steps, step_rows), F32)
+    loss = jax.ShapeDtypeStruct((rows // LOSSES, LOSSES), F32)
     args = list(xs) + [trunk_weight, *weights]
     if not first:
         args += list(prior)
@@ -269,14 +273,14 @@
         pltpu.VMEM((step_rows, shares * share), F32),
     ]
     if last:
-        args += list(losses) + [ids]
+        args += list(losses) + [mine]
         in_specs += [whole()] * len(losses) + [whole(pltpu.SMEM)]
         outs = [acc]
         if in_turns(experts):
             outs += [jax.ShapeDtypeStruct((width // shares, width), F32)] * shares
         else:
             outs += [acc_trunk]
-        outs += [jax.ShapeDtypeStruct((experts * block_rows // step_rows, step_rows), F32)]
+        outs += [jax.ShapeDtypeStruct((experts * block_rows // LOSSES, LOSSES), F32)]
         scratch += [pltpu.VMEM(a.shape, a.dtype) for a in (acc_trunk, loss)]
     else:
         outs = [acc, acc_trunk, loss]
@@ -288,7 +292,7 @@
         in_specs=in_specs,
         out_specs=[whole()] * len(outs),
         scratch_shapes=scratch,
-        compiler_params=pltpu.CompilerParams(vmem_limit_bytes=40 * MIB),
+        compiler_params=pltpu.CompilerParams(vmem_limit_bytes=28 * MIB),
         cost_estimate=pl.CostEstimate(
             flops=12 * rows * width,
             bytes_accessed=rows * width,
@@ -312,10 +316,10 @@
     note_ref[rows + 4 :, :] = jnp.zeros((4, total.shape[1]), F32)
 
 
-def pair_turn_kernel(ids_ref, total_ref, got_ref, loss_ref, *outs):
+def pair_turn_kernel(me_ref, total_ref, got_ref, loss_ref, *outs):
     rows, width = total_ref.shape
     half = rows // 2
-    at = pl.ds(pl.multiple_of((ids_ref[0] & 1) * half, half), half)
+    at = pl.ds(pl.multiple_of((me_ref[0] & 1) * half, half), half)
     for k, ref in enumerate(outs):
         ref[:half, :] = total_ref[at, :] + got_ref[at, :]
         ref[half : half + 1, :] = loss_ref[2 * k : 2 * k + 1, :]
@@ -331,23 +335,23 @@
         loss_ref[2 * k : 2 * k + 2, :] = note[half : half + 2, :]
 
 
-def join_kernel(ids_ref, own_ref, other_ref, both_ref):
+def join_kernel(me_ref, own_ref, other_ref, both_ref):
     half = own_ref.shape[0]
-    core = ids_ref[0] & 1
+    core = me_ref[0] & 1
     both_ref[pl.ds(pl.multiple_of(core * half, half), half), :] = own_ref[...]
     both_ref[pl.ds(pl.multiple_of((1 - core) * half, half), half), :] = other_ref[...]
 
 
-def assemble_kernel(ids_ref, *refs):
+def assemble_kernel(mine_ref, *refs):
     *held, _, trunk_ref = refs
     for j, ref in enumerate(held):
         rows = ref.shape[0]
-        at = pl.multiple_of((ids_ref[1] ^ j) * rows, rows)
+        at = pl.multiple_of((mine_ref[0] ^ j) * rows, rows)
         trunk_ref[pl.ds(at, rows), :] = ref[...]
 
 
-def turn(kernel, held, shapes, name, ids=None):
-    first = [] if ids is None else [ids]
+def turn(kernel, held, shapes, name, index=None):
+    first = [] if index is None else [index]
     width = held[0].shape[1]
     return pl.pallas_call(
         kernel,
@@ -471,7 +475,7 @@
     replicas = lax.axis_size("dp")
     capacity = 2 * rows // experts
     me = lax.axis_index("expert").astype(jnp.int32).reshape(1)
-    ids = jnp.concatenate([me, lax.axis_index("dp").astype(jnp.int32).reshape(1)])
+    mine = lax.axis_index("dp").astype(jnp.int32).reshape(1)
 
     up, down = expert_params[0, 0].astype(BF16), expert_params[0, 1].astype(BF16)
     near_up, near_down = swap(up, "dp", 1), swap(down, "dp", 2)
@@ -479,7 +483,7 @@
     ups, downs = pair(up, near_up, place), pair(down, near_down, place)
     weights = [ups, swap(ups, "dp", 2), downs, swap(downs, "dp", 1)]
     if in_turns(experts):
-        batches, later = ((0, 1), (4, 5), (2,), (3,), (6,), (7,)), (7,)
+        batches, later = ((0, 1), (4, 5), (2,), (3,), (6,), (7,)), (6, 7)
     else:
         batches, later = (range(experts // 2), range(experts // 2, experts)), ()
     order = [s for batch in batches for s in batch]
@@ -489,7 +493,7 @@
         last = k == len(batches) - 1
         relays = [blocks[s] for s in later] if k == 0 else []
         outs = expert_call(
-            [arrived[s] for s in batch], trunk_weight, weights, prior, losses, ids, order, last, relays
+            [arrived[s] for s in batch], trunk_weight, weights, prior, losses, mine, order, last, relays
         )
         if not last:
             prior = outs[:2]
@@ -516,17 +520,17 @@
             [total, swap(note, "expert", 1), losses],
             (quarter // 2 + 8,) * 4,
             "pair_turn",
-            ids,
+            me,
         )
         notes = [swap(note, "expert", 2 * k) for k, note in enumerate(notes)]
         total, loss = turn(z_turn_kernel, notes, (quarter // 2, experts), "z_turn")
         more_up, more_down = pass_on(got, total)
-        (total,) = turn(join_kernel, [total, swap(total, "expert", 1)], (quarter,), "join", ids)
+        (total,) = turn(join_kernel, [total, swap(total, "expert", 1)], (quarter,), "join", me)
         parts = [swap(total, "dp", j) for j in range(replicas)]
         *news, done = adam(
             expert_params, first_moment, second_moment, acc, [*got, more_up, more_down]
         )
-        (trunk_grad,) = turn(assemble_kernel, parts + [done], (width,), "assemble_trunk", ids)
+        (trunk_grad,) = turn(assemble_kernel, parts + [done], (width,), "assemble_trunk", mine)
     else:
         got = send(losses)
         more_up, more_down = pass_on(got, losses)

time: 107 us -> 104 us (0.972)
  Pallas kernels: 38.7 us -> 33.8 us
  starting transfers between devices: 30.3 us -> 31.9 us
    pallas_call x6, Pallas kernels: 28.7 us -> 25.4 us  [expert_call(): pl.pallas_call(functools.partial(expert_kernel, counts, order, first, len...]
    pallas_call x5, Pallas kernels: 2.41 us -> 0.78 us  [turn(): pl.pallas_call(kernel, out_shape=[jax.ShapeDtypeStruct((rows, width), F32...]
    ppermute x26, starting transfers between devices: 30.3 us -> 31.9 us  [swap(): lax.ppermute(value, axis, [(i, i ^ s) for i in range(lax.axis_size(axis))])]
  transfers between devices with their start and end apart: 26 -> 26, of which waited for: 9 -> 11; matrix products, arithmetic and copies ran while one was open for 0% -> 0% of each run, Pallas kernels for 31% -> 28%
where the time goes in v10:
time: 104 us
  Pallas kernels  33.8 us (32%)
  starting transfers between devices  31.9 us (31%)
  waiting for transfers between devices  28.3 us (27%)
  local copies, waits for them, and re-layouts  7.84 us (8%)
  other arithmetic  1.29 us (1%)
    ppermute x26, starting transfers between devices, swap(): lax.ppermute(value, axis, [(i, i ^ s) for i in range(lax.axis_size(axis))])  31.9 us
    ppermute x26, waiting for transfers between devices, swap(): lax.ppermute(value, axis, [(i, i ^ s) for i in range(lax.axis_size(axis))])  28.3 us
    pallas_call x6, Pallas kernels, expert_call(): pl.pallas_call(functools.partial(expert_kernel, counts, order, first, len...  25.4 us
    unnamed x20, local copies, waits for them, and re-layouts  7.81 us
    pallas_call x1, Pallas kernels, pack(): pl.pallas_call(functools.partial(pack_kernel, experts, capacity), out_sha...  4.09 us
    pallas_call x1, Pallas kernels, adam(): pl.pallas_call(adam_kernel, out_shape=[shape] * 3 + [jax.ShapeDtypeStruct...  2.12 us
  transfers between devices with their start and end apart: 26, of which 11 were waited for; matrix products, arithmetic and copies ran while one was open for 0% of the time, Pallas kernels for 28%

profile of v10, /device:TPU:0, one launch (start us, length us, event | category | flops | bytes accessed | tf_op | source)
XLA Modules:
  0.0 104.0 jit_solution(3848722534778746689)
XLA Ops:
  2.0 3.0 %collective-permute-start.3 = (bf16[256,512]{1,0:T(8,128)(2,1)S(1)}, bf16[256,512]{1,0:T(8,128)(2,1)S(1)}, u32[]{:S(2)}, u32[]{:S(2)}) collective-permute-start(bf16[256,512]{1,0:T(8,128)(2,1)S(1)} %get-tuple-element.101.one_ref), channel_id=1, source_target_pairs={{0,16},{8,24},{16,0},{24,8},{1,17},{9,25},{17,1},{25,9},{2,18},{10... | collective-permute-start | bytes 786440 | tf_op jit(solution)/shard_map/ppermute | solution.py:459
  5.0 1.5 %collective-permute-start.1 = (bf16[256,512]{1,0:T(8,128)(2,1)S(1)}, bf16[256,512]{1,0:T(8,128)(2,1)S(1)}, u32[]{:S(2)}, u32[]{:S(2)}) collective-permute-start(bf16[256,512]{1,0:T(8,128)(2,1)S(1)} %get-tuple-element.102.one_ref), channel_id=1, source_target_pairs={{0,8},{8,0},{16,24},{24,16},{1,9},{9,1},{17,25},{25,17},{2,10},{10... | collective-permute-start | bytes 786440 | tf_op jit(solution)/shard_map/ppermute | solution.py:459
  10.1 4.1 %pack_rows.1 = (bf16[256,512]{1,0:T(8,128)(2,1)S(1)}, bf16[256,512]{1,0:T(8,128)(2,1)S(1)}, bf16[256,512]{1,0:T(8,128)(2,1)}, bf16[256,512]{1,0:T(8,128)(2,1)}, ...) custom-call(s32[1]{0:T(128)} %bitcast.1.me_ref, ...), custom_call_target="tpu_custom_call" | custom-call | flops 3221225472 | bytes 6291456 | tf_op jit(solution)/shard_map/pack_rows/pallas_call | solution.py:85
  15.1 3.0 %collective-permute-start.9 = (bf16[256,512]{1,0:T(8,128)(2,1)S(1)}, bf16[256,512]{1,0:T(8,128)(2,1)S(1)}, u32[]{:S(2)}, u32[]{:S(2)}) collective-permute-start(bf16[256,512]{1,0:T(8,128)(2,1)S(1)} %get-tuple-element.62), channel_id=1, source_target_pairs={{0,4},{1,5},{2,6},{3,7},{4,0},{5,1},{6,2},{7,3},{8,12},{9,13},{10,... | collective-permute-start | bytes 786440 | tf_op jit(solution)/shard_map/ppermute | solution.py:459
  19.7 7.7 %collective-permute-done.2.refs_4_.refs_3_ = bf16[2,256,512]{2,1,0:T(8,128)(2,1)S(1)} collective-permute-done((bf16[2,256,512]{2,1,0:T(8,128)(2,1)S(1)}, bf16[2,256,512]{2,1,0:T(8,128)(2,1)S(1)}, u32[]{:S(2)}, u32[]{:S(2)}) %collective-permute-start.2) | collective-permute-done | bytes 524320 | tf_op jit(solution)/shard_map/ppermute | solution.py:459
  27.4 1.6 %collective-permute-start.8 = (bf16[256,512]{1,0:T(8,128)(2,1)}, bf16[256,512]{1,0:T(8,128)(2,1)}, u32[]{:S(2)}, u32[]{:S(2)}) collective-permute-start(bf16[256,512]{1,0:T(8,128)(2,1)} %get-tuple-element.61), channel_id=1, source_target_pairs={{0,2},{1,3},{2,0},{3,1},{4,6},{5,7},{6,4},{7,5},{8,10},{9,11},{10,... | collective-permute-start | bytes 786440 | tf_op jit(solution)/shard_map/ppermute | solution.py:459
  29.0 5.5 %expert_rows.6 = (f32[4,2,256,512]{3,2,1,0:T(8,128)S(1)}, f32[256,256]{1,0:T(8,128)S(1)}, f32[2,256]{1,0:T(2,128)S(1)}, bf16[256,512]{1,0:T(8,128)(2,1)}, bf16[256,512]{1,0:T(8,128)(2,1)}) custom-call(bf16[256,512]{1,0:T(8,128)(2,1)S(1)} %get-tuple-element.53.refs_0_, bf16[256,512]{1,0:T(8,128)(2,1)S(1)} %collective-permute-done.refs_1_, ...), custom_call_target="tpu_custom_call" | custom-call | flops 1572864 | bytes 131072 | tf_op jit(solution)/shard_map/expert_rows/pallas_call | solution.py:289
  34.6 2.0 %copy-done.1 = f32[4,2,256,512]{3,2,1,0:T(8,128)} copy-done((f32[4,2,256,512]{3,2,1,0:T(8,128)}, f32[4,2,256,512]{3,2,1,0:T(8,128)S(1)}, u32[]{:S(2)}) %copy-start.1) | copy-done | bytes 4194328
  36.5 2.5 %collective-permute-start.6 = (bf16[256,512]{1,0:T(8,128)(2,1)}, bf16[256,512]{1,0:T(8,128)(2,1)}, u32[]{:S(2)}, u32[]{:S(2)}) collective-permute-start(bf16[256,512]{1,0:T(8,128)(2,1)} %get-tuple-element.59), channel_id=1, source_target_pairs={{0,6},{1,7},{2,4},{3,5},{4,2},{5,3},{6,0},{7,1},{8,14},{9,15},{10,... | collective-permute-start | bytes 786440 | tf_op jit(solution)/shard_map/ppermute | solution.py:459
  39.6 2.3 %collective-permute-done.10.refs_1_ = bf16[256,512]{1,0:T(8,128)(2,1)S(1)} collective-permute-done((bf16[256,512]{1,0:T(8,128)(2,1)}, bf16[256,512]{1,0:T(8,128)(2,1)S(1)}, u32[]{:S(2)}, u32[]{:S(2)}) %collective-permute-start.10) | collective-permute-done | bytes 262176 | tf_op jit(solution)/shard_map/ppermute | solution.py:459
  41.8 2.2 %copy-done.2 = f32[4,2,256,512]{3,2,1,0:T(8,128)S(1)} copy-done((f32[4,2,256,512]{3,2,1,0:T(8,128)S(1)}, f32[4,2,256,512]{3,2,1,0:T(8,128)}, u32[]{:S(2)}) %copy-start.2) | copy-done | bytes 4194328
  44.0 5.0 %expert_rows.7 = (f32[4,2,256,512]{3,2,1,0:T(8,128)S(1)}, f32[256,256]{1,0:T(8,128)S(1)}, f32[2,256]{1,0:T(2,128)S(1)}) custom-call(bf16[256,512]{1,0:T(8,128)(2,1)S(1)} %collective-permute-done.9.refs_0_, bf16[256,512]{1,0:T(8,128)(2,1)S(1)} %collective-permute-done.10.refs_1_, bf16[256,256]{1,0:T(8,128)(2,1)S(1)} %copy-done, ...), custom_call_target="tpu_custom_call" | custom-call | flops 1572864 | bytes 131072 | tf_op jit(solution)/shard_map/expert_rows/pallas_call | solution.py:289
  49.0 6.6 %collective-permute-done.8.refs_0_ = bf16[256,512]{1,0:T(8,128)(2,1)} collective-permute-done((bf16[256,512]{1,0:T(8,128)(2,1)}, bf16[256,512]{1,0:T(8,128)(2,1)}, u32[]{:S(2)}, u32[]{:S(2)}) %collective-permute-start.8) | collective-permute-done | bytes 262176 | tf_op jit(solution)/shard_map/ppermute | solution.py:459
  55.6 4.2 %expert_rows.8 = (f32[4,2,256,512]{3,2,1,0:T(8,128)S(1)}, f32[256,256]{1,0:T(8,128)S(1)}, f32[1,256]{1,0:T(1,128)S(1)}) custom-call(bf16[256,512]{1,0:T(8,128)(2,1)} %collective-permute-done.8.refs_0_, bf16[256,256]{1,0:T(8,128)(2,1)S(1)} %copy-done, bf16[2,256,512]{2,1,0:T(8,128)(2,1)S(1)} %pair.2.refs_3_.refs_2_, ...), custom_call_target="tpu_custom_call" | custom-call | flops 786432 | bytes 65536 | tf_op jit(solution)/shard_map/expert_rows/pallas_call | solution.py:289
  59.8 3.1 %expert_rows.9 = (f32[4,2,256,512]{3,2,1,0:T(8,128)S(1)}, f32[256,256]{1,0:T(8,128)S(1)}, f32[1,256]{1,0:T(1,128)S(1)}) custom-call(bf16[256,512]{1,0:T(8,128)(2,1)S(1)} %collective-permute-done.7.refs_0_, bf16[256,256]{1,0:T(8,128)(2,1)S(1)} %copy-done, bf16[2,256,512]{2,1,0:T(8,128)(2,1)S(1)} %pair.2.refs_3_.refs_2_, ...), custom_call_target="tpu_custom_call" | custom-call | flops 786432 | bytes 65536 | tf_op jit(solution)/shard_map/expert_rows/pallas_call | solution.py:289
  63.0 4.1 %expert_rows.10 = (f32[4,2,256,512]{3,2,1,0:T(8,128)S(1)}, f32[256,256]{1,0:T(8,128)S(1)}, f32[1,256]{1,0:T(1,128)S(1)}) custom-call(bf16[256,512]{1,0:T(8,128)(2,1)} %collective-permute-done.6.refs_0_, bf16[256,256]{1,0:T(8,128)(2,1)S(1)} %copy-done, bf16[2,256,512]{2,1,0:T(8,128)(2,1)S(1)} %pair.2.refs_3_.refs_2_, ...), custom_call_target="tpu_custom_call" | custom-call | flops 786432 | bytes 65536 | tf_op jit(solution)/shard_map/expert_rows/pallas_call | solution.py:289
  67.1 3.4 %expert_rows.11 = (f32[4,2,256,512]{3,2,1,0:T(8,128)S(1)}, f32[64,256]{1,0:T(8,128)S(1)}, f32[64,256]{1,0:T(8,128)S(1)}, f32[64,256]{1,0:T(8,128)S(1)}, f32[64,256]{1,0:T(8,128)S(1)}, /*index=5*/f32[8,256]{1,0:T(8,128)S(1)}) custom-call(bf16[256,512]{1,0:T(8,128)(2,1)S(1)} %collective-permute-done.5.refs_0_, bf16[256,256]{1,0:T(8,128)(2,1)S(1)} %copy-done, ...), custom_call_target="tpu_custom_call" | custom-call | flops 786432 | bytes 65536 | tf_op jit(solution)/shard_map/expert_rows/pallas_call | solution.py:289
  71.2 2.9 %collective-permute-start.13 = (f32[64,256]{1,0:T(8,128)S(1)}, f32[64,256]{1,0:T(8,128)S(1)}, u32[]{:S(2)}, u32[]{:S(2)}) collective-permute-start(f32[64,256]{1,0:T(8,128)S(1)} %get-tuple-element.82), channel_id=1, source_target_pairs={{0,24},{8,16},{16,8},{24,0},{1,25},{9,17},{17,9},{25,1},{2,26},{10... | collective-permute-start | bytes 196616 | tf_op jit(solution)/shard_map/ppermute | solution.py:459
  77.3 2.0 %collective-permute-start.22 = (bf16[2,256,512]{2,1,0:T(8,128)(2,1)S(1)}, bf16[2,256,512]{2,1,0:T(8,128)(2,1)S(1)}, u32[]{:S(2)}, u32[]{:S(2)}) collective-permute-start(bf16[2,256,512]{2,1,0:T(8,128)(2,1)S(1)} %get-tuple-element.92), channel_id=1, source_target_pairs={{0,8},{8,0},{16,24},{24,16},{1,9},{9,1},{17,25},{25,17},{2,10},{10... | collective-permute-start | bytes 1572872 | tf_op jit(solution)/shard_map/ppermute | solution.py:459
  82.2 5.1 %collective-permute-start.16 = (f32[40,256]{1,0:T(8,128)S(1)}, f32[40,256]{1,0:T(8,128)S(1)}, u32[]{:S(2)}, u32[]{:S(2)}) collective-permute-start(f32[40,256]{1,0:T(8,128)S(1)} %get-tuple-element.88), channel_id=1, source_target_pairs={{0,4},{1,5},{2,6},{3,7},{4,0},{5,1},{6,2},{7,3},{8,12},{9,13},{10,... | collective-permute-start | bytes 122888 | tf_op jit(solution)/shard_map/ppermute | solution.py:459
  87.3 2.8 %collective-permute-done.16.refs_2_ = f32[40,256]{1,0:T(8,128)S(1)} collective-permute-done((f32[40,256]{1,0:T(8,128)S(1)}, f32[40,256]{1,0:T(8,128)S(1)}, u32[]{:S(2)}, u32[]{:S(2)}) %collective-permute-start.16) | collective-permute-done | bytes 40992 | tf_op jit(solution)/shard_map/ppermute | solution.py:459
  90.1 3.0 %collective-permute-done.17.refs_3_ = f32[40,256]{1,0:T(8,128)S(1)} collective-permute-done((f32[40,256]{1,0:T(8,128)S(1)}, f32[40,256]{1,0:T(8,128)S(1)}, u32[]{:S(2)}, u32[]{:S(2)}) %collective-permute-start.17) | collective-permute-done | bytes 40992 | tf_op jit(solution)/shard_map/ppermute | solution.py:459
  96.0 2.0 %collective-permute-start.21 = (f32[64,256]{1,0:T(8,128)S(1)}, f32[64,256]{1,0:T(8,128)S(1)}, u32[]{:S(2)}, u32[]{:S(2)}) collective-permute-start(f32[64,256]{1,0:T(8,128)S(1)} %join.1.refs_0_), channel_id=1, source_target_pairs={{0,24},{8,16},{16,8},{24,0},{1,25},{9,17},{17,9},{25,1},{2,26},{10... | collective-permute-start | bytes 196616 | tf_op jit(solution)/shard_map/ppermute | solution.py:459
  100.8 2.1 %adam.1 = (f32[1,2,256,512]{3,2,1,0:T(8,128)}, f32[1,2,256,512]{3,2,1,0:T(8,128)}, f32[1,2,256,512]{3,2,1,0:T(8,128)}, f32[8,128]{1,0:T(8,128)S(1)}) custom-call(f32[1,2,256,512]{3,2,1,0:T(8,128)S(1)} %copy-done.3, f32[1,2,256,512]{3,2,1,0:T(8,128)S(1)} %copy-done.4, f32[1,2,256,512]{3,2,1,0:T(8,128)S(1)} %copy-done.5, ...), custom_call_target="tpu_custom_call" | custom-call | flops 5242880 | bytes 2097152 | tf_op jit(solution)/shard_map/adam/pallas_call | solution.py:443
  (68 shorter events, 21.4 us)
Async XLA Ops:
  2.0 12.9 %collective-permute-start.3 = (bf16[256,512]{1,0:T(8,128)(2,1)S(1)}, bf16[256,512]{1,0:T(8,128)(2,1)S(1)}, u32[]{:S(2)}, u32[]{:S(2)}) collective-permute-start(bf16[256,512]{1,0:T(8,128)(2,1)S(1)} %get-tuple-element.101.one_ref), channel_id=1, source_target_pairs={{0,16},{8,24},{16,0},{24,8},{1,17},{9,25},{17,1},{25,9},{2,18},{10... | collective-permute-start | bytes 786440 | tf_op jit(solution)/shard_map/ppermute | solution.py:459
  5.0 9.2 %collective-permute-start.1 = (bf16[256,512]{1,0:T(8,128)(2,1)S(1)}, bf16[256,512]{1,0:T(8,128)(2,1)S(1)}, u32[]{:S(2)}, u32[]{:S(2)}) collective-permute-start(bf16[256,512]{1,0:T(8,128)(2,1)S(1)} %get-tuple-element.102.one_ref), channel_id=1, source_target_pairs={{0,8},{8,0},{16,24},{24,16},{1,9},{9,1},{17,25},{25,17},{2,10},{10... | collective-permute-start | bytes 786440 | tf_op jit(solution)/shard_map/ppermute | solution.py:459
  14.3 13.2 %collective-permute-start.2 = (bf16[2,256,512]{2,1,0:T(8,128)(2,1)S(1)}, bf16[2,256,512]{2,1,0:T(8,128)(2,1)S(1)}, u32[]{:S(2)}, u32[]{:S(2)}) collective-permute-start(bf16[2,256,512]{2,1,0:T(8,128)(2,1)S(1)} %pair.2.refs_3_.refs_2_), channel_id=1, source_target_pairs={{0,16},{8,24},{16,0},{24,8},{1,17},{9,25},{17,1},{25,9},{2,18},{10... | collective-permute-start | bytes 1572872 | tf_op jit(solution)/shard_map/ppermute | solution.py:459
  14.9 14.1 %collective-permute-start.4 = (bf16[2,256,512]{2,1,0:T(8,128)(2,1)S(1)}, bf16[2,256,512]{2,1,0:T(8,128)(2,1)S(1)}, u32[]{:S(2)}, u32[]{:S(2)}) collective-permute-start(bf16[2,256,512]{2,1,0:T(8,128)(2,1)S(1)} %pair.3.refs_5_.refs_4_), channel_id=1, source_target_pairs={{0,8},{8,0},{16,24},{24,16},{1,9},{9,1},{17,25},{25,17},{2,10},{10... | collective-permute-start | bytes 1572872 | tf_op jit(solution)/shard_map/ppermute | solution.py:459
  15.1 3.2 %collective-permute-start = (bf16[256,512]{1,0:T(8,128)(2,1)S(1)}, bf16[256,512]{1,0:T(8,128)(2,1)S(1)}, u32[]{:S(2)}, u32[]{:S(2)}) collective-permute-start(bf16[256,512]{1,0:T(8,128)(2,1)S(1)} %get-tuple-element.54), channel_id=1, source_target_pairs={{0,1},{1,0},{2,3},{3,2},{4,5},{5,4},{6,7},{7,6},{8,9},{9,8},{10,11... | collective-permute-start | bytes 786440 | tf_op jit(solution)/shard_map/ppermute | solution.py:459
  15.1 23.9 %collective-permute-start.9 = (bf16[256,512]{1,0:T(8,128)(2,1)S(1)}, bf16[256,512]{1,0:T(8,128)(2,1)S(1)}, u32[]{:S(2)}, u32[]{:S(2)}) collective-permute-start(bf16[256,512]{1,0:T(8,128)(2,1)S(1)} %get-tuple-element.62), channel_id=1, source_target_pairs={{0,4},{1,5},{2,6},{3,7},{4,0},{5,1},{6,2},{7,3},{8,12},{9,13},{10,... | collective-permute-start | bytes 786440 | tf_op jit(solution)/shard_map/ppermute | solution.py:459
  18.1 23.7 %collective-permute-start.10 = (bf16[256,512]{1,0:T(8,128)(2,1)}, bf16[256,512]{1,0:T(8,128)(2,1)S(1)}, u32[]{:S(2)}, u32[]{:S(2)}) collective-permute-start(bf16[256,512]{1,0:T(8,128)(2,1)} %get-tuple-element.63), channel_id=1, source_target_pairs={{0,5},{1,4},{2,7},{3,6},{4,1},{5,0},{6,3},{7,2},{8,13},{9,12},{10,... | collective-permute-start | bytes 786440 | tf_op jit(solution)/shard_map/ppermute | solution.py:459
  18.2 41.6 %collective-permute-start.7 = (bf16[256,512]{1,0:T(8,128)(2,1)}, bf16[256,512]{1,0:T(8,128)(2,1)S(1)}, u32[]{:S(2)}, u32[]{:S(2)}) collective-permute-start(bf16[256,512]{1,0:T(8,128)(2,1)} %get-tuple-element.60), channel_id=1, source_target_pairs={{0,3},{1,2},{2,1},{3,0},{4,7},{5,6},{6,5},{7,4},{8,11},{9,10},{10,... | collective-permute-start | bytes 786440 | tf_op jit(solution)/shard_map/ppermute | solution.py:459
  27.4 28.2 %collective-permute-start.8 = (bf16[256,512]{1,0:T(8,128)(2,1)}, bf16[256,512]{1,0:T(8,128)(2,1)}, u32[]{:S(2)}, u32[]{:S(2)}) collective-permute-start(bf16[256,512]{1,0:T(8,128)(2,1)} %get-tuple-element.61), channel_id=1, source_target_pairs={{0,2},{1,3},{2,0},{3,1},{4,6},{5,7},{6,4},{7,5},{8,10},{9,11},{10,... | collective-permute-start | bytes 786440 | tf_op jit(solution)/shard_map/ppermute | solution.py:459
  36.5 26.4 %collective-permute-start.6 = (bf16[256,512]{1,0:T(8,128)(2,1)}, bf16[256,512]{1,0:T(8,128)(2,1)}, u32[]{:S(2)}, u32[]{:S(2)}) collective-permute-start(bf16[256,512]{1,0:T(8,128)(2,1)} %get-tuple-element.59), channel_id=1, source_target_pairs={{0,6},{1,7},{2,4},{3,5},{4,2},{5,3},{6,0},{7,1},{8,14},{9,15},{10,... | collective-permute-start | bytes 786440 | tf_op jit(solution)/shard_map/ppermute | solution.py:459
  39.0 28.1 %collective-permute-start.5 = (bf16[256,512]{1,0:T(8,128)(2,1)}, bf16[256,512]{1,0:T(8,128)(2,1)S(1)}, u32[]{:S(2)}, u32[]{:S(2)}) collective-permute-start(bf16[256,512]{1,0:T(8,128)(2,1)} %get-tuple-element.58), channel_id=1, source_target_pairs={{0,7},{1,6},{2,5},{3,4},{4,3},{5,2},{6,1},{7,0},{8,15},{9,14},{10,... | collective-permute-start | bytes 786440 | tf_op jit(solution)/shard_map/ppermute | solution.py:459
  70.5 5.0 %collective-permute-start.11 = (f32[64,256]{1,0:T(8,128)S(1)}, f32[64,256]{1,0:T(8,128)S(1)}, u32[]{:S(2)}, u32[]{:S(2)}) collective-permute-start(f32[64,256]{1,0:T(8,128)S(1)} %get-tuple-element.80), channel_id=1, source_target_pairs={{0,8},{8,0},{16,24},{24,16},{1,9},{9,1},{17,25},{25,17},{2,10},{10... | collective-permute-start | bytes 196616 | tf_op jit(solution)/shard_map/ppermute | solution.py:459
  71.2 5.3 %collective-permute-start.12 = (f32[64,256]{1,0:T(8,128)S(1)}, f32[64,256]{1,0:T(8,128)S(1)}, u32[]{:S(2)}, u32[]{:S(2)}) collective-permute-start(f32[64,256]{1,0:T(8,128)S(1)} %get-tuple-element.81), channel_id=1, source_target_pairs={{0,16},{8,24},{16,0},{24,8},{1,17},{9,25},{17,1},{25,9},{2,18},{10... | collective-permute-start | bytes 196616 | tf_op jit(solution)/shard_map/ppermute | solution.py:459
  71.2 5.9 %collective-permute-start.13 = (f32[64,256]{1,0:T(8,128)S(1)}, f32[64,256]{1,0:T(8,128)S(1)}, u32[]{:S(2)}, u32[]{:S(2)}) collective-permute-start(f32[64,256]{1,0:T(8,128)S(1)} %get-tuple-element.82), channel_id=1, source_target_pairs={{0,24},{8,16},{16,8},{24,0},{1,25},{9,17},{17,9},{25,1},{2,26},{10... | collective-permute-start | bytes 196616 | tf_op jit(solution)/shard_map/ppermute | solution.py:459
  77.3 15.8 %collective-permute-start.22 = (bf16[2,256,512]{2,1,0:T(8,128)(2,1)S(1)}, bf16[2,256,512]{2,1,0:T(8,128)(2,1)S(1)}, u32[]{:S(2)}, u32[]{:S(2)}) collective-permute-start(bf16[2,256,512]{2,1,0:T(8,128)(2,1)S(1)} %get-tuple-element.92), channel_id=1, source_target_pairs={{0,8},{8,0},{16,24},{24,16},{1,9},{9,1},{17,25},{25,17},{2,10},{10... | collective-permute-start | bytes 1572872 | tf_op jit(solution)/shard_map/ppermute | solution.py:459
  79.3 13.8 %collective-permute-start.23 = (bf16[2,256,512]{2,1,0:T(8,128)(2,1)S(1)}, bf16[2,256,512]{2,1,0:T(8,128)(2,1)S(1)}, u32[]{:S(2)}, u32[]{:S(2)}) collective-permute-start(bf16[2,256,512]{2,1,0:T(8,128)(2,1)S(1)} %get-tuple-element.93), channel_id=1, source_target_pairs={{0,16},{8,24},{16,0},{24,8},{1,17},{9,25},{17,1},{25,9},{2,18},{10... | collective-permute-start | bytes 1572872 | tf_op jit(solution)/shard_map/ppermute | solution.py:459
  82.1 5.2 %collective-permute-start.15 = (f32[40,256]{1,0:T(8,128)S(1)}, f32[40,256]{1,0:T(8,128)S(1)}, u32[]{:S(2)}, u32[]{:S(2)}) collective-permute-start(f32[40,256]{1,0:T(8,128)S(1)} %get-tuple-element.87), channel_id=1, source_target_pairs={{0,2},{1,3},{2,0},{3,1},{4,6},{5,7},{6,4},{7,5},{8,10},{9,11},{10,... | collective-permute-start | bytes 122888 | tf_op jit(solution)/shard_map/ppermute | solution.py:459
  82.2 7.9 %collective-permute-start.16 = (f32[40,256]{1,0:T(8,128)S(1)}, f32[40,256]{1,0:T(8,128)S(1)}, u32[]{:S(2)}, u32[]{:S(2)}) collective-permute-start(f32[40,256]{1,0:T(8,128)S(1)} %get-tuple-element.88), channel_id=1, source_target_pairs={{0,4},{1,5},{2,6},{3,7},{4,0},{5,1},{6,2},{7,3},{8,12},{9,13},{10,... | collective-permute-start | bytes 122888 | tf_op jit(solution)/shard_map/ppermute | solution.py:459
  87.3 5.8 %collective-permute-start.17 = (f32[40,256]{1,0:T(8,128)S(1)}, f32[40,256]{1,0:T(8,128)S(1)}, u32[]{:S(2)}, u32[]{:S(2)}) collective-permute-start(f32[40,256]{1,0:T(8,128)S(1)} %get-tuple-element.89), channel_id=1, source_target_pairs={{0,6},{1,7},{2,4},{3,5},{4,2},{5,3},{6,0},{7,1},{8,14},{9,15},{10,... | collective-permute-start | bytes 122888 | tf_op jit(solution)/shard_map/ppermute | solution.py:459
  93.2 7.5 %collective-permute-start.24 = (bf16[256,512]{1,0:T(8,128)(2,1)S(1)}, bf16[256,512]{1,0:T(8,128)(2,1)S(1)}, u32[]{:S(2)}, u32[]{:S(2)}) collective-permute-start(bf16[256,512]{1,0:T(8,128)(2,1)S(1)} %get-tuple-element.94), channel_id=1, source_target_pairs={{0,16},{8,24},{16,0},{24,8},{1,17},{9,25},{17,1},{25,9},{2,18},{10... | collective-permute-start | bytes 786440 | tf_op jit(solution)/shard_map/ppermute | solution.py:459
  93.3 7.5 %collective-permute-start.25 = (bf16[256,512]{1,0:T(8,128)(2,1)S(1)}, bf16[256,512]{1,0:T(8,128)(2,1)S(1)}, u32[]{:S(2)}, u32[]{:S(2)}) collective-permute-start(bf16[256,512]{1,0:T(8,128)(2,1)S(1)} %get-tuple-element.95), channel_id=1, source_target_pairs={{0,8},{8,0},{16,24},{24,16},{1,9},{9,1},{17,25},{25,17},{2,10},{10... | collective-permute-start | bytes 786440 | tf_op jit(solution)/shard_map/ppermute | solution.py:459
  96.0 7.2 %collective-permute-start.21 = (f32[64,256]{1,0:T(8,128)S(1)}, f32[64,256]{1,0:T(8,128)S(1)}, u32[]{:S(2)}, u32[]{:S(2)}) collective-permute-start(f32[64,256]{1,0:T(8,128)S(1)} %join.1.refs_0_), channel_id=1, source_target_pairs={{0,24},{8,16},{16,8},{24,0},{1,25},{9,17},{17,9},{25,1},{2,26},{10... | collective-permute-start | bytes 196616 | tf_op jit(solution)/shard_map/ppermute | solution.py:459
  98.1 5.2 %collective-permute-start.20 = (f32[64,256]{1,0:T(8,128)S(1)}, f32[64,256]{1,0:T(8,128)S(1)}, u32[]{:S(2)}, u32[]{:S(2)}) collective-permute-start(f32[64,256]{1,0:T(8,128)S(1)} %join.1.refs_0_), channel_id=1, source_target_pairs={{0,16},{8,24},{16,0},{24,8},{1,17},{9,25},{17,1},{25,9},{2,18},{10... | collective-permute-start | bytes 196616 | tf_op jit(solution)/shard_map/ppermute | solution.py:459
  98.2 5.1 %collective-permute-start.19 = (f32[64,256]{1,0:T(8,128)S(1)}, f32[64,256]{1,0:T(8,128)S(1)}, u32[]{:S(2)}, u32[]{:S(2)}) collective-permute-start(f32[64,256]{1,0:T(8,128)S(1)} %join.1.refs_0_), channel_id=1, source_target_pairs={{0,8},{8,0},{16,24},{24,16},{1,9},{9,1},{17,25},{25,17},{2,10},{10... | collective-permute-start | bytes 196616 | tf_op jit(solution)/shard_map/ppermute | solution.py:459
  (12 other events, 100.0 us)

commit v11 on v10

--- a/solution.py
+++ b/solution.py
@@ -33,7 +33,7 @@
     return pl.BlockSpec(memory_space=memory_space)
 
 
-def pack_kernel(experts, capacity, me_ref, index_ref, region_ref, table_ref, target_ref, *refs):
+def pack_kernel(experts, capacity, me_ref, mine_ref, index_ref, region_ref, table_ref, target_ref, *refs):
     blocks, place_ref, rows_ref = refs[:experts], refs[experts], refs[experts + 1]
     me = me_ref[0]
     groups = index_ref.shape[0]
@@ -79,14 +79,14 @@
         blocks[s][...] = dot(spread, rows_ref[...]).astype(BF16)
 
 
-def pack(me, index, region, table, targets, experts, capacity):
+def pack(me, mine, index, region, table, targets, experts, capacity):
     rows, width = targets.shape
     groups = rows // LANES
     return pl.pallas_call(
         functools.partial(pack_kernel, experts, capacity),
         out_shape=[jax.ShapeDtypeStruct((capacity, 2 * width), BF16)] * experts
         + [jax.ShapeDtypeStruct((groups, LANES), jnp.int32)],
-        in_specs=[whole(pltpu.SMEM)] + [whole()] * 4,
+        in_specs=[whole(pltpu.SMEM)] * 2 + [whole()] * 4,
         out_specs=[whole()] * (experts + 1),
         scratch_shapes=[pltpu.VMEM((rows, 2 * width), BF16)],
         compiler_params=pltpu.CompilerParams(vmem_limit_bytes=24 * MIB),
@@ -96,7 +96,7 @@
             transcendentals=0,
         ),
         name="pack_rows",
-    )(me, index.reshape(groups, LANES), region.reshape(groups, LANES), table, targets)
+    )(me, mine, index.reshape(groups, LANES), region.reshape(groups, LANES), table, targets)
 
 
 def pair_kernel(one_ref, other_ref, ahead_ref, both_ref):
@@ -292,7 +292,7 @@
         in_specs=in_specs,
         out_specs=[whole()] * len(outs),
         scratch_shapes=scratch,
-        compiler_params=pltpu.CompilerParams(vmem_limit_bytes=28 * MIB),
+        compiler_params=pltpu.CompilerParams(vmem_limit_bytes=20 * MIB),
         cost_estimate=pl.CostEstimate(
             flops=12 * rows * width,
             bytes_accessed=rows * width,
@@ -479,7 +479,7 @@
 
     up, down = expert_params[0, 0].astype(BF16), expert_params[0, 1].astype(BF16)
     near_up, near_down = swap(up, "dp", 1), swap(down, "dp", 2)
-    *blocks, place = pack(me, sample_index, region[:, 0], cell_table, targets, experts, capacity)
+    *blocks, place = pack(me, mine, sample_index, region[:, 0], cell_table, targets, experts, capacity)
     ups, downs = pair(up, near_up, place), pair(down, near_down, place)
     weights = [ups, swap(ups, "dp", 2), downs, swap(downs, "dp", 1)]
     if in_turns(experts):

time: 104 us -> 102 us (0.981)
  local copies, waits for them, and re-layouts: 7.84 us -> 3.7 us
  Pallas kernels: 33.8 us -> 31 us
  starting transfers between devices: 31.9 us -> 34.2 us
  waiting for transfers between devices: 28.3 us -> 30.4 us
    unnamed x20 -> x16, local copies, waits for them, and re-layouts: 7.81 us -> 3.66 us
    ppermute x26, starting transfers between devices: 31.9 us -> 34.2 us  [swap(): lax.ppermute(value, axis, [(i, i ^ s) for i in range(lax.axis_size(axis))])]
    pallas_call x6, Pallas kernels: 25.4 us -> 23.2 us  [expert_call(): pl.pallas_call(functools.partial(expert_kernel, counts, order, first, len...]
    ppermute x26, waiting for transfers between devices: 28.3 us -> 30.4 us  [swap(): lax.ppermute(value, axis, [(i, i ^ s) for i in range(lax.axis_size(axis))])]
  transfers between devices with their start and end apart: 26 -> 26, of which waited for: 11 -> 12; matrix products, arithmetic and copies ran while one was open for 0% -> 0% of each run, Pallas kernels for 28% -> 26%
where the time goes in v11:
time: 102 us; the launch traced here: 101 us
  starting transfers between devices  34.2 us (34%)
  Pallas kernels  31 us (30%)
  waiting for transfers between devices  30.4 us (30%)
  local copies, waits for them, and re-layouts  3.7 us (4%)
  other arithmetic  1.29 us (1%)
    ppermute x26, starting transfers between devices, swap(): lax.ppermute(value, axis, [(i, i ^ s) for i in range(lax.axis_size(axis))])  34.2 us
    ppermute x26, waiting for transfers between devices, swap(): lax.ppermute(value, axis, [(i, i ^ s) for i in range(lax.axis_size(axis))])  30.4 us
    pallas_call x6, Pallas kernels, expert_call(): pl.pallas_call(functools.partial(expert_kernel, counts, order, first, len...  23.2 us
    unnamed x16, local copies, waits for them, and re-layouts  3.66 us
    pallas_call x1, Pallas kernels, pack(): pl.pallas_call(functools.partial(pack_kernel, experts, capacity), out_sha...  3.5 us
    pallas_call x1, Pallas kernels, adam(): pl.pallas_call(adam_kernel, out_shape=[shape] * 3 + [jax.ShapeDtypeStruct...  2.07 us
  transfers between devices with their start and end apart: 26, of which 12 were waited for; matrix products, arithmetic and copies ran while one was open for 0% of the time, Pallas kernels for 26%

profile of v11, /device:TPU:0, one launch (start us, length us, event | category | flops | bytes accessed | tf_op | source)
XLA Modules:
  0.0 101.4 jit_solution(17574234424724584811)
XLA Ops:
  2.0 3.0 %collective-permute-start.3 = (bf16[256,512]{1,0:T(8,128)(2,1)S(1)}, bf16[256,512]{1,0:T(8,128)(2,1)S(1)}, u32[]{:S(2)}, u32[]{:S(2)}) collective-permute-start(bf16[256,512]{1,0:T(8,128)(2,1)S(1)} %get-tuple-element.101.one_ref), channel_id=1, source_target_pairs={{0,16},{8,24},{16,0},{24,8},{1,17},{9,25},{17,1},{25,9},{2,18},{10... | collective-permute-start | bytes 786440 | tf_op jit(solution)/shard_map/ppermute | solution.py:459
  10.1 3.5 %pack_rows.1 = (bf16[256,512]{1,0:T(8,128)(2,1)S(1)}, bf16[256,512]{1,0:T(8,128)(2,1)S(1)}, bf16[256,512]{1,0:T(8,128)(2,1)S(1)}, bf16[256,512]{1,0:T(8,128)(2,1...) custom-call(s32[1]{0:T(128)} %bitcast.1.me_ref, ...), custom_call_target="tpu_custom_call" | custom-call | flops 3221225472 | bytes 6291456 | tf_op jit(solution)/shard_map/pack_rows/pallas_call | solution.py:85
  15.0 2.6 %collective-permute-start.9 = (bf16[256,512]{1,0:T(8,128)(2,1)S(1)}, bf16[256,512]{1,0:T(8,128)(2,1)S(1)}, u32[]{:S(2)}, u32[]{:S(2)}) collective-permute-start(bf16[256,512]{1,0:T(8,128)(2,1)S(1)} %get-tuple-element.62), channel_id=1, source_target_pairs={{0,4},{1,5},{2,6},{3,7},{4,0},{5,1},{6,2},{7,3},{8,12},{9,13},{10,... | collective-permute-start | bytes 786440 | tf_op jit(solution)/shard_map/ppermute | solution.py:459
  19.2 7.7 %collective-permute-done.2.refs_4_.refs_3_ = bf16[2,256,512]{2,1,0:T(8,128)(2,1)S(1)} collective-permute-done((bf16[2,256,512]{2,1,0:T(8,128)(2,1)S(1)}, bf16[2,256,512]{2,1,0:T(8,128)(2,1)S(1)}, u32[]{:S(2)}, u32[]{:S(2)}) %collective-permute-start.2) | collective-permute-done | bytes 524320 | tf_op jit(solution)/shard_map/ppermute | solution.py:459
  26.9 1.6 %collective-permute-start.8 = (bf16[256,512]{1,0:T(8,128)(2,1)S(1)}, bf16[256,512]{1,0:T(8,128)(2,1)S(1)}, u32[]{:S(2)}, u32[]{:S(2)}) collective-permute-start(bf16[256,512]{1,0:T(8,128)(2,1)S(1)} %get-tuple-element.61), channel_id=1, source_target_pairs={{0,2},{1,3},{2,0},{3,1},{4,6},{5,7},{6,4},{7,5},{8,10},{9,11},{10,... | collective-permute-start | bytes 786440 | tf_op jit(solution)/shard_map/ppermute | solution.py:459
  28.5 4.9 %expert_rows.6 = (f32[4,2,256,512]{3,2,1,0:T(8,128)S(1)}, f32[256,256]{1,0:T(8,128)S(1)}, f32[2,256]{1,0:T(2,128)S(1)}, bf16[256,512]{1,0:T(8,128)(2,1)S(1)}, bf16[256,512]{1,0:T(8,128)(2,1)S(1)}) custom-call(bf16[256,512]{1,0:T(8,128)(2,1)S(1)} %get-tuple-element.53.refs_0_, bf16[256,512]{1,0:T(8,128)(2,1)S(1)} %collective-permute-done.refs_1_, ...), custom_call_target="tpu_custom_call" | custom-call | flops 1572864 | bytes 131072 | tf_op jit(solution)/shard_map/expert_rows/pallas_call | solution.py:289
  33.4 2.5 %collective-permute-start.6 = (bf16[256,512]{1,0:T(8,128)(2,1)S(1)}, bf16[256,512]{1,0:T(8,128)(2,1)S(1)}, u32[]{:S(2)}, u32[]{:S(2)}) collective-permute-start(bf16[256,512]{1,0:T(8,128)(2,1)S(1)} %get-tuple-element.59), channel_id=1, source_target_pairs={{0,6},{1,7},{2,4},{3,5},{4,2},{5,3},{6,0},{7,1},{8,14},{9,15},{10,... | collective-permute-start | bytes 786440 | tf_op jit(solution)/shard_map/ppermute | solution.py:459
  36.3 2.7 %collective-permute-start.5 = (bf16[256,512]{1,0:T(8,128)(2,1)S(1)}, bf16[256,512]{1,0:T(8,128)(2,1)S(1)}, u32[]{:S(2)}, u32[]{:S(2)}) collective-permute-start(bf16[256,512]{1,0:T(8,128)(2,1)S(1)} %get-tuple-element.58), channel_id=1, source_target_pairs={{0,7},{1,6},{2,5},{3,4},{4,3},{5,2},{6,1},{7,0},{8,15},{9,14},{10,... | collective-permute-start | bytes 786440 | tf_op jit(solution)/shard_map/ppermute | solution.py:459
  39.0 2.1 %collective-permute-done.10.refs_1_ = bf16[256,512]{1,0:T(8,128)(2,1)S(1)} collective-permute-done((bf16[256,512]{1,0:T(8,128)(2,1)S(1)}, bf16[256,512]{1,0:T(8,128)(2,1)S(1)}, u32[]{:S(2)}, u32[]{:S(2)}) %collective-permute-start.10) | collective-permute-done | bytes 262176 | tf_op jit(solution)/shard_map/ppermute | solution.py:459
  41.2 5.1 %expert_rows.7 = (f32[4,2,256,512]{3,2,1,0:T(8,128)S(1)}, f32[256,256]{1,0:T(8,128)S(1)}, f32[2,256]{1,0:T(2,128)S(1)}) custom-call(bf16[256,512]{1,0:T(8,128)(2,1)S(1)} %collective-permute-done.9.refs_0_, bf16[256,512]{1,0:T(8,128)(2,1)S(1)} %collective-permute-done.10.refs_1_, bf16[256,256]{1,0:T(8,128)(2,1)S(1)} %copy-done, ...), custom_call_target="tpu_custom_call" | custom-call | flops 1572864 | bytes 131072 | tf_op jit(solution)/shard_map/expert_rows/pallas_call | solution.py:289
  46.3 8.5 %collective-permute-done.8.refs_0_ = bf16[256,512]{1,0:T(8,128)(2,1)S(1)} collective-permute-done((bf16[256,512]{1,0:T(8,128)(2,1)S(1)}, bf16[256,512]{1,0:T(8,128)(2,1)S(1)}, u32[]{:S(2)}, u32[]{:S(2)}) %collective-permute-start.8) | collective-permute-done | bytes 262176 | tf_op jit(solution)/shard_map/ppermute | solution.py:459
  54.8 3.2 %expert_rows.8 = (f32[4,2,256,512]{3,2,1,0:T(8,128)S(1)}, f32[256,256]{1,0:T(8,128)S(1)}, f32[1,256]{1,0:T(1,128)S(1)}) custom-call(bf16[256,512]{1,0:T(8,128)(2,1)S(1)} %collective-permute-done.8.refs_0_, bf16[256,256]{1,0:T(8,128)(2,1)S(1)} %copy-done, bf16[2,256,512]{2,1,0:T(8,128)(2,1)S(1)} %pair.2.refs_3_.refs_2_, ...), custom_call_target="tpu_custom_call" | custom-call | flops 786432 | bytes 65536 | tf_op jit(solution)/shard_map/expert_rows/pallas_call | solution.py:289
  58.1 3.2 %expert_rows.9 = (f32[4,2,256,512]{3,2,1,0:T(8,128)S(1)}, f32[256,256]{1,0:T(8,128)S(1)}, f32[1,256]{1,0:T(1,128)S(1)}) custom-call(bf16[256,512]{1,0:T(8,128)(2,1)S(1)} %collective-permute-done.7.refs_0_, bf16[256,256]{1,0:T(8,128)(2,1)S(1)} %copy-done, bf16[2,256,512]{2,1,0:T(8,128)(2,1)S(1)} %pair.2.refs_3_.refs_2_, ...), custom_call_target="tpu_custom_call" | custom-call | flops 786432 | bytes 65536 | tf_op jit(solution)/shard_map/expert_rows/pallas_call | solution.py:289
  61.3 3.2 %expert_rows.10 = (f32[4,2,256,512]{3,2,1,0:T(8,128)S(1)}, f32[256,256]{1,0:T(8,128)S(1)}, f32[1,256]{1,0:T(1,128)S(1)}) custom-call(bf16[256,512]{1,0:T(8,128)(2,1)S(1)} %collective-permute-done.6.refs_0_, bf16[256,256]{1,0:T(8,128)(2,1)S(1)} %copy-done, bf16[2,256,512]{2,1,0:T(8,128)(2,1)S(1)} %pair.2.refs_3_.refs_2_, ...), custom_call_target="tpu_custom_call" | custom-call | flops 786432 | bytes 65536 | tf_op jit(solution)/shard_map/expert_rows/pallas_call | solution.py:289
  64.6 3.5 %expert_rows.11 = (f32[4,2,256,512]{3,2,1,0:T(8,128)S(1)}, f32[64,256]{1,0:T(8,128)S(1)}, f32[64,256]{1,0:T(8,128)S(1)}, f32[64,256]{1,0:T(8,128)S(1)}, f32[64,256]{1,0:T(8,128)S(1)}, /*index=5*/f32[8,256]{1,0:T(8,128)S(1)}) custom-call(bf16[256,512]{1,0:T(8,128)(2,1)S(1)} %collective-permute-done.5.refs_0_, bf16[256,256]{1,0:T(8,128)(2,1)S(1)} %copy-done, ...), custom_call_target="tpu_custom_call" | custom-call | flops 786432 | bytes 65536 | tf_op jit(solution)/shard_map/expert_rows/pallas_call | solution.py:289
  68.2 3.4 %collective-permute-start.13 = (f32[64,256]{1,0:T(8,128)S(1)}, f32[64,256]{1,0:T(8,128)S(1)}, u32[]{:S(2)}, u32[]{:S(2)}) collective-permute-start(f32[64,256]{1,0:T(8,128)S(1)} %get-tuple-element.82), channel_id=1, source_target_pairs={{0,24},{8,16},{16,8},{24,0},{1,25},{9,17},{17,9},{25,1},{2,26},{10... | collective-permute-start | bytes 196616 | tf_op jit(solution)/shard_map/ppermute | solution.py:459
  71.6 1.5 %collective-permute-done.11.q1 = f32[64,256]{1,0:T(8,128)S(1)} collective-permute-done((f32[64,256]{1,0:T(8,128)S(1)}, f32[64,256]{1,0:T(8,128)S(1)}, u32[]{:S(2)}, u32[]{:S(2)}) %collective-permute-start.11) | collective-permute-done | bytes 65568 | tf_op jit(solution)/shard_map/ppermute | solution.py:459
  74.8 1.5 %collective-permute-start.22 = (bf16[2,256,512]{2,1,0:T(8,128)(2,1)S(1)}, bf16[2,256,512]{2,1,0:T(8,128)(2,1)S(1)}, u32[]{:S(2)}, u32[]{:S(2)}) collective-permute-start(bf16[2,256,512]{2,1,0:T(8,128)(2,1)S(1)} %get-tuple-element.92), channel_id=1, source_target_pairs={{0,8},{8,0},{16,24},{24,16},{1,9},{9,1},{17,25},{25,17},{2,10},{10... | collective-permute-start | bytes 1572872 | tf_op jit(solution)/shard_map/ppermute | solution.py:459
  76.3 2.0 %collective-permute-start.23 = (bf16[2,256,512]{2,1,0:T(8,128)(2,1)S(1)}, bf16[2,256,512]{2,1,0:T(8,128)(2,1)S(1)}, u32[]{:S(2)}, u32[]{:S(2)}) collective-permute-start(bf16[2,256,512]{2,1,0:T(8,128)(2,1)S(1)} %get-tuple-element.93), channel_id=1, source_target_pairs={{0,16},{8,24},{16,0},{24,8},{1,17},{9,25},{17,1},{25,9},{2,18},{10... | collective-permute-start | bytes 1572872 | tf_op jit(solution)/shard_map/ppermute | solution.py:459
  79.7 5.0 %collective-permute-start.16 = (f32[40,256]{1,0:T(8,128)S(1)}, f32[40,256]{1,0:T(8,128)S(1)}, u32[]{:S(2)}, u32[]{:S(2)}) collective-permute-start(f32[40,256]{1,0:T(8,128)S(1)} %get-tuple-element.88), channel_id=1, source_target_pairs={{0,4},{1,5},{2,6},{3,7},{4,0},{5,1},{6,2},{7,3},{8,12},{9,13},{10,... | collective-permute-start | bytes 122888 | tf_op jit(solution)/shard_map/ppermute | solution.py:459
  84.8 2.8 %collective-permute-done.16.refs_2_ = f32[40,256]{1,0:T(8,128)S(1)} collective-permute-done((f32[40,256]{1,0:T(8,128)S(1)}, f32[40,256]{1,0:T(8,128)S(1)}, u32[]{:S(2)}, u32[]{:S(2)}) %collective-permute-start.16) | collective-permute-done | bytes 40992 | tf_op jit(solution)/shard_map/ppermute | solution.py:459
  87.6 3.0 %collective-permute-done.17.refs_3_ = f32[40,256]{1,0:T(8,128)S(1)} collective-permute-done((f32[40,256]{1,0:T(8,128)S(1)}, f32[40,256]{1,0:T(8,128)S(1)}, u32[]{:S(2)}, u32[]{:S(2)}) %collective-permute-start.17) | collective-permute-done | bytes 40992 | tf_op jit(solution)/shard_map/ppermute | solution.py:459
  93.5 2.0 %collective-permute-start.21 = (f32[64,256]{1,0:T(8,128)S(1)}, f32[64,256]{1,0:T(8,128)S(1)}, u32[]{:S(2)}, u32[]{:S(2)}) collective-permute-start(f32[64,256]{1,0:T(8,128)S(1)} %join.1.refs_0_), channel_id=1, source_target_pairs={{0,24},{8,16},{16,8},{24,0},{1,25},{9,17},{17,9},{25,1},{2,26},{10... | collective-permute-start | bytes 196616 | tf_op jit(solution)/shard_map/ppermute | solution.py:459
  98.3 2.1 %adam.1 = (f32[1,2,256,512]{3,2,1,0:T(8,128)}, f32[1,2,256,512]{3,2,1,0:T(8,128)}, f32[1,2,256,512]{3,2,1,0:T(8,128)}, f32[8,128]{1,0:T(8,128)S(1)}) custom-call(f32[1,2,256,512]{3,2,1,0:T(8,128)S(1)} %copy-done.1, f32[1,2,256,512]{3,2,1,0:T(8,128)S(1)} %copy-done.2, f32[1,2,256,512]{3,2,1,0:T(8,128)S(1)} %copy-done.3, ...), custom_call_target="tpu_custom_call" | custom-call | flops 5242880 | bytes 2097152 | tf_op jit(solution)/shard_map/adam/pallas_call | solution.py:443
  (64 shorter events, 19.7 us)
Async XLA Ops:
  2.0 12.3 %collective-permute-start.3 = (bf16[256,512]{1,0:T(8,128)(2,1)S(1)}, bf16[256,512]{1,0:T(8,128)(2,1)S(1)}, u32[]{:S(2)}, u32[]{:S(2)}) collective-permute-start(bf16[256,512]{1,0:T(8,128)(2,1)S(1)} %get-tuple-element.101.one_ref), channel_id=1, source_target_pairs={{0,16},{8,24},{16,0},{24,8},{1,17},{9,25},{17,1},{25,9},{2,18},{10... | collective-permute-start | bytes 786440 | tf_op jit(solution)/shard_map/ppermute | solution.py:459
  5.0 8.6 %collective-permute-start.1 = (bf16[256,512]{1,0:T(8,128)(2,1)S(1)}, bf16[256,512]{1,0:T(8,128)(2,1)S(1)}, u32[]{:S(2)}, u32[]{:S(2)}) collective-permute-start(bf16[256,512]{1,0:T(8,128)(2,1)S(1)} %get-tuple-element.102.one_ref), channel_id=1, source_target_pairs={{0,8},{8,0},{16,24},{24,16},{1,9},{9,1},{17,25},{25,17},{2,10},{10... | collective-permute-start | bytes 786440 | tf_op jit(solution)/shard_map/ppermute | solution.py:459
  13.7 13.2 %collective-permute-start.2 = (bf16[2,256,512]{2,1,0:T(8,128)(2,1)S(1)}, bf16[2,256,512]{2,1,0:T(8,128)(2,1)S(1)}, u32[]{:S(2)}, u32[]{:S(2)}) collective-permute-start(bf16[2,256,512]{2,1,0:T(8,128)(2,1)S(1)} %pair.2.refs_3_.refs_2_), channel_id=1, source_target_pairs={{0,16},{8,24},{16,0},{24,8},{1,17},{9,25},{17,1},{25,9},{2,18},{10... | collective-permute-start | bytes 1572872 | tf_op jit(solution)/shard_map/ppermute | solution.py:459
  14.3 14.1 %collective-permute-start.4 = (bf16[2,256,512]{2,1,0:T(8,128)(2,1)S(1)}, bf16[2,256,512]{2,1,0:T(8,128)(2,1)S(1)}, u32[]{:S(2)}, u32[]{:S(2)}) collective-permute-start(bf16[2,256,512]{2,1,0:T(8,128)(2,1)S(1)} %pair.3.refs_5_.refs_4_), channel_id=1, source_target_pairs={{0,8},{8,0},{16,24},{24,16},{1,9},{9,1},{17,25},{25,17},{2,10},{10... | collective-permute-start | bytes 1572872 | tf_op jit(solution)/shard_map/ppermute | solution.py:459
  15.0 2.8 %collective-permute-start = (bf16[256,512]{1,0:T(8,128)(2,1)S(1)}, bf16[256,512]{1,0:T(8,128)(2,1)S(1)}, u32[]{:S(2)}, u32[]{:S(2)}) collective-permute-start(bf16[256,512]{1,0:T(8,128)(2,1)S(1)} %get-tuple-element.54), channel_id=1, source_target_pairs={{0,1},{1,0},{2,3},{3,2},{4,5},{5,4},{6,7},{7,6},{8,9},{9,8},{10,11... | collective-permute-start | bytes 786440 | tf_op jit(solution)/shard_map/ppermute | solution.py:459
  15.0 21.3 %collective-permute-start.9 = (bf16[256,512]{1,0:T(8,128)(2,1)S(1)}, bf16[256,512]{1,0:T(8,128)(2,1)S(1)}, u32[]{:S(2)}, u32[]{:S(2)}) collective-permute-start(bf16[256,512]{1,0:T(8,128)(2,1)S(1)} %get-tuple-element.62), channel_id=1, source_target_pairs={{0,4},{1,5},{2,6},{3,7},{4,0},{5,1},{6,2},{7,3},{8,12},{9,13},{10,... | collective-permute-start | bytes 786440 | tf_op jit(solution)/shard_map/ppermute | solution.py:459
  17.6 23.6 %collective-permute-start.10 = (bf16[256,512]{1,0:T(8,128)(2,1)S(1)}, bf16[256,512]{1,0:T(8,128)(2,1)S(1)}, u32[]{:S(2)}, u32[]{:S(2)}) collective-permute-start(bf16[256,512]{1,0:T(8,128)(2,1)S(1)} %get-tuple-element.63), channel_id=1, source_target_pairs={{0,5},{1,4},{2,7},{3,6},{4,1},{5,0},{6,3},{7,2},{8,13},{9,12},{10,... | collective-permute-start | bytes 786440 | tf_op jit(solution)/shard_map/ppermute | solution.py:459
  17.7 40.3 %collective-permute-start.7 = (bf16[256,512]{1,0:T(8,128)(2,1)S(1)}, bf16[256,512]{1,0:T(8,128)(2,1)S(1)}, u32[]{:S(2)}, u32[]{:S(2)}) collective-permute-start(bf16[256,512]{1,0:T(8,128)(2,1)S(1)} %get-tuple-element.60), channel_id=1, source_target_pairs={{0,3},{1,2},{2,1},{3,0},{4,7},{5,6},{6,5},{7,4},{8,11},{9,10},{10,... | collective-permute-start | bytes 786440 | tf_op jit(solution)/shard_map/ppermute | solution.py:459
  26.9 27.9 %collective-permute-start.8 = (bf16[256,512]{1,0:T(8,128)(2,1)S(1)}, bf16[256,512]{1,0:T(8,128)(2,1)S(1)}, u32[]{:S(2)}, u32[]{:S(2)}) collective-permute-start(bf16[256,512]{1,0:T(8,128)(2,1)S(1)} %get-tuple-element.61), channel_id=1, source_target_pairs={{0,2},{1,3},{2,0},{3,1},{4,6},{5,7},{6,4},{7,5},{8,10},{9,11},{10,... | collective-permute-start | bytes 786440 | tf_op jit(solution)/shard_map/ppermute | solution.py:459
  33.4 27.9 %collective-permute-start.6 = (bf16[256,512]{1,0:T(8,128)(2,1)S(1)}, bf16[256,512]{1,0:T(8,128)(2,1)S(1)}, u32[]{:S(2)}, u32[]{:S(2)}) collective-permute-start(bf16[256,512]{1,0:T(8,128)(2,1)S(1)} %get-tuple-element.59), channel_id=1, source_target_pairs={{0,6},{1,7},{2,4},{3,5},{4,2},{5,3},{6,0},{7,1},{8,14},{9,15},{10,... | collective-permute-start | bytes 786440 | tf_op jit(solution)/shard_map/ppermute | solution.py:459
  36.3 28.2 %collective-permute-start.5 = (bf16[256,512]{1,0:T(8,128)(2,1)S(1)}, bf16[256,512]{1,0:T(8,128)(2,1)S(1)}, u32[]{:S(2)}, u32[]{:S(2)}) collective-permute-start(bf16[256,512]{1,0:T(8,128)(2,1)S(1)} %get-tuple-element.58), channel_id=1, source_target_pairs={{0,7},{1,6},{2,5},{3,4},{4,3},{5,2},{6,1},{7,0},{8,15},{9,14},{10,... | collective-permute-start | bytes 786440 | tf_op jit(solution)/shard_map/ppermute | solution.py:459
  68.0 5.1 %collective-permute-start.11 = (f32[64,256]{1,0:T(8,128)S(1)}, f32[64,256]{1,0:T(8,128)S(1)}, u32[]{:S(2)}, u32[]{:S(2)}) collective-permute-start(f32[64,256]{1,0:T(8,128)S(1)} %get-tuple-element.80), channel_id=1, source_target_pairs={{0,8},{8,0},{16,24},{24,16},{1,9},{9,1},{17,25},{25,17},{2,10},{10... | collective-permute-start | bytes 196616 | tf_op jit(solution)/shard_map/ppermute | solution.py:459
  68.1 5.1 %collective-permute-start.12 = (f32[64,256]{1,0:T(8,128)S(1)}, f32[64,256]{1,0:T(8,128)S(1)}, u32[]{:S(2)}, u32[]{:S(2)}) collective-permute-start(f32[64,256]{1,0:T(8,128)S(1)} %get-tuple-element.81), channel_id=1, source_target_pairs={{0,16},{8,24},{16,0},{24,8},{1,17},{9,25},{17,1},{25,9},{2,18},{10... | collective-permute-start | bytes 196616 | tf_op jit(solution)/shard_map/ppermute | solution.py:459
  68.2 6.4 %collective-permute-start.13 = (f32[64,256]{1,0:T(8,128)S(1)}, f32[64,256]{1,0:T(8,128)S(1)}, u32[]{:S(2)}, u32[]{:S(2)}) collective-permute-start(f32[64,256]{1,0:T(8,128)S(1)} %get-tuple-element.82), channel_id=1, source_target_pairs={{0,24},{8,16},{16,8},{24,0},{1,25},{9,17},{17,9},{25,1},{2,26},{10... | collective-permute-start | bytes 196616 | tf_op jit(solution)/shard_map/ppermute | solution.py:459
  74.8 15.8 %collective-permute-start.22 = (bf16[2,256,512]{2,1,0:T(8,128)(2,1)S(1)}, bf16[2,256,512]{2,1,0:T(8,128)(2,1)S(1)}, u32[]{:S(2)}, u32[]{:S(2)}) collective-permute-start(bf16[2,256,512]{2,1,0:T(8,128)(2,1)S(1)} %get-tuple-element.92), channel_id=1, source_target_pairs={{0,8},{8,0},{16,24},{24,16},{1,9},{9,1},{17,25},{25,17},{2,10},{10... | collective-permute-start | bytes 1572872 | tf_op jit(solution)/shard_map/ppermute | solution.py:459
  76.3 14.3 %collective-permute-start.23 = (bf16[2,256,512]{2,1,0:T(8,128)(2,1)S(1)}, bf16[2,256,512]{2,1,0:T(8,128)(2,1)S(1)}, u32[]{:S(2)}, u32[]{:S(2)}) collective-permute-start(bf16[2,256,512]{2,1,0:T(8,128)(2,1)S(1)} %get-tuple-element.93), channel_id=1, source_target_pairs={{0,16},{8,24},{16,0},{24,8},{1,17},{9,25},{17,1},{25,9},{2,18},{10... | collective-permute-start | bytes 1572872 | tf_op jit(solution)/shard_map/ppermute | solution.py:459
  79.6 5.1 %collective-permute-start.15 = (f32[40,256]{1,0:T(8,128)S(1)}, f32[40,256]{1,0:T(8,128)S(1)}, u32[]{:S(2)}, u32[]{:S(2)}) collective-permute-start(f32[40,256]{1,0:T(8,128)S(1)} %get-tuple-element.87), channel_id=1, source_target_pairs={{0,2},{1,3},{2,0},{3,1},{4,6},{5,7},{6,4},{7,5},{8,10},{9,11},{10,... | collective-permute-start | bytes 122888 | tf_op jit(solution)/shard_map/ppermute | solution.py:459
  79.7 7.9 %collective-permute-start.16 = (f32[40,256]{1,0:T(8,128)S(1)}, f32[40,256]{1,0:T(8,128)S(1)}, u32[]{:S(2)}, u32[]{:S(2)}) collective-permute-start(f32[40,256]{1,0:T(8,128)S(1)} %get-tuple-element.88), channel_id=1, source_target_pairs={{0,4},{1,5},{2,6},{3,7},{4,0},{5,1},{6,2},{7,3},{8,12},{9,13},{10,... | collective-permute-start | bytes 122888 | tf_op jit(solution)/shard_map/ppermute | solution.py:459
  84.8 5.8 %collective-permute-start.17 = (f32[40,256]{1,0:T(8,128)S(1)}, f32[40,256]{1,0:T(8,128)S(1)}, u32[]{:S(2)}, u32[]{:S(2)}) collective-permute-start(f32[40,256]{1,0:T(8,128)S(1)} %get-tuple-element.89), channel_id=1, source_target_pairs={{0,6},{1,7},{2,4},{3,5},{4,2},{5,3},{6,0},{7,1},{8,14},{9,15},{10,... | collective-permute-start | bytes 122888 | tf_op jit(solution)/shard_map/ppermute | solution.py:459
  90.7 7.5 %collective-permute-start.24 = (bf16[256,512]{1,0:T(8,128)(2,1)S(1)}, bf16[256,512]{1,0:T(8,128)(2,1)S(1)}, u32[]{:S(2)}, u32[]{:S(2)}) collective-permute-start(bf16[256,512]{1,0:T(8,128)(2,1)S(1)} %get-tuple-element.94), channel_id=1, source_target_pairs={{0,16},{8,24},{16,0},{24,8},{1,17},{9,25},{17,1},{25,9},{2,18},{10... | collective-permute-start | bytes 786440 | tf_op jit(solution)/shard_map/ppermute | solution.py:459
  90.9 7.4 %collective-permute-start.25 = (bf16[256,512]{1,0:T(8,128)(2,1)S(1)}, bf16[256,512]{1,0:T(8,128)(2,1)S(1)}, u32[]{:S(2)}, u32[]{:S(2)}) collective-permute-start(bf16[256,512]{1,0:T(8,128)(2,1)S(1)} %get-tuple-element.95), channel_id=1, source_target_pairs={{0,8},{8,0},{16,24},{24,16},{1,9},{9,1},{17,25},{25,17},{2,10},{10... | collective-permute-start | bytes 786440 | tf_op jit(solution)/shard_map/ppermute | solution.py:459
  93.5 7.2 %collective-permute-start.21 = (f32[64,256]{1,0:T(8,128)S(1)}, f32[64,256]{1,0:T(8,128)S(1)}, u32[]{:S(2)}, u32[]{:S(2)}) collective-permute-start(f32[64,256]{1,0:T(8,128)S(1)} %join.1.refs_0_), channel_id=1, source_target_pairs={{0,24},{8,16},{16,8},{24,0},{1,25},{9,17},{17,9},{25,1},{2,26},{10... | collective-permute-start | bytes 196616 | tf_op jit(solution)/shard_map/ppermute | solution.py:459
  95.5 5.2 %collective-permute-start.20 = (f32[64,256]{1,0:T(8,128)S(1)}, f32[64,256]{1,0:T(8,128)S(1)}, u32[]{:S(2)}, u32[]{:S(2)}) collective-permute-start(f32[64,256]{1,0:T(8,128)S(1)} %join.1.refs_0_), channel_id=1, source_target_pairs={{0,16},{8,24},{16,0},{24,8},{1,17},{9,25},{17,1},{25,9},{2,18},{10... | collective-permute-start | bytes 196616 | tf_op jit(solution)/shard_map/ppermute | solution.py:459
  95.7 5.1 %collective-permute-start.19 = (f32[64,256]{1,0:T(8,128)S(1)}, f32[64,256]{1,0:T(8,128)S(1)}, u32[]{:S(2)}, u32[]{:S(2)}) collective-permute-start(f32[64,256]{1,0:T(8,128)S(1)} %join.1.refs_0_), channel_id=1, source_target_pairs={{0,8},{8,0},{16,24},{24,16},{1,9},{9,1},{17,25},{25,17},{2,10},{10... | collective-permute-start | bytes 196616 | tf_op jit(solution)/shard_map/ppermute | solution.py:459
  (10 other events, 95.3 us)

commit v12 on v11

--- a/solution.py
+++ b/solution.py
@@ -483,7 +483,7 @@
     ups, downs = pair(up, near_up, place), pair(down, near_down, place)
     weights = [ups, swap(ups, "dp", 2), downs, swap(downs, "dp", 1)]
     if in_turns(experts):
-        batches, later = ((0, 1), (4, 5), (2,), (3,), (6,), (7,)), (6, 7)
+        batches, later = ((0, 4), (1, 5), (2, 3), (6, 7)), ()
     else:
         batches, later = (range(experts // 2), range(experts // 2, experts)), ()
     order = [s for batch in batches for s in batch]

time: 102 us -> 101 us (level)
  waiting for transfers between devices: 30.4 us -> 38 us
  starting transfers between devices: 34.2 us -> 29.5 us
  Pallas kernels: 31 us -> 27.5 us
    ppermute x26, waiting for transfers between devices: 30.4 us -> 38 us  [swap(): lax.ppermute(value, axis, [(i, i ^ s) for i in range(lax.axis_size(axis))])]
    ppermute x26, starting transfers between devices: 34.2 us -> 29.5 us  [swap(): lax.ppermute(value, axis, [(i, i ^ s) for i in range(lax.axis_size(axis))])]
    pallas_call x6 -> x4, Pallas kernels: 23.2 us -> 19.7 us  [expert_call(): pl.pallas_call(functools.partial(expert_kernel, counts, order, first, len...]
  transfers between devices with their start and end apart: 26 -> 26, of which waited for: 12 -> 10; matrix products, arithmetic and copies ran while one was open for 0% -> 0% of each run, Pallas kernels for 26% -> 21%
where the time goes in v12:
time: 101 us
  waiting for transfers between devices  38 us (38%)
  starting transfers between devices  29.5 us (29%)
  Pallas kernels  27.5 us (27%)
  local copies, waits for them, and re-layouts  3.7 us (4%)
  other arithmetic  1.29 us (1%)
    ppermute x26, waiting for transfers between devices, swap(): lax.ppermute(value, axis, [(i, i ^ s) for i in range(lax.axis_size(axis))])  38 us
    ppermute x26, starting transfers between devices, swap(): lax.ppermute(value, axis, [(i, i ^ s) for i in range(lax.axis_size(axis))])  29.5 us
    pallas_call x4, Pallas kernels, expert_call(): pl.pallas_call(functools.partial(expert_kernel, counts, order, first, len...  19.7 us
    unnamed x16, local copies, waits for them, and re-layouts  3.66 us
    pallas_call x1, Pallas kernels, pack(): pl.pallas_call(functools.partial(pack_kernel, experts, capacity), out_sha...  3.5 us
    pallas_call x1, Pallas kernels, adam(): pl.pallas_call(adam_kernel, out_shape=[shape] * 3 + [jax.ShapeDtypeStruct...  2.07 us
  transfers between devices with their start and end apart: 26, of which 10 were waited for; matrix products, arithmetic and copies ran while one was open for 0% of the time, Pallas kernels for 21%

profile of v12, /device:TPU:0, one launch (start us, length us, event | category | flops | bytes accessed | tf_op | source)
XLA Modules:
  0.0 100.8 jit_solution(10210315593085024127)
XLA Ops:
  2.0 3.0 %collective-permute-start.4 = (bf16[256,512]{1,0:T(8,128)(2,1)S(1)}, bf16[256,512]{1,0:T(8,128)(2,1)S(1)}, u32[]{:S(2)}, u32[]{:S(2)}) collective-permute-start(bf16[256,512]{1,0:T(8,128)(2,1)S(1)} %get-tuple-element.85.one_ref), channel_id=1, source_target_pairs={{0,16},{8,24},{16,0},{24,8},{1,17},{9,25},{17,1},{25,9},{2,18},{10... | collective-permute-start | bytes 786440 | tf_op jit(solution)/shard_map/ppermute | solution.py:459
  5.0 1.5 %collective-permute-start.2 = (bf16[256,512]{1,0:T(8,128)(2,1)S(1)}, bf16[256,512]{1,0:T(8,128)(2,1)S(1)}, u32[]{:S(2)}, u32[]{:S(2)}) collective-permute-start(bf16[256,512]{1,0:T(8,128)(2,1)S(1)} %get-tuple-element.86.one_ref), channel_id=1, source_target_pairs={{0,8},{8,0},{16,24},{24,16},{1,9},{9,1},{17,25},{25,17},{2,10},{10... | collective-permute-start | bytes 786440 | tf_op jit(solution)/shard_map/ppermute | solution.py:459
  10.1 3.5 %pack_rows.1 = (bf16[256,512]{1,0:T(8,128)(2,1)S(1)}, bf16[256,512]{1,0:T(8,128)(2,1)S(1)}, bf16[256,512]{1,0:T(8,128)(2,1)S(1)}, bf16[256,512]{1,0:T(8,128)(2,1...) custom-call(s32[1]{0:T(128)} %bitcast.1.me_ref, ...), custom_call_target="tpu_custom_call" | custom-call | flops 3221225472 | bytes 6291456 | tf_op jit(solution)/shard_map/pack_rows/pallas_call | solution.py:85
  15.0 2.6 %collective-permute-start.10 = (bf16[256,512]{1,0:T(8,128)(2,1)S(1)}, bf16[256,512]{1,0:T(8,128)(2,1)S(1)}, u32[]{:S(2)}, u32[]{:S(2)}) collective-permute-start(bf16[256,512]{1,0:T(8,128)(2,1)S(1)} %get-tuple-element.53), channel_id=1, source_target_pairs={{0,4},{1,5},{2,6},{3,7},{4,0},{5,1},{6,2},{7,3},{8,12},{9,13},{10,... | collective-permute-start | bytes 786440 | tf_op jit(solution)/shard_map/ppermute | solution.py:459
  17.7 1.6 %collective-permute-start.6 = (bf16[256,512]{1,0:T(8,128)(2,1)S(1)}, bf16[256,512]{1,0:T(8,128)(2,1)S(1)}, u32[]{:S(2)}, u32[]{:S(2)}) collective-permute-start(bf16[256,512]{1,0:T(8,128)(2,1)S(1)} %get-tuple-element.48), channel_id=1, source_target_pairs={{0,2},{1,3},{2,0},{3,1},{4,6},{5,7},{6,4},{7,5},{8,10},{9,11},{10,... | collective-permute-start | bytes 786440 | tf_op jit(solution)/shard_map/ppermute | solution.py:459
  19.3 16.9 %collective-permute-done.10.refs_1_ = bf16[256,512]{1,0:T(8,128)(2,1)S(1)} collective-permute-done((bf16[256,512]{1,0:T(8,128)(2,1)S(1)}, bf16[256,512]{1,0:T(8,128)(2,1)S(1)}, u32[]{:S(2)}, u32[]{:S(2)}) %collective-permute-start.10) | collective-permute-done | bytes 262176 | tf_op jit(solution)/shard_map/ppermute | solution.py:459
  36.2 3.1 %collective-permute-start = (bf16[256,512]{1,0:T(8,128)(2,1)S(1)}, bf16[256,512]{1,0:T(8,128)(2,1)S(1)}, u32[]{:S(2)}, u32[]{:S(2)}) collective-permute-start(bf16[256,512]{1,0:T(8,128)(2,1)S(1)} %get-tuple-element.45), channel_id=1, source_target_pairs={{0,6},{1,7},{2,4},{3,5},{4,2},{5,3},{6,0},{7,1},{8,14},{9,15},{10,... | collective-permute-start | bytes 786440 | tf_op jit(solution)/shard_map/ppermute | solution.py:459
  39.8 4.8 %expert_rows.4 = (f32[4,2,256,512]{3,2,1,0:T(8,128)S(1)}, f32[256,256]{1,0:T(8,128)S(1)}, f32[2,256]{1,0:T(2,128)S(1)}) custom-call(bf16[256,512]{1,0:T(8,128)(2,1)S(1)} %get-tuple-element.52.refs_0_, bf16[256,512]{1,0:T(8,128)(2,1)S(1)} %collective-permute-done.10.refs_1_, bf16[256,256]{1,0:T(8,128)(2,1)S(1)} %copy-done.1, ...), custom_call_target="tpu_custom_call" | custom-call | flops 1572864 | bytes 131072 | tf_op jit(solution)/shard_map/expert_rows/pallas_call | solution.py:289
  44.7 5.0 %expert_rows.5 = (f32[4,2,256,512]{3,2,1,0:T(8,128)S(1)}, f32[256,256]{1,0:T(8,128)S(1)}, f32[2,256]{1,0:T(2,128)S(1)}) custom-call(bf16[256,512]{1,0:T(8,128)(2,1)S(1)} %collective-permute-done.8.refs_0_, bf16[256,512]{1,0:T(8,128)(2,1)S(1)} %collective-permute-done.9.refs_1_, bf16[256,256]{1,0:T(8,128)(2,1)S(1)} %copy-done.1, ...), custom_call_target="tpu_custom_call" | custom-call | flops 1572864 | bytes 131072 | tf_op jit(solution)/shard_map/expert_rows/pallas_call | solution.py:289
  49.7 8.6 %collective-permute-done.7.refs_1_ = bf16[256,512]{1,0:T(8,128)(2,1)S(1)} collective-permute-done((bf16[256,512]{1,0:T(8,128)(2,1)S(1)}, bf16[256,512]{1,0:T(8,128)(2,1)S(1)}, u32[]{:S(2)}, u32[]{:S(2)}) %collective-permute-start.7) | collective-permute-done | bytes 262176 | tf_op jit(solution)/shard_map/ppermute | solution.py:459
  58.3 4.9 %expert_rows.6 = (f32[4,2,256,512]{3,2,1,0:T(8,128)S(1)}, f32[256,256]{1,0:T(8,128)S(1)}, f32[2,256]{1,0:T(2,128)S(1)}) custom-call(bf16[256,512]{1,0:T(8,128)(2,1)S(1)} %collective-permute-done.6.refs_0_, bf16[256,512]{1,0:T(8,128)(2,1)S(1)} %collective-permute-done.7.refs_1_, bf16[256,256]{1,0:T(8,128)(2,1)S(1)} %copy-done.1, ...), custom_call_target="tpu_custom_call" | custom-call | flops 1572864 | bytes 131072 | tf_op jit(solution)/shard_map/expert_rows/pallas_call | solution.py:289
  63.2 4.9 %expert_rows.7 = (f32[4,2,256,512]{3,2,1,0:T(8,128)S(1)}, f32[64,256]{1,0:T(8,128)S(1)}, f32[64,256]{1,0:T(8,128)S(1)}, f32[64,256]{1,0:T(8,128)S(1)}, f32[64,256]{1,0:T(8,128)S(1)}, /*index=5*/f32[8,256]{1,0:T(8,128)S(1)}) custom-call(bf16[256,512]{1,0:T(8,128)(2,1)S(1)} %collective-permute-done.refs_0_, ...), custom_call_target="tpu_custom_call" | custom-call | flops 1572864 | bytes 131072 | tf_op jit(solution)/shard_map/expert_rows/pallas_call | solution.py:289
  68.2 1.5 %collective-permute-start.11 = (f32[64,256]{1,0:T(8,128)S(1)}, f32[64,256]{1,0:T(8,128)S(1)}, u32[]{:S(2)}, u32[]{:S(2)}) collective-permute-start(f32[64,256]{1,0:T(8,128)S(1)} %get-tuple-element.64), channel_id=1, source_target_pairs={{0,8},{8,0},{16,24},{24,16},{1,9},{9,1},{17,25},{25,17},{2,10},{10... | collective-permute-start | bytes 196616 | tf_op jit(solution)/shard_map/ppermute | solution.py:459
  69.7 1.5 %collective-permute-start.12 = (f32[64,256]{1,0:T(8,128)S(1)}, f32[64,256]{1,0:T(8,128)S(1)}, u32[]{:S(2)}, u32[]{:S(2)}) collective-permute-start(f32[64,256]{1,0:T(8,128)S(1)} %get-tuple-element.65), channel_id=1, source_target_pairs={{0,16},{8,24},{16,0},{24,8},{1,17},{9,25},{17,1},{25,9},{2,18},{10... | collective-permute-start | bytes 196616 | tf_op jit(solution)/shard_map/ppermute | solution.py:459
  72.5 1.4 %collective-permute-done.12.q2 = f32[64,256]{1,0:T(8,128)S(1)} collective-permute-done((f32[64,256]{1,0:T(8,128)S(1)}, f32[64,256]{1,0:T(8,128)S(1)}, u32[]{:S(2)}, u32[]{:S(2)}) %collective-permute-start.12) | collective-permute-done | bytes 65568 | tf_op jit(solution)/shard_map/ppermute | solution.py:459
  73.9 2.4 %collective-permute-done.13.q3 = f32[64,256]{1,0:T(8,128)S(1)} collective-permute-done((f32[64,256]{1,0:T(8,128)S(1)}, f32[64,256]{1,0:T(8,128)S(1)}, u32[]{:S(2)}, u32[]{:S(2)}) %collective-permute-start.13) | collective-permute-done | bytes 65568 | tf_op jit(solution)/shard_map/ppermute | solution.py:459
  79.0 1.5 %collective-permute-start.15 = (f32[40,256]{1,0:T(8,128)S(1)}, f32[40,256]{1,0:T(8,128)S(1)}, u32[]{:S(2)}, u32[]{:S(2)}) collective-permute-start(f32[40,256]{1,0:T(8,128)S(1)} %get-tuple-element.71), channel_id=1, source_target_pairs={{0,2},{1,3},{2,0},{3,1},{4,6},{5,7},{6,4},{7,5},{8,10},{9,11},{10,... | collective-permute-start | bytes 122888 | tf_op jit(solution)/shard_map/ppermute | solution.py:459
  80.5 2.6 %collective-permute-start.16 = (f32[40,256]{1,0:T(8,128)S(1)}, f32[40,256]{1,0:T(8,128)S(1)}, u32[]{:S(2)}, u32[]{:S(2)}) collective-permute-start(f32[40,256]{1,0:T(8,128)S(1)} %get-tuple-element.72), channel_id=1, source_target_pairs={{0,4},{1,5},{2,6},{3,7},{4,0},{5,1},{6,2},{7,3},{8,12},{9,13},{10,... | collective-permute-start | bytes 122888 | tf_op jit(solution)/shard_map/ppermute | solution.py:459
  83.8 2.0 %collective-permute-done.16.refs_2_ = f32[40,256]{1,0:T(8,128)S(1)} collective-permute-done((f32[40,256]{1,0:T(8,128)S(1)}, f32[40,256]{1,0:T(8,128)S(1)}, u32[]{:S(2)}, u32[]{:S(2)}) %collective-permute-start.16) | collective-permute-done | bytes 40992 | tf_op jit(solution)/shard_map/ppermute | solution.py:459
  85.8 3.1 %collective-permute-done.17.refs_3_ = f32[40,256]{1,0:T(8,128)S(1)} collective-permute-done((f32[40,256]{1,0:T(8,128)S(1)}, f32[40,256]{1,0:T(8,128)S(1)}, u32[]{:S(2)}, u32[]{:S(2)}) %collective-permute-start.17) | collective-permute-done | bytes 40992 | tf_op jit(solution)/shard_map/ppermute | solution.py:459
  89.3 1.3 %collective-permute-start.24 = (bf16[256,512]{1,0:T(8,128)(2,1)S(1)}, bf16[256,512]{1,0:T(8,128)(2,1)S(1)}, u32[]{:S(2)}, u32[]{:S(2)}) collective-permute-start(bf16[256,512]{1,0:T(8,128)(2,1)S(1)} %get-tuple-element.78), channel_id=1, source_target_pairs={{0,16},{8,24},{16,0},{24,8},{1,17},{9,25},{17,1},{25,9},{2,18},{10... | collective-permute-start | bytes 786440 | tf_op jit(solution)/shard_map/ppermute | solution.py:459
  90.6 1.4 %collective-permute-start.25 = (bf16[256,512]{1,0:T(8,128)(2,1)S(1)}, bf16[256,512]{1,0:T(8,128)(2,1)S(1)}, u32[]{:S(2)}, u32[]{:S(2)}) collective-permute-start(bf16[256,512]{1,0:T(8,128)(2,1)S(1)} %get-tuple-element.79), channel_id=1, source_target_pairs={{0,8},{8,0},{16,24},{24,16},{1,9},{9,1},{17,25},{25,17},{2,10},{10... | collective-permute-start | bytes 786440 | tf_op jit(solution)/shard_map/ppermute | solution.py:459
  95.4 1.4 %collective-permute-start.19 = (f32[64,256]{1,0:T(8,128)S(1)}, f32[64,256]{1,0:T(8,128)S(1)}, u32[]{:S(2)}, u32[]{:S(2)}) collective-permute-start(f32[64,256]{1,0:T(8,128)S(1)} %join.1.refs_0_), channel_id=1, source_target_pairs={{0,8},{8,0},{16,24},{24,16},{1,9},{9,1},{17,25},{25,17},{2,10},{10... | collective-permute-start | bytes 196616 | tf_op jit(solution)/shard_map/ppermute | solution.py:459
  98.0 2.1 %adam.1 = (f32[1,2,256,512]{3,2,1,0:T(8,128)}, f32[1,2,256,512]{3,2,1,0:T(8,128)}, f32[1,2,256,512]{3,2,1,0:T(8,128)}, f32[8,128]{1,0:T(8,128)S(1)}) custom-call(f32[1,2,256,512]{3,2,1,0:T(8,128)S(1)} %copy-done, f32[1,2,256,512]{3,2,1,0:T(8,128)S(1)} %copy-done.2, f32[1,2,256,512]{3,2,1,0:T(8,128)S(1)} %copy-done.3, ...), custom_call_target="tpu_custom_call" | custom-call | flops 5242880 | bytes 2097152 | tf_op jit(solution)/shard_map/adam/pallas_call | solution.py:443
  (62 shorter events, 17.2 us)
Async XLA Ops:
  2.0 12.3 %collective-permute-start.4 = (bf16[256,512]{1,0:T(8,128)(2,1)S(1)}, bf16[256,512]{1,0:T(8,128)(2,1)S(1)}, u32[]{:S(2)}, u32[]{:S(2)}) collective-permute-start(bf16[256,512]{1,0:T(8,128)(2,1)S(1)} %get-tuple-element.85.one_ref), channel_id=1, source_target_pairs={{0,16},{8,24},{16,0},{24,8},{1,17},{9,25},{17,1},{25,9},{2,18},{10... | collective-permute-start | bytes 786440 | tf_op jit(solution)/shard_map/ppermute | solution.py:459
  5.0 8.6 %collective-permute-start.2 = (bf16[256,512]{1,0:T(8,128)(2,1)S(1)}, bf16[256,512]{1,0:T(8,128)(2,1)S(1)}, u32[]{:S(2)}, u32[]{:S(2)}) collective-permute-start(bf16[256,512]{1,0:T(8,128)(2,1)S(1)} %get-tuple-element.86.one_ref), channel_id=1, source_target_pairs={{0,8},{8,0},{16,24},{24,16},{1,9},{9,1},{17,25},{25,17},{2,10},{10... | collective-permute-start | bytes 786440 | tf_op jit(solution)/shard_map/ppermute | solution.py:459
  13.7 22.5 %collective-permute-start.3 = (bf16[2,256,512]{2,1,0:T(8,128)(2,1)S(1)}, bf16[2,256,512]{2,1,0:T(8,128)(2,1)S(1)}, u32[]{:S(2)}, u32[]{:S(2)}) collective-permute-start(bf16[2,256,512]{2,1,0:T(8,128)(2,1)S(1)} %pair.2.refs_3_), channel_id=1, source_target_pairs={{0,16},{8,24},{16,0},{24,8},{1,17},{9,25},{17,1},{25,9},{2,18},{10... | collective-permute-start | bytes 1572872 | tf_op jit(solution)/shard_map/ppermute | solution.py:459
  14.3 25.1 %collective-permute-start.5 = (bf16[2,256,512]{2,1,0:T(8,128)(2,1)S(1)}, bf16[2,256,512]{2,1,0:T(8,128)(2,1)S(1)}, u32[]{:S(2)}, u32[]{:S(2)}) collective-permute-start(bf16[2,256,512]{2,1,0:T(8,128)(2,1)S(1)} %pair.3.refs_5_), channel_id=1, source_target_pairs={{0,8},{8,0},{16,24},{24,16},{1,9},{9,1},{17,25},{25,17},{2,10},{10... | collective-permute-start | bytes 1572872 | tf_op jit(solution)/shard_map/ppermute | solution.py:459
  15.0 2.8 %collective-permute-start.8 = (bf16[256,512]{1,0:T(8,128)(2,1)S(1)}, bf16[256,512]{1,0:T(8,128)(2,1)S(1)}, u32[]{:S(2)}, u32[]{:S(2)}) collective-permute-start(bf16[256,512]{1,0:T(8,128)(2,1)S(1)} %get-tuple-element.50), channel_id=1, source_target_pairs={{0,1},{1,0},{2,3},{3,2},{4,5},{5,4},{6,7},{7,6},{8,9},{9,8},{10,11... | collective-permute-start | bytes 786440 | tf_op jit(solution)/shard_map/ppermute | solution.py:459
  15.0 21.2 %collective-permute-start.10 = (bf16[256,512]{1,0:T(8,128)(2,1)S(1)}, bf16[256,512]{1,0:T(8,128)(2,1)S(1)}, u32[]{:S(2)}, u32[]{:S(2)}) collective-permute-start(bf16[256,512]{1,0:T(8,128)(2,1)S(1)} %get-tuple-element.53), channel_id=1, source_target_pairs={{0,4},{1,5},{2,6},{3,7},{4,0},{5,1},{6,2},{7,3},{8,12},{9,13},{10,... | collective-permute-start | bytes 786440 | tf_op jit(solution)/shard_map/ppermute | solution.py:459
  17.6 27.1 %collective-permute-start.9 = (bf16[256,512]{1,0:T(8,128)(2,1)S(1)}, bf16[256,512]{1,0:T(8,128)(2,1)S(1)}, u32[]{:S(2)}, u32[]{:S(2)}) collective-permute-start(bf16[256,512]{1,0:T(8,128)(2,1)S(1)} %get-tuple-element.51), channel_id=1, source_target_pairs={{0,5},{1,4},{2,7},{3,6},{4,1},{5,0},{6,3},{7,2},{8,13},{9,12},{10,... | collective-permute-start | bytes 786440 | tf_op jit(solution)/shard_map/ppermute | solution.py:459
  17.7 32.0 %collective-permute-start.6 = (bf16[256,512]{1,0:T(8,128)(2,1)S(1)}, bf16[256,512]{1,0:T(8,128)(2,1)S(1)}, u32[]{:S(2)}, u32[]{:S(2)}) collective-permute-start(bf16[256,512]{1,0:T(8,128)(2,1)S(1)} %get-tuple-element.48), channel_id=1, source_target_pairs={{0,2},{1,3},{2,0},{3,1},{4,6},{5,7},{6,4},{7,5},{8,10},{9,11},{10,... | collective-permute-start | bytes 786440 | tf_op jit(solution)/shard_map/ppermute | solution.py:459
  36.2 22.1 %collective-permute-start.7 = (bf16[256,512]{1,0:T(8,128)(2,1)S(1)}, bf16[256,512]{1,0:T(8,128)(2,1)S(1)}, u32[]{:S(2)}, u32[]{:S(2)}) collective-permute-start(bf16[256,512]{1,0:T(8,128)(2,1)S(1)} %get-tuple-element.49), channel_id=1, source_target_pairs={{0,3},{1,2},{2,1},{3,0},{4,7},{5,6},{6,5},{7,4},{8,11},{9,10},{10,... | collective-permute-start | bytes 786440 | tf_op jit(solution)/shard_map/ppermute | solution.py:459
  36.2 27.0 %collective-permute-start = (bf16[256,512]{1,0:T(8,128)(2,1)S(1)}, bf16[256,512]{1,0:T(8,128)(2,1)S(1)}, u32[]{:S(2)}, u32[]{:S(2)}) collective-permute-start(bf16[256,512]{1,0:T(8,128)(2,1)S(1)} %get-tuple-element.45), channel_id=1, source_target_pairs={{0,6},{1,7},{2,4},{3,5},{4,2},{5,3},{6,0},{7,1},{8,14},{9,15},{10,... | collective-permute-start | bytes 786440 | tf_op jit(solution)/shard_map/ppermute | solution.py:459
  39.4 23.9 %collective-permute-start.1 = (bf16[256,512]{1,0:T(8,128)(2,1)S(1)}, bf16[256,512]{1,0:T(8,128)(2,1)S(1)}, u32[]{:S(2)}, u32[]{:S(2)}) collective-permute-start(bf16[256,512]{1,0:T(8,128)(2,1)S(1)} %get-tuple-element.46), channel_id=1, source_target_pairs={{0,7},{1,6},{2,5},{3,4},{4,3},{5,2},{6,1},{7,0},{8,15},{9,14},{10,... | collective-permute-start | bytes 786440 | tf_op jit(solution)/shard_map/ppermute | solution.py:459
  68.2 4.3 %collective-permute-start.11 = (f32[64,256]{1,0:T(8,128)S(1)}, f32[64,256]{1,0:T(8,128)S(1)}, u32[]{:S(2)}, u32[]{:S(2)}) collective-permute-start(f32[64,256]{1,0:T(8,128)S(1)} %get-tuple-element.64), channel_id=1, source_target_pairs={{0,8},{8,0},{16,24},{24,16},{1,9},{9,1},{17,25},{25,17},{2,10},{10... | collective-permute-start | bytes 196616 | tf_op jit(solution)/shard_map/ppermute | solution.py:459
  69.7 4.3 %collective-permute-start.12 = (f32[64,256]{1,0:T(8,128)S(1)}, f32[64,256]{1,0:T(8,128)S(1)}, u32[]{:S(2)}, u32[]{:S(2)}) collective-permute-start(f32[64,256]{1,0:T(8,128)S(1)} %get-tuple-element.65), channel_id=1, source_target_pairs={{0,16},{8,24},{16,0},{24,8},{1,17},{9,25},{17,1},{25,9},{2,18},{10... | collective-permute-start | bytes 196616 | tf_op jit(solution)/shard_map/ppermute | solution.py:459
  71.2 5.2 %collective-permute-start.13 = (f32[64,256]{1,0:T(8,128)S(1)}, f32[64,256]{1,0:T(8,128)S(1)}, u32[]{:S(2)}, u32[]{:S(2)}) collective-permute-start(f32[64,256]{1,0:T(8,128)S(1)} %get-tuple-element.66), channel_id=1, source_target_pairs={{0,24},{8,16},{16,8},{24,0},{1,25},{9,17},{17,9},{25,1},{2,26},{10... | collective-permute-start | bytes 196616 | tf_op jit(solution)/shard_map/ppermute | solution.py:459
  76.5 12.4 %collective-permute-start.22 = (bf16[2,256,512]{2,1,0:T(8,128)(2,1)S(1)}, bf16[2,256,512]{2,1,0:T(8,128)(2,1)S(1)}, u32[]{:S(2)}, u32[]{:S(2)}) collective-permute-start(bf16[2,256,512]{2,1,0:T(8,128)(2,1)S(1)} %get-tuple-element.76), channel_id=1, source_target_pairs={{0,8},{8,0},{16,24},{24,16},{1,9},{9,1},{17,25},{25,17},{2,10},{10... | collective-permute-start | bytes 1572872 | tf_op jit(solution)/shard_map/ppermute | solution.py:459
  77.2 12.0 %collective-permute-start.23 = (bf16[2,256,512]{2,1,0:T(8,128)(2,1)S(1)}, bf16[2,256,512]{2,1,0:T(8,128)(2,1)S(1)}, u32[]{:S(2)}, u32[]{:S(2)}) collective-permute-start(bf16[2,256,512]{2,1,0:T(8,128)(2,1)S(1)} %get-tuple-element.77), channel_id=1, source_target_pairs={{0,16},{8,24},{16,0},{24,8},{1,17},{9,25},{17,1},{25,9},{2,18},{10... | collective-permute-start | bytes 1572872 | tf_op jit(solution)/shard_map/ppermute | solution.py:459
  79.0 4.8 %collective-permute-start.15 = (f32[40,256]{1,0:T(8,128)S(1)}, f32[40,256]{1,0:T(8,128)S(1)}, u32[]{:S(2)}, u32[]{:S(2)}) collective-permute-start(f32[40,256]{1,0:T(8,128)S(1)} %get-tuple-element.71), channel_id=1, source_target_pairs={{0,2},{1,3},{2,0},{3,1},{4,6},{5,7},{6,4},{7,5},{8,10},{9,11},{10,... | collective-permute-start | bytes 122888 | tf_op jit(solution)/shard_map/ppermute | solution.py:459
  80.5 5.3 %collective-permute-start.16 = (f32[40,256]{1,0:T(8,128)S(1)}, f32[40,256]{1,0:T(8,128)S(1)}, u32[]{:S(2)}, u32[]{:S(2)}) collective-permute-start(f32[40,256]{1,0:T(8,128)S(1)} %get-tuple-element.72), channel_id=1, source_target_pairs={{0,4},{1,5},{2,6},{3,7},{4,0},{5,1},{6,2},{7,3},{8,12},{9,13},{10,... | collective-permute-start | bytes 122888 | tf_op jit(solution)/shard_map/ppermute | solution.py:459
  83.1 5.8 %collective-permute-start.17 = (f32[40,256]{1,0:T(8,128)S(1)}, f32[40,256]{1,0:T(8,128)S(1)}, u32[]{:S(2)}, u32[]{:S(2)}) collective-permute-start(f32[40,256]{1,0:T(8,128)S(1)} %get-tuple-element.73), channel_id=1, source_target_pairs={{0,6},{1,7},{2,4},{3,5},{4,2},{5,3},{6,0},{7,1},{8,14},{9,15},{10,... | collective-permute-start | bytes 122888 | tf_op jit(solution)/shard_map/ppermute | solution.py:459
  89.3 8.7 %collective-permute-start.24 = (bf16[256,512]{1,0:T(8,128)(2,1)S(1)}, bf16[256,512]{1,0:T(8,128)(2,1)S(1)}, u32[]{:S(2)}, u32[]{:S(2)}) collective-permute-start(bf16[256,512]{1,0:T(8,128)(2,1)S(1)} %get-tuple-element.78), channel_id=1, source_target_pairs={{0,16},{8,24},{16,0},{24,8},{1,17},{9,25},{17,1},{25,9},{2,18},{10... | collective-permute-start | bytes 786440 | tf_op jit(solution)/shard_map/ppermute | solution.py:459
  90.6 7.4 %collective-permute-start.25 = (bf16[256,512]{1,0:T(8,128)(2,1)S(1)}, bf16[256,512]{1,0:T(8,128)(2,1)S(1)}, u32[]{:S(2)}, u32[]{:S(2)}) collective-permute-start(bf16[256,512]{1,0:T(8,128)(2,1)S(1)} %get-tuple-element.79), channel_id=1, source_target_pairs={{0,8},{8,0},{16,24},{24,16},{1,9},{9,1},{17,25},{25,17},{2,10},{10... | collective-permute-start | bytes 786440 | tf_op jit(solution)/shard_map/ppermute | solution.py:459
  93.3 6.8 %collective-permute-start.21 = (f32[64,256]{1,0:T(8,128)S(1)}, f32[64,256]{1,0:T(8,128)S(1)}, u32[]{:S(2)}, u32[]{:S(2)}) collective-permute-start(f32[64,256]{1,0:T(8,128)S(1)} %join.1.refs_0_), channel_id=1, source_target_pairs={{0,24},{8,16},{16,8},{24,0},{1,25},{9,17},{17,9},{25,1},{2,26},{10... | collective-permute-start | bytes 196616 | tf_op jit(solution)/shard_map/ppermute | solution.py:459
  94.2 6.0 %collective-permute-start.20 = (f32[64,256]{1,0:T(8,128)S(1)}, f32[64,256]{1,0:T(8,128)S(1)}, u32[]{:S(2)}, u32[]{:S(2)}) collective-permute-start(f32[64,256]{1,0:T(8,128)S(1)} %join.1.refs_0_), channel_id=1, source_target_pairs={{0,16},{8,24},{16,0},{24,8},{1,17},{9,25},{17,1},{25,9},{2,18},{10... | collective-permute-start | bytes 196616 | tf_op jit(solution)/shard_map/ppermute | solution.py:459
  95.4 4.7 %collective-permute-start.19 = (f32[64,256]{1,0:T(8,128)S(1)}, f32[64,256]{1,0:T(8,128)S(1)}, u32[]{:S(2)}, u32[]{:S(2)}) collective-permute-start(f32[64,256]{1,0:T(8,128)S(1)} %join.1.refs_0_), channel_id=1, source_target_pairs={{0,8},{8,0},{16,24},{24,16},{1,9},{9,1},{17,25},{25,17},{2,10},{10... | collective-permute-start | bytes 196616 | tf_op jit(solution)/shard_map/ppermute | solution.py:459
  (10 other events, 100.7 us)

commit v13 on v12

--- a/solution.py
+++ b/solution.py
@@ -335,7 +335,7 @@
         loss_ref[2 * k : 2 * k + 2, :] = note[half : half + 2, :]
 
 
-def join_kernel(me_ref, own_ref, other_ref, both_ref):
+def join_kernel(me_ref, own_ref, other_ref, _, both_ref):
     half = own_ref.shape[0]
     core = me_ref[0] & 1
     both_ref[pl.ds(pl.multiple_of(core * half, half), half), :] = own_ref[...]
@@ -387,21 +387,23 @@
 
 def row_loss_kernel(place_ref, loss_ref, row_loss_ref):
     experts, capacity = loss_ref.shape
-    loss = loss_ref[...]
-    for g in range(place_ref.shape[0]):
-        place = place_ref[g : g + 1, :]
-        block = place // capacity
-        slot = place - block * capacity
-        picks = jnp.where(iota((capacity, LANES), 0) == slot, 1.0, 0.0)
-        found = lax.dot_general(
-            loss,
-            picks,
-            (((1,), (0,)), ((), ())),
-            precision=lax.Precision.HIGHEST,
-            preferred_element_type=F32,
-        )
-        mine = jnp.where(iota((experts, LANES), 0) == block, found, 0.0)
-        row_loss_ref[g : g + 1, :] = jnp.sum(mine, axis=0, keepdims=True)
+    groups = place_ref.shape[0]
+    place = jnp.concatenate([place_ref[g : g + 1, :] for g in range(groups)], axis=1)
+    block = place // capacity
+    slot = place - block * capacity
+    picks = jnp.where(iota((capacity, place.shape[1]), 0) == slot, 1.0, 0.0)
+    found = lax.dot_general(
+        loss_ref[...],
+        picks,
+        (((1,), (0,)), ((), ())),
+        precision=lax.Precision.HIGHEST,
+        preferred_element_type=F32,
+    )
+    mine = jnp.sum(
+        jnp.where(iota((experts, place.shape[1]), 0) == block, found, 0.0), axis=0, keepdims=True
+    )
+    for g in range(groups):
+        row_loss_ref[g : g + 1, :] = mine[:, g * LANES : (g + 1) * LANES]
 
 
 def loss_by_row(place, loss):
@@ -483,7 +485,7 @@
     ups, downs = pair(up, near_up, place), pair(down, near_down, place)
     weights = [ups, swap(ups, "dp", 2), downs, swap(downs, "dp", 1)]
     if in_turns(experts):
-        batches, later = ((0, 4), (1, 5), (2, 3), (6, 7)), ()
+        batches, later = ((0, 4), (1, 5), (2,), (6,), (3,), (7,)), ()
     else:
         batches, later = (range(experts // 2), range(experts // 2, experts)), ()
     order = [s for batch in batches for s in batch]
@@ -525,7 +527,9 @@
         notes = [swap(note, "expert", 2 * k) for k, note in enumerate(notes)]
         total, loss = turn(z_turn_kernel, notes, (quarter // 2, experts), "z_turn")
         more_up, more_down = pass_on(got, total)
-        (total,) = turn(join_kernel, [total, swap(total, "expert", 1)], (quarter,), "join", me)
+        row_loss = loss_by_row(place, loss)
+        other = swap(total, "expert", 1)
+        (total,) = turn(join_kernel, [total, other, row_loss], (quarter,), "join", me)
         parts = [swap(total, "dp", j) for j in range(replicas)]
         *news, done = adam(
             expert_params, first_moment, second_moment, acc, [*got, more_up, more_down]
@@ -541,7 +545,7 @@
         places = jnp.arange(experts, dtype=jnp.int32) ^ me
         losses = losses.reshape(experts, capacity)[places]
         loss = lax.all_to_all(losses, "expert", split_axis=0, concat_axis=0, tiled=True)[places]
-    row_loss = loss_by_row(place, loss)
+        row_loss = loss_by_row(place, loss)
 
     return (trunk_grad, row_loss.reshape(rows), *news)
 

time: 101 us -> 100 us (0.990)
  waiting for transfers between devices: 38 us -> 30.3 us
  Pallas kernels: 27.5 us -> 31.1 us
  starting transfers between devices: 29.5 us -> 32 us
    ppermute x26, waiting for transfers between devices: 38 us -> 30.3 us  [swap(): lax.ppermute(value, axis, [(i, i ^ s) for i in range(lax.axis_size(axis))])]
    pallas_call x4 -> x6, Pallas kernels: 19.7 us -> 23.1 us  [expert_call(): pl.pallas_call(functools.partial(expert_kernel, counts, order, first, len...]
    ppermute x26, starting transfers between devices: 29.5 us -> 32 us  [swap(): lax.ppermute(value, axis, [(i, i ^ s) for i in range(lax.axis_size(axis))])]
    unnamed x16 -> x18, local copies, waits for them, and re-layouts: 3.66 us -> 4.35 us
  transfers between devices with their start and end apart: 26 -> 26, of which waited for: 10 -> 12; matrix products, arithmetic and copies ran while one was open for 0% -> 0% of each run, Pallas kernels for 21% -> 27%
where the time goes in v13:
time: 100 us
  starting transfers between devices  32 us (32%)
  Pallas kernels  31.1 us (31%)
  waiting for transfers between devices  30.3 us (30%)
  local copies, waits for them, and re-layouts  4.38 us (4%)
  other arithmetic  1.29 us (1%)
    ppermute x26, starting transfers between devices, swap(): lax.ppermute(value, axis, [(i, i ^ s) for i in range(lax.axis_size(axis))])  32 us
    ppermute x26, waiting for transfers between devices, swap(): lax.ppermute(value, axis, [(i, i ^ s) for i in range(lax.axis_size(axis))])  30.3 us
    pallas_call x6, Pallas kernels, expert_call(): pl.pallas_call(functools.partial(expert_kernel, counts, order, first, len...  23.1 us
    unnamed x18, local copies, waits for them, and re-layouts  4.35 us
    pallas_call x1, Pallas kernels, pack(): pl.pallas_call(functools.partial(pack_kernel, experts, capacity), out_sha...  3.5 us
    pallas_call x1, Pallas kernels, adam(): pl.pallas_call(adam_kernel, out_shape=[shape] * 3 + [jax.ShapeDtypeStruct...  2.07 us
  transfers between devices with their start and end apart: 26, of which 12 were waited for; matrix products, arithmetic and copies ran while one was open for 0% of the time, Pallas kernels for 27%

profile of v13, /device:TPU:0, one launch (start us, length us, event | category | flops | bytes accessed | tf_op | source)
XLA Modules:
  0.0 100.0 jit_solution(2132746199127881224)
XLA Ops:
  2.0 3.0 %collective-permute-start.3 = (bf16[256,512]{1,0:T(8,128)(2,1)S(1)}, bf16[256,512]{1,0:T(8,128)(2,1)S(1)}, u32[]{:S(2)}, u32[]{:S(2)}) collective-permute-start(bf16[256,512]{1,0:T(8,128)(2,1)S(1)} %get-tuple-element.97.one_ref), channel_id=1, source_target_pairs={{0,16},{8,24},{16,0},{24,8},{1,17},{9,25},{17,1},{25,9},{2,18},{10... | collective-permute-start | bytes 786440 | tf_op jit(solution)/shard_map/ppermute | solution.py:461
  5.0 1.5 %collective-permute-start.1 = (bf16[256,512]{1,0:T(8,128)(2,1)S(1)}, bf16[256,512]{1,0:T(8,128)(2,1)S(1)}, u32[]{:S(2)}, u32[]{:S(2)}) collective-permute-start(bf16[256,512]{1,0:T(8,128)(2,1)S(1)} %get-tuple-element.98.one_ref), channel_id=1, source_target_pairs={{0,8},{8,0},{16,24},{24,16},{1,9},{9,1},{17,25},{25,17},{2,10},{10... | collective-permute-start | bytes 786440 | tf_op jit(solution)/shard_map/ppermute | solution.py:461
  10.1 3.5 %pack_rows.1 = (bf16[256,512]{1,0:T(8,128)(2,1)S(1)}, bf16[256,512]{1,0:T(8,128)(2,1)S(1)}, bf16[256,512]{1,0:T(8,128)(2,1)S(1)}, bf16[256,512]{1,0:T(8,128)(2,1...) custom-call(s32[1]{0:T(128)} %bitcast.1.me_ref, ...), custom_call_target="tpu_custom_call" | custom-call | flops 3221225472 | bytes 6291456 | tf_op jit(solution)/shard_map/pack_rows/pallas_call | solution.py:85
  15.0 2.6 %collective-permute-start.10 = (bf16[256,512]{1,0:T(8,128)(2,1)S(1)}, bf16[256,512]{1,0:T(8,128)(2,1)S(1)}, u32[]{:S(2)}, u32[]{:S(2)}) collective-permute-start(bf16[256,512]{1,0:T(8,128)(2,1)S(1)} %get-tuple-element.59), channel_id=1, source_target_pairs={{0,4},{1,5},{2,6},{3,7},{4,0},{5,1},{6,2},{7,3},{8,12},{9,13},{10,... | collective-permute-start | bytes 786440 | tf_op jit(solution)/shard_map/ppermute | solution.py:461
  17.7 1.6 %collective-permute-start.7 = (bf16[256,512]{1,0:T(8,128)(2,1)S(1)}, bf16[256,512]{1,0:T(8,128)(2,1)S(1)}, u32[]{:S(2)}, u32[]{:S(2)}) collective-permute-start(bf16[256,512]{1,0:T(8,128)(2,1)S(1)} %get-tuple-element.55), channel_id=1, source_target_pairs={{0,2},{1,3},{2,0},{3,1},{4,6},{5,7},{6,4},{7,5},{8,10},{9,11},{10,... | collective-permute-start | bytes 786440 | tf_op jit(solution)/shard_map/ppermute | solution.py:461
  19.3 16.9 %collective-permute-done.10.refs_1_ = bf16[256,512]{1,0:T(8,128)(2,1)S(1)} collective-permute-done((bf16[256,512]{1,0:T(8,128)(2,1)S(1)}, bf16[256,512]{1,0:T(8,128)(2,1)S(1)}, u32[]{:S(2)}, u32[]{:S(2)}) %collective-permute-start.10) | collective-permute-done | bytes 262176 | tf_op jit(solution)/shard_map/ppermute | solution.py:461
  36.2 3.1 %collective-permute-start.6 = (bf16[256,512]{1,0:T(8,128)(2,1)S(1)}, bf16[256,512]{1,0:T(8,128)(2,1)S(1)}, u32[]{:S(2)}, u32[]{:S(2)}) collective-permute-start(bf16[256,512]{1,0:T(8,128)(2,1)S(1)} %get-tuple-element.54), channel_id=1, source_target_pairs={{0,6},{1,7},{2,4},{3,5},{4,2},{5,3},{6,0},{7,1},{8,14},{9,15},{10,... | collective-permute-start | bytes 786440 | tf_op jit(solution)/shard_map/ppermute | solution.py:461
  39.5 4.9 %expert_rows.6 = (f32[4,2,256,512]{3,2,1,0:T(8,128)S(1)}, f32[256,256]{1,0:T(8,128)S(1)}, f32[2,256]{1,0:T(2,128)S(1)}) custom-call(bf16[256,512]{1,0:T(8,128)(2,1)S(1)} %get-tuple-element.58.refs_0_, bf16[256,512]{1,0:T(8,128)(2,1)S(1)} %collective-permute-done.10.refs_1_, bf16[256,256]{1,0:T(8,128)(2,1)S(1)} %copy-done, ...), custom_call_target="tpu_custom_call" | custom-call | flops 1572864 | bytes 131072 | tf_op jit(solution)/shard_map/expert_rows/pallas_call | solution.py:289
  44.3 1.9 %collective-permute-done.9.refs_1_ = bf16[256,512]{1,0:T(8,128)(2,1)S(1)} collective-permute-done((bf16[256,512]{1,0:T(8,128)(2,1)S(1)}, bf16[256,512]{1,0:T(8,128)(2,1)S(1)}, u32[]{:S(2)}, u32[]{:S(2)}) %collective-permute-start.9) | collective-permute-done | bytes 262176 | tf_op jit(solution)/shard_map/ppermute | solution.py:461
  46.3 5.1 %expert_rows.7 = (f32[4,2,256,512]{3,2,1,0:T(8,128)S(1)}, f32[256,256]{1,0:T(8,128)S(1)}, f32[2,256]{1,0:T(2,128)S(1)}) custom-call(bf16[256,512]{1,0:T(8,128)(2,1)S(1)} %collective-permute-done.8.refs_0_, bf16[256,512]{1,0:T(8,128)(2,1)S(1)} %collective-permute-done.9.refs_1_, bf16[256,256]{1,0:T(8,128)(2,1)S(1)} %copy-done, ...), custom_call_target="tpu_custom_call" | custom-call | flops 1572864 | bytes 131072 | tf_op jit(solution)/shard_map/expert_rows/pallas_call | solution.py:289
  51.4 3.2 %expert_rows.8 = (f32[4,2,256,512]{3,2,1,0:T(8,128)S(1)}, f32[256,256]{1,0:T(8,128)S(1)}, f32[1,256]{1,0:T(1,128)S(1)}) custom-call(bf16[256,512]{1,0:T(8,128)(2,1)S(1)} %collective-permute-done.7.refs_0_, bf16[256,256]{1,0:T(8,128)(2,1)S(1)} %copy-done, bf16[2,256,512]{2,1,0:T(8,128)(2,1)S(1)} %pair.2.refs_3_.refs_2_, ...), custom_call_target="tpu_custom_call" | custom-call | flops 786432 | bytes 65536 | tf_op jit(solution)/shard_map/expert_rows/pallas_call | solution.py:289
  54.6 3.2 %expert_rows.9 = (f32[4,2,256,512]{3,2,1,0:T(8,128)S(1)}, f32[256,256]{1,0:T(8,128)S(1)}, f32[1,256]{1,0:T(1,128)S(1)}) custom-call(bf16[256,512]{1,0:T(8,128)(2,1)S(1)} %collective-permute-done.6.refs_0_, bf16[256,256]{1,0:T(8,128)(2,1)S(1)} %copy-done, bf16[2,256,512]{2,1,0:T(8,128)(2,1)S(1)} %pair.2.refs_3_.refs_2_, ...), custom_call_target="tpu_custom_call" | custom-call | flops 786432 | bytes 65536 | tf_op jit(solution)/shard_map/expert_rows/pallas_call | solution.py:289
  58.3 3.2 %expert_rows.10 = (f32[4,2,256,512]{3,2,1,0:T(8,128)S(1)}, f32[256,256]{1,0:T(8,128)S(1)}, f32[1,256]{1,0:T(1,128)S(1)}) custom-call(bf16[256,512]{1,0:T(8,128)(2,1)S(1)} %collective-permute-done.5.refs_0_, bf16[256,256]{1,0:T(8,128)(2,1)S(1)} %copy-done, bf16[2,256,512]{2,1,0:T(8,128)(2,1)S(1)} %pair.2.refs_3_.refs_2_, ...), custom_call_target="tpu_custom_call" | custom-call | flops 786432 | bytes 65536 | tf_op jit(solution)/shard_map/expert_rows/pallas_call | solution.py:289
  61.6 3.5 %expert_rows.11 = (f32[4,2,256,512]{3,2,1,0:T(8,128)S(1)}, f32[64,256]{1,0:T(8,128)S(1)}, f32[64,256]{1,0:T(8,128)S(1)}, f32[64,256]{1,0:T(8,128)S(1)}, f32[64,256]{1,0:T(8,128)S(1)}, /*index=5*/f32[8,256]{1,0:T(8,128)S(1)}) custom-call(bf16[256,512]{1,0:T(8,128)(2,1)S(1)} %collective-permute-done.refs_0_, bf16[256,256]{1,0:T(8,128)(2,1)S(1)} %copy-done, ...), custom_call_target="tpu_custom_call" | custom-call | flops 786432 | bytes 65536 | tf_op jit(solution)/shard_map/expert_rows/pallas_call | solution.py:289
  65.0 1.5 %collective-permute-start.11 = (f32[64,256]{1,0:T(8,128)S(1)}, f32[64,256]{1,0:T(8,128)S(1)}, u32[]{:S(2)}, u32[]{:S(2)}) collective-permute-start(f32[64,256]{1,0:T(8,128)S(1)} %get-tuple-element.76), channel_id=1, source_target_pairs={{0,8},{8,0},{16,24},{24,16},{1,9},{9,1},{17,25},{25,17},{2,10},{10... | collective-permute-start | bytes 196616 | tf_op jit(solution)/shard_map/ppermute | solution.py:461
  66.5 1.5 %collective-permute-start.12 = (f32[64,256]{1,0:T(8,128)S(1)}, f32[64,256]{1,0:T(8,128)S(1)}, u32[]{:S(2)}, u32[]{:S(2)}) collective-permute-start(f32[64,256]{1,0:T(8,128)S(1)} %get-tuple-element.77), channel_id=1, source_target_pairs={{0,16},{8,24},{16,0},{24,8},{1,17},{9,25},{17,1},{25,9},{2,18},{10... | collective-permute-start | bytes 196616 | tf_op jit(solution)/shard_map/ppermute | solution.py:461
  70.9 2.3 %collective-permute-done.13.q3 = f32[64,256]{1,0:T(8,128)S(1)} collective-permute-done((f32[64,256]{1,0:T(8,128)S(1)}, f32[64,256]{1,0:T(8,128)S(1)}, u32[]{:S(2)}, u32[]{:S(2)}) %collective-permute-start.13) | collective-permute-done | bytes 65568 | tf_op jit(solution)/shard_map/ppermute | solution.py:461
  76.0 4.1 %collective-permute-start.15 = (f32[40,256]{1,0:T(8,128)S(1)}, f32[40,256]{1,0:T(8,128)S(1)}, u32[]{:S(2)}, u32[]{:S(2)}) collective-permute-start(f32[40,256]{1,0:T(8,128)S(1)} %get-tuple-element.83), channel_id=1, source_target_pairs={{0,2},{1,3},{2,0},{3,1},{4,6},{5,7},{6,4},{7,5},{8,10},{9,11},{10,... | collective-permute-start | bytes 122888 | tf_op jit(solution)/shard_map/ppermute | solution.py:461
  80.1 1.8 %collective-permute-start.16 = (f32[40,256]{1,0:T(8,128)S(1)}, f32[40,256]{1,0:T(8,128)S(1)}, u32[]{:S(2)}, u32[]{:S(2)}) collective-permute-start(f32[40,256]{1,0:T(8,128)S(1)} %get-tuple-element.84), channel_id=1, source_target_pairs={{0,4},{1,5},{2,6},{3,7},{4,0},{5,1},{6,2},{7,3},{8,12},{9,13},{10,... | collective-permute-start | bytes 122888 | tf_op jit(solution)/shard_map/ppermute | solution.py:461
  83.3 2.0 %collective-permute-done.16.refs_2_ = f32[40,256]{1,0:T(8,128)S(1)} collective-permute-done((f32[40,256]{1,0:T(8,128)S(1)}, f32[40,256]{1,0:T(8,128)S(1)}, u32[]{:S(2)}, u32[]{:S(2)}) %collective-permute-start.16) | collective-permute-done | bytes 40992 | tf_op jit(solution)/shard_map/ppermute | solution.py:461
  85.3 2.4 %collective-permute-done.17.refs_3_ = f32[40,256]{1,0:T(8,128)S(1)} collective-permute-done((f32[40,256]{1,0:T(8,128)S(1)}, f32[40,256]{1,0:T(8,128)S(1)}, u32[]{:S(2)}, u32[]{:S(2)}) %collective-permute-start.17) | collective-permute-done | bytes 40992 | tf_op jit(solution)/shard_map/ppermute | solution.py:461
  87.9 1.5 %collective-permute-start.24 = (bf16[256,512]{1,0:T(8,128)(2,1)S(1)}, bf16[256,512]{1,0:T(8,128)(2,1)S(1)}, u32[]{:S(2)}, u32[]{:S(2)}) collective-permute-start(bf16[256,512]{1,0:T(8,128)(2,1)S(1)} %get-tuple-element.91), channel_id=1, source_target_pairs={{0,16},{8,24},{16,0},{24,8},{1,17},{9,25},{17,1},{25,9},{2,18},{10... | collective-permute-start | bytes 786440 | tf_op jit(solution)/shard_map/ppermute | solution.py:461
  93.5 1.5 %collective-permute-start.20 = (f32[64,256]{1,0:T(8,128)S(1)}, f32[64,256]{1,0:T(8,128)S(1)}, u32[]{:S(2)}, u32[]{:S(2)}) collective-permute-start(f32[64,256]{1,0:T(8,128)S(1)} %join.1.refs_0_), channel_id=1, source_target_pairs={{0,16},{8,24},{16,0},{24,8},{1,17},{9,25},{17,1},{25,9},{2,18},{10... | collective-permute-start | bytes 196616 | tf_op jit(solution)/shard_map/ppermute | solution.py:461
  96.5 2.1 %adam.1 = (f32[1,2,256,512]{3,2,1,0:T(8,128)}, f32[1,2,256,512]{3,2,1,0:T(8,128)}, f32[1,2,256,512]{3,2,1,0:T(8,128)}, f32[8,128]{1,0:T(8,128)S(1)}) custom-call(f32[1,2,256,512]{3,2,1,0:T(8,128)S(1)} %copy-done.1, f32[1,2,256,512]{3,2,1,0:T(8,128)S(1)} %copy-done.2, f32[1,2,256,512]{3,2,1,0:T(8,128)S(1)} %copy-done.3, ...), custom_call_target="tpu_custom_call" | custom-call | flops 5242880 | bytes 2097152 | tf_op jit(solution)/shard_map/adam/pallas_call | solution.py:445
  (66 shorter events, 21.1 us)
Async XLA Ops:
  2.0 12.3 %collective-permute-start.3 = (bf16[256,512]{1,0:T(8,128)(2,1)S(1)}, bf16[256,512]{1,0:T(8,128)(2,1)S(1)}, u32[]{:S(2)}, u32[]{:S(2)}) collective-permute-start(bf16[256,512]{1,0:T(8,128)(2,1)S(1)} %get-tuple-element.97.one_ref), channel_id=1, source_target_pairs={{0,16},{8,24},{16,0},{24,8},{1,17},{9,25},{17,1},{25,9},{2,18},{10... | collective-permute-start | bytes 786440 | tf_op jit(solution)/shard_map/ppermute | solution.py:461
  5.0 8.6 %collective-permute-start.1 = (bf16[256,512]{1,0:T(8,128)(2,1)S(1)}, bf16[256,512]{1,0:T(8,128)(2,1)S(1)}, u32[]{:S(2)}, u32[]{:S(2)}) collective-permute-start(bf16[256,512]{1,0:T(8,128)(2,1)S(1)} %get-tuple-element.98.one_ref), channel_id=1, source_target_pairs={{0,8},{8,0},{16,24},{24,16},{1,9},{9,1},{17,25},{25,17},{2,10},{10... | collective-permute-start | bytes 786440 | tf_op jit(solution)/shard_map/ppermute | solution.py:461
  13.7 25.7 %collective-permute-start.2 = (bf16[2,256,512]{2,1,0:T(8,128)(2,1)S(1)}, bf16[2,256,512]{2,1,0:T(8,128)(2,1)S(1)}, u32[]{:S(2)}, u32[]{:S(2)}) collective-permute-start(bf16[2,256,512]{2,1,0:T(8,128)(2,1)S(1)} %pair.2.refs_3_.refs_2_), channel_id=1, source_target_pairs={{0,16},{8,24},{16,0},{24,8},{1,17},{9,25},{17,1},{25,9},{2,18},{10... | collective-permute-start | bytes 1572872 | tf_op jit(solution)/shard_map/ppermute | solution.py:461
  14.3 25.1 %collective-permute-start.4 = (bf16[2,256,512]{2,1,0:T(8,128)(2,1)S(1)}, bf16[2,256,512]{2,1,0:T(8,128)(2,1)S(1)}, u32[]{:S(2)}, u32[]{:S(2)}) collective-permute-start(bf16[2,256,512]{2,1,0:T(8,128)(2,1)S(1)} %pair.3.refs_5_.refs_4_), channel_id=1, source_target_pairs={{0,8},{8,0},{16,24},{24,16},{1,9},{9,1},{17,25},{25,17},{2,10},{10... | collective-permute-start | bytes 1572872 | tf_op jit(solution)/shard_map/ppermute | solution.py:461
  15.0 2.8 %collective-permute-start.8 = (bf16[256,512]{1,0:T(8,128)(2,1)S(1)}, bf16[256,512]{1,0:T(8,128)(2,1)S(1)}, u32[]{:S(2)}, u32[]{:S(2)}) collective-permute-start(bf16[256,512]{1,0:T(8,128)(2,1)S(1)} %get-tuple-element.56), channel_id=1, source_target_pairs={{0,1},{1,0},{2,3},{3,2},{4,5},{5,4},{6,7},{7,6},{8,9},{9,8},{10,11... | collective-permute-start | bytes 786440 | tf_op jit(solution)/shard_map/ppermute | solution.py:461
  15.0 21.2 %collective-permute-start.10 = (bf16[256,512]{1,0:T(8,128)(2,1)S(1)}, bf16[256,512]{1,0:T(8,128)(2,1)S(1)}, u32[]{:S(2)}, u32[]{:S(2)}) collective-permute-start(bf16[256,512]{1,0:T(8,128)(2,1)S(1)} %get-tuple-element.59), channel_id=1, source_target_pairs={{0,4},{1,5},{2,6},{3,7},{4,0},{5,1},{6,2},{7,3},{8,12},{9,13},{10,... | collective-permute-start | bytes 786440 | tf_op jit(solution)/shard_map/ppermute | solution.py:461
  17.6 28.7 %collective-permute-start.9 = (bf16[256,512]{1,0:T(8,128)(2,1)S(1)}, bf16[256,512]{1,0:T(8,128)(2,1)S(1)}, u32[]{:S(2)}, u32[]{:S(2)}) collective-permute-start(bf16[256,512]{1,0:T(8,128)(2,1)S(1)} %get-tuple-element.57), channel_id=1, source_target_pairs={{0,5},{1,4},{2,7},{3,6},{4,1},{5,0},{6,3},{7,2},{8,13},{9,12},{10,... | collective-permute-start | bytes 786440 | tf_op jit(solution)/shard_map/ppermute | solution.py:461
  17.7 33.6 %collective-permute-start.7 = (bf16[256,512]{1,0:T(8,128)(2,1)S(1)}, bf16[256,512]{1,0:T(8,128)(2,1)S(1)}, u32[]{:S(2)}, u32[]{:S(2)}) collective-permute-start(bf16[256,512]{1,0:T(8,128)(2,1)S(1)} %get-tuple-element.55), channel_id=1, source_target_pairs={{0,2},{1,3},{2,0},{3,1},{4,6},{5,7},{6,4},{7,5},{8,10},{9,11},{10,... | collective-permute-start | bytes 786440 | tf_op jit(solution)/shard_map/ppermute | solution.py:461
  36.2 18.4 %collective-permute-start.6 = (bf16[256,512]{1,0:T(8,128)(2,1)S(1)}, bf16[256,512]{1,0:T(8,128)(2,1)S(1)}, u32[]{:S(2)}, u32[]{:S(2)}) collective-permute-start(bf16[256,512]{1,0:T(8,128)(2,1)S(1)} %get-tuple-element.54), channel_id=1, source_target_pairs={{0,6},{1,7},{2,4},{3,5},{4,2},{5,3},{6,0},{7,1},{8,14},{9,15},{10,... | collective-permute-start | bytes 786440 | tf_op jit(solution)/shard_map/ppermute | solution.py:461
  39.4 18.9 %collective-permute-start.5 = (bf16[256,512]{1,0:T(8,128)(2,1)S(1)}, bf16[256,512]{1,0:T(8,128)(2,1)S(1)}, u32[]{:S(2)}, u32[]{:S(2)}) collective-permute-start(bf16[256,512]{1,0:T(8,128)(2,1)S(1)} %get-tuple-element.53), channel_id=1, source_target_pairs={{0,3},{1,2},{2,1},{3,0},{4,7},{5,6},{6,5},{7,4},{8,11},{9,10},{10,... | collective-permute-start | bytes 786440 | tf_op jit(solution)/shard_map/ppermute | solution.py:461
  39.4 22.2 %collective-permute-start = (bf16[256,512]{1,0:T(8,128)(2,1)S(1)}, bf16[256,512]{1,0:T(8,128)(2,1)S(1)}, u32[]{:S(2)}, u32[]{:S(2)}) collective-permute-start(bf16[256,512]{1,0:T(8,128)(2,1)S(1)} %get-tuple-element.51), channel_id=1, source_target_pairs={{0,7},{1,6},{2,5},{3,4},{4,3},{5,2},{6,1},{7,0},{8,15},{9,14},{10,... | collective-permute-start | bytes 786440 | tf_op jit(solution)/shard_map/ppermute | solution.py:461
  65.0 4.7 %collective-permute-start.11 = (f32[64,256]{1,0:T(8,128)S(1)}, f32[64,256]{1,0:T(8,128)S(1)}, u32[]{:S(2)}, u32[]{:S(2)}) collective-permute-start(f32[64,256]{1,0:T(8,128)S(1)} %get-tuple-element.76), channel_id=1, source_target_pairs={{0,8},{8,0},{16,24},{24,16},{1,9},{9,1},{17,25},{25,17},{2,10},{10... | collective-permute-start | bytes 196616 | tf_op jit(solution)/shard_map/ppermute | solution.py:461
  66.5 4.4 %collective-permute-start.12 = (f32[64,256]{1,0:T(8,128)S(1)}, f32[64,256]{1,0:T(8,128)S(1)}, u32[]{:S(2)}, u32[]{:S(2)}) collective-permute-start(f32[64,256]{1,0:T(8,128)S(1)} %get-tuple-element.77), channel_id=1, source_target_pairs={{0,16},{8,24},{16,0},{24,8},{1,17},{9,25},{17,1},{25,9},{2,18},{10... | collective-permute-start | bytes 196616 | tf_op jit(solution)/shard_map/ppermute | solution.py:461
  68.0 5.2 %collective-permute-start.13 = (f32[64,256]{1,0:T(8,128)S(1)}, f32[64,256]{1,0:T(8,128)S(1)}, u32[]{:S(2)}, u32[]{:S(2)}) collective-permute-start(f32[64,256]{1,0:T(8,128)S(1)} %get-tuple-element.78), channel_id=1, source_target_pairs={{0,24},{8,16},{16,8},{24,0},{1,25},{9,17},{17,9},{25,1},{2,26},{10... | collective-permute-start | bytes 196616 | tf_op jit(solution)/shard_map/ppermute | solution.py:461
  73.4 14.4 %collective-permute-start.22 = (bf16[2,256,512]{2,1,0:T(8,128)(2,1)S(1)}, bf16[2,256,512]{2,1,0:T(8,128)(2,1)S(1)}, u32[]{:S(2)}, u32[]{:S(2)}) collective-permute-start(bf16[2,256,512]{2,1,0:T(8,128)(2,1)S(1)} %get-tuple-element.89), channel_id=1, source_target_pairs={{0,8},{8,0},{16,24},{24,16},{1,9},{9,1},{17,25},{25,17},{2,10},{10... | collective-permute-start | bytes 1572872 | tf_op jit(solution)/shard_map/ppermute | solution.py:461
  74.0 13.7 %collective-permute-start.23 = (bf16[2,256,512]{2,1,0:T(8,128)(2,1)S(1)}, bf16[2,256,512]{2,1,0:T(8,128)(2,1)S(1)}, u32[]{:S(2)}, u32[]{:S(2)}) collective-permute-start(bf16[2,256,512]{2,1,0:T(8,128)(2,1)S(1)} %get-tuple-element.90), channel_id=1, source_target_pairs={{0,16},{8,24},{16,0},{24,8},{1,17},{9,25},{17,1},{25,9},{2,18},{10... | collective-permute-start | bytes 1572872 | tf_op jit(solution)/shard_map/ppermute | solution.py:461
  76.0 7.3 %collective-permute-start.15 = (f32[40,256]{1,0:T(8,128)S(1)}, f32[40,256]{1,0:T(8,128)S(1)}, u32[]{:S(2)}, u32[]{:S(2)}) collective-permute-start(f32[40,256]{1,0:T(8,128)S(1)} %get-tuple-element.83), channel_id=1, source_target_pairs={{0,2},{1,3},{2,0},{3,1},{4,6},{5,7},{6,4},{7,5},{8,10},{9,11},{10,... | collective-permute-start | bytes 122888 | tf_op jit(solution)/shard_map/ppermute | solution.py:461
  80.1 5.2 %collective-permute-start.16 = (f32[40,256]{1,0:T(8,128)S(1)}, f32[40,256]{1,0:T(8,128)S(1)}, u32[]{:S(2)}, u32[]{:S(2)}) collective-permute-start(f32[40,256]{1,0:T(8,128)S(1)} %get-tuple-element.84), channel_id=1, source_target_pairs={{0,4},{1,5},{2,6},{3,7},{4,0},{5,1},{6,2},{7,3},{8,12},{9,13},{10,... | collective-permute-start | bytes 122888 | tf_op jit(solution)/shard_map/ppermute | solution.py:461
  81.9 5.8 %collective-permute-start.17 = (f32[40,256]{1,0:T(8,128)S(1)}, f32[40,256]{1,0:T(8,128)S(1)}, u32[]{:S(2)}, u32[]{:S(2)}) collective-permute-start(f32[40,256]{1,0:T(8,128)S(1)} %get-tuple-element.85), channel_id=1, source_target_pairs={{0,6},{1,7},{2,4},{3,5},{4,2},{5,3},{6,0},{7,1},{8,14},{9,15},{10,... | collective-permute-start | bytes 122888 | tf_op jit(solution)/shard_map/ppermute | solution.py:461
  87.9 8.6 %collective-permute-start.24 = (bf16[256,512]{1,0:T(8,128)(2,1)S(1)}, bf16[256,512]{1,0:T(8,128)(2,1)S(1)}, u32[]{:S(2)}, u32[]{:S(2)}) collective-permute-start(bf16[256,512]{1,0:T(8,128)(2,1)S(1)} %get-tuple-element.91), channel_id=1, source_target_pairs={{0,16},{8,24},{16,0},{24,8},{1,17},{9,25},{17,1},{25,9},{2,18},{10... | collective-permute-start | bytes 786440 | tf_op jit(solution)/shard_map/ppermute | solution.py:461
  89.4 7.0 %collective-permute-start.25 = (bf16[256,512]{1,0:T(8,128)(2,1)S(1)}, bf16[256,512]{1,0:T(8,128)(2,1)S(1)}, u32[]{:S(2)}, u32[]{:S(2)}) collective-permute-start(bf16[256,512]{1,0:T(8,128)(2,1)S(1)} %get-tuple-element.92), channel_id=1, source_target_pairs={{0,8},{8,0},{16,24},{24,16},{1,9},{9,1},{17,25},{25,17},{2,10},{10... | collective-permute-start | bytes 786440 | tf_op jit(solution)/shard_map/ppermute | solution.py:461
  92.9 5.9 %collective-permute-start.21 = (f32[64,256]{1,0:T(8,128)S(1)}, f32[64,256]{1,0:T(8,128)S(1)}, u32[]{:S(2)}, u32[]{:S(2)}) collective-permute-start(f32[64,256]{1,0:T(8,128)S(1)} %join.1.refs_0_), channel_id=1, source_target_pairs={{0,24},{8,16},{16,8},{24,0},{1,25},{9,17},{17,9},{25,1},{2,26},{10... | collective-permute-start | bytes 196616 | tf_op jit(solution)/shard_map/ppermute | solution.py:461
  93.5 5.6 %collective-permute-start.20 = (f32[64,256]{1,0:T(8,128)S(1)}, f32[64,256]{1,0:T(8,128)S(1)}, u32[]{:S(2)}, u32[]{:S(2)}) collective-permute-start(f32[64,256]{1,0:T(8,128)S(1)} %join.1.refs_0_), channel_id=1, source_target_pairs={{0,16},{8,24},{16,0},{24,8},{1,17},{9,25},{17,1},{25,9},{2,18},{10... | collective-permute-start | bytes 196616 | tf_op jit(solution)/shard_map/ppermute | solution.py:461
  95.0 4.3 %collective-permute-start.19 = (f32[64,256]{1,0:T(8,128)S(1)}, f32[64,256]{1,0:T(8,128)S(1)}, u32[]{:S(2)}, u32[]{:S(2)}) collective-permute-start(f32[64,256]{1,0:T(8,128)S(1)} %join.1.refs_0_), channel_id=1, source_target_pairs={{0,8},{8,0},{16,24},{24,16},{1,9},{9,1},{17,25},{25,17},{2,10},{10... | collective-permute-start | bytes 196616 | tf_op jit(solution)/shard_map/ppermute | solution.py:461
  (11 other events, 105.9 us)

commit v14 on v13

--- a/solution.py
+++ b/solution.py
@@ -385,7 +385,7 @@
     )(*held, ahead)
 
 
-def row_loss_kernel(place_ref, loss_ref, row_loss_ref):
+def row_loss_kernel(place_ref, loss_ref, row_loss_ref, done_ref):
     experts, capacity = loss_ref.shape
     groups = place_ref.shape[0]
     place = jnp.concatenate([place_ref[g : g + 1, :] for g in range(groups)], axis=1)
@@ -404,14 +404,15 @@
     )
     for g in range(groups):
         row_loss_ref[g : g + 1, :] = mine[:, g * LANES : (g + 1) * LANES]
+    done_ref[...] = jnp.zeros(done_ref.shape, F32)
 
 
 def loss_by_row(place, loss):
     return pl.pallas_call(
         row_loss_kernel,
-        out_shape=jax.ShapeDtypeStruct(place.shape, F32),
+        out_shape=[jax.ShapeDtypeStruct(shape, F32) for shape in (place.shape, (8, LANES))],
         in_specs=[whole()] * 2,
-        out_specs=whole(),
+        out_specs=[whole()] * 2,
         compiler_params=pltpu.CompilerParams(vmem_limit_bytes=16 * MIB),
         name="row_loss",
     )(place, loss)
@@ -485,7 +486,7 @@
     ups, downs = pair(up, near_up, place), pair(down, near_down, place)
     weights = [ups, swap(ups, "dp", 2), downs, swap(downs, "dp", 1)]
     if in_turns(experts):
-        batches, later = ((0, 4), (1, 5), (2,), (6,), (3,), (7,)), ()
+        batches, later = ((0, 4), (1, 5), (2,), (6, 3), (7,)), ()
     else:
         batches, later = (range(experts // 2), range(experts // 2, experts)), ()
     order = [s for batch in batches for s in batch]
@@ -527,9 +528,9 @@
         notes = [swap(note, "expert", 2 * k) for k, note in enumerate(notes)]
         total, loss = turn(z_turn_kernel, notes, (quarter // 2, experts), "z_turn")
         more_up, more_down = pass_on(got, total)
-        row_loss = loss_by_row(place, loss)
+        row_loss, found = loss_by_row(place, loss)
         other = swap(total, "expert", 1)
-        (total,) = turn(join_kernel, [total, other, row_loss], (quarter,), "join", me)
+        (total,) = turn(join_kernel, [total, other, found], (quarter,), "join", me)
         parts = [swap(total, "dp", j) for j in range(replicas)]
         *news, done = adam(
             expert_params, first_moment, second_moment, acc, [*got, more_up, more_down]
@@ -545,7 +546,7 @@
         places = jnp.arange(experts, dtype=jnp.int32) ^ me
         losses = losses.reshape(experts, capacity)[places]
         loss = lax.all_to_all(losses, "expert", split_axis=0, concat_axis=0, tiled=True)[places]
-        row_loss = loss_by_row(place, loss)
+        row_loss, _ = loss_by_row(place, loss)
 
     return (trunk_grad, row_loss.reshape(rows), *news)
 

time: 100 us -> 99.4 us (level)
  waiting for transfers between devices: 30.3 us -> 34.4 us
  starting transfers between devices: 32 us -> 29.6 us
  Pallas kernels: 31.1 us -> 29.3 us
    ppermute x26, waiting for transfers between devices: 30.3 us -> 34.4 us  [swap(): lax.ppermute(value, axis, [(i, i ^ s) for i in range(lax.axis_size(axis))])]
    ppermute x26, starting transfers between devices: 32 us -> 29.6 us  [swap(): lax.ppermute(value, axis, [(i, i ^ s) for i in range(lax.axis_size(axis))])]
    pallas_call x6 -> x5, Pallas kernels: 23.1 us -> 21.4 us  [expert_call(): pl.pallas_call(functools.partial(expert_kernel, counts, order, first, len...]
    unnamed x18 -> x16, local copies, waits for them, and re-layouts: 4.35 us -> 3.66 us
  transfers between devices with their start and end apart: 26 -> 26, of which waited for: 12 -> 13; matrix products, arithmetic and copies ran while one was open for 0% -> 0% of each run, Pallas kernels for 27% -> 25%
where the time goes in v14:
time: 99.4 us; the launch traced here: 99.1 us
  waiting for transfers between devices  34.4 us (35%)
  starting transfers between devices  29.6 us (30%)
  Pallas kernels  29.3 us (29%)
  local copies, waits for them, and re-layouts  3.7 us (4%)
  other arithmetic  1.29 us (1%)
    ppermute x26, waiting for transfers between devices, swap(): lax.ppermute(value, axis, [(i, i ^ s) for i in range(lax.axis_size(axis))])  34.4 us
    ppermute x26, starting transfers between devices, swap(): lax.ppermute(value, axis, [(i, i ^ s) for i in range(lax.axis_size(axis))])  29.6 us
    pallas_call x5, Pallas kernels, expert_call(): pl.pallas_call(functools.partial(expert_kernel, counts, order, first, len...  21.4 us
    unnamed x16, local copies, waits for them, and re-layouts  3.66 us
    pallas_call x1, Pallas kernels, pack(): pl.pallas_call(functools.partial(pack_kernel, experts, capacity), out_sha...  3.5 us
    pallas_call x1, Pallas kernels, adam(): pl.pallas_call(adam_kernel, out_shape=[shape] * 3 + [jax.ShapeDtypeStruct...  2.07 us
  transfers between devices with their start and end apart: 26, of which 13 were waited for; matrix products, arithmetic and copies ran while one was open for 0% of the time, Pallas kernels for 25%

profile of v14, /device:TPU:0, one launch (start us, length us, event | category | flops | bytes accessed | tf_op | source)
XLA Modules:
  0.0 99.1 jit_solution(6959932231264712102)
XLA Ops:
  2.0 3.0 %collective-permute-start.3 = (bf16[256,512]{1,0:T(8,128)(2,1)S(1)}, bf16[256,512]{1,0:T(8,128)(2,1)S(1)}, u32[]{:S(2)}, u32[]{:S(2)}) collective-permute-start(bf16[256,512]{1,0:T(8,128)(2,1)S(1)} %get-tuple-element.95.one_ref), channel_id=1, source_target_pairs={{0,16},{8,24},{16,0},{24,8},{1,17},{9,25},{17,1},{25,9},{2,18},{10... | collective-permute-start | bytes 786440 | tf_op jit(solution)/shard_map/ppermute | solution.py:462
  5.0 1.5 %collective-permute-start.1 = (bf16[256,512]{1,0:T(8,128)(2,1)S(1)}, bf16[256,512]{1,0:T(8,128)(2,1)S(1)}, u32[]{:S(2)}, u32[]{:S(2)}) collective-permute-start(bf16[256,512]{1,0:T(8,128)(2,1)S(1)} %get-tuple-element.96.one_ref), channel_id=1, source_target_pairs={{0,8},{8,0},{16,24},{24,16},{1,9},{9,1},{17,25},{25,17},{2,10},{10... | collective-permute-start | bytes 786440 | tf_op jit(solution)/shard_map/ppermute | solution.py:462
  10.1 3.5 %pack_rows.1 = (bf16[256,512]{1,0:T(8,128)(2,1)S(1)}, bf16[256,512]{1,0:T(8,128)(2,1)S(1)}, bf16[256,512]{1,0:T(8,128)(2,1)S(1)}, bf16[256,512]{1,0:T(8,128)(2,1...) custom-call(s32[1]{0:T(128)} %bitcast.1.me_ref, ...), custom_call_target="tpu_custom_call" | custom-call | flops 3221225472 | bytes 6291456 | tf_op jit(solution)/shard_map/pack_rows/pallas_call | solution.py:85
  15.0 2.6 %collective-permute-start.10 = (bf16[256,512]{1,0:T(8,128)(2,1)S(1)}, bf16[256,512]{1,0:T(8,128)(2,1)S(1)}, u32[]{:S(2)}, u32[]{:S(2)}) collective-permute-start(bf16[256,512]{1,0:T(8,128)(2,1)S(1)} %get-tuple-element.58), channel_id=1, source_target_pairs={{0,4},{1,5},{2,6},{3,7},{4,0},{5,1},{6,2},{7,3},{8,12},{9,13},{10,... | collective-permute-start | bytes 786440 | tf_op jit(solution)/shard_map/ppermute | solution.py:462
  17.7 1.6 %collective-permute-start.7 = (bf16[256,512]{1,0:T(8,128)(2,1)S(1)}, bf16[256,512]{1,0:T(8,128)(2,1)S(1)}, u32[]{:S(2)}, u32[]{:S(2)}) collective-permute-start(bf16[256,512]{1,0:T(8,128)(2,1)S(1)} %get-tuple-element.54), channel_id=1, source_target_pairs={{0,2},{1,3},{2,0},{3,1},{4,6},{5,7},{6,4},{7,5},{8,10},{9,11},{10,... | collective-permute-start | bytes 786440 | tf_op jit(solution)/shard_map/ppermute | solution.py:462
  19.3 16.9 %collective-permute-done.10.refs_1_ = bf16[256,512]{1,0:T(8,128)(2,1)S(1)} collective-permute-done((bf16[256,512]{1,0:T(8,128)(2,1)S(1)}, bf16[256,512]{1,0:T(8,128)(2,1)S(1)}, u32[]{:S(2)}, u32[]{:S(2)}) %collective-permute-start.10) | collective-permute-done | bytes 262176 | tf_op jit(solution)/shard_map/ppermute | solution.py:462
  36.2 3.1 %collective-permute-start.5 = (bf16[256,512]{1,0:T(8,128)(2,1)S(1)}, bf16[256,512]{1,0:T(8,128)(2,1)S(1)}, u32[]{:S(2)}, u32[]{:S(2)}) collective-permute-start(bf16[256,512]{1,0:T(8,128)(2,1)S(1)} %get-tuple-element.52), channel_id=1, source_target_pairs={{0,6},{1,7},{2,4},{3,5},{4,2},{5,3},{6,0},{7,1},{8,14},{9,15},{10,... | collective-permute-start | bytes 786440 | tf_op jit(solution)/shard_map/ppermute | solution.py:462
  39.5 4.9 %expert_rows.5 = (f32[4,2,256,512]{3,2,1,0:T(8,128)S(1)}, f32[256,256]{1,0:T(8,128)S(1)}, f32[2,256]{1,0:T(2,128)S(1)}) custom-call(bf16[256,512]{1,0:T(8,128)(2,1)S(1)} %get-tuple-element.57.refs_0_, bf16[256,512]{1,0:T(8,128)(2,1)S(1)} %collective-permute-done.10.refs_1_, bf16[256,256]{1,0:T(8,128)(2,1)S(1)} %copy-done.1, ...), custom_call_target="tpu_custom_call" | custom-call | flops 1572864 | bytes 131072 | tf_op jit(solution)/shard_map/expert_rows/pallas_call | solution.py:289
  44.3 1.9 %collective-permute-done.9.refs_1_ = bf16[256,512]{1,0:T(8,128)(2,1)S(1)} collective-permute-done((bf16[256,512]{1,0:T(8,128)(2,1)S(1)}, bf16[256,512]{1,0:T(8,128)(2,1)S(1)}, u32[]{:S(2)}, u32[]{:S(2)}) %collective-permute-start.9) | collective-permute-done | bytes 262176 | tf_op jit(solution)/shard_map/ppermute | solution.py:462
  46.3 5.1 %expert_rows.6 = (f32[4,2,256,512]{3,2,1,0:T(8,128)S(1)}, f32[256,256]{1,0:T(8,128)S(1)}, f32[2,256]{1,0:T(2,128)S(1)}) custom-call(bf16[256,512]{1,0:T(8,128)(2,1)S(1)} %collective-permute-done.8.refs_0_, bf16[256,512]{1,0:T(8,128)(2,1)S(1)} %collective-permute-done.9.refs_1_, bf16[256,256]{1,0:T(8,128)(2,1)S(1)} %copy-done.1, ...), custom_call_target="tpu_custom_call" | custom-call | flops 1572864 | bytes 131072 | tf_op jit(solution)/shard_map/expert_rows/pallas_call | solution.py:289
  51.4 3.2 %expert_rows.7 = (f32[4,2,256,512]{3,2,1,0:T(8,128)S(1)}, f32[256,256]{1,0:T(8,128)S(1)}, f32[1,256]{1,0:T(1,128)S(1)}) custom-call(bf16[256,512]{1,0:T(8,128)(2,1)S(1)} %collective-permute-done.7.refs_0_, bf16[256,256]{1,0:T(8,128)(2,1)S(1)} %copy-done.1, bf16[2,256,512]{2,1,0:T(8,128)(2,1)S(1)} %pair.2.refs_3_.refs_2_, ...), custom_call_target="tpu_custom_call" | custom-call | flops 786432 | bytes 65536 | tf_op jit(solution)/shard_map/expert_rows/pallas_call | solution.py:289
  54.6 3.7 %collective-permute-done.6.refs_1_ = bf16[256,512]{1,0:T(8,128)(2,1)S(1)} collective-permute-done((bf16[256,512]{1,0:T(8,128)(2,1)S(1)}, bf16[256,512]{1,0:T(8,128)(2,1)S(1)}, u32[]{:S(2)}, u32[]{:S(2)}) %collective-permute-start.6) | collective-permute-done | bytes 262176 | tf_op jit(solution)/shard_map/ppermute | solution.py:462
  58.3 4.9 %expert_rows.8 = (f32[4,2,256,512]{3,2,1,0:T(8,128)S(1)}, f32[256,256]{1,0:T(8,128)S(1)}, f32[2,256]{1,0:T(2,128)S(1)}) custom-call(bf16[256,512]{1,0:T(8,128)(2,1)S(1)} %collective-permute-done.5.refs_0_, bf16[256,512]{1,0:T(8,128)(2,1)S(1)} %collective-permute-done.6.refs_1_, bf16[256,256]{1,0:T(8,128)(2,1)S(1)} %copy-done.1, ...), custom_call_target="tpu_custom_call" | custom-call | flops 1572864 | bytes 131072 | tf_op jit(solution)/shard_map/expert_rows/pallas_call | solution.py:289
  63.2 3.2 %expert_rows.9 = (f32[4,2,256,512]{3,2,1,0:T(8,128)S(1)}, f32[64,256]{1,0:T(8,128)S(1)}, f32[64,256]{1,0:T(8,128)S(1)}, f32[64,256]{1,0:T(8,128)S(1)}, f32[64,256]{1,0:T(8,128)S(1)}, /*index=5*/f32[8,256]{1,0:T(8,128)S(1)}) custom-call(bf16[256,512]{1,0:T(8,128)(2,1)S(1)} %collective-permute-done.refs_0_, bf16[256,256]{1,0:T(8,128)(2,1)S(1)} %copy-done.1, ...), custom_call_target="tpu_custom_call" | custom-call | flops 786432 | bytes 65536 | tf_op jit(solution)/shard_map/expert_rows/pallas_call | solution.py:289
  66.5 1.5 %collective-permute-start.11 = (f32[64,256]{1,0:T(8,128)S(1)}, f32[64,256]{1,0:T(8,128)S(1)}, u32[]{:S(2)}, u32[]{:S(2)}) collective-permute-start(f32[64,256]{1,0:T(8,128)S(1)} %get-tuple-element.72), channel_id=1, source_target_pairs={{0,8},{8,0},{16,24},{24,16},{1,9},{9,1},{17,25},{25,17},{2,10},{10... | collective-permute-start | bytes 196616 | tf_op jit(solution)/shard_map/ppermute | solution.py:462
  68.0 1.5 %collective-permute-start.12 = (f32[64,256]{1,0:T(8,128)S(1)}, f32[64,256]{1,0:T(8,128)S(1)}, u32[]{:S(2)}, u32[]{:S(2)}) collective-permute-start(f32[64,256]{1,0:T(8,128)S(1)} %get-tuple-element.73), channel_id=1, source_target_pairs={{0,16},{8,24},{16,0},{24,8},{1,17},{9,25},{17,1},{25,9},{2,18},{10... | collective-permute-start | bytes 196616 | tf_op jit(solution)/shard_map/ppermute | solution.py:462
  72.2 2.4 %collective-permute-done.13.q3 = f32[64,256]{1,0:T(8,128)S(1)} collective-permute-done((f32[64,256]{1,0:T(8,128)S(1)}, f32[64,256]{1,0:T(8,128)S(1)}, u32[]{:S(2)}, u32[]{:S(2)}) %collective-permute-start.13) | collective-permute-done | bytes 65568 | tf_op jit(solution)/shard_map/ppermute | solution.py:462
  77.3 1.7 %collective-permute-start.15 = (f32[40,256]{1,0:T(8,128)S(1)}, f32[40,256]{1,0:T(8,128)S(1)}, u32[]{:S(2)}, u32[]{:S(2)}) collective-permute-start(f32[40,256]{1,0:T(8,128)S(1)} %get-tuple-element.79), channel_id=1, source_target_pairs={{0,2},{1,3},{2,0},{3,1},{4,6},{5,7},{6,4},{7,5},{8,10},{9,11},{10,... | collective-permute-start | bytes 122888 | tf_op jit(solution)/shard_map/ppermute | solution.py:462
  79.0 2.6 %collective-permute-start.16 = (f32[40,256]{1,0:T(8,128)S(1)}, f32[40,256]{1,0:T(8,128)S(1)}, u32[]{:S(2)}, u32[]{:S(2)}) collective-permute-start(f32[40,256]{1,0:T(8,128)S(1)} %get-tuple-element.80), channel_id=1, source_target_pairs={{0,4},{1,5},{2,6},{3,7},{4,0},{5,1},{6,2},{7,3},{8,12},{9,13},{10,... | collective-permute-start | bytes 122888 | tf_op jit(solution)/shard_map/ppermute | solution.py:462
  82.3 2.0 %collective-permute-done.16.refs_2_ = f32[40,256]{1,0:T(8,128)S(1)} collective-permute-done((f32[40,256]{1,0:T(8,128)S(1)}, f32[40,256]{1,0:T(8,128)S(1)}, u32[]{:S(2)}, u32[]{:S(2)}) %collective-permute-start.16) | collective-permute-done | bytes 40992 | tf_op jit(solution)/shard_map/ppermute | solution.py:462
  84.3 3.1 %collective-permute-done.17.refs_3_ = f32[40,256]{1,0:T(8,128)S(1)} collective-permute-done((f32[40,256]{1,0:T(8,128)S(1)}, f32[40,256]{1,0:T(8,128)S(1)}, u32[]{:S(2)}, u32[]{:S(2)}) %collective-permute-start.17) | collective-permute-done | bytes 40992 | tf_op jit(solution)/shard_map/ppermute | solution.py:462
  87.6 1.5 %collective-permute-start.24 = (bf16[256,512]{1,0:T(8,128)(2,1)S(1)}, bf16[256,512]{1,0:T(8,128)(2,1)S(1)}, u32[]{:S(2)}, u32[]{:S(2)}) collective-permute-start(bf16[256,512]{1,0:T(8,128)(2,1)S(1)} %get-tuple-element.88), channel_id=1, source_target_pairs={{0,16},{8,24},{16,0},{24,8},{1,17},{9,25},{17,1},{25,9},{2,18},{10... | collective-permute-start | bytes 786440 | tf_op jit(solution)/shard_map/ppermute | solution.py:462
  92.6 1.5 %collective-permute-start.20 = (f32[64,256]{1,0:T(8,128)S(1)}, f32[64,256]{1,0:T(8,128)S(1)}, u32[]{:S(2)}, u32[]{:S(2)}) collective-permute-start(f32[64,256]{1,0:T(8,128)S(1)} %join.1.refs_0_), channel_id=1, source_target_pairs={{0,16},{8,24},{16,0},{24,8},{1,17},{9,25},{17,1},{25,9},{2,18},{10... | collective-permute-start | bytes 196616 | tf_op jit(solution)/shard_map/ppermute | solution.py:462
  96.0 2.1 %adam.1 = (f32[1,2,256,512]{3,2,1,0:T(8,128)}, f32[1,2,256,512]{3,2,1,0:T(8,128)}, f32[1,2,256,512]{3,2,1,0:T(8,128)}, f32[8,128]{1,0:T(8,128)S(1)}) custom-call(f32[1,2,256,512]{3,2,1,0:T(8,128)S(1)} %copy-done, f32[1,2,256,512]{3,2,1,0:T(8,128)S(1)} %copy-done.2, f32[1,2,256,512]{3,2,1,0:T(8,128)S(1)} %copy-done.3, ...), custom_call_target="tpu_custom_call" | custom-call | flops 5242880 | bytes 2097152 | tf_op jit(solution)/shard_map/adam/pallas_call | solution.py:446
  (63 shorter events, 19.1 us)
Async XLA Ops:
  2.0 12.3 %collective-permute-start.3 = (bf16[256,512]{1,0:T(8,128)(2,1)S(1)}, bf16[256,512]{1,0:T(8,128)(2,1)S(1)}, u32[]{:S(2)}, u32[]{:S(2)}) collective-permute-start(bf16[256,512]{1,0:T(8,128)(2,1)S(1)} %get-tuple-element.95.one_ref), channel_id=1, source_target_pairs={{0,16},{8,24},{16,0},{24,8},{1,17},{9,25},{17,1},{25,9},{2,18},{10... | collective-permute-start | bytes 786440 | tf_op jit(solution)/shard_map/ppermute | solution.py:462
  5.0 8.6 %collective-permute-start.1 = (bf16[256,512]{1,0:T(8,128)(2,1)S(1)}, bf16[256,512]{1,0:T(8,128)(2,1)S(1)}, u32[]{:S(2)}, u32[]{:S(2)}) collective-permute-start(bf16[256,512]{1,0:T(8,128)(2,1)S(1)} %get-tuple-element.96.one_ref), channel_id=1, source_target_pairs={{0,8},{8,0},{16,24},{24,16},{1,9},{9,1},{17,25},{25,17},{2,10},{10... | collective-permute-start | bytes 786440 | tf_op jit(solution)/shard_map/ppermute | solution.py:462
  13.7 25.7 %collective-permute-start.2 = (bf16[2,256,512]{2,1,0:T(8,128)(2,1)S(1)}, bf16[2,256,512]{2,1,0:T(8,128)(2,1)S(1)}, u32[]{:S(2)}, u32[]{:S(2)}) collective-permute-start(bf16[2,256,512]{2,1,0:T(8,128)(2,1)S(1)} %pair.2.refs_3_.refs_2_), channel_id=1, source_target_pairs={{0,16},{8,24},{16,0},{24,8},{1,17},{9,25},{17,1},{25,9},{2,18},{10... | collective-permute-start | bytes 1572872 | tf_op jit(solution)/shard_map/ppermute | solution.py:462
  14.3 25.1 %collective-permute-start.4 = (bf16[2,256,512]{2,1,0:T(8,128)(2,1)S(1)}, bf16[2,256,512]{2,1,0:T(8,128)(2,1)S(1)}, u32[]{:S(2)}, u32[]{:S(2)}) collective-permute-start(bf16[2,256,512]{2,1,0:T(8,128)(2,1)S(1)} %pair.3.refs_5_.refs_4_), channel_id=1, source_target_pairs={{0,8},{8,0},{16,24},{24,16},{1,9},{9,1},{17,25},{25,17},{2,10},{10... | collective-permute-start | bytes 1572872 | tf_op jit(solution)/shard_map/ppermute | solution.py:462
  15.0 2.8 %collective-permute-start.8 = (bf16[256,512]{1,0:T(8,128)(2,1)S(1)}, bf16[256,512]{1,0:T(8,128)(2,1)S(1)}, u32[]{:S(2)}, u32[]{:S(2)}) collective-permute-start(bf16[256,512]{1,0:T(8,128)(2,1)S(1)} %get-tuple-element.55), channel_id=1, source_target_pairs={{0,1},{1,0},{2,3},{3,2},{4,5},{5,4},{6,7},{7,6},{8,9},{9,8},{10,11... | collective-permute-start | bytes 786440 | tf_op jit(solution)/shard_map/ppermute | solution.py:462
  15.0 21.2 %collective-permute-start.10 = (bf16[256,512]{1,0:T(8,128)(2,1)S(1)}, bf16[256,512]{1,0:T(8,128)(2,1)S(1)}, u32[]{:S(2)}, u32[]{:S(2)}) collective-permute-start(bf16[256,512]{1,0:T(8,128)(2,1)S(1)} %get-tuple-element.58), channel_id=1, source_target_pairs={{0,4},{1,5},{2,6},{3,7},{4,0},{5,1},{6,2},{7,3},{8,12},{9,13},{10,... | collective-permute-start | bytes 786440 | tf_op jit(solution)/shard_map/ppermute | solution.py:462
  17.6 28.7 %collective-permute-start.9 = (bf16[256,512]{1,0:T(8,128)(2,1)S(1)}, bf16[256,512]{1,0:T(8,128)(2,1)S(1)}, u32[]{:S(2)}, u32[]{:S(2)}) collective-permute-start(bf16[256,512]{1,0:T(8,128)(2,1)S(1)} %get-tuple-element.56), channel_id=1, source_target_pairs={{0,5},{1,4},{2,7},{3,6},{4,1},{5,0},{6,3},{7,2},{8,13},{9,12},{10,... | collective-permute-start | bytes 786440 | tf_op jit(solution)/shard_map/ppermute | solution.py:462
  17.7 33.6 %collective-permute-start.7 = (bf16[256,512]{1,0:T(8,128)(2,1)S(1)}, bf16[256,512]{1,0:T(8,128)(2,1)S(1)}, u32[]{:S(2)}, u32[]{:S(2)}) collective-permute-start(bf16[256,512]{1,0:T(8,128)(2,1)S(1)} %get-tuple-element.54), channel_id=1, source_target_pairs={{0,2},{1,3},{2,0},{3,1},{4,6},{5,7},{6,4},{7,5},{8,10},{9,11},{10,... | collective-permute-start | bytes 786440 | tf_op jit(solution)/shard_map/ppermute | solution.py:462
  36.2 18.4 %collective-permute-start.5 = (bf16[256,512]{1,0:T(8,128)(2,1)S(1)}, bf16[256,512]{1,0:T(8,128)(2,1)S(1)}, u32[]{:S(2)}, u32[]{:S(2)}) collective-permute-start(bf16[256,512]{1,0:T(8,128)(2,1)S(1)} %get-tuple-element.52), channel_id=1, source_target_pairs={{0,6},{1,7},{2,4},{3,5},{4,2},{5,3},{6,0},{7,1},{8,14},{9,15},{10,... | collective-permute-start | bytes 786440 | tf_op jit(solution)/shard_map/ppermute | solution.py:462
  39.4 18.9 %collective-permute-start.6 = (bf16[256,512]{1,0:T(8,128)(2,1)S(1)}, bf16[256,512]{1,0:T(8,128)(2,1)S(1)}, u32[]{:S(2)}, u32[]{:S(2)}) collective-permute-start(bf16[256,512]{1,0:T(8,128)(2,1)S(1)} %get-tuple-element.53), channel_id=1, source_target_pairs={{0,3},{1,2},{2,1},{3,0},{4,7},{5,6},{6,5},{7,4},{8,11},{9,10},{10,... | collective-permute-start | bytes 786440 | tf_op jit(solution)/shard_map/ppermute | solution.py:462
  39.4 23.9 %collective-permute-start = (bf16[256,512]{1,0:T(8,128)(2,1)S(1)}, bf16[256,512]{1,0:T(8,128)(2,1)S(1)}, u32[]{:S(2)}, u32[]{:S(2)}) collective-permute-start(bf16[256,512]{1,0:T(8,128)(2,1)S(1)} %get-tuple-element.50), channel_id=1, source_target_pairs={{0,7},{1,6},{2,5},{3,4},{4,3},{5,2},{6,1},{7,0},{8,15},{9,14},{10,... | collective-permute-start | bytes 786440 | tf_op jit(solution)/shard_map/ppermute | solution.py:462
  66.5 4.3 %collective-permute-start.11 = (f32[64,256]{1,0:T(8,128)S(1)}, f32[64,256]{1,0:T(8,128)S(1)}, u32[]{:S(2)}, u32[]{:S(2)}) collective-permute-start(f32[64,256]{1,0:T(8,128)S(1)} %get-tuple-element.72), channel_id=1, source_target_pairs={{0,8},{8,0},{16,24},{24,16},{1,9},{9,1},{17,25},{25,17},{2,10},{10... | collective-permute-start | bytes 196616 | tf_op jit(solution)/shard_map/ppermute | solution.py:462
  68.0 4.3 %collective-permute-start.12 = (f32[64,256]{1,0:T(8,128)S(1)}, f32[64,256]{1,0:T(8,128)S(1)}, u32[]{:S(2)}, u32[]{:S(2)}) collective-permute-start(f32[64,256]{1,0:T(8,128)S(1)} %get-tuple-element.73), channel_id=1, source_target_pairs={{0,16},{8,24},{16,0},{24,8},{1,17},{9,25},{17,1},{25,9},{2,18},{10... | collective-permute-start | bytes 196616 | tf_op jit(solution)/shard_map/ppermute | solution.py:462
  69.5 5.2 %collective-permute-start.13 = (f32[64,256]{1,0:T(8,128)S(1)}, f32[64,256]{1,0:T(8,128)S(1)}, u32[]{:S(2)}, u32[]{:S(2)}) collective-permute-start(f32[64,256]{1,0:T(8,128)S(1)} %get-tuple-element.74), channel_id=1, source_target_pairs={{0,24},{8,16},{16,8},{24,0},{1,25},{9,17},{17,9},{25,1},{2,26},{10... | collective-permute-start | bytes 196616 | tf_op jit(solution)/shard_map/ppermute | solution.py:462
  74.8 12.6 %collective-permute-start.22 = (bf16[2,256,512]{2,1,0:T(8,128)(2,1)S(1)}, bf16[2,256,512]{2,1,0:T(8,128)(2,1)S(1)}, u32[]{:S(2)}, u32[]{:S(2)}) collective-permute-start(bf16[2,256,512]{2,1,0:T(8,128)(2,1)S(1)} %get-tuple-element.86), channel_id=1, source_target_pairs={{0,8},{8,0},{16,24},{24,16},{1,9},{9,1},{17,25},{25,17},{2,10},{10... | collective-permute-start | bytes 1572872 | tf_op jit(solution)/shard_map/ppermute | solution.py:462
  75.5 12.0 %collective-permute-start.23 = (bf16[2,256,512]{2,1,0:T(8,128)(2,1)S(1)}, bf16[2,256,512]{2,1,0:T(8,128)(2,1)S(1)}, u32[]{:S(2)}, u32[]{:S(2)}) collective-permute-start(bf16[2,256,512]{2,1,0:T(8,128)(2,1)S(1)} %get-tuple-element.87), channel_id=1, source_target_pairs={{0,16},{8,24},{16,0},{24,8},{1,17},{9,25},{17,1},{25,9},{2,18},{10... | collective-permute-start | bytes 1572872 | tf_op jit(solution)/shard_map/ppermute | solution.py:462
  77.3 5.0 %collective-permute-start.15 = (f32[40,256]{1,0:T(8,128)S(1)}, f32[40,256]{1,0:T(8,128)S(1)}, u32[]{:S(2)}, u32[]{:S(2)}) collective-permute-start(f32[40,256]{1,0:T(8,128)S(1)} %get-tuple-element.79), channel_id=1, source_target_pairs={{0,2},{1,3},{2,0},{3,1},{4,6},{5,7},{6,4},{7,5},{8,10},{9,11},{10,... | collective-permute-start | bytes 122888 | tf_op jit(solution)/shard_map/ppermute | solution.py:462
  79.0 5.3 %collective-permute-start.16 = (f32[40,256]{1,0:T(8,128)S(1)}, f32[40,256]{1,0:T(8,128)S(1)}, u32[]{:S(2)}, u32[]{:S(2)}) collective-permute-start(f32[40,256]{1,0:T(8,128)S(1)} %get-tuple-element.80), channel_id=1, source_target_pairs={{0,4},{1,5},{2,6},{3,7},{4,0},{5,1},{6,2},{7,3},{8,12},{9,13},{10,... | collective-permute-start | bytes 122888 | tf_op jit(solution)/shard_map/ppermute | solution.py:462
  81.6 5.8 %collective-permute-start.17 = (f32[40,256]{1,0:T(8,128)S(1)}, f32[40,256]{1,0:T(8,128)S(1)}, u32[]{:S(2)}, u32[]{:S(2)}) collective-permute-start(f32[40,256]{1,0:T(8,128)S(1)} %get-tuple-element.81), channel_id=1, source_target_pairs={{0,6},{1,7},{2,4},{3,5},{4,2},{5,3},{6,0},{7,1},{8,14},{9,15},{10,... | collective-permute-start | bytes 122888 | tf_op jit(solution)/shard_map/ppermute | solution.py:462
  87.6 7.8 %collective-permute-start.24 = (bf16[256,512]{1,0:T(8,128)(2,1)S(1)}, bf16[256,512]{1,0:T(8,128)(2,1)S(1)}, u32[]{:S(2)}, u32[]{:S(2)}) collective-permute-start(bf16[256,512]{1,0:T(8,128)(2,1)S(1)} %get-tuple-element.88), channel_id=1, source_target_pairs={{0,16},{8,24},{16,0},{24,8},{1,17},{9,25},{17,1},{25,9},{2,18},{10... | collective-permute-start | bytes 786440 | tf_op jit(solution)/shard_map/ppermute | solution.py:462
  89.2 6.9 %collective-permute-start.25 = (bf16[256,512]{1,0:T(8,128)(2,1)S(1)}, bf16[256,512]{1,0:T(8,128)(2,1)S(1)}, u32[]{:S(2)}, u32[]{:S(2)}) collective-permute-start(bf16[256,512]{1,0:T(8,128)(2,1)S(1)} %get-tuple-element.89), channel_id=1, source_target_pairs={{0,8},{8,0},{16,24},{24,16},{1,9},{9,1},{17,25},{25,17},{2,10},{10... | collective-permute-start | bytes 786440 | tf_op jit(solution)/shard_map/ppermute | solution.py:462
  91.9 6.2 %collective-permute-start.21 = (f32[64,256]{1,0:T(8,128)S(1)}, f32[64,256]{1,0:T(8,128)S(1)}, u32[]{:S(2)}, u32[]{:S(2)}) collective-permute-start(f32[64,256]{1,0:T(8,128)S(1)} %join.1.refs_0_), channel_id=1, source_target_pairs={{0,24},{8,16},{16,8},{24,0},{1,25},{9,17},{17,9},{25,1},{2,26},{10... | collective-permute-start | bytes 196616 | tf_op jit(solution)/shard_map/ppermute | solution.py:462
  92.6 5.6 %collective-permute-start.20 = (f32[64,256]{1,0:T(8,128)S(1)}, f32[64,256]{1,0:T(8,128)S(1)}, u32[]{:S(2)}, u32[]{:S(2)}) collective-permute-start(f32[64,256]{1,0:T(8,128)S(1)} %join.1.refs_0_), channel_id=1, source_target_pairs={{0,16},{8,24},{16,0},{24,8},{1,17},{9,25},{17,1},{25,9},{2,18},{10... | collective-permute-start | bytes 196616 | tf_op jit(solution)/shard_map/ppermute | solution.py:462
  94.0 4.3 %collective-permute-start.19 = (f32[64,256]{1,0:T(8,128)S(1)}, f32[64,256]{1,0:T(8,128)S(1)}, u32[]{:S(2)}, u32[]{:S(2)}) collective-permute-start(f32[64,256]{1,0:T(8,128)S(1)} %join.1.refs_0_), channel_id=1, source_target_pairs={{0,8},{8,0},{16,24},{24,16},{1,9},{9,1},{17,25},{25,17},{2,10},{10... | collective-permute-start | bytes 196616 | tf_op jit(solution)/shard_map/ppermute | solution.py:462
  (10 other events, 99.5 us)

commit v15 on v14

--- a/solution.py
+++ b/solution.py
@@ -486,7 +486,7 @@
     ups, downs = pair(up, near_up, place), pair(down, near_down, place)
     weights = [ups, swap(ups, "dp", 2), downs, swap(downs, "dp", 1)]
     if in_turns(experts):
-        batches, later = ((0, 4), (1, 5), (2,), (6, 3), (7,)), ()
+        batches, later = ((0, 4), (1, 5), (2,), (6,), (7, 3)), ()
     else:
         batches, later = (range(experts // 2), range(experts // 2, experts)), ()
     order = [s for batch in batches for s in batch]

time: 99.4 us -> 103 us (1.036)
  waiting for transfers between devices: 34.4 us -> 38.3 us
    ppermute x26, waiting for transfers between devices: 34.4 us -> 38.3 us  [swap(): lax.ppermute(value, axis, [(i, i ^ s) for i in range(lax.axis_size(axis))])]
  transfers between devices with their start and end apart: 26 -> 26, of which waited for: 13 -> 12; matrix products, arithmetic and copies ran while one was open for 0% -> 0% of each run, Pallas kernels for 25% -> 23%
where the time goes in v15:
time: 103 us
  waiting for transfers between devices  38.3 us (37%)
  Pallas kernels  29.3 us (28%)
  starting transfers between devices  29 us (28%)
  local copies, waits for them, and re-layouts  3.7 us (4%)
  other arithmetic  1.29 us (1%)
    ppermute x26, waiting for transfers between devices, swap(): lax.ppermute(value, axis, [(i, i ^ s) for i in range(lax.axis_size(axis))])  38.3 us
    ppermute x26, starting transfers between devices, swap(): lax.ppermute(value, axis, [(i, i ^ s) for i in range(lax.axis_size(axis))])  29 us
    pallas_call x5, Pallas kernels, expert_call(): pl.pallas_call(functools.partial(expert_kernel, counts, order, first, len...  21.4 us
    unnamed x16, local copies, waits for them, and re-layouts  3.66 us
    pallas_call x1, Pallas kernels, pack(): pl.pallas_call(functools.partial(pack_kernel, experts, capacity), out_sha...  3.5 us
    pallas_call x1, Pallas kernels, adam(): pl.pallas_call(adam_kernel, out_shape=[shape] * 3 + [jax.ShapeDtypeStruct...  2.07 us
  transfers between devices with their start and end apart: 26, of which 12 were waited for; matrix products, arithmetic and copies ran while one was open for 0% of the time, Pallas kernels for 23%

profile of v15, /device:TPU:0, one launch (start us, length us, event | category | flops | bytes accessed | tf_op | source)
XLA Modules:
  0.0 102.5 jit_solution(15890863045851901172)
XLA Ops:
  2.0 3.0 %collective-permute-start.4 = (bf16[256,512]{1,0:T(8,128)(2,1)S(1)}, bf16[256,512]{1,0:T(8,128)(2,1)S(1)}, u32[]{:S(2)}, u32[]{:S(2)}) collective-permute-start(bf16[256,512]{1,0:T(8,128)(2,1)S(1)} %get-tuple-element.95.one_ref), channel_id=1, source_target_pairs={{0,16},{8,24},{16,0},{24,8},{1,17},{9,25},{17,1},{25,9},{2,18},{10... | collective-permute-start | bytes 786440 | tf_op jit(solution)/shard_map/ppermute | solution.py:462
  5.0 1.5 %collective-permute-start.2 = (bf16[256,512]{1,0:T(8,128)(2,1)S(1)}, bf16[256,512]{1,0:T(8,128)(2,1)S(1)}, u32[]{:S(2)}, u32[]{:S(2)}) collective-permute-start(bf16[256,512]{1,0:T(8,128)(2,1)S(1)} %get-tuple-element.96.one_ref), channel_id=1, source_target_pairs={{0,8},{8,0},{16,24},{24,16},{1,9},{9,1},{17,25},{25,17},{2,10},{10... | collective-permute-start | bytes 786440 | tf_op jit(solution)/shard_map/ppermute | solution.py:462
  10.1 3.5 %pack_rows.1 = (bf16[256,512]{1,0:T(8,128)(2,1)S(1)}, bf16[256,512]{1,0:T(8,128)(2,1)S(1)}, bf16[256,512]{1,0:T(8,128)(2,1)S(1)}, bf16[256,512]{1,0:T(8,128)(2,1...) custom-call(s32[1]{0:T(128)} %bitcast.1.me_ref, ...), custom_call_target="tpu_custom_call" | custom-call | flops 3221225472 | bytes 6291456 | tf_op jit(solution)/shard_map/pack_rows/pallas_call | solution.py:85
  15.0 2.6 %collective-permute-start.10 = (bf16[256,512]{1,0:T(8,128)(2,1)S(1)}, bf16[256,512]{1,0:T(8,128)(2,1)S(1)}, u32[]{:S(2)}, u32[]{:S(2)}) collective-permute-start(bf16[256,512]{1,0:T(8,128)(2,1)S(1)} %get-tuple-element.58), channel_id=1, source_target_pairs={{0,4},{1,5},{2,6},{3,7},{4,0},{5,1},{6,2},{7,3},{8,12},{9,13},{10,... | collective-permute-start | bytes 786440 | tf_op jit(solution)/shard_map/ppermute | solution.py:462
  17.7 1.6 %collective-permute-start.7 = (bf16[256,512]{1,0:T(8,128)(2,1)S(1)}, bf16[256,512]{1,0:T(8,128)(2,1)S(1)}, u32[]{:S(2)}, u32[]{:S(2)}) collective-permute-start(bf16[256,512]{1,0:T(8,128)(2,1)S(1)} %get-tuple-element.54), channel_id=1, source_target_pairs={{0,2},{1,3},{2,0},{3,1},{4,6},{5,7},{6,4},{7,5},{8,10},{9,11},{10,... | collective-permute-start | bytes 786440 | tf_op jit(solution)/shard_map/ppermute | solution.py:462
  19.3 16.9 %collective-permute-done.10.refs_1_ = bf16[256,512]{1,0:T(8,128)(2,1)S(1)} collective-permute-done((bf16[256,512]{1,0:T(8,128)(2,1)S(1)}, bf16[256,512]{1,0:T(8,128)(2,1)S(1)}, u32[]{:S(2)}, u32[]{:S(2)}) %collective-permute-start.10) | collective-permute-done | bytes 262176 | tf_op jit(solution)/shard_map/ppermute | solution.py:462
  36.2 3.1 %collective-permute-start.6 = (bf16[256,512]{1,0:T(8,128)(2,1)S(1)}, bf16[256,512]{1,0:T(8,128)(2,1)S(1)}, u32[]{:S(2)}, u32[]{:S(2)}) collective-permute-start(bf16[256,512]{1,0:T(8,128)(2,1)S(1)} %get-tuple-element.53), channel_id=1, source_target_pairs={{0,6},{1,7},{2,4},{3,5},{4,2},{5,3},{6,0},{7,1},{8,14},{9,15},{10,... | collective-permute-start | bytes 786440 | tf_op jit(solution)/shard_map/ppermute | solution.py:462
  39.5 4.9 %expert_rows.5 = (f32[4,2,256,512]{3,2,1,0:T(8,128)S(1)}, f32[256,256]{1,0:T(8,128)S(1)}, f32[2,256]{1,0:T(2,128)S(1)}) custom-call(bf16[256,512]{1,0:T(8,128)(2,1)S(1)} %get-tuple-element.57.refs_0_, bf16[256,512]{1,0:T(8,128)(2,1)S(1)} %collective-permute-done.10.refs_1_, bf16[256,256]{1,0:T(8,128)(2,1)S(1)} %copy-done.1, ...), custom_call_target="tpu_custom_call" | custom-call | flops 1572864 | bytes 131072 | tf_op jit(solution)/shard_map/expert_rows/pallas_call | solution.py:289
  44.3 7.5 %collective-permute-done.9.refs_1_ = bf16[256,512]{1,0:T(8,128)(2,1)S(1)} collective-permute-done((bf16[256,512]{1,0:T(8,128)(2,1)S(1)}, bf16[256,512]{1,0:T(8,128)(2,1)S(1)}, u32[]{:S(2)}, u32[]{:S(2)}) %collective-permute-start.9) | collective-permute-done | bytes 262176 | tf_op jit(solution)/shard_map/ppermute | solution.py:462
  51.8 5.1 %expert_rows.6 = (f32[4,2,256,512]{3,2,1,0:T(8,128)S(1)}, f32[256,256]{1,0:T(8,128)S(1)}, f32[2,256]{1,0:T(2,128)S(1)}) custom-call(bf16[256,512]{1,0:T(8,128)(2,1)S(1)} %collective-permute-done.8.refs_0_, bf16[256,512]{1,0:T(8,128)(2,1)S(1)} %collective-permute-done.9.refs_1_, bf16[256,256]{1,0:T(8,128)(2,1)S(1)} %copy-done.1, ...), custom_call_target="tpu_custom_call" | custom-call | flops 1572864 | bytes 131072 | tf_op jit(solution)/shard_map/expert_rows/pallas_call | solution.py:289
  57.0 3.2 %expert_rows.7 = (f32[4,2,256,512]{3,2,1,0:T(8,128)S(1)}, f32[256,256]{1,0:T(8,128)S(1)}, f32[1,256]{1,0:T(1,128)S(1)}) custom-call(bf16[256,512]{1,0:T(8,128)(2,1)S(1)} %collective-permute-done.7.refs_0_, bf16[256,256]{1,0:T(8,128)(2,1)S(1)} %copy-done.1, bf16[2,256,512]{2,1,0:T(8,128)(2,1)S(1)} %pair.2.refs_3_.refs_2_, ...), custom_call_target="tpu_custom_call" | custom-call | flops 786432 | bytes 65536 | tf_op jit(solution)/shard_map/expert_rows/pallas_call | solution.py:289
  60.2 3.2 %expert_rows.8 = (f32[4,2,256,512]{3,2,1,0:T(8,128)S(1)}, f32[256,256]{1,0:T(8,128)S(1)}, f32[1,256]{1,0:T(1,128)S(1)}) custom-call(bf16[256,512]{1,0:T(8,128)(2,1)S(1)} %collective-permute-done.6.refs_0_, bf16[256,256]{1,0:T(8,128)(2,1)S(1)} %copy-done.1, bf16[2,256,512]{2,1,0:T(8,128)(2,1)S(1)} %pair.2.refs_3_.refs_2_, ...), custom_call_target="tpu_custom_call" | custom-call | flops 786432 | bytes 65536 | tf_op jit(solution)/shard_map/expert_rows/pallas_call | solution.py:289
  63.5 5.0 %expert_rows.9 = (f32[4,2,256,512]{3,2,1,0:T(8,128)S(1)}, f32[64,256]{1,0:T(8,128)S(1)}, f32[64,256]{1,0:T(8,128)S(1)}, f32[64,256]{1,0:T(8,128)S(1)}, f32[64,256]{1,0:T(8,128)S(1)}, /*index=5*/f32[8,256]{1,0:T(8,128)S(1)}) custom-call(bf16[256,512]{1,0:T(8,128)(2,1)S(1)} %collective-permute-done.refs_0_, ...), custom_call_target="tpu_custom_call" | custom-call | flops 1572864 | bytes 131072 | tf_op jit(solution)/shard_map/expert_rows/pallas_call | solution.py:289
  68.5 1.5 %collective-permute-start.11 = (f32[64,256]{1,0:T(8,128)S(1)}, f32[64,256]{1,0:T(8,128)S(1)}, u32[]{:S(2)}, u32[]{:S(2)}) collective-permute-start(f32[64,256]{1,0:T(8,128)S(1)} %get-tuple-element.72), channel_id=1, source_target_pairs={{0,8},{8,0},{16,24},{24,16},{1,9},{9,1},{17,25},{25,17},{2,10},{10... | collective-permute-start | bytes 196616 | tf_op jit(solution)/shard_map/ppermute | solution.py:462
  69.9 1.5 %collective-permute-start.12 = (f32[64,256]{1,0:T(8,128)S(1)}, f32[64,256]{1,0:T(8,128)S(1)}, u32[]{:S(2)}, u32[]{:S(2)}) collective-permute-start(f32[64,256]{1,0:T(8,128)S(1)} %get-tuple-element.73), channel_id=1, source_target_pairs={{0,16},{8,24},{16,0},{24,8},{1,17},{9,25},{17,1},{25,9},{2,18},{10... | collective-permute-start | bytes 196616 | tf_op jit(solution)/shard_map/ppermute | solution.py:462
  72.0 1.3 %collective-permute-done.11.q1 = f32[64,256]{1,0:T(8,128)S(1)} collective-permute-done((f32[64,256]{1,0:T(8,128)S(1)}, f32[64,256]{1,0:T(8,128)S(1)}, u32[]{:S(2)}, u32[]{:S(2)}) %collective-permute-start.11) | collective-permute-done | bytes 65568 | tf_op jit(solution)/shard_map/ppermute | solution.py:462
  73.3 1.9 %collective-permute-done.12.q2 = f32[64,256]{1,0:T(8,128)S(1)} collective-permute-done((f32[64,256]{1,0:T(8,128)S(1)}, f32[64,256]{1,0:T(8,128)S(1)}, u32[]{:S(2)}, u32[]{:S(2)}) %collective-permute-start.12) | collective-permute-done | bytes 65568 | tf_op jit(solution)/shard_map/ppermute | solution.py:462
  75.3 1.7 %collective-permute-done.13.q3 = f32[64,256]{1,0:T(8,128)S(1)} collective-permute-done((f32[64,256]{1,0:T(8,128)S(1)}, f32[64,256]{1,0:T(8,128)S(1)}, u32[]{:S(2)}, u32[]{:S(2)}) %collective-permute-start.13) | collective-permute-done | bytes 65568 | tf_op jit(solution)/shard_map/ppermute | solution.py:462
  81.1 3.4 %collective-permute-start.16 = (f32[40,256]{1,0:T(8,128)S(1)}, f32[40,256]{1,0:T(8,128)S(1)}, u32[]{:S(2)}, u32[]{:S(2)}) collective-permute-start(f32[40,256]{1,0:T(8,128)S(1)} %get-tuple-element.80), channel_id=1, source_target_pairs={{0,4},{1,5},{2,6},{3,7},{4,0},{5,1},{6,2},{7,3},{8,12},{9,13},{10,... | collective-permute-start | bytes 122888 | tf_op jit(solution)/shard_map/ppermute | solution.py:462
  84.5 2.8 %collective-permute-done.16.refs_2_ = f32[40,256]{1,0:T(8,128)S(1)} collective-permute-done((f32[40,256]{1,0:T(8,128)S(1)}, f32[40,256]{1,0:T(8,128)S(1)}, u32[]{:S(2)}, u32[]{:S(2)}) %collective-permute-start.16) | collective-permute-done | bytes 40992 | tf_op jit(solution)/shard_map/ppermute | solution.py:462
  87.3 3.0 %collective-permute-done.17.refs_3_ = f32[40,256]{1,0:T(8,128)S(1)} collective-permute-done((f32[40,256]{1,0:T(8,128)S(1)}, f32[40,256]{1,0:T(8,128)S(1)}, u32[]{:S(2)}, u32[]{:S(2)}) %collective-permute-start.17) | collective-permute-done | bytes 40992 | tf_op jit(solution)/shard_map/ppermute | solution.py:462
  92.2 1.4 %collective-permute-start.25 = (bf16[256,512]{1,0:T(8,128)(2,1)S(1)}, bf16[256,512]{1,0:T(8,128)(2,1)S(1)}, u32[]{:S(2)}, u32[]{:S(2)}) collective-permute-start(bf16[256,512]{1,0:T(8,128)(2,1)S(1)} %get-tuple-element.89), channel_id=1, source_target_pairs={{0,8},{8,0},{16,24},{24,16},{1,9},{9,1},{17,25},{25,17},{2,10},{10... | collective-permute-start | bytes 786440 | tf_op jit(solution)/shard_map/ppermute | solution.py:462
  97.1 1.4 %collective-permute-start.19 = (f32[64,256]{1,0:T(8,128)S(1)}, f32[64,256]{1,0:T(8,128)S(1)}, u32[]{:S(2)}, u32[]{:S(2)}) collective-permute-start(f32[64,256]{1,0:T(8,128)S(1)} %join.1.refs_0_), channel_id=1, source_target_pairs={{0,8},{8,0},{16,24},{24,16},{1,9},{9,1},{17,25},{25,17},{2,10},{10... | collective-permute-start | bytes 196616 | tf_op jit(solution)/shard_map/ppermute | solution.py:462
  99.3 2.1 %adam.1 = (f32[1,2,256,512]{3,2,1,0:T(8,128)}, f32[1,2,256,512]{3,2,1,0:T(8,128)}, f32[1,2,256,512]{3,2,1,0:T(8,128)}, f32[8,128]{1,0:T(8,128)S(1)}) custom-call(f32[1,2,256,512]{3,2,1,0:T(8,128)S(1)} %copy-done, f32[1,2,256,512]{3,2,1,0:T(8,128)S(1)} %copy-done.2, f32[1,2,256,512]{3,2,1,0:T(8,128)S(1)} %copy-done.3, ...), custom_call_target="tpu_custom_call" | custom-call | flops 5242880 | bytes 2097152 | tf_op jit(solution)/shard_map/adam/pallas_call | solution.py:446
  (63 shorter events, 18.5 us)
Async XLA Ops:
  2.0 12.3 %collective-permute-start.4 = (bf16[256,512]{1,0:T(8,128)(2,1)S(1)}, bf16[256,512]{1,0:T(8,128)(2,1)S(1)}, u32[]{:S(2)}, u32[]{:S(2)}) collective-permute-start(bf16[256,512]{1,0:T(8,128)(2,1)S(1)} %get-tuple-element.95.one_ref), channel_id=1, source_target_pairs={{0,16},{8,24},{16,0},{24,8},{1,17},{9,25},{17,1},{25,9},{2,18},{10... | collective-permute-start | bytes 786440 | tf_op jit(solution)/shard_map/ppermute | solution.py:462
  5.0 8.6 %collective-permute-start.2 = (bf16[256,512]{1,0:T(8,128)(2,1)S(1)}, bf16[256,512]{1,0:T(8,128)(2,1)S(1)}, u32[]{:S(2)}, u32[]{:S(2)}) collective-permute-start(bf16[256,512]{1,0:T(8,128)(2,1)S(1)} %get-tuple-element.96.one_ref), channel_id=1, source_target_pairs={{0,8},{8,0},{16,24},{24,16},{1,9},{9,1},{17,25},{25,17},{2,10},{10... | collective-permute-start | bytes 786440 | tf_op jit(solution)/shard_map/ppermute | solution.py:462
  13.7 25.7 %collective-permute-start.3 = (bf16[2,256,512]{2,1,0:T(8,128)(2,1)S(1)}, bf16[2,256,512]{2,1,0:T(8,128)(2,1)S(1)}, u32[]{:S(2)}, u32[]{:S(2)}) collective-permute-start(bf16[2,256,512]{2,1,0:T(8,128)(2,1)S(1)} %pair.2.refs_3_.refs_2_), channel_id=1, source_target_pairs={{0,16},{8,24},{16,0},{24,8},{1,17},{9,25},{17,1},{25,9},{2,18},{10... | collective-permute-start | bytes 1572872 | tf_op jit(solution)/shard_map/ppermute | solution.py:462
  14.3 25.1 %collective-permute-start.5 = (bf16[2,256,512]{2,1,0:T(8,128)(2,1)S(1)}, bf16[2,256,512]{2,1,0:T(8,128)(2,1)S(1)}, u32[]{:S(2)}, u32[]{:S(2)}) collective-permute-start(bf16[2,256,512]{2,1,0:T(8,128)(2,1)S(1)} %pair.3.refs_5_.refs_4_), channel_id=1, source_target_pairs={{0,8},{8,0},{16,24},{24,16},{1,9},{9,1},{17,25},{25,17},{2,10},{10... | collective-permute-start | bytes 1572872 | tf_op jit(solution)/shard_map/ppermute | solution.py:462
  15.0 2.8 %collective-permute-start.8 = (bf16[256,512]{1,0:T(8,128)(2,1)S(1)}, bf16[256,512]{1,0:T(8,128)(2,1)S(1)}, u32[]{:S(2)}, u32[]{:S(2)}) collective-permute-start(bf16[256,512]{1,0:T(8,128)(2,1)S(1)} %get-tuple-element.55), channel_id=1, source_target_pairs={{0,1},{1,0},{2,3},{3,2},{4,5},{5,4},{6,7},{7,6},{8,9},{9,8},{10,11... | collective-permute-start | bytes 786440 | tf_op jit(solution)/shard_map/ppermute | solution.py:462
  15.0 21.2 %collective-permute-start.10 = (bf16[256,512]{1,0:T(8,128)(2,1)S(1)}, bf16[256,512]{1,0:T(8,128)(2,1)S(1)}, u32[]{:S(2)}, u32[]{:S(2)}) collective-permute-start(bf16[256,512]{1,0:T(8,128)(2,1)S(1)} %get-tuple-element.58), channel_id=1, source_target_pairs={{0,4},{1,5},{2,6},{3,7},{4,0},{5,1},{6,2},{7,3},{8,12},{9,13},{10,... | collective-permute-start | bytes 786440 | tf_op jit(solution)/shard_map/ppermute | solution.py:462
  17.6 34.3 %collective-permute-start.9 = (bf16[256,512]{1,0:T(8,128)(2,1)S(1)}, bf16[256,512]{1,0:T(8,128)(2,1)S(1)}, u32[]{:S(2)}, u32[]{:S(2)}) collective-permute-start(bf16[256,512]{1,0:T(8,128)(2,1)S(1)} %get-tuple-element.56), channel_id=1, source_target_pairs={{0,5},{1,4},{2,7},{3,6},{4,1},{5,0},{6,3},{7,2},{8,13},{9,12},{10,... | collective-permute-start | bytes 786440 | tf_op jit(solution)/shard_map/ppermute | solution.py:462
  17.7 39.2 %collective-permute-start.7 = (bf16[256,512]{1,0:T(8,128)(2,1)S(1)}, bf16[256,512]{1,0:T(8,128)(2,1)S(1)}, u32[]{:S(2)}, u32[]{:S(2)}) collective-permute-start(bf16[256,512]{1,0:T(8,128)(2,1)S(1)} %get-tuple-element.54), channel_id=1, source_target_pairs={{0,2},{1,3},{2,0},{3,1},{4,6},{5,7},{6,4},{7,5},{8,10},{9,11},{10,... | collective-permute-start | bytes 786440 | tf_op jit(solution)/shard_map/ppermute | solution.py:462
  36.2 24.0 %collective-permute-start.6 = (bf16[256,512]{1,0:T(8,128)(2,1)S(1)}, bf16[256,512]{1,0:T(8,128)(2,1)S(1)}, u32[]{:S(2)}, u32[]{:S(2)}) collective-permute-start(bf16[256,512]{1,0:T(8,128)(2,1)S(1)} %get-tuple-element.53), channel_id=1, source_target_pairs={{0,6},{1,7},{2,4},{3,5},{4,2},{5,3},{6,0},{7,1},{8,14},{9,15},{10,... | collective-permute-start | bytes 786440 | tf_op jit(solution)/shard_map/ppermute | solution.py:462
  39.4 24.1 %collective-permute-start = (bf16[256,512]{1,0:T(8,128)(2,1)S(1)}, bf16[256,512]{1,0:T(8,128)(2,1)S(1)}, u32[]{:S(2)}, u32[]{:S(2)}) collective-permute-start(bf16[256,512]{1,0:T(8,128)(2,1)S(1)} %get-tuple-element.50), channel_id=1, source_target_pairs={{0,7},{1,6},{2,5},{3,4},{4,3},{5,2},{6,1},{7,0},{8,15},{9,14},{10,... | collective-permute-start | bytes 786440 | tf_op jit(solution)/shard_map/ppermute | solution.py:462
  39.4 24.1 %collective-permute-start.1 = (bf16[256,512]{1,0:T(8,128)(2,1)S(1)}, bf16[256,512]{1,0:T(8,128)(2,1)S(1)}, u32[]{:S(2)}, u32[]{:S(2)}) collective-permute-start(bf16[256,512]{1,0:T(8,128)(2,1)S(1)} %get-tuple-element.51), channel_id=1, source_target_pairs={{0,3},{1,2},{2,1},{3,0},{4,7},{5,6},{6,5},{7,4},{8,11},{9,10},{10,... | collective-permute-start | bytes 786440 | tf_op jit(solution)/shard_map/ppermute | solution.py:462
  68.5 4.9 %collective-permute-start.11 = (f32[64,256]{1,0:T(8,128)S(1)}, f32[64,256]{1,0:T(8,128)S(1)}, u32[]{:S(2)}, u32[]{:S(2)}) collective-permute-start(f32[64,256]{1,0:T(8,128)S(1)} %get-tuple-element.72), channel_id=1, source_target_pairs={{0,8},{8,0},{16,24},{24,16},{1,9},{9,1},{17,25},{25,17},{2,10},{10... | collective-permute-start | bytes 196616 | tf_op jit(solution)/shard_map/ppermute | solution.py:462
  69.9 5.3 %collective-permute-start.12 = (f32[64,256]{1,0:T(8,128)S(1)}, f32[64,256]{1,0:T(8,128)S(1)}, u32[]{:S(2)}, u32[]{:S(2)}) collective-permute-start(f32[64,256]{1,0:T(8,128)S(1)} %get-tuple-element.73), channel_id=1, source_target_pairs={{0,16},{8,24},{16,0},{24,8},{1,17},{9,25},{17,1},{25,9},{2,18},{10... | collective-permute-start | bytes 196616 | tf_op jit(solution)/shard_map/ppermute | solution.py:462
  71.5 5.4 %collective-permute-start.13 = (f32[64,256]{1,0:T(8,128)S(1)}, f32[64,256]{1,0:T(8,128)S(1)}, u32[]{:S(2)}, u32[]{:S(2)}) collective-permute-start(f32[64,256]{1,0:T(8,128)S(1)} %get-tuple-element.74), channel_id=1, source_target_pairs={{0,24},{8,16},{16,8},{24,0},{1,25},{9,17},{17,9},{25,1},{2,26},{10... | collective-permute-start | bytes 196616 | tf_op jit(solution)/shard_map/ppermute | solution.py:462
  77.1 13.7 %collective-permute-start.22 = (bf16[2,256,512]{2,1,0:T(8,128)(2,1)S(1)}, bf16[2,256,512]{2,1,0:T(8,128)(2,1)S(1)}, u32[]{:S(2)}, u32[]{:S(2)}) collective-permute-start(bf16[2,256,512]{2,1,0:T(8,128)(2,1)S(1)} %get-tuple-element.86), channel_id=1, source_target_pairs={{0,8},{8,0},{16,24},{24,16},{1,9},{9,1},{17,25},{25,17},{2,10},{10... | collective-permute-start | bytes 1572872 | tf_op jit(solution)/shard_map/ppermute | solution.py:462
  77.7 13.3 %collective-permute-start.23 = (bf16[2,256,512]{2,1,0:T(8,128)(2,1)S(1)}, bf16[2,256,512]{2,1,0:T(8,128)(2,1)S(1)}, u32[]{:S(2)}, u32[]{:S(2)}) collective-permute-start(bf16[2,256,512]{2,1,0:T(8,128)(2,1)S(1)} %get-tuple-element.87), channel_id=1, source_target_pairs={{0,16},{8,24},{16,0},{24,8},{1,17},{9,25},{17,1},{25,9},{2,18},{10... | collective-permute-start | bytes 1572872 | tf_op jit(solution)/shard_map/ppermute | solution.py:462
  79.8 4.7 %collective-permute-start.15 = (f32[40,256]{1,0:T(8,128)S(1)}, f32[40,256]{1,0:T(8,128)S(1)}, u32[]{:S(2)}, u32[]{:S(2)}) collective-permute-start(f32[40,256]{1,0:T(8,128)S(1)} %get-tuple-element.79), channel_id=1, source_target_pairs={{0,2},{1,3},{2,0},{3,1},{4,6},{5,7},{6,4},{7,5},{8,10},{9,11},{10,... | collective-permute-start | bytes 122888 | tf_op jit(solution)/shard_map/ppermute | solution.py:462
  81.1 6.1 %collective-permute-start.16 = (f32[40,256]{1,0:T(8,128)S(1)}, f32[40,256]{1,0:T(8,128)S(1)}, u32[]{:S(2)}, u32[]{:S(2)}) collective-permute-start(f32[40,256]{1,0:T(8,128)S(1)} %get-tuple-element.80), channel_id=1, source_target_pairs={{0,4},{1,5},{2,6},{3,7},{4,0},{5,1},{6,2},{7,3},{8,12},{9,13},{10,... | collective-permute-start | bytes 122888 | tf_op jit(solution)/shard_map/ppermute | solution.py:462
  84.5 5.8 %collective-permute-start.17 = (f32[40,256]{1,0:T(8,128)S(1)}, f32[40,256]{1,0:T(8,128)S(1)}, u32[]{:S(2)}, u32[]{:S(2)}) collective-permute-start(f32[40,256]{1,0:T(8,128)S(1)} %get-tuple-element.81), channel_id=1, source_target_pairs={{0,6},{1,7},{2,4},{3,5},{4,2},{5,3},{6,0},{7,1},{8,14},{9,15},{10,... | collective-permute-start | bytes 122888 | tf_op jit(solution)/shard_map/ppermute | solution.py:462
  91.2 7.4 %collective-permute-start.24 = (bf16[256,512]{1,0:T(8,128)(2,1)S(1)}, bf16[256,512]{1,0:T(8,128)(2,1)S(1)}, u32[]{:S(2)}, u32[]{:S(2)}) collective-permute-start(bf16[256,512]{1,0:T(8,128)(2,1)S(1)} %get-tuple-element.88), channel_id=1, source_target_pairs={{0,16},{8,24},{16,0},{24,8},{1,17},{9,25},{17,1},{25,9},{2,18},{10... | collective-permute-start | bytes 786440 | tf_op jit(solution)/shard_map/ppermute | solution.py:462
  92.2 7.0 %collective-permute-start.25 = (bf16[256,512]{1,0:T(8,128)(2,1)S(1)}, bf16[256,512]{1,0:T(8,128)(2,1)S(1)}, u32[]{:S(2)}, u32[]{:S(2)}) collective-permute-start(bf16[256,512]{1,0:T(8,128)(2,1)S(1)} %get-tuple-element.89), channel_id=1, source_target_pairs={{0,8},{8,0},{16,24},{24,16},{1,9},{9,1},{17,25},{25,17},{2,10},{10... | collective-permute-start | bytes 786440 | tf_op jit(solution)/shard_map/ppermute | solution.py:462
  95.0 6.3 %collective-permute-start.21 = (f32[64,256]{1,0:T(8,128)S(1)}, f32[64,256]{1,0:T(8,128)S(1)}, u32[]{:S(2)}, u32[]{:S(2)}) collective-permute-start(f32[64,256]{1,0:T(8,128)S(1)} %join.1.refs_0_), channel_id=1, source_target_pairs={{0,24},{8,16},{16,8},{24,0},{1,25},{9,17},{17,9},{25,1},{2,26},{10... | collective-permute-start | bytes 196616 | tf_op jit(solution)/shard_map/ppermute | solution.py:462
  96.1 5.6 %collective-permute-start.20 = (f32[64,256]{1,0:T(8,128)S(1)}, f32[64,256]{1,0:T(8,128)S(1)}, u32[]{:S(2)}, u32[]{:S(2)}) collective-permute-start(f32[64,256]{1,0:T(8,128)S(1)} %join.1.refs_0_), channel_id=1, source_target_pairs={{0,16},{8,24},{16,0},{24,8},{1,17},{9,25},{17,1},{25,9},{2,18},{10... | collective-permute-start | bytes 196616 | tf_op jit(solution)/shard_map/ppermute | solution.py:462
  97.1 4.7 %collective-permute-start.19 = (f32[64,256]{1,0:T(8,128)S(1)}, f32[64,256]{1,0:T(8,128)S(1)}, u32[]{:S(2)}, u32[]{:S(2)}) collective-permute-start(f32[64,256]{1,0:T(8,128)S(1)} %join.1.refs_0_), channel_id=1, source_target_pairs={{0,8},{8,0},{16,24},{24,16},{1,9},{9,1},{17,25},{25,17},{2,10},{10... | collective-permute-start | bytes 196616 | tf_op jit(solution)/shard_map/ppermute | solution.py:462
  (10 other events, 102.4 us)

commit v16 on v15

--- a/solution.py
+++ b/solution.py
@@ -486,7 +486,7 @@
     ups, downs = pair(up, near_up, place), pair(down, near_down, place)
     weights = [ups, swap(ups, "dp", 2), downs, swap(downs, "dp", 1)]
     if in_turns(experts):
-        batches, later = ((0, 4), (1, 5), (2,), (6,), (7, 3)), ()
+        batches, later = ((0, 1), (4, 5), (2,), (6, 3), (7,)), ()
     else:
         batches, later = (range(experts // 2), range(experts // 2, experts)), ()
     order = [s for batch in batches for s in batch]

time: 103 us -> 103 us (level)
  transfers between devices with their start and end apart: 26 -> 26, of which waited for: 12 -> 13; matrix products, arithmetic and copies ran while one was open for 0% -> 0% of each run, Pallas kernels for 23% -> 24%
where the time goes in v16:
time: 103 us
  waiting for transfers between devices  38.4 us (37%)
  starting transfers between devices  29.3 us (28%)
  Pallas kernels  29.3 us (28%)
  local copies, waits for them, and re-layouts  3.7 us (4%)
  other arithmetic  1.29 us (1%)
    ppermute x26, waiting for transfers between devices, swap(): lax.ppermute(value, axis, [(i, i ^ s) for i in range(lax.axis_size(axis))])  38.4 us
    ppermute x26, starting transfers between devices, swap(): lax.ppermute(value, axis, [(i, i ^ s) for i in range(lax.axis_size(axis))])  29.3 us
    pallas_call x5, Pallas kernels, expert_call(): pl.pallas_call(functools.partial(expert_kernel, counts, order, first, len...  21.4 us
    unnamed x16, local copies, waits for them, and re-layouts  3.66 us
    pallas_call x1, Pallas kernels, pack(): pl.pallas_call(functools.partial(pack_kernel, experts, capacity), out_sha...  3.5 us
    pallas_call x1, Pallas kernels, adam(): pl.pallas_call(adam_kernel, out_shape=[shape] * 3 + [jax.ShapeDtypeStruct...  2.07 us
  transfers between devices with their start and end apart: 26, of which 13 were waited for; matrix products, arithmetic and copies ran while one was open for 0% of the time, Pallas kernels for 24%

profile of v16, /device:TPU:0, one launch (start us, length us, event | category | flops | bytes accessed | tf_op | source)
XLA Modules:
  0.0 102.7 jit_solution(15174293702545503321)
XLA Ops:
  2.0 3.0 %collective-permute-start.3 = (bf16[256,512]{1,0:T(8,128)(2,1)S(1)}, bf16[256,512]{1,0:T(8,128)(2,1)S(1)}, u32[]{:S(2)}, u32[]{:S(2)}) collective-permute-start(bf16[256,512]{1,0:T(8,128)(2,1)S(1)} %get-tuple-element.95.one_ref), channel_id=1, source_target_pairs={{0,16},{8,24},{16,0},{24,8},{1,17},{9,25},{17,1},{25,9},{2,18},{10... | collective-permute-start | bytes 786440 | tf_op jit(solution)/shard_map/ppermute | solution.py:462
  5.0 1.5 %collective-permute-start.1 = (bf16[256,512]{1,0:T(8,128)(2,1)S(1)}, bf16[256,512]{1,0:T(8,128)(2,1)S(1)}, u32[]{:S(2)}, u32[]{:S(2)}) collective-permute-start(bf16[256,512]{1,0:T(8,128)(2,1)S(1)} %get-tuple-element.96.one_ref), channel_id=1, source_target_pairs={{0,8},{8,0},{16,24},{24,16},{1,9},{9,1},{17,25},{25,17},{2,10},{10... | collective-permute-start | bytes 786440 | tf_op jit(solution)/shard_map/ppermute | solution.py:462
  10.1 3.5 %pack_rows.1 = (bf16[256,512]{1,0:T(8,128)(2,1)S(1)}, bf16[256,512]{1,0:T(8,128)(2,1)S(1)}, bf16[256,512]{1,0:T(8,128)(2,1)S(1)}, bf16[256,512]{1,0:T(8,128)(2,1...) custom-call(s32[1]{0:T(128)} %bitcast.1.me_ref, ...), custom_call_target="tpu_custom_call" | custom-call | flops 3221225472 | bytes 6291456 | tf_op jit(solution)/shard_map/pack_rows/pallas_call | solution.py:85
  15.0 2.6 %collective-permute-start.8 = (bf16[256,512]{1,0:T(8,128)(2,1)S(1)}, bf16[256,512]{1,0:T(8,128)(2,1)S(1)}, u32[]{:S(2)}, u32[]{:S(2)}) collective-permute-start(bf16[256,512]{1,0:T(8,128)(2,1)S(1)} %get-tuple-element.55), channel_id=1, source_target_pairs={{0,4},{1,5},{2,6},{3,7},{4,0},{5,1},{6,2},{7,3},{8,12},{9,13},{10,... | collective-permute-start | bytes 786440 | tf_op jit(solution)/shard_map/ppermute | solution.py:462
  18.0 17.1 %collective-permute-done.8.refs_0_ = bf16[256,512]{1,0:T(8,128)(2,1)S(1)} collective-permute-done((bf16[256,512]{1,0:T(8,128)(2,1)S(1)}, bf16[256,512]{1,0:T(8,128)(2,1)S(1)}, u32[]{:S(2)}, u32[]{:S(2)}) %collective-permute-start.8) | collective-permute-done | bytes 262176 | tf_op jit(solution)/shard_map/ppermute | solution.py:462
  35.2 2.4 %collective-permute-start.5 = (bf16[256,512]{1,0:T(8,128)(2,1)S(1)}, bf16[256,512]{1,0:T(8,128)(2,1)S(1)}, u32[]{:S(2)}, u32[]{:S(2)}) collective-permute-start(bf16[256,512]{1,0:T(8,128)(2,1)S(1)} %get-tuple-element.52), channel_id=1, source_target_pairs={{0,6},{1,7},{2,4},{3,5},{4,2},{5,3},{6,0},{7,1},{8,14},{9,15},{10,... | collective-permute-start | bytes 786440 | tf_op jit(solution)/shard_map/ppermute | solution.py:462
  37.7 2.2 %collective-permute-start = (bf16[256,512]{1,0:T(8,128)(2,1)S(1)}, bf16[256,512]{1,0:T(8,128)(2,1)S(1)}, u32[]{:S(2)}, u32[]{:S(2)}) collective-permute-start(bf16[256,512]{1,0:T(8,128)(2,1)S(1)} %get-tuple-element.50), channel_id=1, source_target_pairs={{0,7},{1,6},{2,5},{3,4},{4,3},{5,2},{6,1},{7,0},{8,15},{9,14},{10,... | collective-permute-start | bytes 786440 | tf_op jit(solution)/shard_map/ppermute | solution.py:462
  39.8 4.9 %expert_rows.5 = (f32[4,2,256,512]{3,2,1,0:T(8,128)S(1)}, f32[256,256]{1,0:T(8,128)S(1)}, f32[2,256]{1,0:T(2,128)S(1)}) custom-call(bf16[256,512]{1,0:T(8,128)(2,1)S(1)} %get-tuple-element.57.refs_0_, bf16[256,512]{1,0:T(8,128)(2,1)S(1)} %collective-permute-done.10.refs_1_, bf16[256,256]{1,0:T(8,128)(2,1)S(1)} %copy-done.1, ...), custom_call_target="tpu_custom_call" | custom-call | flops 1572864 | bytes 131072 | tf_op jit(solution)/shard_map/expert_rows/pallas_call | solution.py:289
  44.7 5.1 %expert_rows.6 = (f32[4,2,256,512]{3,2,1,0:T(8,128)S(1)}, f32[256,256]{1,0:T(8,128)S(1)}, f32[2,256]{1,0:T(2,128)S(1)}) custom-call(bf16[256,512]{1,0:T(8,128)(2,1)S(1)} %collective-permute-done.8.refs_0_, bf16[256,512]{1,0:T(8,128)(2,1)S(1)} %collective-permute-done.9.refs_1_, bf16[256,256]{1,0:T(8,128)(2,1)S(1)} %copy-done.1, ...), custom_call_target="tpu_custom_call" | custom-call | flops 1572864 | bytes 131072 | tf_op jit(solution)/shard_map/expert_rows/pallas_call | solution.py:289
  50.9 3.2 %expert_rows.7 = (f32[4,2,256,512]{3,2,1,0:T(8,128)S(1)}, f32[256,256]{1,0:T(8,128)S(1)}, f32[1,256]{1,0:T(1,128)S(1)}) custom-call(bf16[256,512]{1,0:T(8,128)(2,1)S(1)} %collective-permute-done.7.refs_0_, bf16[256,256]{1,0:T(8,128)(2,1)S(1)} %copy-done.1, bf16[2,256,512]{2,1,0:T(8,128)(2,1)S(1)} %pair.2.refs_3_.refs_2_, ...), custom_call_target="tpu_custom_call" | custom-call | flops 786432 | bytes 65536 | tf_op jit(solution)/shard_map/expert_rows/pallas_call | solution.py:289
  54.1 7.8 %collective-permute-done.6.refs_1_ = bf16[256,512]{1,0:T(8,128)(2,1)S(1)} collective-permute-done((bf16[256,512]{1,0:T(8,128)(2,1)S(1)}, bf16[256,512]{1,0:T(8,128)(2,1)S(1)}, u32[]{:S(2)}, u32[]{:S(2)}) %collective-permute-start.6) | collective-permute-done | bytes 262176 | tf_op jit(solution)/shard_map/ppermute | solution.py:462
  61.9 4.9 %expert_rows.8 = (f32[4,2,256,512]{3,2,1,0:T(8,128)S(1)}, f32[256,256]{1,0:T(8,128)S(1)}, f32[2,256]{1,0:T(2,128)S(1)}) custom-call(bf16[256,512]{1,0:T(8,128)(2,1)S(1)} %collective-permute-done.5.refs_0_, bf16[256,512]{1,0:T(8,128)(2,1)S(1)} %collective-permute-done.6.refs_1_, bf16[256,256]{1,0:T(8,128)(2,1)S(1)} %copy-done.1, ...), custom_call_target="tpu_custom_call" | custom-call | flops 1572864 | bytes 131072 | tf_op jit(solution)/shard_map/expert_rows/pallas_call | solution.py:289
  66.9 3.2 %expert_rows.9 = (f32[4,2,256,512]{3,2,1,0:T(8,128)S(1)}, f32[64,256]{1,0:T(8,128)S(1)}, f32[64,256]{1,0:T(8,128)S(1)}, f32[64,256]{1,0:T(8,128)S(1)}, f32[64,256]{1,0:T(8,128)S(1)}, /*index=5*/f32[8,256]{1,0:T(8,128)S(1)}) custom-call(bf16[256,512]{1,0:T(8,128)(2,1)S(1)} %collective-permute-done.refs_0_, bf16[256,256]{1,0:T(8,128)(2,1)S(1)} %copy-done.1, ...), custom_call_target="tpu_custom_call" | custom-call | flops 786432 | bytes 65536 | tf_op jit(solution)/shard_map/expert_rows/pallas_call | solution.py:289
  70.1 1.6 %collective-permute-start.11 = (f32[64,256]{1,0:T(8,128)S(1)}, f32[64,256]{1,0:T(8,128)S(1)}, u32[]{:S(2)}, u32[]{:S(2)}) collective-permute-start(f32[64,256]{1,0:T(8,128)S(1)} %get-tuple-element.72), channel_id=1, source_target_pairs={{0,8},{8,0},{16,24},{24,16},{1,9},{9,1},{17,25},{25,17},{2,10},{10... | collective-permute-start | bytes 196616 | tf_op jit(solution)/shard_map/ppermute | solution.py:462
  71.7 1.5 %collective-permute-start.12 = (f32[64,256]{1,0:T(8,128)S(1)}, f32[64,256]{1,0:T(8,128)S(1)}, u32[]{:S(2)}, u32[]{:S(2)}) collective-permute-start(f32[64,256]{1,0:T(8,128)S(1)} %get-tuple-element.73), channel_id=1, source_target_pairs={{0,16},{8,24},{16,0},{24,8},{1,17},{9,25},{17,1},{25,9},{2,18},{10... | collective-permute-start | bytes 196616 | tf_op jit(solution)/shard_map/ppermute | solution.py:462
  74.4 1.6 %collective-permute-done.12.q2 = f32[64,256]{1,0:T(8,128)S(1)} collective-permute-done((f32[64,256]{1,0:T(8,128)S(1)}, f32[64,256]{1,0:T(8,128)S(1)}, u32[]{:S(2)}, u32[]{:S(2)}) %collective-permute-start.12) | collective-permute-done | bytes 65568 | tf_op jit(solution)/shard_map/ppermute | solution.py:462
  76.0 2.4 %collective-permute-done.13.q3 = f32[64,256]{1,0:T(8,128)S(1)} collective-permute-done((f32[64,256]{1,0:T(8,128)S(1)}, f32[64,256]{1,0:T(8,128)S(1)}, u32[]{:S(2)}, u32[]{:S(2)}) %collective-permute-start.13) | collective-permute-done | bytes 65568 | tf_op jit(solution)/shard_map/ppermute | solution.py:462
  81.2 4.1 %collective-permute-start.16 = (f32[40,256]{1,0:T(8,128)S(1)}, f32[40,256]{1,0:T(8,128)S(1)}, u32[]{:S(2)}, u32[]{:S(2)}) collective-permute-start(f32[40,256]{1,0:T(8,128)S(1)} %get-tuple-element.80), channel_id=1, source_target_pairs={{0,4},{1,5},{2,6},{3,7},{4,0},{5,1},{6,2},{7,3},{8,12},{9,13},{10,... | collective-permute-start | bytes 122888 | tf_op jit(solution)/shard_map/ppermute | solution.py:462
  85.6 2.5 %collective-permute-done.16.refs_2_ = f32[40,256]{1,0:T(8,128)S(1)} collective-permute-done((f32[40,256]{1,0:T(8,128)S(1)}, f32[40,256]{1,0:T(8,128)S(1)}, u32[]{:S(2)}, u32[]{:S(2)}) %collective-permute-start.16) | collective-permute-done | bytes 40992 | tf_op jit(solution)/shard_map/ppermute | solution.py:462
  88.1 3.0 %collective-permute-done.17.refs_3_ = f32[40,256]{1,0:T(8,128)S(1)} collective-permute-done((f32[40,256]{1,0:T(8,128)S(1)}, f32[40,256]{1,0:T(8,128)S(1)}, u32[]{:S(2)}, u32[]{:S(2)}) %collective-permute-start.17) | collective-permute-done | bytes 40992 | tf_op jit(solution)/shard_map/ppermute | solution.py:462
  91.4 1.5 %collective-permute-start.24 = (bf16[256,512]{1,0:T(8,128)(2,1)S(1)}, bf16[256,512]{1,0:T(8,128)(2,1)S(1)}, u32[]{:S(2)}, u32[]{:S(2)}) collective-permute-start(bf16[256,512]{1,0:T(8,128)(2,1)S(1)} %get-tuple-element.88), channel_id=1, source_target_pairs={{0,16},{8,24},{16,0},{24,8},{1,17},{9,25},{17,1},{25,9},{2,18},{10... | collective-permute-start | bytes 786440 | tf_op jit(solution)/shard_map/ppermute | solution.py:462
  92.8 1.5 %collective-permute-start.25 = (bf16[256,512]{1,0:T(8,128)(2,1)S(1)}, bf16[256,512]{1,0:T(8,128)(2,1)S(1)}, u32[]{:S(2)}, u32[]{:S(2)}) collective-permute-start(bf16[256,512]{1,0:T(8,128)(2,1)S(1)} %get-tuple-element.89), channel_id=1, source_target_pairs={{0,8},{8,0},{16,24},{24,16},{1,9},{9,1},{17,25},{25,17},{2,10},{10... | collective-permute-start | bytes 786440 | tf_op jit(solution)/shard_map/ppermute | solution.py:462
  97.7 1.5 %collective-permute-start.19 = (f32[64,256]{1,0:T(8,128)S(1)}, f32[64,256]{1,0:T(8,128)S(1)}, u32[]{:S(2)}, u32[]{:S(2)}) collective-permute-start(f32[64,256]{1,0:T(8,128)S(1)} %join.1.refs_0_), channel_id=1, source_target_pairs={{0,8},{8,0},{16,24},{24,16},{1,9},{9,1},{17,25},{25,17},{2,10},{10... | collective-permute-start | bytes 196616 | tf_op jit(solution)/shard_map/ppermute | solution.py:462
  99.6 2.1 %adam.1 = (f32[1,2,256,512]{3,2,1,0:T(8,128)}, f32[1,2,256,512]{3,2,1,0:T(8,128)}, f32[1,2,256,512]{3,2,1,0:T(8,128)}, f32[8,128]{1,0:T(8,128)S(1)}) custom-call(f32[1,2,256,512]{3,2,1,0:T(8,128)S(1)} %copy-done, f32[1,2,256,512]{3,2,1,0:T(8,128)S(1)} %copy-done.2, f32[1,2,256,512]{3,2,1,0:T(8,128)S(1)} %copy-done.3, ...), custom_call_target="tpu_custom_call" | custom-call | flops 5242880 | bytes 2097152 | tf_op jit(solution)/shard_map/adam/pallas_call | solution.py:446
  (63 shorter events, 17.2 us)
Async XLA Ops:
  2.0 12.3 %collective-permute-start.3 = (bf16[256,512]{1,0:T(8,128)(2,1)S(1)}, bf16[256,512]{1,0:T(8,128)(2,1)S(1)}, u32[]{:S(2)}, u32[]{:S(2)}) collective-permute-start(bf16[256,512]{1,0:T(8,128)(2,1)S(1)} %get-tuple-element.95.one_ref), channel_id=1, source_target_pairs={{0,16},{8,24},{16,0},{24,8},{1,17},{9,25},{17,1},{25,9},{2,18},{10... | collective-permute-start | bytes 786440 | tf_op jit(solution)/shard_map/ppermute | solution.py:462
  5.0 8.6 %collective-permute-start.1 = (bf16[256,512]{1,0:T(8,128)(2,1)S(1)}, bf16[256,512]{1,0:T(8,128)(2,1)S(1)}, u32[]{:S(2)}, u32[]{:S(2)}) collective-permute-start(bf16[256,512]{1,0:T(8,128)(2,1)S(1)} %get-tuple-element.96.one_ref), channel_id=1, source_target_pairs={{0,8},{8,0},{16,24},{24,16},{1,9},{9,1},{17,25},{25,17},{2,10},{10... | collective-permute-start | bytes 786440 | tf_op jit(solution)/shard_map/ppermute | solution.py:462
  13.7 23.9 %collective-permute-start.2 = (bf16[2,256,512]{2,1,0:T(8,128)(2,1)S(1)}, bf16[2,256,512]{2,1,0:T(8,128)(2,1)S(1)}, u32[]{:S(2)}, u32[]{:S(2)}) collective-permute-start(bf16[2,256,512]{2,1,0:T(8,128)(2,1)S(1)} %pair.2.refs_3_.refs_2_), channel_id=1, source_target_pairs={{0,16},{8,24},{16,0},{24,8},{1,17},{9,25},{17,1},{25,9},{2,18},{10... | collective-permute-start | bytes 1572872 | tf_op jit(solution)/shard_map/ppermute | solution.py:462
  14.3 23.4 %collective-permute-start.4 = (bf16[2,256,512]{2,1,0:T(8,128)(2,1)S(1)}, bf16[2,256,512]{2,1,0:T(8,128)(2,1)S(1)}, u32[]{:S(2)}, u32[]{:S(2)}) collective-permute-start(bf16[2,256,512]{2,1,0:T(8,128)(2,1)S(1)} %pair.3.refs_5_.refs_4_), channel_id=1, source_target_pairs={{0,8},{8,0},{16,24},{24,16},{1,9},{9,1},{17,25},{25,17},{2,10},{10... | collective-permute-start | bytes 1572872 | tf_op jit(solution)/shard_map/ppermute | solution.py:462
  15.0 20.2 %collective-permute-start.8 = (bf16[256,512]{1,0:T(8,128)(2,1)S(1)}, bf16[256,512]{1,0:T(8,128)(2,1)S(1)}, u32[]{:S(2)}, u32[]{:S(2)}) collective-permute-start(bf16[256,512]{1,0:T(8,128)(2,1)S(1)} %get-tuple-element.55), channel_id=1, source_target_pairs={{0,4},{1,5},{2,6},{3,7},{4,0},{5,1},{6,2},{7,3},{8,12},{9,13},{10,... | collective-permute-start | bytes 786440 | tf_op jit(solution)/shard_map/ppermute | solution.py:462
  17.6 17.6 %collective-permute-start.10 = (bf16[256,512]{1,0:T(8,128)(2,1)S(1)}, bf16[256,512]{1,0:T(8,128)(2,1)S(1)}, u32[]{:S(2)}, u32[]{:S(2)}) collective-permute-start(bf16[256,512]{1,0:T(8,128)(2,1)S(1)} %get-tuple-element.58), channel_id=1, source_target_pairs={{0,1},{1,0},{2,3},{3,2},{4,5},{5,4},{6,7},{7,6},{8,9},{9,8},{10,11... | collective-permute-start | bytes 786440 | tf_op jit(solution)/shard_map/ppermute | solution.py:462
  17.6 27.1 %collective-permute-start.9 = (bf16[256,512]{1,0:T(8,128)(2,1)S(1)}, bf16[256,512]{1,0:T(8,128)(2,1)S(1)}, u32[]{:S(2)}, u32[]{:S(2)}) collective-permute-start(bf16[256,512]{1,0:T(8,128)(2,1)S(1)} %get-tuple-element.56), channel_id=1, source_target_pairs={{0,5},{1,4},{2,7},{3,6},{4,1},{5,0},{6,3},{7,2},{8,13},{9,12},{10,... | collective-permute-start | bytes 786440 | tf_op jit(solution)/shard_map/ppermute | solution.py:462
  35.1 15.7 %collective-permute-start.7 = (bf16[256,512]{1,0:T(8,128)(2,1)S(1)}, bf16[256,512]{1,0:T(8,128)(2,1)S(1)}, u32[]{:S(2)}, u32[]{:S(2)}) collective-permute-start(bf16[256,512]{1,0:T(8,128)(2,1)S(1)} %get-tuple-element.54), channel_id=1, source_target_pairs={{0,2},{1,3},{2,0},{3,1},{4,6},{5,7},{6,4},{7,5},{8,10},{9,11},{10,... | collective-permute-start | bytes 786440 | tf_op jit(solution)/shard_map/ppermute | solution.py:462
  35.2 19.0 %collective-permute-start.5 = (bf16[256,512]{1,0:T(8,128)(2,1)S(1)}, bf16[256,512]{1,0:T(8,128)(2,1)S(1)}, u32[]{:S(2)}, u32[]{:S(2)}) collective-permute-start(bf16[256,512]{1,0:T(8,128)(2,1)S(1)} %get-tuple-element.52), channel_id=1, source_target_pairs={{0,6},{1,7},{2,4},{3,5},{4,2},{5,3},{6,0},{7,1},{8,14},{9,15},{10,... | collective-permute-start | bytes 786440 | tf_op jit(solution)/shard_map/ppermute | solution.py:462
  37.6 24.3 %collective-permute-start.6 = (bf16[256,512]{1,0:T(8,128)(2,1)S(1)}, bf16[256,512]{1,0:T(8,128)(2,1)S(1)}, u32[]{:S(2)}, u32[]{:S(2)}) collective-permute-start(bf16[256,512]{1,0:T(8,128)(2,1)S(1)} %get-tuple-element.53), channel_id=1, source_target_pairs={{0,3},{1,2},{2,1},{3,0},{4,7},{5,6},{6,5},{7,4},{8,11},{9,10},{10,... | collective-permute-start | bytes 786440 | tf_op jit(solution)/shard_map/ppermute | solution.py:462
  37.7 29.2 %collective-permute-start = (bf16[256,512]{1,0:T(8,128)(2,1)S(1)}, bf16[256,512]{1,0:T(8,128)(2,1)S(1)}, u32[]{:S(2)}, u32[]{:S(2)}) collective-permute-start(bf16[256,512]{1,0:T(8,128)(2,1)S(1)} %get-tuple-element.50), channel_id=1, source_target_pairs={{0,7},{1,6},{2,5},{3,4},{4,3},{5,2},{6,1},{7,0},{8,15},{9,14},{10,... | collective-permute-start | bytes 786440 | tf_op jit(solution)/shard_map/ppermute | solution.py:462
  70.1 4.3 %collective-permute-start.11 = (f32[64,256]{1,0:T(8,128)S(1)}, f32[64,256]{1,0:T(8,128)S(1)}, u32[]{:S(2)}, u32[]{:S(2)}) collective-permute-start(f32[64,256]{1,0:T(8,128)S(1)} %get-tuple-element.72), channel_id=1, source_target_pairs={{0,8},{8,0},{16,24},{24,16},{1,9},{9,1},{17,25},{25,17},{2,10},{10... | collective-permute-start | bytes 196616 | tf_op jit(solution)/shard_map/ppermute | solution.py:462
  71.7 4.3 %collective-permute-start.12 = (f32[64,256]{1,0:T(8,128)S(1)}, f32[64,256]{1,0:T(8,128)S(1)}, u32[]{:S(2)}, u32[]{:S(2)}) collective-permute-start(f32[64,256]{1,0:T(8,128)S(1)} %get-tuple-element.73), channel_id=1, source_target_pairs={{0,16},{8,24},{16,0},{24,8},{1,17},{9,25},{17,1},{25,9},{2,18},{10... | collective-permute-start | bytes 196616 | tf_op jit(solution)/shard_map/ppermute | solution.py:462
  73.2 5.2 %collective-permute-start.13 = (f32[64,256]{1,0:T(8,128)S(1)}, f32[64,256]{1,0:T(8,128)S(1)}, u32[]{:S(2)}, u32[]{:S(2)}) collective-permute-start(f32[64,256]{1,0:T(8,128)S(1)} %get-tuple-element.74), channel_id=1, source_target_pairs={{0,24},{8,16},{16,8},{24,0},{1,25},{9,17},{17,9},{25,1},{2,26},{10... | collective-permute-start | bytes 196616 | tf_op jit(solution)/shard_map/ppermute | solution.py:462
  78.6 12.5 %collective-permute-start.22 = (bf16[2,256,512]{2,1,0:T(8,128)(2,1)S(1)}, bf16[2,256,512]{2,1,0:T(8,128)(2,1)S(1)}, u32[]{:S(2)}, u32[]{:S(2)}) collective-permute-start(bf16[2,256,512]{2,1,0:T(8,128)(2,1)S(1)} %get-tuple-element.86), channel_id=1, source_target_pairs={{0,8},{8,0},{16,24},{24,16},{1,9},{9,1},{17,25},{25,17},{2,10},{10... | collective-permute-start | bytes 1572872 | tf_op jit(solution)/shard_map/ppermute | solution.py:462
  79.2 12.1 %collective-permute-start.23 = (bf16[2,256,512]{2,1,0:T(8,128)(2,1)S(1)}, bf16[2,256,512]{2,1,0:T(8,128)(2,1)S(1)}, u32[]{:S(2)}, u32[]{:S(2)}) collective-permute-start(bf16[2,256,512]{2,1,0:T(8,128)(2,1)S(1)} %get-tuple-element.87), channel_id=1, source_target_pairs={{0,16},{8,24},{16,0},{24,8},{1,17},{9,25},{17,1},{25,9},{2,18},{10... | collective-permute-start | bytes 1572872 | tf_op jit(solution)/shard_map/ppermute | solution.py:462
  80.9 4.7 %collective-permute-start.15 = (f32[40,256]{1,0:T(8,128)S(1)}, f32[40,256]{1,0:T(8,128)S(1)}, u32[]{:S(2)}, u32[]{:S(2)}) collective-permute-start(f32[40,256]{1,0:T(8,128)S(1)} %get-tuple-element.79), channel_id=1, source_target_pairs={{0,2},{1,3},{2,0},{3,1},{4,6},{5,7},{6,4},{7,5},{8,10},{9,11},{10,... | collective-permute-start | bytes 122888 | tf_op jit(solution)/shard_map/ppermute | solution.py:462
  81.2 6.9 %collective-permute-start.16 = (f32[40,256]{1,0:T(8,128)S(1)}, f32[40,256]{1,0:T(8,128)S(1)}, u32[]{:S(2)}, u32[]{:S(2)}) collective-permute-start(f32[40,256]{1,0:T(8,128)S(1)} %get-tuple-element.80), channel_id=1, source_target_pairs={{0,4},{1,5},{2,6},{3,7},{4,0},{5,1},{6,2},{7,3},{8,12},{9,13},{10,... | collective-permute-start | bytes 122888 | tf_op jit(solution)/shard_map/ppermute | solution.py:462
  85.3 5.8 %collective-permute-start.17 = (f32[40,256]{1,0:T(8,128)S(1)}, f32[40,256]{1,0:T(8,128)S(1)}, u32[]{:S(2)}, u32[]{:S(2)}) collective-permute-start(f32[40,256]{1,0:T(8,128)S(1)} %get-tuple-element.81), channel_id=1, source_target_pairs={{0,6},{1,7},{2,4},{3,5},{4,2},{5,3},{6,0},{7,1},{8,14},{9,15},{10,... | collective-permute-start | bytes 122888 | tf_op jit(solution)/shard_map/ppermute | solution.py:462
  91.4 7.8 %collective-permute-start.24 = (bf16[256,512]{1,0:T(8,128)(2,1)S(1)}, bf16[256,512]{1,0:T(8,128)(2,1)S(1)}, u32[]{:S(2)}, u32[]{:S(2)}) collective-permute-start(bf16[256,512]{1,0:T(8,128)(2,1)S(1)} %get-tuple-element.88), channel_id=1, source_target_pairs={{0,16},{8,24},{16,0},{24,8},{1,17},{9,25},{17,1},{25,9},{2,18},{10... | collective-permute-start | bytes 786440 | tf_op jit(solution)/shard_map/ppermute | solution.py:462
  92.8 6.8 %collective-permute-start.25 = (bf16[256,512]{1,0:T(8,128)(2,1)S(1)}, bf16[256,512]{1,0:T(8,128)(2,1)S(1)}, u32[]{:S(2)}, u32[]{:S(2)}) collective-permute-start(bf16[256,512]{1,0:T(8,128)(2,1)S(1)} %get-tuple-element.89), channel_id=1, source_target_pairs={{0,8},{8,0},{16,24},{24,16},{1,9},{9,1},{17,25},{25,17},{2,10},{10... | collective-permute-start | bytes 786440 | tf_op jit(solution)/shard_map/ppermute | solution.py:462
  95.6 6.0 %collective-permute-start.21 = (f32[64,256]{1,0:T(8,128)S(1)}, f32[64,256]{1,0:T(8,128)S(1)}, u32[]{:S(2)}, u32[]{:S(2)}) collective-permute-start(f32[64,256]{1,0:T(8,128)S(1)} %join.1.refs_0_), channel_id=1, source_target_pairs={{0,24},{8,16},{16,8},{24,0},{1,25},{9,17},{17,9},{25,1},{2,26},{10... | collective-permute-start | bytes 196616 | tf_op jit(solution)/shard_map/ppermute | solution.py:462
  96.3 5.6 %collective-permute-start.20 = (f32[64,256]{1,0:T(8,128)S(1)}, f32[64,256]{1,0:T(8,128)S(1)}, u32[]{:S(2)}, u32[]{:S(2)}) collective-permute-start(f32[64,256]{1,0:T(8,128)S(1)} %join.1.refs_0_), channel_id=1, source_target_pairs={{0,16},{8,24},{16,0},{24,8},{1,17},{9,25},{17,1},{25,9},{2,18},{10... | collective-permute-start | bytes 196616 | tf_op jit(solution)/shard_map/ppermute | solution.py:462
  97.7 4.3 %collective-permute-start.19 = (f32[64,256]{1,0:T(8,128)S(1)}, f32[64,256]{1,0:T(8,128)S(1)}, u32[]{:S(2)}, u32[]{:S(2)}) collective-permute-start(f32[64,256]{1,0:T(8,128)S(1)} %join.1.refs_0_), channel_id=1, source_target_pairs={{0,8},{8,0},{16,24},{24,16},{1,9},{9,1},{17,25},{25,17},{2,10},{10... | collective-permute-start | bytes 196616 | tf_op jit(solution)/shard_map/ppermute | solution.py:462
  (10 other events, 99.4 us)

commit v17 on v14

--- a/solution.py
+++ b/solution.py
@@ -335,23 +335,24 @@
         loss_ref[2 * k : 2 * k + 2, :] = note[half : half + 2, :]
 
 
-def join_kernel(me_ref, own_ref, other_ref, _, both_ref):
-    half = own_ref.shape[0]
-    core = me_ref[0] & 1
-    both_ref[pl.ds(pl.multiple_of(core * half, half), half), :] = own_ref[...]
-    both_ref[pl.ds(pl.multiple_of((1 - core) * half, half), half), :] = other_ref[...]
-
-
-def assemble_kernel(mine_ref, *refs):
-    *held, _, trunk_ref = refs
+def stack_kernel(*refs):
+    *held, _, all_ref = refs
     for j, ref in enumerate(held):
         rows = ref.shape[0]
-        at = pl.multiple_of((mine_ref[0] ^ j) * rows, rows)
-        trunk_ref[pl.ds(at, rows), :] = ref[...]
-
-
-def turn(kernel, held, shapes, name, index=None):
-    first = [] if index is None else [index]
+        all_ref[j * rows : (j + 1) * rows, :] = ref[...]
+
+
+def assemble_kernel(me_ref, mine_ref, own_ref, other_ref, _, trunk_ref):
+    core = me_ref[0] & 1
+    half = own_ref.shape[0] // 4
+    for ref, side in ((own_ref, core), (other_ref, 1 - core)):
+        for j in range(4):
+            at = pl.multiple_of(((mine_ref[0] ^ j) * 2 + side) * half, half)
+            trunk_ref[pl.ds(at, half), :] = ref[j * half : (j + 1) * half, :]
+
+
+def turn(kernel, held, shapes, name, indices=()):
+    first = list(indices)
     width = held[0].shape[1]
     return pl.pallas_call(
         kernel,
@@ -523,19 +524,21 @@
             [total, swap(note, "expert", 1), losses],
             (quarter // 2 + 8,) * 4,
             "pair_turn",
-            me,
+            (me,),
         )
         notes = [swap(note, "expert", 2 * k) for k, note in enumerate(notes)]
         total, loss = turn(z_turn_kernel, notes, (quarter // 2, experts), "z_turn")
         more_up, more_down = pass_on(got, total)
         row_loss, found = loss_by_row(place, loss)
-        other = swap(total, "expert", 1)
-        (total,) = turn(join_kernel, [total, other, found], (quarter,), "join", me)
         parts = [swap(total, "dp", j) for j in range(replicas)]
+        (parts,) = turn(stack_kernel, parts + [found], (width // 2,), "stack_parts")
+        other = swap(parts, "expert", 1)
         *news, done = adam(
             expert_params, first_moment, second_moment, acc, [*got, more_up, more_down]
         )
-        (trunk_grad,) = turn(assemble_kernel, parts + [done], (width,), "assemble_trunk", mine)
+        (trunk_grad,) = turn(
+            assemble_kernel, [parts, other, done], (width,), "assemble_trunk", (me, mine)
+        )
     else:
         got = send(losses)
         more_up, more_down = pass_on(got, losses)

time: 99.4 us -> 100 us (level)
  transfers between devices with their start and end apart: 26 -> 26, of which waited for: 13 -> 12; matrix products, arithmetic and copies ran while one was open for 0% -> 0% of each run, Pallas kernels for 25% -> 25%
where the time goes in v17:
time: 100 us; the launch traced here: 99.9 us
  waiting for transfers between devices  35.2 us (35%)
  starting transfers between devices  29.6 us (30%)
  Pallas kernels  29.3 us (29%)
  local copies, waits for them, and re-layouts  3.7 us (4%)
  other arithmetic  1.29 us (1%)
    ppermute x26, waiting for transfers between devices, swap(): lax.ppermute(value, axis, [(i, i ^ s) for i in range(lax.axis_size(axis))])  35.2 us
    ppermute x26, starting transfers between devices, swap(): lax.ppermute(value, axis, [(i, i ^ s) for i in range(lax.axis_size(axis))])  29.6 us
    pallas_call x5, Pallas kernels, expert_call(): pl.pallas_call(functools.partial(expert_kernel, counts, order, first, len...  21.4 us
    unnamed x16, local copies, waits for them, and re-layouts  3.66 us
    pallas_call x1, Pallas kernels, pack(): pl.pallas_call(functools.partial(pack_kernel, experts, capacity), out_sha...  3.5 us
    pallas_call x1, Pallas kernels, adam(): pl.pallas_call(adam_kernel, out_shape=[shape] * 3 + [jax.ShapeDtypeStruct...  2.07 us
  transfers between devices with their start and end apart: 26, of which 12 were waited for; matrix products, arithmetic and copies ran while one was open for 0% of the time, Pallas kernels for 25%

profile of v17, /device:TPU:0, one launch (start us, length us, event | category | flops | bytes accessed | tf_op | source)
XLA Modules:
  0.0 99.9 jit_solution(18161211011297931782)
XLA Ops:
  2.0 3.0 %collective-permute-start.3 = (bf16[256,512]{1,0:T(8,128)(2,1)S(1)}, bf16[256,512]{1,0:T(8,128)(2,1)S(1)}, u32[]{:S(2)}, u32[]{:S(2)}) collective-permute-start(bf16[256,512]{1,0:T(8,128)(2,1)S(1)} %get-tuple-element.95.one_ref), channel_id=1, source_target_pairs={{0,16},{8,24},{16,0},{24,8},{1,17},{9,25},{17,1},{25,9},{2,18},{10... | collective-permute-start | bytes 786440 | tf_op jit(solution)/shard_map/ppermute | solution.py:463
  5.0 1.5 %collective-permute-start.1 = (bf16[256,512]{1,0:T(8,128)(2,1)S(1)}, bf16[256,512]{1,0:T(8,128)(2,1)S(1)}, u32[]{:S(2)}, u32[]{:S(2)}) collective-permute-start(bf16[256,512]{1,0:T(8,128)(2,1)S(1)} %get-tuple-element.96.one_ref), channel_id=1, source_target_pairs={{0,8},{8,0},{16,24},{24,16},{1,9},{9,1},{17,25},{25,17},{2,10},{10... | collective-permute-start | bytes 786440 | tf_op jit(solution)/shard_map/ppermute | solution.py:463
  10.1 3.5 %pack_rows.1 = (bf16[256,512]{1,0:T(8,128)(2,1)S(1)}, bf16[256,512]{1,0:T(8,128)(2,1)S(1)}, bf16[256,512]{1,0:T(8,128)(2,1)S(1)}, bf16[256,512]{1,0:T(8,128)(2,1...) custom-call(s32[1]{0:T(128)} %bitcast.me_ref, ...), custom_call_target="tpu_custom_call" | custom-call | flops 3221225472 | bytes 6291456 | tf_op jit(solution)/shard_map/pack_rows/pallas_call | solution.py:85
  15.0 2.6 %collective-permute-start.10 = (bf16[256,512]{1,0:T(8,128)(2,1)S(1)}, bf16[256,512]{1,0:T(8,128)(2,1)S(1)}, u32[]{:S(2)}, u32[]{:S(2)}) collective-permute-start(bf16[256,512]{1,0:T(8,128)(2,1)S(1)} %get-tuple-element.58), channel_id=1, source_target_pairs={{0,4},{1,5},{2,6},{3,7},{4,0},{5,1},{6,2},{7,3},{8,12},{9,13},{10,... | collective-permute-start | bytes 786440 | tf_op jit(solution)/shard_map/ppermute | solution.py:463
  17.7 1.6 %collective-permute-start.7 = (bf16[256,512]{1,0:T(8,128)(2,1)S(1)}, bf16[256,512]{1,0:T(8,128)(2,1)S(1)}, u32[]{:S(2)}, u32[]{:S(2)}) collective-permute-start(bf16[256,512]{1,0:T(8,128)(2,1)S(1)} %get-tuple-element.54), channel_id=1, source_target_pairs={{0,2},{1,3},{2,0},{3,1},{4,6},{5,7},{6,4},{7,5},{8,10},{9,11},{10,... | collective-permute-start | bytes 786440 | tf_op jit(solution)/shard_map/ppermute | solution.py:463
  19.3 16.9 %collective-permute-done.10.refs_1_ = bf16[256,512]{1,0:T(8,128)(2,1)S(1)} collective-permute-done((bf16[256,512]{1,0:T(8,128)(2,1)S(1)}, bf16[256,512]{1,0:T(8,128)(2,1)S(1)}, u32[]{:S(2)}, u32[]{:S(2)}) %collective-permute-start.10) | collective-permute-done | bytes 262176 | tf_op jit(solution)/shard_map/ppermute | solution.py:463
  36.2 3.1 %collective-permute-start.5 = (bf16[256,512]{1,0:T(8,128)(2,1)S(1)}, bf16[256,512]{1,0:T(8,128)(2,1)S(1)}, u32[]{:S(2)}, u32[]{:S(2)}) collective-permute-start(bf16[256,512]{1,0:T(8,128)(2,1)S(1)} %get-tuple-element.52), channel_id=1, source_target_pairs={{0,6},{1,7},{2,4},{3,5},{4,2},{5,3},{6,0},{7,1},{8,14},{9,15},{10,... | collective-permute-start | bytes 786440 | tf_op jit(solution)/shard_map/ppermute | solution.py:463
  39.5 4.9 %expert_rows.5 = (f32[4,2,256,512]{3,2,1,0:T(8,128)S(1)}, f32[256,256]{1,0:T(8,128)S(1)}, f32[2,256]{1,0:T(2,128)S(1)}) custom-call(bf16[256,512]{1,0:T(8,128)(2,1)S(1)} %get-tuple-element.57.refs_0_, bf16[256,512]{1,0:T(8,128)(2,1)S(1)} %collective-permute-done.10.refs_1_, bf16[256,256]{1,0:T(8,128)(2,1)S(1)} %copy-done.1, ...), custom_call_target="tpu_custom_call" | custom-call | flops 1572864 | bytes 131072 | tf_op jit(solution)/shard_map/expert_rows/pallas_call | solution.py:289
  44.3 1.9 %collective-permute-done.9.refs_1_ = bf16[256,512]{1,0:T(8,128)(2,1)S(1)} collective-permute-done((bf16[256,512]{1,0:T(8,128)(2,1)S(1)}, bf16[256,512]{1,0:T(8,128)(2,1)S(1)}, u32[]{:S(2)}, u32[]{:S(2)}) %collective-permute-start.9) | collective-permute-done | bytes 262176 | tf_op jit(solution)/shard_map/ppermute | solution.py:463
  46.3 5.1 %expert_rows.6 = (f32[4,2,256,512]{3,2,1,0:T(8,128)S(1)}, f32[256,256]{1,0:T(8,128)S(1)}, f32[2,256]{1,0:T(2,128)S(1)}) custom-call(bf16[256,512]{1,0:T(8,128)(2,1)S(1)} %collective-permute-done.8.refs_0_, bf16[256,512]{1,0:T(8,128)(2,1)S(1)} %collective-permute-done.9.refs_1_, bf16[256,256]{1,0:T(8,128)(2,1)S(1)} %copy-done.1, ...), custom_call_target="tpu_custom_call" | custom-call | flops 1572864 | bytes 131072 | tf_op jit(solution)/shard_map/expert_rows/pallas_call | solution.py:289
  51.4 3.2 %expert_rows.7 = (f32[4,2,256,512]{3,2,1,0:T(8,128)S(1)}, f32[256,256]{1,0:T(8,128)S(1)}, f32[1,256]{1,0:T(1,128)S(1)}) custom-call(bf16[256,512]{1,0:T(8,128)(2,1)S(1)} %collective-permute-done.7.refs_0_, bf16[256,256]{1,0:T(8,128)(2,1)S(1)} %copy-done.1, bf16[2,256,512]{2,1,0:T(8,128)(2,1)S(1)} %pair.2.refs_3_.refs_2_, ...), custom_call_target="tpu_custom_call" | custom-call | flops 786432 | bytes 65536 | tf_op jit(solution)/shard_map/expert_rows/pallas_call | solution.py:289
  54.6 3.7 %collective-permute-done.6.refs_1_ = bf16[256,512]{1,0:T(8,128)(2,1)S(1)} collective-permute-done((bf16[256,512]{1,0:T(8,128)(2,1)S(1)}, bf16[256,512]{1,0:T(8,128)(2,1)S(1)}, u32[]{:S(2)}, u32[]{:S(2)}) %collective-permute-start.6) | collective-permute-done | bytes 262176 | tf_op jit(solution)/shard_map/ppermute | solution.py:463
  58.3 4.9 %expert_rows.8 = (f32[4,2,256,512]{3,2,1,0:T(8,128)S(1)}, f32[256,256]{1,0:T(8,128)S(1)}, f32[2,256]{1,0:T(2,128)S(1)}) custom-call(bf16[256,512]{1,0:T(8,128)(2,1)S(1)} %collective-permute-done.5.refs_0_, bf16[256,512]{1,0:T(8,128)(2,1)S(1)} %collective-permute-done.6.refs_1_, bf16[256,256]{1,0:T(8,128)(2,1)S(1)} %copy-done.1, ...), custom_call_target="tpu_custom_call" | custom-call | flops 1572864 | bytes 131072 | tf_op jit(solution)/shard_map/expert_rows/pallas_call | solution.py:289
  63.2 3.2 %expert_rows.9 = (f32[4,2,256,512]{3,2,1,0:T(8,128)S(1)}, f32[64,256]{1,0:T(8,128)S(1)}, f32[64,256]{1,0:T(8,128)S(1)}, f32[64,256]{1,0:T(8,128)S(1)}, f32[64,256]{1,0:T(8,128)S(1)}, /*index=5*/f32[8,256]{1,0:T(8,128)S(1)}) custom-call(bf16[256,512]{1,0:T(8,128)(2,1)S(1)} %collective-permute-done.refs_0_, bf16[256,256]{1,0:T(8,128)(2,1)S(1)} %copy-done.1, ...), custom_call_target="tpu_custom_call" | custom-call | flops 786432 | bytes 65536 | tf_op jit(solution)/shard_map/expert_rows/pallas_call | solution.py:289
  66.5 1.5 %collective-permute-start.11 = (f32[64,256]{1,0:T(8,128)S(1)}, f32[64,256]{1,0:T(8,128)S(1)}, u32[]{:S(2)}, u32[]{:S(2)}) collective-permute-start(f32[64,256]{1,0:T(8,128)S(1)} %get-tuple-element.72), channel_id=1, source_target_pairs={{0,8},{8,0},{16,24},{24,16},{1,9},{9,1},{17,25},{25,17},{2,10},{10... | collective-permute-start | bytes 196616 | tf_op jit(solution)/shard_map/ppermute | solution.py:463
  68.0 1.5 %collective-permute-start.12 = (f32[64,256]{1,0:T(8,128)S(1)}, f32[64,256]{1,0:T(8,128)S(1)}, u32[]{:S(2)}, u32[]{:S(2)}) collective-permute-start(f32[64,256]{1,0:T(8,128)S(1)} %get-tuple-element.73), channel_id=1, source_target_pairs={{0,16},{8,24},{16,0},{24,8},{1,17},{9,25},{17,1},{25,9},{2,18},{10... | collective-permute-start | bytes 196616 | tf_op jit(solution)/shard_map/ppermute | solution.py:463
  72.2 2.4 %collective-permute-done.13.q3 = f32[64,256]{1,0:T(8,128)S(1)} collective-permute-done((f32[64,256]{1,0:T(8,128)S(1)}, f32[64,256]{1,0:T(8,128)S(1)}, u32[]{:S(2)}, u32[]{:S(2)}) %collective-permute-start.13) | collective-permute-done | bytes 65568 | tf_op jit(solution)/shard_map/ppermute | solution.py:463
  77.3 1.7 %collective-permute-start.15 = (f32[40,256]{1,0:T(8,128)S(1)}, f32[40,256]{1,0:T(8,128)S(1)}, u32[]{:S(2)}, u32[]{:S(2)}) collective-permute-start(f32[40,256]{1,0:T(8,128)S(1)} %get-tuple-element.79), channel_id=1, source_target_pairs={{0,2},{1,3},{2,0},{3,1},{4,6},{5,7},{6,4},{7,5},{8,10},{9,11},{10,... | collective-permute-start | bytes 122888 | tf_op jit(solution)/shard_map/ppermute | solution.py:463
  79.0 2.6 %collective-permute-start.16 = (f32[40,256]{1,0:T(8,128)S(1)}, f32[40,256]{1,0:T(8,128)S(1)}, u32[]{:S(2)}, u32[]{:S(2)}) collective-permute-start(f32[40,256]{1,0:T(8,128)S(1)} %get-tuple-element.80), channel_id=1, source_target_pairs={{0,4},{1,5},{2,6},{3,7},{4,0},{5,1},{6,2},{7,3},{8,12},{9,13},{10,... | collective-permute-start | bytes 122888 | tf_op jit(solution)/shard_map/ppermute | solution.py:463
  82.3 2.0 %collective-permute-done.16.refs_2_ = f32[40,256]{1,0:T(8,128)S(1)} collective-permute-done((f32[40,256]{1,0:T(8,128)S(1)}, f32[40,256]{1,0:T(8,128)S(1)}, u32[]{:S(2)}, u32[]{:S(2)}) %collective-permute-start.16) | collective-permute-done | bytes 40992 | tf_op jit(solution)/shard_map/ppermute | solution.py:463
  84.3 3.1 %collective-permute-done.17.refs_3_ = f32[40,256]{1,0:T(8,128)S(1)} collective-permute-done((f32[40,256]{1,0:T(8,128)S(1)}, f32[40,256]{1,0:T(8,128)S(1)}, u32[]{:S(2)}, u32[]{:S(2)}) %collective-permute-start.17) | collective-permute-done | bytes 40992 | tf_op jit(solution)/shard_map/ppermute | solution.py:463
  87.6 1.5 %collective-permute-start.24 = (bf16[256,512]{1,0:T(8,128)(2,1)S(1)}, bf16[256,512]{1,0:T(8,128)(2,1)S(1)}, u32[]{:S(2)}, u32[]{:S(2)}) collective-permute-start(bf16[256,512]{1,0:T(8,128)(2,1)S(1)} %get-tuple-element.88), channel_id=1, source_target_pairs={{0,16},{8,24},{16,0},{24,8},{1,17},{9,25},{17,1},{25,9},{2,18},{10... | collective-permute-start | bytes 786440 | tf_op jit(solution)/shard_map/ppermute | solution.py:463
  91.2 1.5 %collective-permute-start.19 = (f32[32,256]{1,0:T(8,128)S(1)}, f32[32,256]{1,0:T(8,128)S(1)}, u32[]{:S(2)}, u32[]{:S(2)}) collective-permute-start(f32[32,256]{1,0:T(8,128)S(1)} %get-tuple-element.82.refs_0_.ahead_ref), channel_id=1, source_target_pairs={{0,16},{8,24},{16,0},{24,8},{1,17},{9,25},{17,1},{25,9},{2,18},{10... | collective-permute-start | bytes 98312 | tf_op jit(solution)/shard_map/ppermute | solution.py:463
  97.1 2.1 %adam.1 = (f32[1,2,256,512]{3,2,1,0:T(8,128)}, f32[1,2,256,512]{3,2,1,0:T(8,128)}, f32[1,2,256,512]{3,2,1,0:T(8,128)}, f32[8,128]{1,0:T(8,128)S(1)}) custom-call(f32[1,2,256,512]{3,2,1,0:T(8,128)S(1)} %copy-done, f32[1,2,256,512]{3,2,1,0:T(8,128)S(1)} %copy-done.2, f32[1,2,256,512]{3,2,1,0:T(8,128)S(1)} %copy-done.3, ...), custom_call_target="tpu_custom_call" | custom-call | flops 5242880 | bytes 2097152 | tf_op jit(solution)/shard_map/adam/pallas_call | solution.py:447
  (63 shorter events, 19.9 us)
Async XLA Ops:
  2.0 12.3 %collective-permute-start.3 = (bf16[256,512]{1,0:T(8,128)(2,1)S(1)}, bf16[256,512]{1,0:T(8,128)(2,1)S(1)}, u32[]{:S(2)}, u32[]{:S(2)}) collective-permute-start(bf16[256,512]{1,0:T(8,128)(2,1)S(1)} %get-tuple-element.95.one_ref), channel_id=1, source_target_pairs={{0,16},{8,24},{16,0},{24,8},{1,17},{9,25},{17,1},{25,9},{2,18},{10... | collective-permute-start | bytes 786440 | tf_op jit(solution)/shard_map/ppermute | solution.py:463
  5.0 8.6 %collective-permute-start.1 = (bf16[256,512]{1,0:T(8,128)(2,1)S(1)}, bf16[256,512]{1,0:T(8,128)(2,1)S(1)}, u32[]{:S(2)}, u32[]{:S(2)}) collective-permute-start(bf16[256,512]{1,0:T(8,128)(2,1)S(1)} %get-tuple-element.96.one_ref), channel_id=1, source_target_pairs={{0,8},{8,0},{16,24},{24,16},{1,9},{9,1},{17,25},{25,17},{2,10},{10... | collective-permute-start | bytes 786440 | tf_op jit(solution)/shard_map/ppermute | solution.py:463
  13.7 25.7 %collective-permute-start.2 = (bf16[2,256,512]{2,1,0:T(8,128)(2,1)S(1)}, bf16[2,256,512]{2,1,0:T(8,128)(2,1)S(1)}, u32[]{:S(2)}, u32[]{:S(2)}) collective-permute-start(bf16[2,256,512]{2,1,0:T(8,128)(2,1)S(1)} %pair.2.refs_3_.refs_2_), channel_id=1, source_target_pairs={{0,16},{8,24},{16,0},{24,8},{1,17},{9,25},{17,1},{25,9},{2,18},{10... | collective-permute-start | bytes 1572872 | tf_op jit(solution)/shard_map/ppermute | solution.py:463
  14.3 25.1 %collective-permute-start.4 = (bf16[2,256,512]{2,1,0:T(8,128)(2,1)S(1)}, bf16[2,256,512]{2,1,0:T(8,128)(2,1)S(1)}, u32[]{:S(2)}, u32[]{:S(2)}) collective-permute-start(bf16[2,256,512]{2,1,0:T(8,128)(2,1)S(1)} %pair.3.refs_5_.refs_4_), channel_id=1, source_target_pairs={{0,8},{8,0},{16,24},{24,16},{1,9},{9,1},{17,25},{25,17},{2,10},{10... | collective-permute-start | bytes 1572872 | tf_op jit(solution)/shard_map/ppermute | solution.py:463
  15.0 2.8 %collective-permute-start.8 = (bf16[256,512]{1,0:T(8,128)(2,1)S(1)}, bf16[256,512]{1,0:T(8,128)(2,1)S(1)}, u32[]{:S(2)}, u32[]{:S(2)}) collective-permute-start(bf16[256,512]{1,0:T(8,128)(2,1)S(1)} %get-tuple-element.55), channel_id=1, source_target_pairs={{0,1},{1,0},{2,3},{3,2},{4,5},{5,4},{6,7},{7,6},{8,9},{9,8},{10,11... | collective-permute-start | bytes 786440 | tf_op jit(solution)/shard_map/ppermute | solution.py:463
  15.0 21.2 %collective-permute-start.10 = (bf16[256,512]{1,0:T(8,128)(2,1)S(1)}, bf16[256,512]{1,0:T(8,128)(2,1)S(1)}, u32[]{:S(2)}, u32[]{:S(2)}) collective-permute-start(bf16[256,512]{1,0:T(8,128)(2,1)S(1)} %get-tuple-element.58), channel_id=1, source_target_pairs={{0,4},{1,5},{2,6},{3,7},{4,0},{5,1},{6,2},{7,3},{8,12},{9,13},{10,... | collective-permute-start | bytes 786440 | tf_op jit(solution)/shard_map/ppermute | solution.py:463
  17.6 28.7 %collective-permute-start.9 = (bf16[256,512]{1,0:T(8,128)(2,1)S(1)}, bf16[256,512]{1,0:T(8,128)(2,1)S(1)}, u32[]{:S(2)}, u32[]{:S(2)}) collective-permute-start(bf16[256,512]{1,0:T(8,128)(2,1)S(1)} %get-tuple-element.56), channel_id=1, source_target_pairs={{0,5},{1,4},{2,7},{3,6},{4,1},{5,0},{6,3},{7,2},{8,13},{9,12},{10,... | collective-permute-start | bytes 786440 | tf_op jit(solution)/shard_map/ppermute | solution.py:463
  17.7 33.6 %collective-permute-start.7 = (bf16[256,512]{1,0:T(8,128)(2,1)S(1)}, bf16[256,512]{1,0:T(8,128)(2,1)S(1)}, u32[]{:S(2)}, u32[]{:S(2)}) collective-permute-start(bf16[256,512]{1,0:T(8,128)(2,1)S(1)} %get-tuple-element.54), channel_id=1, source_target_pairs={{0,2},{1,3},{2,0},{3,1},{4,6},{5,7},{6,4},{7,5},{8,10},{9,11},{10,... | collective-permute-start | bytes 786440 | tf_op jit(solution)/shard_map/ppermute | solution.py:463
  36.2 18.4 %collective-permute-start.5 = (bf16[256,512]{1,0:T(8,128)(2,1)S(1)}, bf16[256,512]{1,0:T(8,128)(2,1)S(1)}, u32[]{:S(2)}, u32[]{:S(2)}) collective-permute-start(bf16[256,512]{1,0:T(8,128)(2,1)S(1)} %get-tuple-element.52), channel_id=1, source_target_pairs={{0,6},{1,7},{2,4},{3,5},{4,2},{5,3},{6,0},{7,1},{8,14},{9,15},{10,... | collective-permute-start | bytes 786440 | tf_op jit(solution)/shard_map/ppermute | solution.py:463
  39.4 18.9 %collective-permute-start.6 = (bf16[256,512]{1,0:T(8,128)(2,1)S(1)}, bf16[256,512]{1,0:T(8,128)(2,1)S(1)}, u32[]{:S(2)}, u32[]{:S(2)}) collective-permute-start(bf16[256,512]{1,0:T(8,128)(2,1)S(1)} %get-tuple-element.53), channel_id=1, source_target_pairs={{0,3},{1,2},{2,1},{3,0},{4,7},{5,6},{6,5},{7,4},{8,11},{9,10},{10,... | collective-permute-start | bytes 786440 | tf_op jit(solution)/shard_map/ppermute | solution.py:463
  39.4 23.9 %collective-permute-start = (bf16[256,512]{1,0:T(8,128)(2,1)S(1)}, bf16[256,512]{1,0:T(8,128)(2,1)S(1)}, u32[]{:S(2)}, u32[]{:S(2)}) collective-permute-start(bf16[256,512]{1,0:T(8,128)(2,1)S(1)} %get-tuple-element.50), channel_id=1, source_target_pairs={{0,7},{1,6},{2,5},{3,4},{4,3},{5,2},{6,1},{7,0},{8,15},{9,14},{10,... | collective-permute-start | bytes 786440 | tf_op jit(solution)/shard_map/ppermute | solution.py:463
  66.5 4.3 %collective-permute-start.11 = (f32[64,256]{1,0:T(8,128)S(1)}, f32[64,256]{1,0:T(8,128)S(1)}, u32[]{:S(2)}, u32[]{:S(2)}) collective-permute-start(f32[64,256]{1,0:T(8,128)S(1)} %get-tuple-element.72), channel_id=1, source_target_pairs={{0,8},{8,0},{16,24},{24,16},{1,9},{9,1},{17,25},{25,17},{2,10},{10... | collective-permute-start | bytes 196616 | tf_op jit(solution)/shard_map/ppermute | solution.py:463
  68.0 4.3 %collective-permute-start.12 = (f32[64,256]{1,0:T(8,128)S(1)}, f32[64,256]{1,0:T(8,128)S(1)}, u32[]{:S(2)}, u32[]{:S(2)}) collective-permute-start(f32[64,256]{1,0:T(8,128)S(1)} %get-tuple-element.73), channel_id=1, source_target_pairs={{0,16},{8,24},{16,0},{24,8},{1,17},{9,25},{17,1},{25,9},{2,18},{10... | collective-permute-start | bytes 196616 | tf_op jit(solution)/shard_map/ppermute | solution.py:463
  69.5 5.2 %collective-permute-start.13 = (f32[64,256]{1,0:T(8,128)S(1)}, f32[64,256]{1,0:T(8,128)S(1)}, u32[]{:S(2)}, u32[]{:S(2)}) collective-permute-start(f32[64,256]{1,0:T(8,128)S(1)} %get-tuple-element.74), channel_id=1, source_target_pairs={{0,24},{8,16},{16,8},{24,0},{1,25},{9,17},{17,9},{25,1},{2,26},{10... | collective-permute-start | bytes 196616 | tf_op jit(solution)/shard_map/ppermute | solution.py:463
  74.8 12.6 %collective-permute-start.22 = (bf16[2,256,512]{2,1,0:T(8,128)(2,1)S(1)}, bf16[2,256,512]{2,1,0:T(8,128)(2,1)S(1)}, u32[]{:S(2)}, u32[]{:S(2)}) collective-permute-start(bf16[2,256,512]{2,1,0:T(8,128)(2,1)S(1)} %get-tuple-element.86), channel_id=1, source_target_pairs={{0,8},{8,0},{16,24},{24,16},{1,9},{9,1},{17,25},{25,17},{2,10},{10... | collective-permute-start | bytes 1572872 | tf_op jit(solution)/shard_map/ppermute | solution.py:463
  75.5 12.0 %collective-permute-start.23 = (bf16[2,256,512]{2,1,0:T(8,128)(2,1)S(1)}, bf16[2,256,512]{2,1,0:T(8,128)(2,1)S(1)}, u32[]{:S(2)}, u32[]{:S(2)}) collective-permute-start(bf16[2,256,512]{2,1,0:T(8,128)(2,1)S(1)} %get-tuple-element.87), channel_id=1, source_target_pairs={{0,16},{8,24},{16,0},{24,8},{1,17},{9,25},{17,1},{25,9},{2,18},{10... | collective-permute-start | bytes 1572872 | tf_op jit(solution)/shard_map/ppermute | solution.py:463
  77.3 5.0 %collective-permute-start.15 = (f32[40,256]{1,0:T(8,128)S(1)}, f32[40,256]{1,0:T(8,128)S(1)}, u32[]{:S(2)}, u32[]{:S(2)}) collective-permute-start(f32[40,256]{1,0:T(8,128)S(1)} %get-tuple-element.79), channel_id=1, source_target_pairs={{0,2},{1,3},{2,0},{3,1},{4,6},{5,7},{6,4},{7,5},{8,10},{9,11},{10,... | collective-permute-start | bytes 122888 | tf_op jit(solution)/shard_map/ppermute | solution.py:463
  79.0 5.3 %collective-permute-start.16 = (f32[40,256]{1,0:T(8,128)S(1)}, f32[40,256]{1,0:T(8,128)S(1)}, u32[]{:S(2)}, u32[]{:S(2)}) collective-permute-start(f32[40,256]{1,0:T(8,128)S(1)} %get-tuple-element.80), channel_id=1, source_target_pairs={{0,4},{1,5},{2,6},{3,7},{4,0},{5,1},{6,2},{7,3},{8,12},{9,13},{10,... | collective-permute-start | bytes 122888 | tf_op jit(solution)/shard_map/ppermute | solution.py:463
  81.6 5.8 %collective-permute-start.17 = (f32[40,256]{1,0:T(8,128)S(1)}, f32[40,256]{1,0:T(8,128)S(1)}, u32[]{:S(2)}, u32[]{:S(2)}) collective-permute-start(f32[40,256]{1,0:T(8,128)S(1)} %get-tuple-element.81), channel_id=1, source_target_pairs={{0,6},{1,7},{2,4},{3,5},{4,2},{5,3},{6,0},{7,1},{8,14},{9,15},{10,... | collective-permute-start | bytes 122888 | tf_op jit(solution)/shard_map/ppermute | solution.py:463
  87.6 9.4 %collective-permute-start.24 = (bf16[256,512]{1,0:T(8,128)(2,1)S(1)}, bf16[256,512]{1,0:T(8,128)(2,1)S(1)}, u32[]{:S(2)}, u32[]{:S(2)}) collective-permute-start(bf16[256,512]{1,0:T(8,128)(2,1)S(1)} %get-tuple-element.88), channel_id=1, source_target_pairs={{0,16},{8,24},{16,0},{24,8},{1,17},{9,25},{17,1},{25,9},{2,18},{10... | collective-permute-start | bytes 786440 | tf_op jit(solution)/shard_map/ppermute | solution.py:463
  89.2 7.9 %collective-permute-start.25 = (bf16[256,512]{1,0:T(8,128)(2,1)S(1)}, bf16[256,512]{1,0:T(8,128)(2,1)S(1)}, u32[]{:S(2)}, u32[]{:S(2)}) collective-permute-start(bf16[256,512]{1,0:T(8,128)(2,1)S(1)} %get-tuple-element.89), channel_id=1, source_target_pairs={{0,8},{8,0},{16,24},{24,16},{1,9},{9,1},{17,25},{25,17},{2,10},{10... | collective-permute-start | bytes 786440 | tf_op jit(solution)/shard_map/ppermute | solution.py:463
  90.6 6.0 %collective-permute-start.20 = (f32[32,256]{1,0:T(8,128)S(1)}, f32[32,256]{1,0:T(8,128)S(1)}, u32[]{:S(2)}, u32[]{:S(2)}) collective-permute-start(f32[32,256]{1,0:T(8,128)S(1)} %get-tuple-element.82.refs_0_.ahead_ref), channel_id=1, source_target_pairs={{0,24},{8,16},{16,8},{24,0},{1,25},{9,17},{17,9},{25,1},{2,26},{10... | collective-permute-start | bytes 98312 | tf_op jit(solution)/shard_map/ppermute | solution.py:463
  91.2 5.4 %collective-permute-start.19 = (f32[32,256]{1,0:T(8,128)S(1)}, f32[32,256]{1,0:T(8,128)S(1)}, u32[]{:S(2)}, u32[]{:S(2)}) collective-permute-start(f32[32,256]{1,0:T(8,128)S(1)} %get-tuple-element.82.refs_0_.ahead_ref), channel_id=1, source_target_pairs={{0,16},{8,24},{16,0},{24,8},{1,17},{9,25},{17,1},{25,9},{2,18},{10... | collective-permute-start | bytes 98312 | tf_op jit(solution)/shard_map/ppermute | solution.py:463
  92.7 4.3 %collective-permute-start.18 = (f32[32,256]{1,0:T(8,128)S(1)}, f32[32,256]{1,0:T(8,128)S(1)}, u32[]{:S(2)}, u32[]{:S(2)}) collective-permute-start(f32[32,256]{1,0:T(8,128)S(1)} %get-tuple-element.82.refs_0_.ahead_ref), channel_id=1, source_target_pairs={{0,8},{8,0},{16,24},{24,16},{1,9},{9,1},{17,25},{25,17},{2,10},{10... | collective-permute-start | bytes 98312 | tf_op jit(solution)/shard_map/ppermute | solution.py:463
  (10 other events, 103.6 us)

commit v18 on v17

--- a/solution.py
+++ b/solution.py
@@ -526,9 +526,9 @@
             "pair_turn",
             (me,),
         )
+        more_up, more_down = pass_on(got, notes[0])
         notes = [swap(note, "expert", 2 * k) for k, note in enumerate(notes)]
         total, loss = turn(z_turn_kernel, notes, (quarter // 2, experts), "z_turn")
-        more_up, more_down = pass_on(got, total)
         row_loss, found = loss_by_row(place, loss)
         parts = [swap(total, "dp", j) for j in range(replicas)]
         (parts,) = turn(stack_kernel, parts + [found], (width // 2,), "stack_parts")

time: 100 us -> 109 us (1.090)
  waiting for transfers between devices: 35.2 us -> 45 us
  starting transfers between devices: 29.6 us -> 28.4 us
    ppermute x26, waiting for transfers between devices: 35.2 us -> 45 us  [swap(): lax.ppermute(value, axis, [(i, i ^ s) for i in range(lax.axis_size(axis))])]
    ppermute x26, starting transfers between devices: 29.6 us -> 28.4 us  [swap(): lax.ppermute(value, axis, [(i, i ^ s) for i in range(lax.axis_size(axis))])]
  transfers between devices with their start and end apart: 26 -> 26, of which waited for: 12 -> 13; matrix products, arithmetic and copies ran while one was open for 0% -> 0% of each run, Pallas kernels for 25% -> 23%
where the time goes in v18:
time: 109 us
  waiting for transfers between devices  45 us (41%)
  Pallas kernels  29.5 us (27%)
  starting transfers between devices  28.4 us (26%)
  local copies, waits for them, and re-layouts  3.7 us (3%)
  other arithmetic  1.29 us (1%)
    ppermute x26, waiting for transfers between devices, swap(): lax.ppermute(value, axis, [(i, i ^ s) for i in range(lax.axis_size(axis))])  45 us
    ppermute x26, starting transfers between devices, swap(): lax.ppermute(value, axis, [(i, i ^ s) for i in range(lax.axis_size(axis))])  28.4 us
    pallas_call x5, Pallas kernels, expert_call(): pl.pallas_call(functools.partial(expert_kernel, counts, order, first, len...  21.4 us
    unnamed x16, local copies, waits for them, and re-layouts  3.66 us
    pallas_call x1, Pallas kernels, pack(): pl.pallas_call(functools.partial(pack_kernel, experts, capacity), out_sha...  3.5 us
  transfers between devices with their start and end apart: 26, of which 13 were waited for; matrix products, arithmetic and copies ran while one was open for 0% of the time, Pallas kernels for 23%

profile of v18, /device:TPU:0, one launch (start us, length us, event | category | flops | bytes accessed | tf_op | source)
XLA Modules:
  0.0 108.8 jit_solution(15187745564990638266)
XLA Ops:
  2.0 3.0 %collective-permute-start.3 = (bf16[256,512]{1,0:T(8,128)(2,1)S(1)}, bf16[256,512]{1,0:T(8,128)(2,1)S(1)}, u32[]{:S(2)}, u32[]{:S(2)}) collective-permute-start(bf16[256,512]{1,0:T(8,128)(2,1)S(1)} %get-tuple-element.95.one_ref), channel_id=1, source_target_pairs={{0,16},{8,24},{16,0},{24,8},{1,17},{9,25},{17,1},{25,9},{2,18},{10... | collective-permute-start | bytes 786440 | tf_op jit(solution)/shard_map/ppermute | solution.py:463
  5.0 1.5 %collective-permute-start.1 = (bf16[256,512]{1,0:T(8,128)(2,1)S(1)}, bf16[256,512]{1,0:T(8,128)(2,1)S(1)}, u32[]{:S(2)}, u32[]{:S(2)}) collective-permute-start(bf16[256,512]{1,0:T(8,128)(2,1)S(1)} %get-tuple-element.96.one_ref), channel_id=1, source_target_pairs={{0,8},{8,0},{16,24},{24,16},{1,9},{9,1},{17,25},{25,17},{2,10},{10... | collective-permute-start | bytes 786440 | tf_op jit(solution)/shard_map/ppermute | solution.py:463
  10.1 3.5 %pack_rows.1 = (bf16[256,512]{1,0:T(8,128)(2,1)S(1)}, bf16[256,512]{1,0:T(8,128)(2,1)S(1)}, bf16[256,512]{1,0:T(8,128)(2,1)S(1)}, bf16[256,512]{1,0:T(8,128)(2,1...) custom-call(s32[1]{0:T(128)} %bitcast.me_ref, ...), custom_call_target="tpu_custom_call" | custom-call | flops 3221225472 | bytes 6291456 | tf_op jit(solution)/shard_map/pack_rows/pallas_call | solution.py:85
  15.0 2.6 %collective-permute-start.10 = (bf16[256,512]{1,0:T(8,128)(2,1)S(1)}, bf16[256,512]{1,0:T(8,128)(2,1)S(1)}, u32[]{:S(2)}, u32[]{:S(2)}) collective-permute-start(bf16[256,512]{1,0:T(8,128)(2,1)S(1)} %get-tuple-element.58), channel_id=1, source_target_pairs={{0,4},{1,5},{2,6},{3,7},{4,0},{5,1},{6,2},{7,3},{8,12},{9,13},{10,... | collective-permute-start | bytes 786440 | tf_op jit(solution)/shard_map/ppermute | solution.py:463
  17.7 1.6 %collective-permute-start.7 = (bf16[256,512]{1,0:T(8,128)(2,1)S(1)}, bf16[256,512]{1,0:T(8,128)(2,1)S(1)}, u32[]{:S(2)}, u32[]{:S(2)}) collective-permute-start(bf16[256,512]{1,0:T(8,128)(2,1)S(1)} %get-tuple-element.54), channel_id=1, source_target_pairs={{0,2},{1,3},{2,0},{3,1},{4,6},{5,7},{6,4},{7,5},{8,10},{9,11},{10,... | collective-permute-start | bytes 786440 | tf_op jit(solution)/shard_map/ppermute | solution.py:463
  19.3 16.9 %collective-permute-done.10.refs_1_ = bf16[256,512]{1,0:T(8,128)(2,1)S(1)} collective-permute-done((bf16[256,512]{1,0:T(8,128)(2,1)S(1)}, bf16[256,512]{1,0:T(8,128)(2,1)S(1)}, u32[]{:S(2)}, u32[]{:S(2)}) %collective-permute-start.10) | collective-permute-done | bytes 262176 | tf_op jit(solution)/shard_map/ppermute | solution.py:463
  36.2 3.1 %collective-permute-start.5 = (bf16[256,512]{1,0:T(8,128)(2,1)S(1)}, bf16[256,512]{1,0:T(8,128)(2,1)S(1)}, u32[]{:S(2)}, u32[]{:S(2)}) collective-permute-start(bf16[256,512]{1,0:T(8,128)(2,1)S(1)} %get-tuple-element.52), channel_id=1, source_target_pairs={{0,6},{1,7},{2,4},{3,5},{4,2},{5,3},{6,0},{7,1},{8,14},{9,15},{10,... | collective-permute-start | bytes 786440 | tf_op jit(solution)/shard_map/ppermute | solution.py:463
  39.5 4.9 %expert_rows.5 = (f32[4,2,256,512]{3,2,1,0:T(8,128)S(1)}, f32[256,256]{1,0:T(8,128)S(1)}, f32[2,256]{1,0:T(2,128)S(1)}) custom-call(bf16[256,512]{1,0:T(8,128)(2,1)S(1)} %get-tuple-element.57.refs_0_, bf16[256,512]{1,0:T(8,128)(2,1)S(1)} %collective-permute-done.10.refs_1_, bf16[256,256]{1,0:T(8,128)(2,1)S(1)} %copy-done.1, ...), custom_call_target="tpu_custom_call" | custom-call | flops 1572864 | bytes 131072 | tf_op jit(solution)/shard_map/expert_rows/pallas_call | solution.py:289
  44.3 1.9 %collective-permute-done.9.refs_1_ = bf16[256,512]{1,0:T(8,128)(2,1)S(1)} collective-permute-done((bf16[256,512]{1,0:T(8,128)(2,1)S(1)}, bf16[256,512]{1,0:T(8,128)(2,1)S(1)}, u32[]{:S(2)}, u32[]{:S(2)}) %collective-permute-start.9) | collective-permute-done | bytes 262176 | tf_op jit(solution)/shard_map/ppermute | solution.py:463
  46.3 5.1 %expert_rows.6 = (f32[4,2,256,512]{3,2,1,0:T(8,128)S(1)}, f32[256,256]{1,0:T(8,128)S(1)}, f32[2,256]{1,0:T(2,128)S(1)}) custom-call(bf16[256,512]{1,0:T(8,128)(2,1)S(1)} %collective-permute-done.8.refs_0_, bf16[256,512]{1,0:T(8,128)(2,1)S(1)} %collective-permute-done.9.refs_1_, bf16[256,256]{1,0:T(8,128)(2,1)S(1)} %copy-done.1, ...), custom_call_target="tpu_custom_call" | custom-call | flops 1572864 | bytes 131072 | tf_op jit(solution)/shard_map/expert_rows/pallas_call | solution.py:289
  51.4 3.2 %expert_rows.7 = (f32[4,2,256,512]{3,2,1,0:T(8,128)S(1)}, f32[256,256]{1,0:T(8,128)S(1)}, f32[1,256]{1,0:T(1,128)S(1)}) custom-call(bf16[256,512]{1,0:T(8,128)(2,1)S(1)} %collective-permute-done.7.refs_0_, bf16[256,256]{1,0:T(8,128)(2,1)S(1)} %copy-done.1, bf16[2,256,512]{2,1,0:T(8,128)(2,1)S(1)} %pair.2.refs_3_.refs_2_, ...), custom_call_target="tpu_custom_call" | custom-call | flops 786432 | bytes 65536 | tf_op jit(solution)/shard_map/expert_rows/pallas_call | solution.py:289
  54.6 3.7 %collective-permute-done.6.refs_1_ = bf16[256,512]{1,0:T(8,128)(2,1)S(1)} collective-permute-done((bf16[256,512]{1,0:T(8,128)(2,1)S(1)}, bf16[256,512]{1,0:T(8,128)(2,1)S(1)}, u32[]{:S(2)}, u32[]{:S(2)}) %collective-permute-start.6) | collective-permute-done | bytes 262176 | tf_op jit(solution)/shard_map/ppermute | solution.py:463
  58.3 4.9 %expert_rows.8 = (f32[4,2,256,512]{3,2,1,0:T(8,128)S(1)}, f32[256,256]{1,0:T(8,128)S(1)}, f32[2,256]{1,0:T(2,128)S(1)}) custom-call(bf16[256,512]{1,0:T(8,128)(2,1)S(1)} %collective-permute-done.5.refs_0_, bf16[256,512]{1,0:T(8,128)(2,1)S(1)} %collective-permute-done.6.refs_1_, bf16[256,256]{1,0:T(8,128)(2,1)S(1)} %copy-done.1, ...), custom_call_target="tpu_custom_call" | custom-call | flops 1572864 | bytes 131072 | tf_op jit(solution)/shard_map/expert_rows/pallas_call | solution.py:289
  63.2 3.2 %expert_rows.9 = (f32[4,2,256,512]{3,2,1,0:T(8,128)S(1)}, f32[64,256]{1,0:T(8,128)S(1)}, f32[64,256]{1,0:T(8,128)S(1)}, f32[64,256]{1,0:T(8,128)S(1)}, f32[64,256]{1,0:T(8,128)S(1)}, /*index=5*/f32[8,256]{1,0:T(8,128)S(1)}) custom-call(bf16[256,512]{1,0:T(8,128)(2,1)S(1)} %collective-permute-done.refs_0_, bf16[256,256]{1,0:T(8,128)(2,1)S(1)} %copy-done.1, ...), custom_call_target="tpu_custom_call" | custom-call | flops 786432 | bytes 65536 | tf_op jit(solution)/shard_map/expert_rows/pallas_call | solution.py:289
  66.5 1.5 %collective-permute-start.11 = (f32[64,256]{1,0:T(8,128)S(1)}, f32[64,256]{1,0:T(8,128)S(1)}, u32[]{:S(2)}, u32[]{:S(2)}) collective-permute-start(f32[64,256]{1,0:T(8,128)S(1)} %get-tuple-element.72), channel_id=1, source_target_pairs={{0,8},{8,0},{16,24},{24,16},{1,9},{9,1},{17,25},{25,17},{2,10},{10... | collective-permute-start | bytes 196616 | tf_op jit(solution)/shard_map/ppermute | solution.py:463
  68.0 1.5 %collective-permute-start.12 = (f32[64,256]{1,0:T(8,128)S(1)}, f32[64,256]{1,0:T(8,128)S(1)}, u32[]{:S(2)}, u32[]{:S(2)}) collective-permute-start(f32[64,256]{1,0:T(8,128)S(1)} %get-tuple-element.73), channel_id=1, source_target_pairs={{0,16},{8,24},{16,0},{24,8},{1,17},{9,25},{17,1},{25,9},{2,18},{10... | collective-permute-start | bytes 196616 | tf_op jit(solution)/shard_map/ppermute | solution.py:463
  70.8 1.4 %collective-permute-done.12.q2 = f32[64,256]{1,0:T(8,128)S(1)} collective-permute-done((f32[64,256]{1,0:T(8,128)S(1)}, f32[64,256]{1,0:T(8,128)S(1)}, u32[]{:S(2)}, u32[]{:S(2)}) %collective-permute-start.12) | collective-permute-done | bytes 65568 | tf_op jit(solution)/shard_map/ppermute | solution.py:463
  72.2 2.4 %collective-permute-done.13.q3 = f32[64,256]{1,0:T(8,128)S(1)} collective-permute-done((f32[64,256]{1,0:T(8,128)S(1)}, f32[64,256]{1,0:T(8,128)S(1)}, u32[]{:S(2)}, u32[]{:S(2)}) %collective-permute-start.13) | collective-permute-done | bytes 65568 | tf_op jit(solution)/shard_map/ppermute | solution.py:463
  77.3 9.8 %collective-permute-done.22.got_up_ref.refs_4_ = bf16[2,256,512]{2,1,0:T(8,128)(2,1)S(1)} collective-permute-done((bf16[2,256,512]{2,1,0:T(8,128)(2,1)S(1)}, bf16[2,256,512]{2,1,0:T(8,128)(2,1)S(1)}, u32[]{:S(2)}, u32[]{:S(2)}) %collective-permute-start.22) | collective-permute-done | bytes 524320 | tf_op jit(solution)/shard_map/ppermute | solution.py:463
  91.2 2.7 %collective-permute-start.16 = (f32[40,256]{1,0:T(8,128)S(1)}, f32[40,256]{1,0:T(8,128)S(1)}, u32[]{:S(2)}, u32[]{:S(2)}) collective-permute-start(f32[40,256]{1,0:T(8,128)S(1)} %get-tuple-element.80), channel_id=1, source_target_pairs={{0,4},{1,5},{2,6},{3,7},{4,0},{5,1},{6,2},{7,3},{8,12},{9,13},{10,... | collective-permute-start | bytes 122888 | tf_op jit(solution)/shard_map/ppermute | solution.py:463
  94.6 1.5 %collective-permute-done.16.refs_2_ = f32[40,256]{1,0:T(8,128)S(1)} collective-permute-done((f32[40,256]{1,0:T(8,128)S(1)}, f32[40,256]{1,0:T(8,128)S(1)}, u32[]{:S(2)}, u32[]{:S(2)}) %collective-permute-start.16) | collective-permute-done | bytes 40992 | tf_op jit(solution)/shard_map/ppermute | solution.py:463
  96.1 3.6 %collective-permute-done.17.refs_3_ = f32[40,256]{1,0:T(8,128)S(1)} collective-permute-done((f32[40,256]{1,0:T(8,128)S(1)}, f32[40,256]{1,0:T(8,128)S(1)}, u32[]{:S(2)}, u32[]{:S(2)}) %collective-permute-start.17) | collective-permute-done | bytes 40992 | tf_op jit(solution)/shard_map/ppermute | solution.py:463
  99.7 1.6 %collective-permute-start.20 = (f32[32,256]{1,0:T(8,128)S(1)}, f32[32,256]{1,0:T(8,128)S(1)}, u32[]{:S(2)}, u32[]{:S(2)}) collective-permute-start(f32[32,256]{1,0:T(8,128)S(1)} %get-tuple-element.82.refs_0_), channel_id=1, source_target_pairs={{0,24},{8,16},{16,8},{24,0},{1,25},{9,17},{17,9},{25,1},{2,26},{10... | collective-permute-start | bytes 98312 | tf_op jit(solution)/shard_map/ppermute | solution.py:463
  105.9 2.1 %adam.1 = (f32[1,2,256,512]{3,2,1,0:T(8,128)}, f32[1,2,256,512]{3,2,1,0:T(8,128)}, f32[1,2,256,512]{3,2,1,0:T(8,128)}, f32[8,128]{1,0:T(8,128)S(1)}) custom-call(f32[1,2,256,512]{3,2,1,0:T(8,128)S(1)} %copy-done, f32[1,2,256,512]{3,2,1,0:T(8,128)S(1)} %copy-done.2, f32[1,2,256,512]{3,2,1,0:T(8,128)S(1)} %copy-done.3, ...), custom_call_target="tpu_custom_call" | custom-call | flops 5242880 | bytes 2097152 | tf_op jit(solution)/shard_map/adam/pallas_call | solution.py:447
  (63 shorter events, 20.5 us)
Async XLA Ops:
  2.0 12.3 %collective-permute-start.3 = (bf16[256,512]{1,0:T(8,128)(2,1)S(1)}, bf16[256,512]{1,0:T(8,128)(2,1)S(1)}, u32[]{:S(2)}, u32[]{:S(2)}) collective-permute-start(bf16[256,512]{1,0:T(8,128)(2,1)S(1)} %get-tuple-element.95.one_ref), channel_id=1, source_target_pairs={{0,16},{8,24},{16,0},{24,8},{1,17},{9,25},{17,1},{25,9},{2,18},{10... | collective-permute-start | bytes 786440 | tf_op jit(solution)/shard_map/ppermute | solution.py:463
  5.0 8.6 %collective-permute-start.1 = (bf16[256,512]{1,0:T(8,128)(2,1)S(1)}, bf16[256,512]{1,0:T(8,128)(2,1)S(1)}, u32[]{:S(2)}, u32[]{:S(2)}) collective-permute-start(bf16[256,512]{1,0:T(8,128)(2,1)S(1)} %get-tuple-element.96.one_ref), channel_id=1, source_target_pairs={{0,8},{8,0},{16,24},{24,16},{1,9},{9,1},{17,25},{25,17},{2,10},{10... | collective-permute-start | bytes 786440 | tf_op jit(solution)/shard_map/ppermute | solution.py:463
  13.7 25.7 %collective-permute-start.2 = (bf16[2,256,512]{2,1,0:T(8,128)(2,1)S(1)}, bf16[2,256,512]{2,1,0:T(8,128)(2,1)S(1)}, u32[]{:S(2)}, u32[]{:S(2)}) collective-permute-start(bf16[2,256,512]{2,1,0:T(8,128)(2,1)S(1)} %pair.2.refs_3_.refs_2_), channel_id=1, source_target_pairs={{0,16},{8,24},{16,0},{24,8},{1,17},{9,25},{17,1},{25,9},{2,18},{10... | collective-permute-start | bytes 1572872 | tf_op jit(solution)/shard_map/ppermute | solution.py:463
  14.3 25.1 %collective-permute-start.4 = (bf16[2,256,512]{2,1,0:T(8,128)(2,1)S(1)}, bf16[2,256,512]{2,1,0:T(8,128)(2,1)S(1)}, u32[]{:S(2)}, u32[]{:S(2)}) collective-permute-start(bf16[2,256,512]{2,1,0:T(8,128)(2,1)S(1)} %pair.3.refs_5_.refs_4_), channel_id=1, source_target_pairs={{0,8},{8,0},{16,24},{24,16},{1,9},{9,1},{17,25},{25,17},{2,10},{10... | collective-permute-start | bytes 1572872 | tf_op jit(solution)/shard_map/ppermute | solution.py:463
  15.0 2.8 %collective-permute-start.8 = (bf16[256,512]{1,0:T(8,128)(2,1)S(1)}, bf16[256,512]{1,0:T(8,128)(2,1)S(1)}, u32[]{:S(2)}, u32[]{:S(2)}) collective-permute-start(bf16[256,512]{1,0:T(8,128)(2,1)S(1)} %get-tuple-element.55), channel_id=1, source_target_pairs={{0,1},{1,0},{2,3},{3,2},{4,5},{5,4},{6,7},{7,6},{8,9},{9,8},{10,11... | collective-permute-start | bytes 786440 | tf_op jit(solution)/shard_map/ppermute | solution.py:463
  15.0 21.2 %collective-permute-start.10 = (bf16[256,512]{1,0:T(8,128)(2,1)S(1)}, bf16[256,512]{1,0:T(8,128)(2,1)S(1)}, u32[]{:S(2)}, u32[]{:S(2)}) collective-permute-start(bf16[256,512]{1,0:T(8,128)(2,1)S(1)} %get-tuple-element.58), channel_id=1, source_target_pairs={{0,4},{1,5},{2,6},{3,7},{4,0},{5,1},{6,2},{7,3},{8,12},{9,13},{10,... | collective-permute-start | bytes 786440 | tf_op jit(solution)/shard_map/ppermute | solution.py:463
  17.6 28.7 %collective-permute-start.9 = (bf16[256,512]{1,0:T(8,128)(2,1)S(1)}, bf16[256,512]{1,0:T(8,128)(2,1)S(1)}, u32[]{:S(2)}, u32[]{:S(2)}) collective-permute-start(bf16[256,512]{1,0:T(8,128)(2,1)S(1)} %get-tuple-element.56), channel_id=1, source_target_pairs={{0,5},{1,4},{2,7},{3,6},{4,1},{5,0},{6,3},{7,2},{8,13},{9,12},{10,... | collective-permute-start | bytes 786440 | tf_op jit(solution)/shard_map/ppermute | solution.py:463
  17.7 33.6 %collective-permute-start.7 = (bf16[256,512]{1,0:T(8,128)(2,1)S(1)}, bf16[256,512]{1,0:T(8,128)(2,1)S(1)}, u32[]{:S(2)}, u32[]{:S(2)}) collective-permute-start(bf16[256,512]{1,0:T(8,128)(2,1)S(1)} %get-tuple-element.54), channel_id=1, source_target_pairs={{0,2},{1,3},{2,0},{3,1},{4,6},{5,7},{6,4},{7,5},{8,10},{9,11},{10,... | collective-permute-start | bytes 786440 | tf_op jit(solution)/shard_map/ppermute | solution.py:463
  36.2 18.4 %collective-permute-start.5 = (bf16[256,512]{1,0:T(8,128)(2,1)S(1)}, bf16[256,512]{1,0:T(8,128)(2,1)S(1)}, u32[]{:S(2)}, u32[]{:S(2)}) collective-permute-start(bf16[256,512]{1,0:T(8,128)(2,1)S(1)} %get-tuple-element.52), channel_id=1, source_target_pairs={{0,6},{1,7},{2,4},{3,5},{4,2},{5,3},{6,0},{7,1},{8,14},{9,15},{10,... | collective-permute-start | bytes 786440 | tf_op jit(solution)/shard_map/ppermute | solution.py:463
  39.4 18.9 %collective-permute-start.6 = (bf16[256,512]{1,0:T(8,128)(2,1)S(1)}, bf16[256,512]{1,0:T(8,128)(2,1)S(1)}, u32[]{:S(2)}, u32[]{:S(2)}) collective-permute-start(bf16[256,512]{1,0:T(8,128)(2,1)S(1)} %get-tuple-element.53), channel_id=1, source_target_pairs={{0,3},{1,2},{2,1},{3,0},{4,7},{5,6},{6,5},{7,4},{8,11},{9,10},{10,... | collective-permute-start | bytes 786440 | tf_op jit(solution)/shard_map/ppermute | solution.py:463
  39.4 23.9 %collective-permute-start = (bf16[256,512]{1,0:T(8,128)(2,1)S(1)}, bf16[256,512]{1,0:T(8,128)(2,1)S(1)}, u32[]{:S(2)}, u32[]{:S(2)}) collective-permute-start(bf16[256,512]{1,0:T(8,128)(2,1)S(1)} %get-tuple-element.50), channel_id=1, source_target_pairs={{0,7},{1,6},{2,5},{3,4},{4,3},{5,2},{6,1},{7,0},{8,15},{9,14},{10,... | collective-permute-start | bytes 786440 | tf_op jit(solution)/shard_map/ppermute | solution.py:463
  66.5 4.3 %collective-permute-start.11 = (f32[64,256]{1,0:T(8,128)S(1)}, f32[64,256]{1,0:T(8,128)S(1)}, u32[]{:S(2)}, u32[]{:S(2)}) collective-permute-start(f32[64,256]{1,0:T(8,128)S(1)} %get-tuple-element.72), channel_id=1, source_target_pairs={{0,8},{8,0},{16,24},{24,16},{1,9},{9,1},{17,25},{25,17},{2,10},{10... | collective-permute-start | bytes 196616 | tf_op jit(solution)/shard_map/ppermute | solution.py:463
  68.0 4.3 %collective-permute-start.12 = (f32[64,256]{1,0:T(8,128)S(1)}, f32[64,256]{1,0:T(8,128)S(1)}, u32[]{:S(2)}, u32[]{:S(2)}) collective-permute-start(f32[64,256]{1,0:T(8,128)S(1)} %get-tuple-element.73), channel_id=1, source_target_pairs={{0,16},{8,24},{16,0},{24,8},{1,17},{9,25},{17,1},{25,9},{2,18},{10... | collective-permute-start | bytes 196616 | tf_op jit(solution)/shard_map/ppermute | solution.py:463
  69.5 5.2 %collective-permute-start.13 = (f32[64,256]{1,0:T(8,128)S(1)}, f32[64,256]{1,0:T(8,128)S(1)}, u32[]{:S(2)}, u32[]{:S(2)}) collective-permute-start(f32[64,256]{1,0:T(8,128)S(1)} %get-tuple-element.74), channel_id=1, source_target_pairs={{0,24},{8,16},{16,8},{24,0},{1,25},{9,17},{17,9},{25,1},{2,26},{10... | collective-permute-start | bytes 196616 | tf_op jit(solution)/shard_map/ppermute | solution.py:463
  74.8 12.3 %collective-permute-start.22 = (bf16[2,256,512]{2,1,0:T(8,128)(2,1)S(1)}, bf16[2,256,512]{2,1,0:T(8,128)(2,1)S(1)}, u32[]{:S(2)}, u32[]{:S(2)}) collective-permute-start(bf16[2,256,512]{2,1,0:T(8,128)(2,1)S(1)} %get-tuple-element.86), channel_id=1, source_target_pairs={{0,8},{8,0},{16,24},{24,16},{1,9},{9,1},{17,25},{25,17},{2,10},{10... | collective-permute-start | bytes 1572872 | tf_op jit(solution)/shard_map/ppermute | solution.py:463
  75.5 12.0 %collective-permute-start.23 = (bf16[2,256,512]{2,1,0:T(8,128)(2,1)S(1)}, bf16[2,256,512]{2,1,0:T(8,128)(2,1)S(1)}, u32[]{:S(2)}, u32[]{:S(2)}) collective-permute-start(bf16[2,256,512]{2,1,0:T(8,128)(2,1)S(1)} %get-tuple-element.87), channel_id=1, source_target_pairs={{0,16},{8,24},{16,0},{24,8},{1,17},{9,25},{17,1},{25,9},{2,18},{10... | collective-permute-start | bytes 1572872 | tf_op jit(solution)/shard_map/ppermute | solution.py:463
  87.8 18.1 %collective-permute-start.24 = (bf16[256,512]{1,0:T(8,128)(2,1)S(1)}, bf16[256,512]{1,0:T(8,128)(2,1)S(1)}, u32[]{:S(2)}, u32[]{:S(2)}) collective-permute-start(bf16[256,512]{1,0:T(8,128)(2,1)S(1)} %get-tuple-element.88), channel_id=1, source_target_pairs={{0,16},{8,24},{16,0},{24,8},{1,17},{9,25},{17,1},{25,9},{2,18},{10... | collective-permute-start | bytes 786440 | tf_op jit(solution)/shard_map/ppermute | solution.py:463
  88.5 17.4 %collective-permute-start.25 = (bf16[256,512]{1,0:T(8,128)(2,1)S(1)}, bf16[256,512]{1,0:T(8,128)(2,1)S(1)}, u32[]{:S(2)}, u32[]{:S(2)}) collective-permute-start(bf16[256,512]{1,0:T(8,128)(2,1)S(1)} %get-tuple-element.89), channel_id=1, source_target_pairs={{0,8},{8,0},{16,24},{24,16},{1,9},{9,1},{17,25},{25,17},{2,10},{10... | collective-permute-start | bytes 786440 | tf_op jit(solution)/shard_map/ppermute | solution.py:463
  89.8 4.7 %collective-permute-start.15 = (f32[40,256]{1,0:T(8,128)S(1)}, f32[40,256]{1,0:T(8,128)S(1)}, u32[]{:S(2)}, u32[]{:S(2)}) collective-permute-start(f32[40,256]{1,0:T(8,128)S(1)} %get-tuple-element.79), channel_id=1, source_target_pairs={{0,2},{1,3},{2,0},{3,1},{4,6},{5,7},{6,4},{7,5},{8,10},{9,11},{10,... | collective-permute-start | bytes 122888 | tf_op jit(solution)/shard_map/ppermute | solution.py:463
  91.2 4.9 %collective-permute-start.16 = (f32[40,256]{1,0:T(8,128)S(1)}, f32[40,256]{1,0:T(8,128)S(1)}, u32[]{:S(2)}, u32[]{:S(2)}) collective-permute-start(f32[40,256]{1,0:T(8,128)S(1)} %get-tuple-element.80), channel_id=1, source_target_pairs={{0,4},{1,5},{2,6},{3,7},{4,0},{5,1},{6,2},{7,3},{8,12},{9,13},{10,... | collective-permute-start | bytes 122888 | tf_op jit(solution)/shard_map/ppermute | solution.py:463
  93.9 5.8 %collective-permute-start.17 = (f32[40,256]{1,0:T(8,128)S(1)}, f32[40,256]{1,0:T(8,128)S(1)}, u32[]{:S(2)}, u32[]{:S(2)}) collective-permute-start(f32[40,256]{1,0:T(8,128)S(1)} %get-tuple-element.81), channel_id=1, source_target_pairs={{0,6},{1,7},{2,4},{3,5},{4,2},{5,3},{6,0},{7,1},{8,14},{9,15},{10,... | collective-permute-start | bytes 122888 | tf_op jit(solution)/shard_map/ppermute | solution.py:463
  99.7 4.9 %collective-permute-start.20 = (f32[32,256]{1,0:T(8,128)S(1)}, f32[32,256]{1,0:T(8,128)S(1)}, u32[]{:S(2)}, u32[]{:S(2)}) collective-permute-start(f32[32,256]{1,0:T(8,128)S(1)} %get-tuple-element.82.refs_0_), channel_id=1, source_target_pairs={{0,24},{8,16},{16,8},{24,0},{1,25},{9,17},{17,9},{25,1},{2,26},{10... | collective-permute-start | bytes 98312 | tf_op jit(solution)/shard_map/ppermute | solution.py:463
  101.3 3.9 %collective-permute-start.19 = (f32[32,256]{1,0:T(8,128)S(1)}, f32[32,256]{1,0:T(8,128)S(1)}, u32[]{:S(2)}, u32[]{:S(2)}) collective-permute-start(f32[32,256]{1,0:T(8,128)S(1)} %get-tuple-element.82.refs_0_), channel_id=1, source_target_pairs={{0,16},{8,24},{16,0},{24,8},{1,17},{9,25},{17,1},{25,9},{2,18},{10... | collective-permute-start | bytes 98312 | tf_op jit(solution)/shard_map/ppermute | solution.py:463
  101.9 3.9 %collective-permute-start.18 = (f32[32,256]{1,0:T(8,128)S(1)}, f32[32,256]{1,0:T(8,128)S(1)}, u32[]{:S(2)}, u32[]{:S(2)}) collective-permute-start(f32[32,256]{1,0:T(8,128)S(1)} %get-tuple-element.82.refs_0_), channel_id=1, source_target_pairs={{0,8},{8,0},{16,24},{24,16},{1,9},{9,1},{17,25},{25,17},{2,10},{10... | collective-permute-start | bytes 98312 | tf_op jit(solution)/shard_map/ppermute | solution.py:463
  (10 other events, 130.1 us)
